TPU v7x, 32 devices: a whole 2x2x4 slice. The times are simulated.
32 devices in a mesh: row: 4 (over y, core), col: 8 (over z, x).
Axes of the slice: x: 2, y: 2, z: 4, core: 2. Of those that a mesh axis runs over, the one named last changes fastest.
Arguments:
- cond_orbitals: bfloat16 [32, 48, 2304], P(('row', 'col')), may hold values from -6 to 6
- occ_orbitals: bfloat16 [32, 48, 2304], P(('row', 'col')), may hold values from -6 to 6
- cond_energy: float32 [32], replicated, may hold values from 0.02 to 1
- occ_energy: float32 [32], replicated, may hold values from -1 to -0.02
- occ_band: int32 [32], replicated, may hold values from 0 to 31, each once
- sphere_index: int32 [3, 8192], replicated, may hold values from 0 to 47, as said below
Outputs:
- chi_zero: float32 [16384, 16384], P('row', 'col')
Inputs may be any that keep to these rules, and one draw needn't show every extreme that they name: `sphere_index`: columns are 8192 distinct wave vectors (gx, gy, gz) stored modulo 48, with gx and gy from -18 to 18 and gz from 1 to 18. `occ_band`: each occupied band number appears once.
All inputs are finite; a program needn't handle non-finite values.
Results may differ from a plain program's by a relative error of at most 0.013.
Values may be sent and summed in bfloat16 or wider, within the bound.
No kernel may reach another device: no remote copies, remote signals or barrier semaphores. Data moves between devices by JAX's collectives and lax.ppermute only.
A program may use at most 128 MiB of HBM per device.

v0:
```python
import math

import jax
import jax.numpy as jnp
from jax import lax
from jax.sharding import PartitionSpec as P

GMAX = 18
STEPS = 2


omega_squared = 0.0625
triple = lax.Precision.HIGH


def from_behind(value, axis, by):
    devices = lax.axis_size(axis)
    return lax.ppermute(value, axis, [(i, (i + by) % devices) for i in range(devices)])


def dft_tables(freq_count, freq_first, grid_size):
    frequency = lax.iota(jnp.int32, freq_count) + freq_first
    places = lax.iota(jnp.int32, grid_size)
    phase_int = frequency[:, None] * places[None, :] % grid_size
    angle_rad = phase_int.astype(jnp.float32) * (2.0 * math.pi / grid_size)
    return (jnp.cos(angle_rad), jnp.sin(angle_rad))


def split_table(table):
    upper = table.astype(jnp.bfloat16)
    lower = (table - upper.astype(jnp.float32)).astype(jnp.bfloat16)
    return (upper, lower)


def first_section(table, density):
    upper, lower = split_table(table)
    return jnp.einsum(
        "kx,lxm->lkm", upper, density, preferred_element_type=jnp.float32
    ) + jnp.einsum("kx,lxm->lkm", lower, density, preferred_element_type=jnp.float32)


def rotation(cos_part, sin_part):
    return jnp.stack([jnp.stack([cos_part, sin_part]), jnp.stack([-sin_part, cos_part])])


def cube_positions(sphere_index, grid_size):
    signed = jnp.where(sphere_index >= grid_size // 2, sphere_index - grid_size, sphere_index)
    span_count = 2 * GMAX + 1
    return ((signed[0] + GMAX) * span_count + signed[1] + GMAX) * GMAX + signed[2] - 1


def transform(density, cube_index):
    batch_size = density.shape[0]
    grid_size = density.shape[1]
    span_count = 2 * GMAX + 1
    cos_side, sin_side = dft_tables(span_count, -GMAX, grid_size)
    cos_last, sin_last = dft_tables(GMAX, 1, grid_size)
    stacked_table = jnp.concatenate([cos_side, -sin_side], axis=0)
    section_one = first_section(stacked_table, density)
    section_one = section_one.reshape(batch_size, 2, span_count, grid_size, grid_size)
    section_two = jnp.einsum(
        "abjy,lbkyz->lakjz", rotation(cos_side, sin_side), section_one, precision=triple
    )
    section_three = jnp.einsum(
        "caqz,lakjz->lckjq", rotation(cos_last, sin_last), section_two, precision=triple
    )
    flat_parts = section_three.reshape(batch_size, 2, -1)
    coef_parts = jnp.take(flat_parts, cube_index, axis=2).reshape(batch_size, -1)
    return (coef_parts * grid_size ** (-1.5)).astype(jnp.bfloat16)


def lookup(energy_table, indices):
    match_mask = indices[:, None] == lax.iota(jnp.int32, energy_table.shape[0])[None, :]
    return jnp.sum(jnp.where(match_mask, energy_table[None, :], jnp.float32(0.0)), axis=1)


def on_device(cond_orbitals, occ_orbitals, cond_energy, occ_energy, occ_band, sphere_index):
    row_count = lax.axis_size("row")
    col_count = lax.axis_size("col")
    device_count = row_count * col_count
    position = lax.axis_index("row") * col_count + lax.axis_index("col")
    occ_count = occ_orbitals.shape[0]
    grid_size = cond_orbitals.shape[1]
    pair_total = device_count * STEPS * occ_count
    cube_index = cube_positions(sphere_index, grid_size)
    occ_now = occ_orbitals
    coef_list = []
    gap_list = []
    for turn_number in range(STEPS):
        if turn_number > 0:
            occ_now = from_behind(occ_now, "row", 1)
        occ_block = (position - turn_number * col_count) % device_count
        density = (cond_orbitals.astype(jnp.float32) * occ_now.astype(jnp.float32)).astype(
            jnp.bfloat16
        )
        coef_list.append(transform(density, cube_index))
        band_ids = lax.dynamic_slice_in_dim(occ_band, occ_block * occ_count, occ_count)
        cond_level = lax.dynamic_slice_in_dim(cond_energy, position, 1)
        gap_list.append(cond_level - lookup(occ_energy, band_ids))
    coefficients = jnp.concatenate(coef_list, axis=0)
    energy_gap = jnp.concatenate(gap_list, axis=0)
    weight = -4.0 * energy_gap / (energy_gap * energy_gap + omega_squared) / pair_total
    scaled = (weight[:, None] * coefficients.astype(jnp.float32)).astype(jnp.bfloat16)
    row_blocks = lax.all_to_all(coefficients[None], "row", split_axis=2, concat_axis=0, tiled=True)
    col_blocks = lax.all_to_all(scaled, "col", split_axis=1, concat_axis=0, tiled=True)
    row_panel = lax.all_gather(row_blocks, "col", axis=1, tiled=True)
    col_panel = lax.all_gather(col_blocks[None], "row", axis=0, tiled=True)
    chi_tile = jnp.einsum("kpg,kph->gh", row_panel, col_panel, preferred_element_type=jnp.float32)
    return chi_tile


def solution(mesh):
    placed = (P(("row", "col"), None, None), P(("row", "col"), None, None), P(), P(), P(), P())
    return jax.shard_map(
        on_device, mesh=mesh, in_specs=placed, out_specs=P("row", "col"), check_vma=False
    )
```

profile of v0, /device:TPU:1, one launch (start us, length us, event | category | flops | bytes accessed | tf_op | source)
XLA Modules:
  0.0 313.2 jit_solution(17164633032863843207)
XLA Ops:
  0.0 2.6 collective-permute-start
  2.6 0.2 fusion.47
  2.8 0.2 fusion.43
  3.0 1.2 dynamic_slice.10
  4.3 1.4 fusion.70
  5.6 2.5 fusion.61
  10.7 0.1 fusion.54
  10.8 0.9 compare_select_fusion
  11.7 0.1 fusion.33
  11.9 0.0 copy-start.2
  11.9 1.3 fusion.23
  13.2 0.0 copy-done.1
  13.2 0.0 copy-done
  13.2 0.2 fusion
  13.4 1.1 reshape.426
  14.6 0.0 copy-done.2
  14.6 0.0 copy-start.5
  14.6 0.0 copy-start.7
  14.6 0.8 fusion.4
  15.5 1.5 fusion.10
  16.9 0.0 copy-done.5
  16.9 0.0 copy-done.7
  16.9 0.6 copy.50
  17.6 0.8 reshape.428
  18.4 7.0 %copy.51 = f32[1,2,24642]{1,2,0:T(8,128)} copy(f32[1,2,24642]{2,1,0:T(2,128)S(1)} %reshape.428) | data formatting | bytes 394272 | tf_op jit(solution)/shard_map/reshape | solution.py:67
  25.4 32.3 %gather_fusion = f32[8192,2]{1,0:T(8,128)} fusion(f32[2,24642]{0,1:T(8,128)} %bitcast.126, s32[8192]{0:T(1024)S(1)} %fusion.36), kind=kCustom, calls=%fused_computation.clone | custom fusion | bytes 163840 | tf_op jit(solution)/shard_map/jit(_take)/gather | solution.py:68
  57.7 3.5 %copy.52 = f32[8192,2]{0,1:T(2,128)} copy(f32[8192,2]{1,0:T(8,128)} %gather_fusion) | data formatting | bytes 131072 | tf_op jit(solution)/shard_map/jit(_take)/gather | solution.py:68
  61.2 0.1 fusion.63
  61.2 0.0 copy-done.3
  61.3 0.0 collective-permute-done
  61.3 1.2 fusion.25
  62.5 1.2 fusion.1
  63.6 1.1 reshape.430
  64.8 0.0 copy-start.6
  64.8 0.0 copy-start.8
  64.8 0.8 fusion.2
  65.6 0.0 copy-done.6
  65.6 1.5 fusion.13
  67.1 0.6 copy.54
  67.7 0.8 reshape.432
  68.5 6.8 %copy.55 = f32[1,2,24642]{1,2,0:T(8,128)} copy(f32[1,2,24642]{2,1,0:T(2,128)S(1)} %reshape.432) | data formatting | bytes 394272 | tf_op jit(solution)/shard_map/reshape | solution.py:67
  75.4 32.3 %gather_fusion.1 = f32[8192,2]{1,0:T(8,128)} fusion(f32[2,24642]{0,1:T(8,128)} %bitcast.125, s32[8192]{0:T(1024)S(1)} %fusion.36), kind=kCustom, calls=%fused_computation.1.clone | custom fusion | bytes 163840 | tf_op jit(solution)/shard_map/jit(_take)/gather | solution.py:68
  107.7 2.9 copy.56
  110.5 0.0 copy-done.4
  110.6 0.1 fusion.31
  110.7 0.1 copy.75
  110.8 0.1 copy.74
  110.8 0.2 maximum_bitcast_fusion.3
  111.0 12.8 %copy.57 = bf16[1,2,16384]{1,0,2:T(2,128)(2,1)} copy(bf16[1,2,16384]{2,1,0:T(2,128)(2,1)S(1)} %maximum_bitcast_fusion.3) | data formatting | bytes 131072 | tf_op jit(solution)/shard_map/broadcast_in_dim | solution.py:104
  123.7 0.6 broadcast.437
  124.3 91.0 %reduce.4 = bf16[16384,2]{1,0:T(8,128)(2,1)} reduce(bf16[16384,1,2]{2,1,0:T(2,128)(2,1)} %bitcast.123, bf16[]{:T(256)} %broadcast.437), dimensions={1}, to_apply=%bitcast.114.reduce_sub_computation | reduce | bytes 131074
  215.3 7.8 %reshape.480 = bf16[4,2,4096]{2,1,0:T(2,128)(2,1)} reshape(bf16[16384,2]{1,0:T(8,128)(2,1)} %reduce.4) | data formatting | bytes 131072
  223.1 3.3 %all-to-all-start = ((bf16[4,2,4096]{2,1,0:T(2,128)(2,1)}), bf16[4,2,4096]{2,1,0:T(2,128)(2,1)S(1)}, u32[]{:S(2)}, u32[]{:S(2)}) async-start(bf16[4,2,4096]{2,1,0:T(2,128)(2,1)} %reshape.480), calls=%async_computation | async-start | bytes 131072 | tf_op jit(solution)/shard_map/all_to_all | solution.py:104
  226.4 0.1 multiply_convert_fusion
  226.5 0.7 copy.61
  227.2 1.0 all-to-all-done
  228.1 5.9 %all-to-all-start.1 = ((bf16[2,8,2048]{2,0,1:T(2,128)(2,1)}), bf16[2,8,2048]{2,0,1:T(2,128)(2,1)S(1)}, u32[]{:S(2)}, u32[]{:S(2)}) async-start(bf16[2,8,2048]{2,0,1:T(2,128)(2,1)} %copy.61), calls=%async_computation.1 | async-start | bytes 131072 | tf_op jit(solution)/shard_map/all_to_all | solution.py:105
  234.1 11.1 %reshape.481 = bf16[16384,1,2]{2,1,0:T(2,128)(2,1)} reshape(bf16[4,2,4096]{2,1,0:T(2,128)(2,1)S(1)} %all-to-all-done) | data formatting | bytes 131072
  245.2 15.3 %copy.58 = bf16[1,2,16384]{2,1,0:T(2,128)(2,1)S(1)} copy(bf16[1,2,16384]{1,0,2:T(2,128)(2,1)} %bitcast.124) | data formatting | bytes 131072 | tf_op jit(solution)/shard_map/all_to_all | solution.py:104
  260.5 0.1 all_to_all.24
  260.6 25.1 %all-gather = bf16[4,1,16,4096]{3,0,1,2:T(4,128)(2,1)S(1)} all-gather(bf16[4,1,2,4096]{3,0,1,2:T(4,128)(2,1)S(1)} %bitcast.133), channel_id=2, replica_groups=mesh['row'=4,'col'=8] {'col'}, dimensions={2}, use_global_device_ids=true | all-gather | bytes 589824 | tf_op jit(solution)/shard_map/all_gather | solution.py:106
  285.7 0.0 all-to-all-done.1
  285.7 13.4 %all_gather.7 = bf16[4,16,2048]{2,1,0:T(8,128)(2,1)S(1)} all-gather(bf16[1,16,2048]{2,1,0:T(8,128)(2,1)S(1)} %broadcast_in_dim.20), channel_id=1, replica_groups=mesh['row'=4,'col'=8] {'row'}, dimensions={0}, use_global_device_ids=true | all-gather | bytes 327680 | tf_op jit(solution)/shard_map/all_gather | solution.py:107
  299.2 14.1 %convolution_bitcast_fusion = f32[4096,2048]{1,0:T(8,128)} fusion(bf16[4,16,2048]{2,1,0:T(8,128)(2,1)S(1)} %all_gather.7, bf16[4,1,16,4096]{3,0,1,2:T(4,128)(2,1)S(1)} %all-gather), kind=kOutput, calls=%fused_computation.2 | convolution fusion | flops 1073741824 | bytes 34340864 | tf_op jit(solution)/shard_map/kpg,kph->gh/dot_general | solution.py:108
  (14 shorter events, 0.1 us)
Async XLA Ops:
  0.0 13.2 %copy-start.1 = (bf16[1,48,2304]{2,1,0:T(8,128)(2,1)S(1)}, bf16[1,48,2304]{2,1,0:T(8,128)(2,1)}, u32[]{:S(2)}) copy-start(bf16[1,48,2304]{2,1,0:T(8,128)(2,1)} %param.9) | copy-start | bytes 663556
  0.0 13.2 %copy-start = (bf16[1,48,2304]{2,1,0:T(8,128)(2,1)S(1)}, bf16[1,48,2304]{2,1,0:T(8,128)(2,1)}, u32[]{:S(2)}) copy-start(bf16[1,48,2304]{2,1,0:T(8,128)(2,1)} %param.8) | copy-start | bytes 663556
  0.0 61.3 %collective-permute-start = (bf16[1,48,2304]{2,1,0:T(8,128)(2,1)}, bf16[1,48,2304]{2,1,0:T(8,128)(2,1)}, u32[]{:S(2)}, u32[]{:S(2)}) collective-permute-start(bf16[1,48,2304]{2,1,0:T(8,128)(2,1)} %param.9), channel_id=1, source_target_pairs={{0,8},{8,16},{16,24},{24,0},{1,9},{9,17},{17,25},{25,1},{2,10},{10... | collective-permute-start | bytes 663560 | tf_op jit(solution)/shard_map/ppermute | solution.py:18
  11.9 2.7 copy-start.2
  14.6 2.3 copy-start.5
  14.6 2.3 copy-start.7
  57.7 3.5 %copy-start.3 = (s32[1,8192]{1,0:T(1,128)S(1)}, s32[1,8192]{1,0:T(1,128)}, u32[]{:S(2)}) copy-start(s32[1,8192]{1,0:T(1,128)} %copy-done.2) | copy-start | bytes 98308
  64.8 0.8 copy-start.6
  64.8 0.8 copy-start.8
  107.7 2.9 copy-start.4
  223.1 5.0 %all-to-all-start = ((bf16[4,2,4096]{2,1,0:T(2,128)(2,1)}), bf16[4,2,4096]{2,1,0:T(2,128)(2,1)S(1)}, u32[]{:S(2)}, u32[]{:S(2)}) async-start(bf16[4,2,4096]{2,1,0:T(2,128)(2,1)} %reshape.480), calls=%async_computation | async-start | bytes 131072 | tf_op jit(solution)/shard_map/all_to_all | solution.py:104
  228.1 57.6 %all-to-all-start.1 = ((bf16[2,8,2048]{2,0,1:T(2,128)(2,1)}), bf16[2,8,2048]{2,0,1:T(2,128)(2,1)S(1)}, u32[]{:S(2)}, u32[]{:S(2)}) async-start(bf16[2,8,2048]{2,0,1:T(2,128)(2,1)} %copy.61), calls=%async_computation.1 | async-start | bytes 131072 | tf_op jit(solution)/shard_map/all_to_all | solution.py:105
where the time goes:
time: 314 us; the launch traced here: 313 us
  local copies, waits for them, and re-layouts  141 us (45%)
  other arithmetic  95.5 us (30%)
  blocking collectives  38.5 us (12%)
  matrix products  22.5 us (7%)
  starting transfers between devices  11.8 us (4%)
    unnamed x1, other arithmetic  91 us
    gather x4, local copies, waits for them, and re-layouts, transform(): jnp.take(flat_parts, cube_index, axis=2).reshape(batch_size, -1)  70.9 us
    all_gather x1, blocking collectives, on_device(): row_panel = lax.all_gather(row_blocks, 'col', axis=1, tiled=True)  25.1 us
    unnamed x23, local copies, waits for them, and re-layouts  19.6 us
    reshape x4, local copies, waits for them, and re-layouts, transform(): flat_parts = section_three.reshape(batch_size, 2, -1)  15.5 us
    all_to_all x2, local copies, waits for them, and re-layouts, on_device(): lax.all_to_all(coefficients[None], 'row', split_axis=2, concat_axis=0, ti...  15.4 us
    dot_general x1, matrix products, on_device(): jnp.einsum('kpg,kph->gh', row_panel, col_panel, preferred_element_type=jn...  14.1 us
    all_gather x1, blocking collectives, on_device(): col_panel = lax.all_gather(col_blocks[None], 'row', axis=0, tiled=True)  13.4 us
  transfers between devices with their start and end apart: 3, of which 1 were waited for; matrix products, arithmetic and copies ran while one was open for 27% of the time, Pallas kernels for 0%

commit v1 on v0

v1 whole, which is shorter than its diff:
```python
import functools
import math

import jax
import jax.numpy as jnp
import numpy as np
from jax import lax
from jax.experimental import pallas as pl
from jax.experimental.pallas import tpu as pltpu
from jax.sharding import PartitionSpec as P

GMAX = 18
STEPS = 2
RADIX = 6
SPAN = 2 * GMAX + 1
KX_ROWS = 40
LANES = 128
OMEGA_SQUARED = 0.0625
TILE = 512


def split_table(table):
    upper = table.astype(jnp.bfloat16)
    lower = (table - upper.astype(np.float64)).astype(jnp.bfloat16)
    return upper, lower


def tables(grid):
    y_lo_count = grid // RADIX
    turn = 2.0 * np.pi / grid
    kx = np.arange(SPAN) - GMAX
    angle = turn * (kx[:, None] * np.arange(grid)[None, :] % grid)
    x_table = np.zeros((2 * KX_ROWS, grid))
    x_table[:SPAN] = np.cos(angle)
    x_table[KX_ROWS : KX_ROWS + SPAN] = -np.sin(angle)
    x_table = np.concatenate(split_table(x_table), axis=1)

    width = y_lo_count * grid
    y_lo = np.arange(width) // grid
    z = np.arange(width) % grid
    angle = turn * (np.arange(RADIX)[:, None] * y_lo[None, :] % grid)
    twiddle = np.concatenate([np.cos(angle), -np.sin(angle)], axis=0).astype(np.float32)

    column = np.arange((2 * GMAX // RADIX + 1) * GMAX)
    q = column // GMAX - GMAX // RADIX
    kz = column % GMAX + 1
    phase = (RADIX * q[None, :] * y_lo[:, None] + kz[None, :] * z[:, None]) % grid
    cos_part = np.zeros((width, LANES))
    sin_part = np.zeros((width, LANES))
    cos_part[:, : column.size] = np.cos(turn * phase)
    sin_part[:, : column.size] = -np.sin(turn * phase)
    last = np.block([[cos_part, sin_part], [-sin_part, cos_part]])
    upper, lower = split_table(last)
    return x_table, twiddle, upper, lower


def dft_six(re, im):
    half = 0.5
    root = math.sqrt(3.0) / 2.0
    s_re = [re[h] + re[h + 3] for h in range(3)]
    s_im = [im[h] + im[h + 3] for h in range(3)]
    d_re = [re[h] - re[h + 3] for h in range(3)]
    d_im = [im[h] - im[h + 3] for h in range(3)]
    out = [None] * 6
    sum_re, sum_im = s_re[1] + s_re[2], s_im[1] + s_im[2]
    dif_re, dif_im = (s_re[1] - s_re[2]) * root, (s_im[1] - s_im[2]) * root
    out[0] = (s_re[0] + sum_re, s_im[0] + sum_im)
    mid_re, mid_im = s_re[0] - half * sum_re, s_im[0] - half * sum_im
    out[2] = (mid_re + dif_im, mid_im - dif_re)
    out[4] = (mid_re - dif_im, mid_im + dif_re)
    sum_re, sum_im = (d_re[1] + d_re[2]) * root, (d_im[1] + d_im[2]) * root
    dif_re, dif_im = d_re[1] - d_re[2], d_im[1] - d_im[2]
    out[3] = (d_re[0] - dif_re, d_im[0] - dif_im)
    mid_re, mid_im = d_re[0] + half * dif_re, d_im[0] + half * dif_im
    out[1] = (mid_re + sum_im, mid_im - sum_re)
    out[5] = (mid_re - sum_im, mid_im + sum_re)
    return out


def dot(a, b):
    return jnp.dot(a, b, preferred_element_type=jnp.float32)


def transform_kernel(grid, cond_ref, occ0_ref, occ1_ref, sphere_ref, x_table_ref, twiddle_ref, upper_ref, lower_ref, out_ref, cube_ref):
    norm = np.float32(grid ** (-1.5))
    width = (grid // RADIX) * grid
    for pair, occ_ref in enumerate((occ0_ref, occ1_ref)):
        density = (cond_ref[0].astype(jnp.float32) * occ_ref[0].astype(jnp.float32)).astype(jnp.bfloat16)
        section = dot(x_table_ref[...], jnp.concatenate([density, density], axis=0))
        re = [section[:KX_ROWS, h * width : (h + 1) * width] for h in range(RADIX)]
        im = [section[KX_ROWS:, h * width : (h + 1) * width] for h in range(RADIX)]
        rows = []
        for residue, (d_re, d_im) in enumerate(dft_six(re, im)):
            if residue > 0:
                t_re = twiddle_ref[residue : residue + 1, :]
                t_im = twiddle_ref[RADIX + residue : RADIX + residue + 1, :]
                d_re, d_im = d_re * t_re - d_im * t_im, d_re * t_im + d_im * t_re
            rows.append(jnp.concatenate([d_re, d_im], axis=1))
        whole = jnp.concatenate(rows, axis=0)
        whole_hi = whole.astype(jnp.bfloat16)
        whole_lo = (whole - whole_hi.astype(jnp.float32)).astype(jnp.bfloat16)
        spectrum = dot(whole_hi, upper_ref[...]) + dot(whole_lo, upper_ref[...]) + dot(whole_hi, lower_ref[...])
        spectrum = spectrum * norm
        parts = []
        for side in range(2):
            own = spectrum[:, side * LANES : (side + 1) * LANES]
            for group in range(RADIX // 2):
                first = 2 * group * KX_ROWS
                parts.append(jnp.concatenate([own[first : first + KX_ROWS], own[first + KX_ROWS : first + 2 * KX_ROWS]], axis=1))
        rows_per_pair = RADIX * KX_ROWS
        cube_ref[pair * rows_per_pair : (pair + 1) * rows_per_pair, :] = jnp.concatenate(parts, axis=0).astype(jnp.bfloat16)

    half = grid // 2
    picks = RADIX // 2 * KX_ROWS
    half_count = sphere_ref.shape[1]
    for first in range(0, half_count, TILE):
        here = slice(first, first + TILE)
        sx, sy, kz = sphere_ref[0:1, here], sphere_ref[1:2, here], sphere_ref[2:3, here]
        kx = jnp.where(sx >= half, sx - grid, sx) + GMAX
        ky = jnp.where(sy >= half, sy - grid, sy) + GMAX
        q = (ky * 43) >> 8
        residue = ky - q * RADIX
        lane = (residue & 1) * LANES + q * GMAX + kz - 1
        row = (residue >> 1) * KX_ROWS + kx
        one_hot = (lax.broadcasted_iota(jnp.int32, (2 * LANES, TILE), 0) == lane).astype(jnp.float32).astype(jnp.bfloat16)
        chosen = lax.broadcasted_iota(jnp.int32, (picks, TILE), 0) == row
        found = dot(cube_ref[...], one_hot)
        for pair in range(2):
            for side in range(2):
                start = (pair * 2 + side) * picks
                value = jnp.sum(jnp.where(chosen, found[start : start + picks], 0.0), axis=0, keepdims=True)
                out_ref[pair : pair + 1, side * half_count + first : side * half_count + first + TILE] = value.astype(jnp.bfloat16)


def transform(cond_orbitals, occ_first, occ_second, sphere_index):
    grid = cond_orbitals.shape[1]
    held = [jnp.asarray(t) for t in tables(grid)]
    half_count = sphere_index.shape[1]
    return pl.pallas_call(
        functools.partial(transform_kernel, grid),
        out_shape=jax.ShapeDtypeStruct((STEPS, 2 * half_count), jnp.bfloat16),
        scratch_shapes=[pltpu.VMEM((STEPS * 2 * RADIX // 2 * KX_ROWS, 2 * LANES), jnp.bfloat16)],
        compiler_params=pltpu.CompilerParams(vmem_limit_bytes=40 * 2**20),
        name="transform",
    )(cond_orbitals, occ_first, occ_second, sphere_index, *held)


def pack_kernel(rows, cols, sources, place_ref, cond_energy_ref, occ_energy_ref, occ_band_ref, *refs):
    arrived, outs, mixed_ref = refs[: len(sources)], refs[len(sources) : -1], refs[-1]
    r, c = place_ref[0], place_ref[1]
    devices = rows * cols
    pairs = STEPS * len(sources)
    total = 2 * mixed_ref.shape[1]
    entries = mixed_ref.shape[1]
    row_width, col_width = entries // rows, entries // cols
    line = lax.broadcasted_iota(jnp.int32, (pairs, LANES), 0)
    gap = jnp.zeros((pairs, LANES), jnp.float32)
    for j, (ref, source) in enumerate(zip(arrived, sources)):
        mixed_ref[STEPS * j : STEPS * (j + 1), :] = ref[...].astype(jnp.float32)
        band = r * cols + source(c)
        for step in range(STEPS):
            slot = lax.rem(band - step * cols + devices, devices)
            value = cond_energy_ref[band] - occ_energy_ref[occ_band_ref[slot]]
            gap = jnp.where(line == STEPS * j + step, value, gap)
    weight = -4.0 * gap / (gap * gap + OMEGA_SQUARED) / (devices * STEPS)
    weight = weight[:, :1]
    column = mixed_ref[:, pl.ds(pl.multiple_of(c * col_width, LANES), col_width)]
    column = (weight * column).astype(jnp.bfloat16)
    for k, out_ref in enumerate(outs):
        block = lax.rem(r + k, rows)
        out_ref[:, :row_width] = mixed_ref[:, pl.ds(pl.multiple_of(block * row_width, LANES), row_width)].astype(jnp.bfloat16)
        out_ref[:, row_width:] = column


def pack(arrived, sources, place, cond_energy, occ_energy, occ_band, rows, cols):
    entries = arrived[0].shape[1]
    pairs = STEPS * len(arrived)
    message = jax.ShapeDtypeStruct((pairs, entries // rows + entries // cols), jnp.bfloat16)
    smem = pl.BlockSpec(memory_space=pltpu.SMEM)
    vmem = pl.BlockSpec(memory_space=pltpu.VMEM)
    return pl.pallas_call(
        functools.partial(pack_kernel, rows, cols, sources),
        out_shape=[message] * rows,
        in_specs=[smem] * 4 + [vmem] * len(arrived),
        out_specs=[vmem] * rows,
        scratch_shapes=[pltpu.VMEM((pairs, entries), jnp.float32)],
        compiler_params=pltpu.CompilerParams(vmem_limit_bytes=40 * 2**20),
        name="pack",
    )(place, cond_energy, occ_energy, occ_band, *arrived)


def outer_kernel(row_width, block, *refs):
    messages, out_ref, left_ref, right_ref = refs[:-3], refs[-3], refs[-2], refs[-1]
    depth = messages[0].shape[0]

    @pl.when(pl.program_id(0) == 0)
    def _():
        for j, ref in enumerate(messages):
            left_ref[depth * j : depth * (j + 1), :] = ref[:, :row_width]
            right_ref[depth * j : depth * (j + 1), :] = ref[:, row_width:]

    here = pl.ds(pl.multiple_of(pl.program_id(0) * block, block), block)
    out_ref[...] = lax.dot_general(
        left_ref[:, here], right_ref[...], (((0,), (0,)), ((), ())), preferred_element_type=jnp.float32
    )


def outer(messages, row_width):
    depth, width = messages[0].shape
    col_width = width - row_width
    block = min(256, row_width)
    vmem = pl.BlockSpec(memory_space=pltpu.VMEM)
    return pl.pallas_call(
        functools.partial(outer_kernel, row_width, block),
        grid=(row_width // block,),
        out_shape=jax.ShapeDtypeStruct((row_width, col_width), jnp.float32),
        in_specs=[vmem] * len(messages),
        out_specs=pl.BlockSpec((block, col_width), lambda i: (i, 0)),
        scratch_shapes=[
            pltpu.VMEM((depth * len(messages), row_width), jnp.bfloat16),
            pltpu.VMEM((depth * len(messages), col_width), jnp.bfloat16),
        ],
        compiler_params=pltpu.CompilerParams(vmem_limit_bytes=40 * 2**20),
        name="outer",
    )(*messages)


def shifted(value, axis, by):
    devices = lax.axis_size(axis)
    return lax.ppermute(value, axis, [(i, (i + by) % devices) for i in range(devices)])


def swapped(value, axis):
    devices = lax.axis_size(axis)
    return lax.ppermute(value, axis, [(i, i ^ 1) for i in range(devices)])


def on_device(cond_orbitals, occ_orbitals, cond_energy, occ_energy, occ_band, sphere_index):
    rows = lax.axis_size("row")
    cols = lax.axis_size("col")
    place = jnp.stack([lax.axis_index("row"), lax.axis_index("col")]).astype(jnp.int32)
    occ_second = shifted(occ_orbitals, "row", 1)
    own = transform(cond_orbitals, occ_orbitals, occ_second, sphere_index)
    arrived = [own]
    sources = [lambda c: c]
    for k in range(1, cols // 2):
        arrived.append(shifted(own, "col", 2 * k))
        sources.append(lambda c, k=k: lax.rem(c - 2 * k + cols, cols))
    arrived += [swapped(value, "col") for value in arrived]
    sources += [lambda c, source=source: source(c ^ 1) for source in sources]
    messages = pack(arrived, sources, place, cond_energy, occ_energy, occ_band, rows, cols)
    gathered = [messages[0]] + [shifted(messages[k], "row", k) for k in range(1, rows)]
    return outer(gathered, own.shape[1] // rows)


def solution(mesh):
    placed = (P(("row", "col"), None, None), P(("row", "col"), None, None), P(), P(), P(), P())
    return jax.shard_map(
        on_device, mesh=mesh, in_specs=placed, out_specs=P("row", "col"), check_vma=False
    )
```

time: 314 us -> 61.3 us (0.20)
  local copies, waits for them, and re-layouts: 141 us -> 8.19 us
  other arithmetic: 95.5 us -> 0.07 us
  blocking collectives: 38.5 us -> 0 us
  matrix products: 22.5 us -> 0 us
  Pallas kernels: 0 us -> 20.1 us
  waiting for transfers between devices: 0.99 us -> 19.1 us
    unnamed x1 -> x0, other arithmetic: 91 us -> none
    gather x4 -> x0, local copies, waits for them, and re-layouts: 70.9 us -> none  [transform(): jnp.take(flat_parts, cube_index, axis=2).reshape(batch_size, -1)]
    all_gather x2 -> x0, blocking collectives: 38.5 us -> none  [the longest x1 25.1 us: on_device(): row_panel = lax.all_gather(row_blocks, 'col', axis=1, tiled=True)]
    dot_general x9 -> x0, matrix products: 22.5 us -> none  [the longest x1 14.1 us: on_device(): jnp.einsum('kpg,kph->gh', row_panel, col_panel, preferred_element_type=jn...]
    pallas_call x0 -> x3, Pallas kernels: none -> 20.1 us  [the longest x1 15 us: outer(): pl.pallas_call(functools.partial(outer_kernel, row_width, block), grid=(r...]
    ppermute x1 -> x11, waiting for transfers between devices: 0.01 us -> 19.1 us  [the longest x7 15.7 us: shifted(): lax.ppermute(value, axis, [(i, (i + by) % devices) for i in range(devices)])]
    reshape x4 -> x0, local copies, waits for them, and re-layouts: 15.5 us -> none  [transform(): flat_parts = section_three.reshape(batch_size, 2, -1)]
    all_to_all x2 -> x0, local copies, waits for them, and re-layouts: 15.4 us -> none  [on_device(): lax.all_to_all(coefficients[None], 'row', split_axis=2, concat_axis=0, ti...]
  transfers between devices with their start and end apart: 3 -> 11, of which waited for: 1 -> 7; matrix products, arithmetic and copies ran while one was open for 27% -> 0% of each run, Pallas kernels for 0% -> 0%
where the time goes in v1:
time: 61.3 us; the launch traced here: 60.9 us
  Pallas kernels  20.1 us (33%)
  waiting for transfers between devices  19.1 us (31%)
  starting transfers between devices  13.3 us (22%)
  local copies, waits for them, and re-layouts  8.19 us (13%)
    ppermute x7, waiting for transfers between devices, shifted(): lax.ppermute(value, axis, [(i, (i + by) % devices) for i in range(devices)])  15.7 us
    pallas_call x1, Pallas kernels, outer(): pl.pallas_call(functools.partial(outer_kernel, row_width, block), grid=(r...  15 us
    ppermute x7, starting transfers between devices, shifted(): lax.ppermute(value, axis, [(i, (i + by) % devices) for i in range(devices)])  9.75 us
    unnamed x20, local copies, waits for them, and re-layouts  8.19 us
    pallas_call x1, Pallas kernels, transform(): pl.pallas_call(functools.partial(transform_kernel, grid), out_shape=jax.S...  4.2 us
    ppermute x4, starting transfers between devices, swapped(): return lax.ppermute(value, axis, [(i, i ^ 1) for i in range(devices)])  3.56 us
    ppermute x4, waiting for transfers between devices, swapped(): return lax.ppermute(value, axis, [(i, i ^ 1) for i in range(devices)])  3.49 us
  transfers between devices with their start and end apart: 11, of which 7 were waited for; matrix products, arithmetic and copies ran while one was open for 0% of the time, Pallas kernels for 0%

profile of v1, /device:TPU:1, one launch (start us, length us, event | category | flops | bytes accessed | tf_op | source)
XLA Modules:
  0.0 60.9 jit_solution(18156913816596886952)
XLA Ops:
  0.0 2.6 %collective-permute-start = (bf16[1,48,2304]{2,1,0:T(8,128)(2,1)}, bf16[1,48,2304]{2,1,0:T(8,128)(2,1)S(1)}, u32[]{:S(2)}, u32[]{:S(2)}) collective-permute-start(bf16[1,48,2304]{2,1,0:T(8,128)(2,1)} %occ0_ref.1), channel_id=1, source_target_pairs={{0,8},{8,16},{16,24},{24,0},{1,9},{9,17},{17,25},{25,1},{2,10},{10... | collective-permute-start | bytes 663560 | tf_op jit(solution)/shard_map/ppermute | solution.py:230
  2.6 3.2 %collective-permute-done.occ1_ref = bf16[1,48,2304]{2,1,0:T(8,128)(2,1)S(1)} collective-permute-done((bf16[1,48,2304]{2,1,0:T(8,128)(2,1)}, bf16[1,48,2304]{2,1,0:T(8,128)(2,1)S(1)}, u32[]{:S(2)}, u32[]{:S(2)}) %collective-permute-start) | collective-permute-done | bytes 221216 | tf_op jit(solution)/shard_map/ppermute | solution.py:230
  5.8 0.0 copy-start
  5.8 1.0 %copy-done = bf16[768,256]{1,0:T(8,128)(2,1)S(1)} copy-done((bf16[768,256]{1,0:T(8,128)(2,1)S(1)}, bf16[768,256]{1,0:T(8,128)(2,1)}, u32[]{:S(2)}) %copy-start) | copy-done | bytes 393240
  6.8 0.0 copy-start.1
  6.8 1.0 %copy-done.1 = bf16[768,256]{1,0:T(8,128)(2,1)S(1)} copy-done((bf16[768,256]{1,0:T(8,128)(2,1)S(1)}, bf16[768,256]{1,0:T(8,128)(2,1)}, u32[]{:S(2)}) %copy-start.1) | copy-done | bytes 393240
  7.8 0.0 copy-start.2
  7.8 0.9 %copy-done.2 = bf16[1,48,2304]{2,1,0:T(8,128)(2,1)S(1)} copy-done((bf16[1,48,2304]{2,1,0:T(8,128)(2,1)S(1)}, bf16[1,48,2304]{2,1,0:T(8,128)(2,1)}, u32[]{:S(2)}) %copy-start.2) | copy-done | bytes 221208
  8.8 0.0 copy-start.3
  8.8 0.9 %copy-done.3 = bf16[1,48,2304]{2,1,0:T(8,128)(2,1)S(1)} copy-done((bf16[1,48,2304]{2,1,0:T(8,128)(2,1)S(1)}, bf16[1,48,2304]{2,1,0:T(8,128)(2,1)}, u32[]{:S(2)}) %copy-start.3) | copy-done | bytes 221208
  9.7 0.0 copy-start.4
  9.7 0.9 %copy-done.4 = s32[3,8192]{1,0:T(4,128)S(1)} copy-done((s32[3,8192]{1,0:T(4,128)S(1)}, s32[3,8192]{1,0:T(4,128)}, u32[]{:S(2)}) %copy-start.4) | copy-done | bytes 98328
  10.6 0.0 copy-start.5
  10.6 0.7 %copy-done.5 = f32[12,384]{1,0:T(8,128)S(1)} copy-done((f32[12,384]{1,0:T(8,128)S(1)}, f32[12,384]{1,0:T(8,128)}, u32[]{:S(2)}) %copy-start.5) | copy-done | bytes 18456
  11.3 0.0 copy-start.6
  11.3 0.7 %copy-done.6 = bf16[80,96]{1,0:T(8,128)(2,1)S(1)} copy-done((bf16[80,96]{1,0:T(8,128)(2,1)S(1)}, bf16[80,96]{1,0:T(8,128)(2,1)}, u32[]{:S(2)}) %copy-start.6) | copy-done | bytes 15384
  12.1 4.2 %transform.1.refs_0_ = bf16[2,16384]{1,0:T(2,128)(2,1)S(1)} custom-call(bf16[1,48,2304]{2,1,0:T(8,128)(2,1)S(1)} %copy-done.2, bf16[1,48,2304]{2,1,0:T(8,128)(2,1)S(1)} %copy-done.3, bf16[1,48,2304]{2,1,0:T(8,128)(2,1)S(1)} %collective-permute-done.occ1_ref, s32[3,8192]{1,0:T(4,128)S(1)} %copy-done.4, bf16[80,96]{1,0:T(8,128)(2,1)S(1)} %copy-done.6, ...), custom_call_target="tpu_custom_call" | custom-call | tf_op jit(solution)/shard_map/transform/pallas_call | solution.py:139
  16.3 3.4 %collective-permute-start.3 = (bf16[2,16384]{1,0:T(2,128)(2,1)S(1)}, bf16[2,16384]{1,0:T(2,128)(2,1)S(1)}, u32[]{:S(2)}, u32[]{:S(2)}) collective-permute-start(bf16[2,16384]{1,0:T(2,128)(2,1)S(1)} %transform.1.refs_0_), channel_id=1, source_target_pairs={{0,6},{1,7},{2,0},{3,1},{4,2},{5,3},{6,4},{7,5},{8,14},{9,15},{10,... | collective-permute-start | bytes 196616 | tf_op jit(solution)/shard_map/ppermute | solution.py:230
  19.6 0.0 collective-permute-start.2
  19.6 0.4 collective-permute-start.1
  20.1 1.2 %collective-permute-start.4 = (bf16[2,16384]{1,0:T(2,128)(2,1)S(1)}, bf16[2,16384]{1,0:T(2,128)(2,1)S(1)}, u32[]{:S(2)}, u32[]{:S(2)}) collective-permute-start(bf16[2,16384]{1,0:T(2,128)(2,1)S(1)} %transform.1.refs_0_), channel_id=1, source_target_pairs={{0,1},{1,0},{2,3},{3,2},{4,5},{5,4},{6,7},{7,6},{8,9},{9,8},{10,11... | collective-permute-start | bytes 196616 | tf_op jit(solution)/shard_map/ppermute | solution.py:235
  21.3 0.0 collective-permute-done.3.refs_3_
  21.3 0.9 %collective-permute-start.7 = (bf16[2,16384]{1,0:T(2,128)(2,1)S(1)}, bf16[2,16384]{1,0:T(2,128)(2,1)S(1)}, u32[]{:S(2)}, u32[]{:S(2)}) collective-permute-start(bf16[2,16384]{1,0:T(2,128)(2,1)S(1)} %collective-permute-done.3.refs_3_), channel_id=1, source_target_pairs={{0,1},{1,0},{2,3},{3,2},{4,5},{5,4},{6,7},{7,6},{8,9},{9,8},{10,11... | collective-permute-start | bytes 196616 | tf_op jit(solution)/shard_map/ppermute | solution.py:235
  22.2 3.2 %collective-permute-done.2.refs_2_ = bf16[2,16384]{1,0:T(2,128)(2,1)S(1)} collective-permute-done((bf16[2,16384]{1,0:T(2,128)(2,1)S(1)}, bf16[2,16384]{1,0:T(2,128)(2,1)S(1)}, u32[]{:S(2)}, u32[]{:S(2)}) %collective-permute-start.2) | collective-permute-done | bytes 65568 | tf_op jit(solution)/shard_map/ppermute | solution.py:230
  25.4 1.2 %collective-permute-start.6 = (bf16[2,16384]{1,0:T(2,128)(2,1)S(1)}, bf16[2,16384]{1,0:T(2,128)(2,1)S(1)}, u32[]{:S(2)}, u32[]{:S(2)}) collective-permute-start(bf16[2,16384]{1,0:T(2,128)(2,1)S(1)} %collective-permute-done.2.refs_2_), channel_id=1, source_target_pairs={{0,1},{1,0},{2,3},{3,2},{4,5},{5,4},{6,7},{7,6},{8,9},{9,8},{10,11... | collective-permute-start | bytes 196616 | tf_op jit(solution)/shard_map/ppermute | solution.py:235
  26.6 0.0 collective-permute-done.1.refs_1_
  26.6 0.3 collective-permute-start.5
  26.9 0.1 pad_add_fusion.place_ref
  26.9 0.0 collective-permute-done.4.refs_4_
  26.9 0.0 collective-permute-done.7.refs_7_
  26.9 1.6 %collective-permute-done.6.refs_6_ = bf16[2,16384]{1,0:T(2,128)(2,1)S(1)} collective-permute-done((bf16[2,16384]{1,0:T(2,128)(2,1)S(1)}, bf16[2,16384]{1,0:T(2,128)(2,1)S(1)}, u32[]{:S(2)}, u32[]{:S(2)}) %collective-permute-start.6) | collective-permute-done | bytes 65568 | tf_op jit(solution)/shard_map/ppermute | solution.py:235
  28.5 1.9 %collective-permute-done.5.refs_5_ = bf16[2,16384]{1,0:T(2,128)(2,1)S(1)} collective-permute-done((bf16[2,16384]{1,0:T(2,128)(2,1)S(1)}, bf16[2,16384]{1,0:T(2,128)(2,1)S(1)}, u32[]{:S(2)}, u32[]{:S(2)}) %collective-permute-start.5) | collective-permute-done | bytes 65568 | tf_op jit(solution)/shard_map/ppermute | solution.py:235
  30.4 0.0 copy-start.7
  30.4 0.7 %copy-done.7 = f32[32]{0:T(128)S(1)} copy-done((f32[32]{0:T(128)S(1)}, f32[32]{0:T(128)}, u32[]{:S(2)}) %copy-start.7) | copy-done | bytes 152
  31.1 0.0 copy-start.8
  31.1 0.7 %copy-done.8 = f32[32]{0:T(128)S(1)} copy-done((f32[32]{0:T(128)S(1)}, f32[32]{0:T(128)}, u32[]{:S(2)}) %copy-start.8) | copy-done | bytes 152
  31.7 0.0 copy-start.9
  31.7 0.7 %copy-done.9 = s32[32]{0:T(128)S(1)} copy-done((s32[32]{0:T(128)S(1)}, s32[32]{0:T(128)}, u32[]{:S(2)}) %copy-start.9) | copy-done | bytes 152
  32.4 0.9 %pack.1 = (bf16[16,6144]{1,0:T(8,128)(2,1)S(1)}, bf16[16,6144]{1,0:T(8,128)(2,1)S(1)}, bf16[16,6144]{1,0:T(8,128)(2,1)S(1)}, bf16[16,6144]{1,0:T(8,128)(2,1)S(1)}) custom-call(s32[2]{0:T(128)S(1)} %pad_add_fusion.place_ref, f32[32]{0:T(128)S(1)} %copy-done.7, f32[32]{0:T(128)S(1)} %copy-done.8, s32[32]{0:T(128)S(1)} %copy-done.9, ...), custom_call_target="tpu_custom_call" | custom-call | tf_op jit(solution)/shard_map/pack/pallas_call | solution.py:181
  33.3 2.8 %collective-permute-start.8 = (bf16[16,6144]{1,0:T(8,128)(2,1)S(1)}, bf16[16,6144]{1,0:T(8,128)(2,1)S(1)}, u32[]{:S(2)}, u32[]{:S(2)}) collective-permute-start(bf16[16,6144]{1,0:T(8,128)(2,1)S(1)} %get-tuple-element.10), channel_id=1, source_target_pairs={{0,8},{8,16},{16,24},{24,0},{1,9},{9,17},{17,25},{25,1},{2,10},{10... | collective-permute-start | bytes 589832 | tf_op jit(solution)/shard_map/ppermute | solution.py:230
  36.2 0.3 collective-permute-start.9
  36.5 0.1 collective-permute-start.10
  36.7 3.6 %collective-permute-done.8.refs_1_ = bf16[16,6144]{1,0:T(8,128)(2,1)S(1)} collective-permute-done((bf16[16,6144]{1,0:T(8,128)(2,1)S(1)}, bf16[16,6144]{1,0:T(8,128)(2,1)S(1)}, u32[]{:S(2)}, u32[]{:S(2)}) %collective-permute-start.8) | collective-permute-done | bytes 196640 | tf_op jit(solution)/shard_map/ppermute | solution.py:230
  40.3 5.0 %collective-permute-done.9.refs_2_ = bf16[16,6144]{1,0:T(8,128)(2,1)S(1)} collective-permute-done((bf16[16,6144]{1,0:T(8,128)(2,1)S(1)}, bf16[16,6144]{1,0:T(8,128)(2,1)S(1)}, u32[]{:S(2)}, u32[]{:S(2)}) %collective-permute-start.9) | collective-permute-done | bytes 196640 | tf_op jit(solution)/shard_map/ppermute | solution.py:230
  45.3 0.6 collective-permute-done.10.refs_3_
  45.9 15.0 %outer.1 = f32[4096,2048]{1,0:T(8,128)} custom-call(bf16[16,6144]{1,0:T(8,128)(2,1)S(1)} %get-tuple-element.9.refs_0_, bf16[16,6144]{1,0:T(8,128)(2,1)S(1)} %collective-permute-done.8.refs_1_, bf16[16,6144]{1,0:T(8,128)(2,1)S(1)} %collective-permute-done.9.refs_2_, bf16[16,6144]{1,0:T(8,128)(2,1)S(1)} %collective-permute-done.10.refs_3_), custom_call_target="tpu_custom_call" | custom-call | tf_op jit(solution)/shard_map/outer/pallas_call | solution.py:213
Async XLA Ops:
  0.0 5.8 %collective-permute-start = (bf16[1,48,2304]{2,1,0:T(8,128)(2,1)}, bf16[1,48,2304]{2,1,0:T(8,128)(2,1)S(1)}, u32[]{:S(2)}, u32[]{:S(2)}) collective-permute-start(bf16[1,48,2304]{2,1,0:T(8,128)(2,1)} %occ0_ref.1), channel_id=1, source_target_pairs={{0,8},{8,16},{16,24},{24,0},{1,9},{9,17},{17,25},{25,1},{2,10},{10... | collective-permute-start | bytes 663560 | tf_op jit(solution)/shard_map/ppermute | solution.py:230
  5.8 1.0 %copy-start = (bf16[768,256]{1,0:T(8,128)(2,1)S(1)}, bf16[768,256]{1,0:T(8,128)(2,1)}, u32[]{:S(2)}) copy-start(bf16[768,256]{1,0:T(8,128)(2,1)} %constant.19.clone.lower_ref) | copy-start | bytes 1179652
  6.8 1.0 %copy-start.1 = (bf16[768,256]{1,0:T(8,128)(2,1)S(1)}, bf16[768,256]{1,0:T(8,128)(2,1)}, u32[]{:S(2)}) copy-start(bf16[768,256]{1,0:T(8,128)(2,1)} %constant.18.clone.upper_ref) | copy-start | bytes 1179652
  7.8 0.9 %copy-start.2 = (bf16[1,48,2304]{2,1,0:T(8,128)(2,1)S(1)}, bf16[1,48,2304]{2,1,0:T(8,128)(2,1)}, u32[]{:S(2)}) copy-start(bf16[1,48,2304]{2,1,0:T(8,128)(2,1)} %cond_ref.1) | copy-start | bytes 663556
  8.8 0.9 %copy-start.3 = (bf16[1,48,2304]{2,1,0:T(8,128)(2,1)S(1)}, bf16[1,48,2304]{2,1,0:T(8,128)(2,1)}, u32[]{:S(2)}) copy-start(bf16[1,48,2304]{2,1,0:T(8,128)(2,1)} %occ0_ref.1) | copy-start | bytes 663556
  9.7 0.9 %copy-start.4 = (s32[3,8192]{1,0:T(4,128)S(1)}, s32[3,8192]{1,0:T(4,128)}, u32[]{:S(2)}) copy-start(s32[3,8192]{1,0:T(4,128)} %sphere_ref.1) | copy-start | bytes 294916
  10.6 0.7 %copy-start.5 = (f32[12,384]{1,0:T(8,128)S(1)}, f32[12,384]{1,0:T(8,128)}, u32[]{:S(2)}) copy-start(f32[12,384]{1,0:T(8,128)} %constant.17.clone.twiddle_ref) | copy-start | bytes 55300
  11.3 0.7 %copy-start.6 = (bf16[80,96]{1,0:T(8,128)(2,1)S(1)}, bf16[80,96]{1,0:T(8,128)(2,1)}, u32[]{:S(2)}) copy-start(bf16[80,96]{1,0:T(8,128)(2,1)} %constant.16.clone.x_table_ref) | copy-start | bytes 46084
  16.3 5.0 %collective-permute-start.3 = (bf16[2,16384]{1,0:T(2,128)(2,1)S(1)}, bf16[2,16384]{1,0:T(2,128)(2,1)S(1)}, u32[]{:S(2)}, u32[]{:S(2)}) collective-permute-start(bf16[2,16384]{1,0:T(2,128)(2,1)S(1)} %transform.1.refs_0_), channel_id=1, source_target_pairs={{0,6},{1,7},{2,0},{3,1},{4,2},{5,3},{6,4},{7,5},{8,14},{9,15},{10,... | collective-permute-start | bytes 196616 | tf_op jit(solution)/shard_map/ppermute | solution.py:230
  19.6 5.8 %collective-permute-start.2 = (bf16[2,16384]{1,0:T(2,128)(2,1)S(1)}, bf16[2,16384]{1,0:T(2,128)(2,1)S(1)}, u32[]{:S(2)}, u32[]{:S(2)}) collective-permute-start(bf16[2,16384]{1,0:T(2,128)(2,1)S(1)} %transform.1.refs_0_), channel_id=1, source_target_pairs={{0,4},{1,5},{2,6},{3,7},{4,0},{5,1},{6,2},{7,3},{8,12},{9,13},{10,... | collective-permute-start | bytes 196616 | tf_op jit(solution)/shard_map/ppermute | solution.py:230
  19.6 7.0 %collective-permute-start.1 = (bf16[2,16384]{1,0:T(2,128)(2,1)S(1)}, bf16[2,16384]{1,0:T(2,128)(2,1)S(1)}, u32[]{:S(2)}, u32[]{:S(2)}) collective-permute-start(bf16[2,16384]{1,0:T(2,128)(2,1)S(1)} %transform.1.refs_0_), channel_id=1, source_target_pairs={{0,2},{1,3},{2,4},{3,5},{4,6},{5,7},{6,0},{7,1},{8,10},{9,11},{10,... | collective-permute-start | bytes 196616 | tf_op jit(solution)/shard_map/ppermute | solution.py:230
  20.1 6.9 %collective-permute-start.4 = (bf16[2,16384]{1,0:T(2,128)(2,1)S(1)}, bf16[2,16384]{1,0:T(2,128)(2,1)S(1)}, u32[]{:S(2)}, u32[]{:S(2)}) collective-permute-start(bf16[2,16384]{1,0:T(2,128)(2,1)S(1)} %transform.1.refs_0_), channel_id=1, source_target_pairs={{0,1},{1,0},{2,3},{3,2},{4,5},{5,4},{6,7},{7,6},{8,9},{9,8},{10,11... | collective-permute-start | bytes 196616 | tf_op jit(solution)/shard_map/ppermute | solution.py:235
  21.3 5.6 %collective-permute-start.7 = (bf16[2,16384]{1,0:T(2,128)(2,1)S(1)}, bf16[2,16384]{1,0:T(2,128)(2,1)S(1)}, u32[]{:S(2)}, u32[]{:S(2)}) collective-permute-start(bf16[2,16384]{1,0:T(2,128)(2,1)S(1)} %collective-permute-done.3.refs_3_), channel_id=1, source_target_pairs={{0,1},{1,0},{2,3},{3,2},{4,5},{5,4},{6,7},{7,6},{8,9},{9,8},{10,11... | collective-permute-start | bytes 196616 | tf_op jit(solution)/shard_map/ppermute | solution.py:235
  25.4 3.1 %collective-permute-start.6 = (bf16[2,16384]{1,0:T(2,128)(2,1)S(1)}, bf16[2,16384]{1,0:T(2,128)(2,1)S(1)}, u32[]{:S(2)}, u32[]{:S(2)}) collective-permute-start(bf16[2,16384]{1,0:T(2,128)(2,1)S(1)} %collective-permute-done.2.refs_2_), channel_id=1, source_target_pairs={{0,1},{1,0},{2,3},{3,2},{4,5},{5,4},{6,7},{7,6},{8,9},{9,8},{10,11... | collective-permute-start | bytes 196616 | tf_op jit(solution)/shard_map/ppermute | solution.py:235
  26.6 3.8 %collective-permute-start.5 = (bf16[2,16384]{1,0:T(2,128)(2,1)S(1)}, bf16[2,16384]{1,0:T(2,128)(2,1)S(1)}, u32[]{:S(2)}, u32[]{:S(2)}) collective-permute-start(bf16[2,16384]{1,0:T(2,128)(2,1)S(1)} %collective-permute-done.1.refs_1_), channel_id=1, source_target_pairs={{0,1},{1,0},{2,3},{3,2},{4,5},{5,4},{6,7},{7,6},{8,9},{9,8},{10,11... | collective-permute-start | bytes 196616 | tf_op jit(solution)/shard_map/ppermute | solution.py:235
  30.4 0.7 %copy-start.7 = (f32[32]{0:T(128)S(1)}, f32[32]{0:T(128)}, u32[]{:S(2)}) copy-start(f32[32]{0:T(128)} %cond_energy_ref.1) | copy-start | bytes 388
  31.1 0.7 %copy-start.8 = (f32[32]{0:T(128)S(1)}, f32[32]{0:T(128)}, u32[]{:S(2)}) copy-start(f32[32]{0:T(128)} %occ_energy_ref.1) | copy-start | bytes 388
  31.7 0.7 %copy-start.9 = (s32[32]{0:T(128)S(1)}, s32[32]{0:T(128)}, u32[]{:S(2)}) copy-start(s32[32]{0:T(128)} %occ_band_ref.1) | copy-start | bytes 388
  33.3 6.9 %collective-permute-start.8 = (bf16[16,6144]{1,0:T(8,128)(2,1)S(1)}, bf16[16,6144]{1,0:T(8,128)(2,1)S(1)}, u32[]{:S(2)}, u32[]{:S(2)}) collective-permute-start(bf16[16,6144]{1,0:T(8,128)(2,1)S(1)} %get-tuple-element.10), channel_id=1, source_target_pairs={{0,8},{8,16},{16,24},{24,0},{1,9},{9,17},{17,25},{25,1},{2,10},{10... | collective-permute-start | bytes 589832 | tf_op jit(solution)/shard_map/ppermute | solution.py:230
  36.2 9.1 %collective-permute-start.9 = (bf16[16,6144]{1,0:T(8,128)(2,1)S(1)}, bf16[16,6144]{1,0:T(8,128)(2,1)S(1)}, u32[]{:S(2)}, u32[]{:S(2)}) collective-permute-start(bf16[16,6144]{1,0:T(8,128)(2,1)S(1)} %get-tuple-element.11), channel_id=1, source_target_pairs={{0,16},{8,24},{16,0},{24,8},{1,17},{9,25},{17,1},{25,9},{2,18},{10... | collective-permute-start | bytes 589832 | tf_op jit(solution)/shard_map/ppermute | solution.py:230
  36.5 9.4 %collective-permute-start.10 = (bf16[16,6144]{1,0:T(8,128)(2,1)S(1)}, bf16[16,6144]{1,0:T(8,128)(2,1)S(1)}, u32[]{:S(2)}, u32[]{:S(2)}) collective-permute-start(bf16[16,6144]{1,0:T(8,128)(2,1)S(1)} %get-tuple-element.12), channel_id=1, source_target_pairs={{0,24},{8,0},{16,8},{24,16},{1,25},{9,1},{17,9},{25,17},{2,26},{10... | collective-permute-start | bytes 589832 | tf_op jit(solution)/shard_map/ppermute | solution.py:230

commit v2 on v1

v2 whole, which is shorter than its diff:
```python
import functools
import math

import jax
import jax.numpy as jnp
import numpy as np
from jax import lax
from jax.experimental import pallas as pl
from jax.experimental.pallas import tpu as pltpu
from jax.sharding import PartitionSpec as P

GMAX = 18
STEPS = 2
RADIX = 6
SPAN = 2 * GMAX + 1
KX_ROWS = 40
LANES = 128
OMEGA_SQUARED = 0.0625
TILE = 512
FULL_VMEM = 56 * 2**20


def split_table(table):
    upper = table.astype(jnp.bfloat16)
    lower = (table - upper.astype(np.float64)).astype(jnp.bfloat16)
    return upper, lower


def tables(grid):
    y_lo_count = grid // RADIX
    turn = 2.0 * np.pi / grid
    kx = np.arange(SPAN) - GMAX
    angle = turn * (kx[:, None] * np.arange(grid)[None, :] % grid)
    x_table = np.zeros((2 * KX_ROWS, grid))
    x_table[:SPAN] = np.cos(angle)
    x_table[KX_ROWS : KX_ROWS + SPAN] = -np.sin(angle)
    x_table = np.concatenate(split_table(x_table), axis=1)

    width = y_lo_count * grid
    y_lo = np.arange(width) // grid
    z = np.arange(width) % grid
    angle = turn * (np.arange(RADIX)[:, None] * y_lo[None, :] % grid)
    twiddle = np.concatenate([np.cos(angle), -np.sin(angle)], axis=0).astype(np.float32)

    column = np.arange((2 * GMAX // RADIX + 1) * GMAX)
    q = column // GMAX - GMAX // RADIX
    kz = column % GMAX + 1
    phase = (RADIX * q[None, :] * y_lo[:, None] + kz[None, :] * z[:, None]) % grid
    cos_part = np.zeros((width, LANES))
    sin_part = np.zeros((width, LANES))
    cos_part[:, : column.size] = np.cos(turn * phase)
    sin_part[:, : column.size] = -np.sin(turn * phase)
    last = np.block([[cos_part, sin_part], [-sin_part, cos_part]])
    upper, lower = split_table(last)
    return x_table, twiddle, upper, lower


def dft_six(re, im):
    half = 0.5
    root = math.sqrt(3.0) / 2.0
    s_re = [re[h] + re[h + 3] for h in range(3)]
    s_im = [im[h] + im[h + 3] for h in range(3)]
    d_re = [re[h] - re[h + 3] for h in range(3)]
    d_im = [im[h] - im[h + 3] for h in range(3)]
    out = [None] * 6
    sum_re, sum_im = s_re[1] + s_re[2], s_im[1] + s_im[2]
    dif_re, dif_im = (s_re[1] - s_re[2]) * root, (s_im[1] - s_im[2]) * root
    out[0] = (s_re[0] + sum_re, s_im[0] + sum_im)
    mid_re, mid_im = s_re[0] - half * sum_re, s_im[0] - half * sum_im
    out[2] = (mid_re + dif_im, mid_im - dif_re)
    out[4] = (mid_re - dif_im, mid_im + dif_re)
    sum_re, sum_im = (d_re[1] + d_re[2]) * root, (d_im[1] + d_im[2]) * root
    dif_re, dif_im = d_re[1] - d_re[2], d_im[1] - d_im[2]
    out[3] = (d_re[0] - dif_re, d_im[0] - dif_im)
    mid_re, mid_im = d_re[0] + half * dif_re, d_im[0] + half * dif_im
    out[1] = (mid_re + sum_im, mid_im - sum_re)
    out[5] = (mid_re - sum_im, mid_im + sum_re)
    return out


def dot(a, b):
    return jnp.dot(a, b, preferred_element_type=jnp.float32)


def spectrum_of(grid, cond_ref, occ_ref, x_table_ref, twiddle_ref, upper_ref, lower_ref):
    norm = np.float32(grid ** (-1.5))
    width = (grid // RADIX) * grid
    density = (cond_ref[0].astype(jnp.float32) * occ_ref[0].astype(jnp.float32)).astype(jnp.bfloat16)
    section = dot(x_table_ref[...], jnp.concatenate([density, density], axis=0))
    re = [section[:KX_ROWS, h * width : (h + 1) * width] for h in range(RADIX)]
    im = [section[KX_ROWS:, h * width : (h + 1) * width] for h in range(RADIX)]
    rows = []
    for residue, (d_re, d_im) in enumerate(dft_six(re, im)):
        if residue > 0:
            t_re = twiddle_ref[residue : residue + 1, :]
            t_im = twiddle_ref[RADIX + residue : RADIX + residue + 1, :]
            d_re, d_im = d_re * t_re - d_im * t_im, d_re * t_im + d_im * t_re
        rows.append(jnp.concatenate([d_re, d_im], axis=1))
    whole = jnp.concatenate(rows, axis=0)
    whole_hi = whole.astype(jnp.bfloat16)
    whole_lo = (whole - whole_hi.astype(jnp.float32)).astype(jnp.bfloat16)
    spectrum = dot(whole_hi, upper_ref[...]) + dot(whole_lo, upper_ref[...]) + dot(whole_hi, lower_ref[...])
    spectrum = spectrum * norm
    parts = []
    for side in range(2):
        own = spectrum[:, side * LANES : (side + 1) * LANES]
        for group in range(RADIX // 2):
            first = 2 * group * KX_ROWS
            parts.append(jnp.concatenate([own[first : first + KX_ROWS], own[first + KX_ROWS : first + 2 * KX_ROWS]], axis=1))
    return jnp.concatenate(parts, axis=0).astype(jnp.bfloat16)


def cube_places(grid, sphere):
    half = grid // 2
    sx, sy, kz = sphere[0:1], sphere[1:2], sphere[2:3]
    kx = jnp.where(sx >= half, sx - grid, sx) + GMAX
    ky = jnp.where(sy >= half, sy - grid, sy) + GMAX
    q = (ky * 43) >> 8
    residue = ky - q * RADIX
    lane = (residue & 1) * LANES + q * GMAX + kz - 1
    row = (residue >> 1) * KX_ROWS + kx
    return lane, row


def pick(cube_ref, places_ref, pair, out_ref):
    picks = RADIX // 2 * KX_ROWS
    half_count = places_ref.shape[1]
    for first in range(0, half_count, TILE):
        here = slice(first, first + TILE)
        lane, row = places_ref[0:1, here], places_ref[1:2, here]
        one_hot = (lax.broadcasted_iota(jnp.int32, (2 * LANES, TILE), 0) == lane).astype(jnp.float32).astype(jnp.bfloat16)
        chosen = lax.broadcasted_iota(jnp.int32, (picks, TILE), 0) == row
        found = dot(cube_ref[...], one_hot)
        for side in range(2):
            part = found[side * picks : (side + 1) * picks]
            value = jnp.sum(jnp.where(chosen, part, 0.0), axis=0, keepdims=True)
            out_ref[pair : pair + 1, side * half_count + first : side * half_count + first + TILE] = value.astype(jnp.bfloat16)


def own_place():
    return lax.axis_index("row"), lax.axis_index("col")


def weight_line(step, levels_ref, occ_levels_ref, bands_ref):
    rows, cols = lax.axis_size("row"), lax.axis_size("col")
    r, c = own_place()
    devices = rows * cols
    band = r * cols + c
    slot = lax.rem(band - step * cols + devices, devices)
    gap = jnp.full((1, LANES), levels_ref[band] - occ_levels_ref[bands_ref[slot]], jnp.float32)
    weight = -4.0 * gap / (gap * gap + OMEGA_SQUARED) / (devices * STEPS)
    lane = lax.broadcasted_iota(jnp.int32, weight.shape, 1)
    line = jnp.zeros_like(weight)
    for i in range(3):
        piece = weight.astype(jnp.bfloat16).astype(jnp.float32)
        line = jnp.where(lane == i, piece, line)
        weight = weight - piece
    return line.astype(jnp.bfloat16)


def start_all(sources, targets, sems):
    copies = [pltpu.make_async_copy(source, target, sems.at[i]) for i, (source, target) in enumerate(zip(sources, targets))]
    for copy in copies:
        copy.start()
    return copies


def pair_row(grid, step, copies, held, cube_ref, places_ref, out_ref):
    cond_ref, occ_ref, x_ref, twiddle_ref, upper_ref, lower_ref, vectors_ref, levels_ref, occ_levels_ref, bands_ref = held
    ready = len(copies) - 4 - step
    for copy in copies[:ready]:
        copy.wait()
    cube_ref[...] = spectrum_of(grid, cond_ref, occ_ref, x_ref, twiddle_ref, upper_ref, lower_ref)
    for copy in copies[ready:]:
        copy.wait()
    if step == 0:
        lane, row = cube_places(grid, vectors_ref[...])
        places_ref[0:1, :] = lane
        places_ref[1:2, :] = row
    else:
        places_ref = vectors_ref
    out_ref[step : step + 1, 2 * places_ref.shape[1] :] = weight_line(step, levels_ref, occ_levels_ref, bands_ref)
    pick(cube_ref, places_ref, step, out_ref)


def first_kernel(grid, *refs):
    sources, (out_ref, places_ref, *held, cube_ref, sems) = refs[:10], refs[10:]
    copies = start_all(sources, held, sems)
    pair_row(grid, 0, copies, held, cube_ref, places_ref, out_ref)


def second_kernel(grid, *refs):
    (cond_in, occ_ref, *sources), (out_ref, cond_ref, *held, first_ref, cube_ref, sems) = refs[:11], refs[11:]
    copies = start_all((cond_in, *sources), (cond_ref, *held, first_ref), sems)
    pair_row(grid, 1, copies, (cond_ref, occ_ref, *held), cube_ref, None, out_ref)
    out_ref[0:1, :] = first_ref[...]


def transform(cond_orbitals, occ_orbitals, occ_second, sphere_index, levels):
    grid = cond_orbitals.shape[1]
    tabled = [jnp.asarray(t) for t in tables(grid)]
    half_count = sphere_index.shape[1]
    width = 2 * half_count + LANES
    hbm = pl.BlockSpec(memory_space=pltpu.HBM)
    vmem = pl.BlockSpec(memory_space=pltpu.VMEM)
    places = jax.ShapeDtypeStruct((2, half_count), jnp.int32)

    def scratch(kept, more=()):
        return [
            *[pltpu.VMEM(a.shape, a.dtype) for a in kept],
            *[pltpu.SMEM(a.shape, a.dtype) for a in levels],
            *more,
            pltpu.VMEM((RADIX * KX_ROWS, 2 * LANES), jnp.bfloat16),
            pltpu.SemaphoreType.DMA((11,)),
        ]

    params = dict(
        compiler_params=pltpu.CompilerParams(vmem_limit_bytes=FULL_VMEM),
        cost_estimate=pl.CostEstimate(flops=2 * 10**9, bytes_accessed=2 * 10**6, transcendentals=0),
    )
    first_row = jax.ShapeDtypeStruct((1, width), jnp.bfloat16)
    first, places = pl.pallas_call(
        functools.partial(first_kernel, grid),
        out_shape=[first_row, places],
        in_specs=[hbm] * 10,
        out_specs=[vmem] * 2,
        scratch_shapes=scratch([cond_orbitals, occ_orbitals, *tabled, sphere_index]),
        name="first_pair",
        **params,
    )(cond_orbitals, occ_orbitals, *tabled, sphere_index, *levels)
    return pl.pallas_call(
        functools.partial(second_kernel, grid),
        out_shape=jax.ShapeDtypeStruct((STEPS, width), jnp.bfloat16),
        in_specs=[hbm, vmem] + [hbm] * 9,
        out_specs=vmem,
        scratch_shapes=scratch([cond_orbitals, *tabled, places], [pltpu.VMEM(first_row.shape, first_row.dtype)]),
        name="second_pair",
        **params,
    )(cond_orbitals, occ_second, *tabled, places, *levels, first)


def pack_kernel(rows, cols, *refs):
    arrived, outs, mixed_ref = refs[: -1 - rows], refs[-1 - rows : -1], refs[-1]
    r, c = own_place()
    entries = mixed_ref.shape[1] - LANES
    row_width, col_width = entries // rows, entries // cols
    for j, ref in enumerate(arrived):
        mixed_ref[STEPS * j : STEPS * (j + 1), :] = ref[...].astype(jnp.float32)
    weight = mixed_ref[:, entries : entries + 1]
    for i in range(1, 3):
        weight = weight + mixed_ref[:, entries + i : entries + i + 1]
    column = mixed_ref[:, pl.ds(pl.multiple_of(c * col_width, LANES), col_width)]
    column = (weight * column).astype(jnp.bfloat16)
    for k, out_ref in enumerate(outs):
        block = lax.rem(r + k, rows)
        out_ref[:, :row_width] = mixed_ref[:, pl.ds(pl.multiple_of(block * row_width, LANES), row_width)].astype(jnp.bfloat16)
        out_ref[:, row_width:] = column


def pack(arrived, rows, cols):
    entries = arrived[0].shape[1] - LANES
    pairs = STEPS * len(arrived)
    message = jax.ShapeDtypeStruct((pairs, entries // rows + entries // cols), jnp.bfloat16)
    vmem = pl.BlockSpec(memory_space=pltpu.VMEM)
    return pl.pallas_call(
        functools.partial(pack_kernel, rows, cols),
        out_shape=[message] * rows,
        in_specs=[vmem] * len(arrived),
        out_specs=[vmem] * rows,
        scratch_shapes=[pltpu.VMEM((pairs, entries + LANES), jnp.float32)],
        compiler_params=pltpu.CompilerParams(vmem_limit_bytes=30 * 2**20),
        cost_estimate=pl.CostEstimate(flops=4 * 10**9, bytes_accessed=2 * 10**6, transcendentals=0),
        name="pack",
    )(*arrived)


def outer_kernel(row_width, block, slots, *refs):
    messages, (out_ref, left_ref, right_ref, held_ref, sems) = refs[:-5], refs[-5:]
    depth = messages[0].shape[0]
    merge = max(1, 16 // depth)
    for j in range(0, len(messages), merge):
        whole = jnp.concatenate([ref[...].astype(jnp.float32) for ref in messages[j : j + merge]], axis=0).astype(jnp.bfloat16)
        left_ref[depth * j : depth * (j + merge), :] = whole[:, :row_width]
        right_ref[depth * j : depth * (j + merge), :] = whole[:, row_width:]
    count = row_width // block

    def copy_out(i, slot):
        rows = pl.ds(pl.multiple_of(i * block, block), block)
        return pltpu.make_async_copy(held_ref.at[slot], out_ref.at[rows], sems.at[slot])

    def step(i, carry):
        slot = lax.rem(i, slots)

        @pl.when(i >= slots)
        def _():
            copy_out(i - slots, slot).wait()

        here = pl.ds(pl.multiple_of(i * block, block), block)
        held_ref[slot] = lax.dot_general(
            left_ref[:, here], right_ref[...], (((0,), (0,)), ((), ())), preferred_element_type=jnp.float32
        )
        copy_out(i, slot).start()
        return carry

    lax.fori_loop(0, count, step, 0)
    for i in range(max(0, count - slots), count):
        copy_out(i, i % slots).wait()


def outer(messages, row_width):
    depth, width = messages[0].shape
    col_width = width - row_width
    block = min(256, row_width)
    slots = min(4, row_width // block)
    vmem = pl.BlockSpec(memory_space=pltpu.VMEM)
    return pl.pallas_call(
        functools.partial(outer_kernel, row_width, block, slots),
        out_shape=jax.ShapeDtypeStruct((row_width, col_width), jnp.float32),
        in_specs=[vmem] * len(messages),
        out_specs=pl.BlockSpec(memory_space=pltpu.HBM),
        scratch_shapes=[
            pltpu.VMEM((depth * len(messages), row_width), jnp.bfloat16),
            pltpu.VMEM((depth * len(messages), col_width), jnp.bfloat16),
            pltpu.VMEM((slots, block, col_width), jnp.float32),
            pltpu.SemaphoreType.DMA((slots,)),
        ],
        compiler_params=pltpu.CompilerParams(vmem_limit_bytes=30 * 2**20),
        name="outer",
    )(*messages)


def shifted(value, axis, by):
    devices = lax.axis_size(axis)
    return lax.ppermute(value, axis, [(i, (i + by) % devices) for i in range(devices)])


def swapped(value, axis):
    devices = lax.axis_size(axis)
    return lax.ppermute(value, axis, [(i, i ^ 1) for i in range(devices)])


def on_device(cond_orbitals, occ_orbitals, cond_energy, occ_energy, occ_band, sphere_index):
    rows = lax.axis_size("row")
    cols = lax.axis_size("col")
    occ_second = shifted(occ_orbitals, "row", 1)
    own = transform(cond_orbitals, occ_orbitals, occ_second, sphere_index, (cond_energy, occ_energy, occ_band))
    straight = [own] + [shifted(own, "col", 2 * k) for k in range(1, cols // 2)]
    crossed = [swapped(value, "col") for value in straight]
    gathered = []
    for arrived in (straight, crossed):
        messages = pack(arrived, rows, cols)
        gathered += [messages[0]] + [shifted(messages[k], "row", k) for k in range(1, rows)]
    return outer(gathered, 2 * sphere_index.shape[1] // rows)


def solution(mesh):
    placed = (P(("row", "col"), None, None), P(("row", "col"), None, None), P(), P(), P(), P())
    return jax.shard_map(
        on_device, mesh=mesh, in_specs=placed, out_specs=P("row", "col"), check_vma=False
    )
```

time: 61.3 us -> 51.2 us (0.84)
  waiting for transfers between devices: 19.1 us -> 10.1 us
  local copies, waits for them, and re-layouts: 8.19 us -> 1.56 us
  Pallas kernels: 20.1 us -> 23.6 us
  starting transfers between devices: 13.3 us -> 15.5 us
    unnamed x20 -> x4, local copies, waits for them, and re-layouts: 8.19 us -> 1.56 us
    ppermute x7 -> x10, waiting for transfers between devices: 15.7 us -> 10.1 us  [shifted(): lax.ppermute(value, axis, [(i, (i + by) % devices) for i in range(devices)])]
    pallas_call x3 -> x5, Pallas kernels: 20.1 us -> 23.6 us  [the longest x1 11.4 us: outer(): pl.pallas_call(functools.partial(outer_kernel, row_width, block, slots),...]
    ppermute x4, waiting for transfers between devices: 3.49 us -> 0.01 us  [swapped(): return lax.ppermute(value, axis, [(i, i ^ 1) for i in range(devices)])]
    ppermute x7 -> x10, starting transfers between devices: 9.75 us -> 11.7 us  [shifted(): lax.ppermute(value, axis, [(i, (i + by) % devices) for i in range(devices)])]
  transfers between devices with their start and end apart: 11 -> 14, of which waited for: 7 -> 6; matrix products, arithmetic and copies ran while one was open for 0% -> 0% of each run, Pallas kernels for 0% -> 12%
where the time goes in v2:
time: 51.2 us; the launch traced here: 51 us
  Pallas kernels  23.6 us (46%)
  starting transfers between devices  15.5 us (30%)
  waiting for transfers between devices  10.1 us (20%)
  local copies, waits for them, and re-layouts  1.56 us (3%)
    ppermute x10, starting transfers between devices, shifted(): lax.ppermute(value, axis, [(i, (i + by) % devices) for i in range(devices)])  11.7 us
    pallas_call x1, Pallas kernels, outer(): pl.pallas_call(functools.partial(outer_kernel, row_width, block, slots),...  11.4 us
    ppermute x10, waiting for transfers between devices, shifted(): lax.ppermute(value, axis, [(i, (i + by) % devices) for i in range(devices)])  10.1 us
    pallas_call x1, Pallas kernels, transform(): pl.pallas_call(functools.partial(second_kernel, grid), out_shape=jax.Shap...  6.32 us
    pallas_call x1, Pallas kernels, transform(): pl.pallas_call(functools.partial(first_kernel, grid), out_shape=[first_ro...  5.39 us
    ppermute x4, starting transfers between devices, swapped(): return lax.ppermute(value, axis, [(i, i ^ 1) for i in range(devices)])  3.88 us
    unnamed x4, local copies, waits for them, and re-layouts  1.56 us
  transfers between devices with their start and end apart: 14, of which 6 were waited for; matrix products, arithmetic and copies ran while one was open for 0% of the time, Pallas kernels for 12%

profile of v2, /device:TPU:1, one launch (start us, length us, event | category | flops | bytes accessed | tf_op | source)
XLA Modules:
  0.0 51.0 jit_solution(11967894542856520091)
XLA Ops:
  0.0 2.6 %collective-permute-start = (bf16[1,48,2304]{2,1,0:T(8,128)(2,1)}, bf16[1,48,2304]{2,1,0:T(8,128)(2,1)S(1)}, u32[]{:S(2)}, u32[]{:S(2)}) collective-permute-start(bf16[1,48,2304]{2,1,0:T(8,128)(2,1)} %refs_1_.1), channel_id=1, source_target_pairs={{0,8},{8,16},{16,24},{24,0},{1,9},{9,17},{17,25},{25,1},{2,10},{10... | collective-permute-start | bytes 663560 | tf_op jit(solution)/shard_map/ppermute | solution.py:334
  2.6 5.4 %first_pair.1 = (bf16[1,16512]{1,0:T(2,128)(2,1)}, s32[2,8192]{1,0:T(2,128)}) custom-call(bf16[1,48,2304]{2,1,0:T(8,128)(2,1)} %refs_0_.3, bf16[1,48,2304]{2,1,0:T(8,128)(2,1)} %refs_1_.1, bf16[80,96]{1,0:T(8,128)(2,1)} %constant.8.clone.refs_2_, f32[12,384]{1,0:T(8,128)} %constant.9.clone.refs_3_, bf16[768,256]{1,0:T(8,128)(2,1)} %constant.10.clone.refs_4_, ...), custom_call_target="tpu_custom_call" | custom-call | flops 2000000000 | bytes 2000000 | tf_op jit(solution)/shard_map/first_pair/pallas_call | solution.py:222
  8.0 0.0 collective-permute-done.refs_1_
  8.0 0.0 copy-start.1
  8.1 0.7 %copy-done.1 = bf16[1,48,2304]{2,1,0:T(8,128)(2,1)} copy-done((bf16[1,48,2304]{2,1,0:T(8,128)(2,1)}, bf16[1,48,2304]{2,1,0:T(8,128)(2,1)S(1)}, u32[]{:S(2)}) %copy-start.1) | copy-done | bytes 221208
  8.7 6.3 %second_pair.1.refs_0_ = bf16[2,16512]{1,0:T(2,128)(2,1)} custom-call(bf16[1,48,2304]{2,1,0:T(8,128)(2,1)} %refs_0_.3, bf16[1,48,2304]{2,1,0:T(8,128)(2,1)} %copy-done.1, bf16[80,96]{1,0:T(8,128)(2,1)} %constant.8.clone.refs_2_, f32[12,384]{1,0:T(8,128)} %constant.9.clone.refs_3_, bf16[768,256]{1,0:T(8,128)(2,1)} %constant.10.clone.refs_4_, ...), custom_call_target="tpu_custom_call" | custom-call | flops 2000000000 | bytes 2000000 | tf_op jit(solution)/shard_map/second_pair/pallas_call | solution.py:231
  15.1 3.4 %collective-permute-start.3 = (bf16[2,16512]{1,0:T(2,128)(2,1)}, bf16[2,16512]{1,0:T(2,128)(2,1)S(1)}, u32[]{:S(2)}, u32[]{:S(2)}) collective-permute-start(bf16[2,16512]{1,0:T(2,128)(2,1)} %second_pair.1.refs_0_), channel_id=1, source_target_pairs={{0,6},{1,7},{2,0},{3,1},{4,2},{5,3},{6,4},{7,5},{8,14},{9,15},{10,... | collective-permute-start | bytes 198152 | tf_op jit(solution)/shard_map/ppermute | solution.py:334
  18.4 0.0 collective-permute-start.2
  18.4 0.4 collective-permute-start.1
  18.9 1.2 %collective-permute-start.7 = (bf16[2,16512]{1,0:T(2,128)(2,1)}, bf16[2,16512]{1,0:T(2,128)(2,1)S(1)}, u32[]{:S(2)}, u32[]{:S(2)}) collective-permute-start(bf16[2,16512]{1,0:T(2,128)(2,1)} %second_pair.1.refs_0_), channel_id=1, source_target_pairs={{0,1},{1,0},{2,3},{3,2},{4,5},{5,4},{6,7},{7,6},{8,9},{9,8},{10,11... | collective-permute-start | bytes 198152 | tf_op jit(solution)/shard_map/ppermute | solution.py:339
  20.1 0.6 %collective-permute-done.3.refs_3_ = bf16[2,16512]{1,0:T(2,128)(2,1)S(1)} collective-permute-done((bf16[2,16512]{1,0:T(2,128)(2,1)}, bf16[2,16512]{1,0:T(2,128)(2,1)S(1)}, u32[]{:S(2)}, u32[]{:S(2)}) %collective-permute-start.3) | collective-permute-done | bytes 66080 | tf_op jit(solution)/shard_map/ppermute | solution.py:334
  20.6 1.2 %collective-permute-start.10 = (bf16[2,16512]{1,0:T(2,128)(2,1)S(1)}, bf16[2,16512]{1,0:T(2,128)(2,1)S(1)}, u32[]{:S(2)}, u32[]{:S(2)}) collective-permute-start(bf16[2,16512]{1,0:T(2,128)(2,1)S(1)} %collective-permute-done.3.refs_3_), channel_id=1, source_target_pairs={{0,1},{1,0},{2,3},{3,2},{4,5},{5,4},{6,7},{7,6},{8,9},{9,8},{10,11... | collective-permute-start | bytes 198152 | tf_op jit(solution)/shard_map/ppermute | solution.py:339
  21.9 3.3 %collective-permute-done.2.refs_2_ = bf16[2,16512]{1,0:T(2,128)(2,1)S(1)} collective-permute-done((bf16[2,16512]{1,0:T(2,128)(2,1)}, bf16[2,16512]{1,0:T(2,128)(2,1)S(1)}, u32[]{:S(2)}, u32[]{:S(2)}) %collective-permute-start.2) | collective-permute-done | bytes 66080 | tf_op jit(solution)/shard_map/ppermute | solution.py:334
  25.2 1.2 %collective-permute-start.9 = (bf16[2,16512]{1,0:T(2,128)(2,1)S(1)}, bf16[2,16512]{1,0:T(2,128)(2,1)S(1)}, u32[]{:S(2)}, u32[]{:S(2)}) collective-permute-start(bf16[2,16512]{1,0:T(2,128)(2,1)S(1)} %collective-permute-done.2.refs_2_), channel_id=1, source_target_pairs={{0,1},{1,0},{2,3},{3,2},{4,5},{5,4},{6,7},{7,6},{8,9},{9,8},{10,11... | collective-permute-start | bytes 198152 | tf_op jit(solution)/shard_map/ppermute | solution.py:339
  26.4 0.0 collective-permute-done.1.refs_1_
  26.4 0.3 collective-permute-start.8
  26.7 0.0 copy-start
  26.7 0.9 %copy-done = bf16[2,16512]{1,0:T(2,128)(2,1)S(1)} copy-done((bf16[2,16512]{1,0:T(2,128)(2,1)S(1)}, bf16[2,16512]{1,0:T(2,128)(2,1)}, u32[]{:S(2)}) %copy-start) | copy-done | bytes 66072
  27.5 0.2 pack.2
  27.8 1.7 %collective-permute-start.4 = (bf16[8,6144]{1,0:T(8,128)(2,1)S(1)}, bf16[8,6144]{1,0:T(8,128)(2,1)S(1)}, u32[]{:S(2)}, u32[]{:S(2)}) collective-permute-start(bf16[8,6144]{1,0:T(8,128)(2,1)S(1)} %get-tuple-element.18), channel_id=1, source_target_pairs={{0,8},{8,16},{16,24},{24,0},{1,9},{9,17},{17,25},{25,1},{2,10},{10... | collective-permute-start | bytes 294920 | tf_op jit(solution)/shard_map/ppermute | solution.py:334
  29.4 0.0 collective-permute-done.7.refs_0_
  29.4 0.7 %collective-permute-start.5 = (bf16[8,6144]{1,0:T(8,128)(2,1)S(1)}, bf16[8,6144]{1,0:T(8,128)(2,1)S(1)}, u32[]{:S(2)}, u32[]{:S(2)}) collective-permute-start(bf16[8,6144]{1,0:T(8,128)(2,1)S(1)} %get-tuple-element.19), channel_id=1, source_target_pairs={{0,16},{8,24},{16,0},{24,8},{1,17},{9,25},{17,1},{25,9},{2,18},{10... | collective-permute-start | bytes 294920 | tf_op jit(solution)/shard_map/ppermute | solution.py:334
  30.2 0.0 collective-permute-done.10.refs_3_
  30.2 0.0 collective-permute-start.6
  30.2 0.0 collective-permute-done.9.refs_2_
  30.2 0.0 collective-permute-done.8.refs_1_
  30.2 0.2 pack.3
  30.4 1.9 %collective-permute-start.11 = (bf16[8,6144]{1,0:T(8,128)(2,1)S(1)}, bf16[8,6144]{1,0:T(8,128)(2,1)S(1)}, u32[]{:S(2)}, u32[]{:S(2)}) collective-permute-start(bf16[8,6144]{1,0:T(8,128)(2,1)S(1)} %get-tuple-element.22), channel_id=1, source_target_pairs={{0,8},{8,16},{16,24},{24,0},{1,9},{9,17},{17,25},{25,1},{2,10},{10... | collective-permute-start | bytes 294920 | tf_op jit(solution)/shard_map/ppermute | solution.py:334
  32.3 0.7 %collective-permute-start.12 = (bf16[8,6144]{1,0:T(8,128)(2,1)S(1)}, bf16[8,6144]{1,0:T(8,128)(2,1)S(1)}, u32[]{:S(2)}, u32[]{:S(2)}) collective-permute-start(bf16[8,6144]{1,0:T(8,128)(2,1)S(1)} %get-tuple-element.23), channel_id=1, source_target_pairs={{0,16},{8,24},{16,0},{24,8},{1,17},{9,25},{17,1},{25,9},{2,18},{10... | collective-permute-start | bytes 294920 | tf_op jit(solution)/shard_map/ppermute | solution.py:334
  33.0 0.0 collective-permute-done.4.refs_1_
  33.0 0.3 collective-permute-start.13
  33.3 1.4 %collective-permute-done.5.refs_2_ = bf16[8,6144]{1,0:T(8,128)(2,1)S(1)} collective-permute-done((bf16[8,6144]{1,0:T(8,128)(2,1)S(1)}, bf16[8,6144]{1,0:T(8,128)(2,1)S(1)}, u32[]{:S(2)}, u32[]{:S(2)}) %collective-permute-start.5) | collective-permute-done | bytes 98336 | tf_op jit(solution)/shard_map/ppermute | solution.py:334
  34.7 1.5 %collective-permute-done.6.refs_3_ = bf16[8,6144]{1,0:T(8,128)(2,1)S(1)} collective-permute-done((bf16[8,6144]{1,0:T(8,128)(2,1)S(1)}, bf16[8,6144]{1,0:T(8,128)(2,1)S(1)}, u32[]{:S(2)}, u32[]{:S(2)}) %collective-permute-start.6) | collective-permute-done | bytes 98336 | tf_op jit(solution)/shard_map/ppermute | solution.py:334
  36.2 0.0 collective-permute-done.11.refs_5_
  36.2 2.7 %collective-permute-done.12.refs_6_ = bf16[8,6144]{1,0:T(8,128)(2,1)S(1)} collective-permute-done((bf16[8,6144]{1,0:T(8,128)(2,1)S(1)}, bf16[8,6144]{1,0:T(8,128)(2,1)S(1)}, u32[]{:S(2)}, u32[]{:S(2)}) %collective-permute-start.12) | collective-permute-done | bytes 98336 | tf_op jit(solution)/shard_map/ppermute | solution.py:334
  38.9 0.6 %collective-permute-done.13.refs_7_ = bf16[8,6144]{1,0:T(8,128)(2,1)S(1)} collective-permute-done((bf16[8,6144]{1,0:T(8,128)(2,1)S(1)}, bf16[8,6144]{1,0:T(8,128)(2,1)S(1)}, u32[]{:S(2)}, u32[]{:S(2)}) %collective-permute-start.13) | collective-permute-done | bytes 98336 | tf_op jit(solution)/shard_map/ppermute | solution.py:334
  39.5 11.4 %outer.1 = f32[4096,2048]{1,0:T(8,128)} custom-call(bf16[8,6144]{1,0:T(8,128)(2,1)S(1)} %get-tuple-element.17.refs_0_, bf16[8,6144]{1,0:T(8,128)(2,1)S(1)} %collective-permute-done.4.refs_1_, bf16[8,6144]{1,0:T(8,128)(2,1)S(1)} %collective-permute-done.5.refs_2_, bf16[8,6144]{1,0:T(8,128)(2,1)S(1)} %collective-permute-done.6.refs_3_, ...), custom_call_target="tpu_custom_call" | custom-call | tf_op jit(solution)/shard_map/outer/pallas_call | solution.py:316
Async XLA Ops:
  0.0 8.0 %collective-permute-start = (bf16[1,48,2304]{2,1,0:T(8,128)(2,1)}, bf16[1,48,2304]{2,1,0:T(8,128)(2,1)S(1)}, u32[]{:S(2)}, u32[]{:S(2)}) collective-permute-start(bf16[1,48,2304]{2,1,0:T(8,128)(2,1)} %refs_1_.1), channel_id=1, source_target_pairs={{0,8},{8,16},{16,24},{24,0},{1,9},{9,17},{17,25},{25,1},{2,10},{10... | collective-permute-start | bytes 663560 | tf_op jit(solution)/shard_map/ppermute | solution.py:334
  8.0 0.7 %copy-start.1 = (bf16[1,48,2304]{2,1,0:T(8,128)(2,1)}, bf16[1,48,2304]{2,1,0:T(8,128)(2,1)S(1)}, u32[]{:S(2)}) copy-start(bf16[1,48,2304]{2,1,0:T(8,128)(2,1)S(1)} %collective-permute-done.refs_1_) | copy-start | bytes 663556
  15.1 5.6 %collective-permute-start.3 = (bf16[2,16512]{1,0:T(2,128)(2,1)}, bf16[2,16512]{1,0:T(2,128)(2,1)S(1)}, u32[]{:S(2)}, u32[]{:S(2)}) collective-permute-start(bf16[2,16512]{1,0:T(2,128)(2,1)} %second_pair.1.refs_0_), channel_id=1, source_target_pairs={{0,6},{1,7},{2,0},{3,1},{4,2},{5,3},{6,4},{7,5},{8,14},{9,15},{10,... | collective-permute-start | bytes 198152 | tf_op jit(solution)/shard_map/ppermute | solution.py:334
  18.4 6.8 %collective-permute-start.2 = (bf16[2,16512]{1,0:T(2,128)(2,1)}, bf16[2,16512]{1,0:T(2,128)(2,1)S(1)}, u32[]{:S(2)}, u32[]{:S(2)}) collective-permute-start(bf16[2,16512]{1,0:T(2,128)(2,1)} %second_pair.1.refs_0_), channel_id=1, source_target_pairs={{0,4},{1,5},{2,6},{3,7},{4,0},{5,1},{6,2},{7,3},{8,12},{9,13},{10,... | collective-permute-start | bytes 198152 | tf_op jit(solution)/shard_map/ppermute | solution.py:334
  18.4 8.0 %collective-permute-start.1 = (bf16[2,16512]{1,0:T(2,128)(2,1)}, bf16[2,16512]{1,0:T(2,128)(2,1)S(1)}, u32[]{:S(2)}, u32[]{:S(2)}) collective-permute-start(bf16[2,16512]{1,0:T(2,128)(2,1)} %second_pair.1.refs_0_), channel_id=1, source_target_pairs={{0,2},{1,3},{2,4},{3,5},{4,6},{5,7},{6,0},{7,1},{8,10},{9,11},{10,... | collective-permute-start | bytes 198152 | tf_op jit(solution)/shard_map/ppermute | solution.py:334
  18.9 10.6 %collective-permute-start.7 = (bf16[2,16512]{1,0:T(2,128)(2,1)}, bf16[2,16512]{1,0:T(2,128)(2,1)S(1)}, u32[]{:S(2)}, u32[]{:S(2)}) collective-permute-start(bf16[2,16512]{1,0:T(2,128)(2,1)} %second_pair.1.refs_0_), channel_id=1, source_target_pairs={{0,1},{1,0},{2,3},{3,2},{4,5},{5,4},{6,7},{7,6},{8,9},{9,8},{10,11... | collective-permute-start | bytes 198152 | tf_op jit(solution)/shard_map/ppermute | solution.py:339
  20.6 9.5 %collective-permute-start.10 = (bf16[2,16512]{1,0:T(2,128)(2,1)S(1)}, bf16[2,16512]{1,0:T(2,128)(2,1)S(1)}, u32[]{:S(2)}, u32[]{:S(2)}) collective-permute-start(bf16[2,16512]{1,0:T(2,128)(2,1)S(1)} %collective-permute-done.3.refs_3_), channel_id=1, source_target_pairs={{0,1},{1,0},{2,3},{3,2},{4,5},{5,4},{6,7},{7,6},{8,9},{9,8},{10,11... | collective-permute-start | bytes 198152 | tf_op jit(solution)/shard_map/ppermute | solution.py:339
  25.2 5.0 %collective-permute-start.9 = (bf16[2,16512]{1,0:T(2,128)(2,1)S(1)}, bf16[2,16512]{1,0:T(2,128)(2,1)S(1)}, u32[]{:S(2)}, u32[]{:S(2)}) collective-permute-start(bf16[2,16512]{1,0:T(2,128)(2,1)S(1)} %collective-permute-done.2.refs_2_), channel_id=1, source_target_pairs={{0,1},{1,0},{2,3},{3,2},{4,5},{5,4},{6,7},{7,6},{8,9},{9,8},{10,11... | collective-permute-start | bytes 198152 | tf_op jit(solution)/shard_map/ppermute | solution.py:339
  26.4 3.8 %collective-permute-start.8 = (bf16[2,16512]{1,0:T(2,128)(2,1)S(1)}, bf16[2,16512]{1,0:T(2,128)(2,1)S(1)}, u32[]{:S(2)}, u32[]{:S(2)}) collective-permute-start(bf16[2,16512]{1,0:T(2,128)(2,1)S(1)} %collective-permute-done.1.refs_1_), channel_id=1, source_target_pairs={{0,1},{1,0},{2,3},{3,2},{4,5},{5,4},{6,7},{7,6},{8,9},{9,8},{10,11... | collective-permute-start | bytes 198152 | tf_op jit(solution)/shard_map/ppermute | solution.py:339
  26.7 0.9 %copy-start = (bf16[2,16512]{1,0:T(2,128)(2,1)S(1)}, bf16[2,16512]{1,0:T(2,128)(2,1)}, u32[]{:S(2)}) copy-start(bf16[2,16512]{1,0:T(2,128)(2,1)} %second_pair.1.refs_0_) | copy-start | bytes 198148
  27.8 5.2 %collective-permute-start.4 = (bf16[8,6144]{1,0:T(8,128)(2,1)S(1)}, bf16[8,6144]{1,0:T(8,128)(2,1)S(1)}, u32[]{:S(2)}, u32[]{:S(2)}) collective-permute-start(bf16[8,6144]{1,0:T(8,128)(2,1)S(1)} %get-tuple-element.18), channel_id=1, source_target_pairs={{0,8},{8,16},{16,24},{24,0},{1,9},{9,17},{17,25},{25,1},{2,10},{10... | collective-permute-start | bytes 294920 | tf_op jit(solution)/shard_map/ppermute | solution.py:334
  29.4 5.2 %collective-permute-start.5 = (bf16[8,6144]{1,0:T(8,128)(2,1)S(1)}, bf16[8,6144]{1,0:T(8,128)(2,1)S(1)}, u32[]{:S(2)}, u32[]{:S(2)}) collective-permute-start(bf16[8,6144]{1,0:T(8,128)(2,1)S(1)} %get-tuple-element.19), channel_id=1, source_target_pairs={{0,16},{8,24},{16,0},{24,8},{1,17},{9,25},{17,1},{25,9},{2,18},{10... | collective-permute-start | bytes 294920 | tf_op jit(solution)/shard_map/ppermute | solution.py:334
  30.2 6.1 %collective-permute-start.6 = (bf16[8,6144]{1,0:T(8,128)(2,1)S(1)}, bf16[8,6144]{1,0:T(8,128)(2,1)S(1)}, u32[]{:S(2)}, u32[]{:S(2)}) collective-permute-start(bf16[8,6144]{1,0:T(8,128)(2,1)S(1)} %get-tuple-element.20), channel_id=1, source_target_pairs={{0,24},{8,0},{16,8},{24,16},{1,25},{9,1},{17,9},{25,17},{2,26},{10... | collective-permute-start | bytes 294920 | tf_op jit(solution)/shard_map/ppermute | solution.py:334
  30.4 5.8 %collective-permute-start.11 = (bf16[8,6144]{1,0:T(8,128)(2,1)S(1)}, bf16[8,6144]{1,0:T(8,128)(2,1)S(1)}, u32[]{:S(2)}, u32[]{:S(2)}) collective-permute-start(bf16[8,6144]{1,0:T(8,128)(2,1)S(1)} %get-tuple-element.22), channel_id=1, source_target_pairs={{0,8},{8,16},{16,24},{24,0},{1,9},{9,17},{17,25},{25,1},{2,10},{10... | collective-permute-start | bytes 294920 | tf_op jit(solution)/shard_map/ppermute | solution.py:334
  32.3 6.6 %collective-permute-start.12 = (bf16[8,6144]{1,0:T(8,128)(2,1)S(1)}, bf16[8,6144]{1,0:T(8,128)(2,1)S(1)}, u32[]{:S(2)}, u32[]{:S(2)}) collective-permute-start(bf16[8,6144]{1,0:T(8,128)(2,1)S(1)} %get-tuple-element.23), channel_id=1, source_target_pairs={{0,16},{8,24},{16,0},{24,8},{1,17},{9,25},{17,1},{25,9},{2,18},{10... | collective-permute-start | bytes 294920 | tf_op jit(solution)/shard_map/ppermute | solution.py:334
  33.0 6.5 %collective-permute-start.13 = (bf16[8,6144]{1,0:T(8,128)(2,1)S(1)}, bf16[8,6144]{1,0:T(8,128)(2,1)S(1)}, u32[]{:S(2)}, u32[]{:S(2)}) collective-permute-start(bf16[8,6144]{1,0:T(8,128)(2,1)S(1)} %get-tuple-element.24), channel_id=1, source_target_pairs={{0,24},{8,0},{16,8},{24,16},{1,25},{9,1},{17,9},{25,17},{2,26},{10... | collective-permute-start | bytes 294920 | tf_op jit(solution)/shard_map/ppermute | solution.py:334

commit v3 on v0

v3 whole, which is shorter than its diff:
```python
import functools
import math

import jax
import jax.numpy as jnp
import ml_dtypes
import numpy as np
from jax import lax
from jax.experimental import pallas as pl
from jax.experimental.pallas import tpu as pltpu
from jax.sharding import PartitionSpec as P

GMAX = 18
STEPS = 2
RADIX = 6
SPAN = 2 * GMAX + 1
KX_ROWS = 40
LANES = 128
OMEGA_SQUARED = 0.0625
TILE = 512
VMEM_LIMIT = 40 * 2**20


def split(values, count):
    parts = []
    for _ in range(count):
        parts.append(values.astype(ml_dtypes.bfloat16))
        values = values - parts[-1].astype(np.float64)
    return parts


def table_rows(grid):
    width = (grid // RADIX) * grid
    x_first = 4 * width
    twiddle_first = x_first + 2 * KX_ROWS
    return width, x_first, twiddle_first


def packed_tables(grid):
    turn = 2.0 * np.pi / grid
    width, _, _ = table_rows(grid)
    y_lo = np.arange(width) // grid
    z = np.arange(width) % grid

    column = np.arange((2 * GMAX // RADIX + 1) * GMAX)
    q = column // GMAX - GMAX // RADIX
    kz = column % GMAX + 1
    phase = (RADIX * q[None, :] * y_lo[:, None] + kz[None, :] * z[:, None]) % grid
    last = np.zeros((2 * width, LANES))
    last[:width, : column.size] = np.cos(turn * phase)
    last[width:, : column.size] = -np.sin(turn * phase)
    pieces = split(last, 2)

    kx = np.arange(SPAN) - GMAX
    angle = turn * (kx[:, None] * np.arange(grid)[None, :] % grid)
    x_table = np.zeros((2 * KX_ROWS, grid))
    x_table[:SPAN] = np.cos(angle)
    x_table[KX_ROWS : KX_ROWS + SPAN] = -np.sin(angle)
    x_table = np.concatenate(split(x_table, 2), axis=1)
    pieces.append(np.pad(x_table, ((0, 0), (0, LANES - 2 * grid))))

    angle = turn * (np.arange(RADIX)[:, None] * y_lo[None, :] % grid)
    twiddle = np.zeros((16, width))
    twiddle[:RADIX] = np.cos(angle)
    twiddle[RADIX : 2 * RADIX] = -np.sin(angle)
    for part in split(twiddle, 3):
        pieces += [part[:, first : first + LANES] for first in range(0, width, LANES)]
    return np.concatenate(pieces, axis=0)


def dft_six(re, im):
    half = 0.5
    root = math.sqrt(3.0) / 2.0
    s_re = [re[h] + re[h + 3] for h in range(3)]
    s_im = [im[h] + im[h + 3] for h in range(3)]
    d_re = [re[h] - re[h + 3] for h in range(3)]
    d_im = [im[h] - im[h + 3] for h in range(3)]
    out = [None] * 6
    sum_re, sum_im = s_re[1] + s_re[2], s_im[1] + s_im[2]
    dif_re, dif_im = (s_re[1] - s_re[2]) * root, (s_im[1] - s_im[2]) * root
    out[0] = (s_re[0] + sum_re, s_im[0] + sum_im)
    mid_re, mid_im = s_re[0] - half * sum_re, s_im[0] - half * sum_im
    out[2] = (mid_re + dif_im, mid_im - dif_re)
    out[4] = (mid_re - dif_im, mid_im + dif_re)
    sum_re, sum_im = (d_re[1] + d_re[2]) * root, (d_im[1] + d_im[2]) * root
    dif_re, dif_im = d_re[1] - d_re[2], d_im[1] - d_im[2]
    out[3] = (d_re[0] - dif_re, d_im[0] - dif_im)
    mid_re, mid_im = d_re[0] + half * dif_re, d_im[0] + half * dif_im
    out[1] = (mid_re + sum_im, mid_im - sum_re)
    out[5] = (mid_re - sum_im, mid_im + sum_re)
    return out


def dot(a, b):
    return jnp.dot(a, b, preferred_element_type=jnp.float32)


def own_place():
    return lax.axis_index("row"), lax.axis_index("col")


def spectrum_of(grid, cond, occ, table_ref):
    norm = np.float32(grid ** (-1.5))
    width, x_first, twiddle_first = table_rows(grid)
    density = (cond.astype(jnp.float32) * occ.astype(jnp.float32)).astype(jnp.bfloat16)
    x_table = table_ref[x_first:twiddle_first, : 2 * grid]
    section = dot(x_table, jnp.concatenate([density, density], axis=0))
    re = [section[:KX_ROWS, h * width : (h + 1) * width] for h in range(RADIX)]
    im = [section[KX_ROWS:, h * width : (h + 1) * width] for h in range(RADIX)]
    chunks = width // LANES
    twiddle = 0.0
    for part in range(3):
        first = twiddle_first + 16 * chunks * part
        whole = [table_ref[first + 16 * i : first + 16 * (i + 1), :].astype(jnp.float32) for i in range(chunks)]
        twiddle = twiddle + jnp.concatenate(whole, axis=1)
    rows = []
    for residue, (d_re, d_im) in enumerate(dft_six(re, im)):
        if residue > 0:
            t_re = twiddle[residue : residue + 1, :]
            t_im = twiddle[RADIX + residue : RADIX + residue + 1, :]
            d_re, d_im = d_re * t_re - d_im * t_im, d_re * t_im + d_im * t_re
        rows.append(jnp.concatenate([d_re, d_im], axis=1))
    whole = jnp.concatenate(rows, axis=0)
    whole_hi = whole.astype(jnp.bfloat16)
    whole_lo = (whole - whole_hi.astype(jnp.float32)).astype(jnp.bfloat16)

    def rotation(first):
        cos_part = table_ref[first : first + width, :]
        sin_part = table_ref[first + width : first + 2 * width, :]
        upper = jnp.concatenate([cos_part, sin_part], axis=1)
        return jnp.concatenate([upper, jnp.concatenate([-sin_part, cos_part], axis=1)], axis=0)

    upper, lower = rotation(0), rotation(2 * width)
    spectrum = (dot(whole_hi, upper) + dot(whole_lo, upper) + dot(whole_hi, lower)) * norm
    parts = []
    for side in range(2):
        own = spectrum[:, side * LANES : (side + 1) * LANES]
        for group in range(RADIX // 2):
            first = 2 * group * KX_ROWS
            parts.append(jnp.concatenate([own[first : first + KX_ROWS], own[first + KX_ROWS : first + 2 * KX_ROWS]], axis=1))
    return jnp.concatenate(parts, axis=0).astype(jnp.bfloat16)


def pair_weight(step, levels_ref):
    rows, cols = lax.axis_size("row"), lax.axis_size("col")
    r, c = own_place()
    devices = rows * cols
    band = r * cols + c
    slot = lax.rem(band - step * cols + devices, devices)
    lane = lax.broadcasted_iota(jnp.int32, (1, levels_ref.shape[1]), 1)

    def at(line, chosen):
        return jnp.sum(jnp.where(chosen, levels_ref[line : line + 1, :], 0.0), axis=1, keepdims=True)

    occ_band = at(2, lane == slot).astype(jnp.int32)
    gap = at(0, lane == band) - at(1, lane == occ_band)
    gap = jnp.broadcast_to(gap, (1, LANES))
    return -4.0 * gap / (gap * gap + OMEGA_SQUARED) / (devices * STEPS)


def first_kernel(grid, orbitals_ref, table_ref, levels_ref, sphere_ref, cube_ref, weight_ref, places_ref, table_out):
    half = grid // 2
    sx, sy, kz = sphere_ref[0:1, :], sphere_ref[1:2, :], sphere_ref[2:3, :]
    kx = jnp.where(sx >= half, sx - grid, sx) + GMAX
    ky = jnp.where(sy >= half, sy - grid, sy) + GMAX
    q = (ky * 43) >> 8
    residue = ky - q * RADIX
    places_ref[0:1, :] = (residue & 1) * LANES + q * GMAX + kz - 1
    places_ref[1:2, :] = (residue >> 1) * KX_ROWS + kx
    table_out[...] = table_ref[...]
    cube_ref[...] = spectrum_of(grid, orbitals_ref[0], orbitals_ref[1], table_ref)
    for step in range(STEPS):
        weight_ref[step : step + 1, :] = pair_weight(step, levels_ref)


def pick(cube_ref, places_ref, coef_ref):
    groups = RADIX // 2 * KX_ROWS // 8
    half_count = places_ref.shape[1]
    counted = lax.broadcasted_iota(jnp.int32, (2 * LANES, TILE), 0).astype(jnp.float32).astype(jnp.bfloat16)
    line = lax.broadcasted_iota(jnp.int32, (8, TILE), 0)
    for first in range(0, half_count, TILE):
        here = slice(first, first + TILE)
        lane = places_ref[0:1, here].astype(jnp.float32).astype(jnp.bfloat16)
        row = places_ref[1:2, here]
        one_hot = jnp.where(counted == lane, jnp.bfloat16(1), jnp.bfloat16(0))
        found = dot(cube_ref[...], one_hot)
        away = line - row
        values = [jnp.zeros((8, TILE), jnp.float32)] * 4
        for group in range(groups):
            chosen = away == -8 * group
            for which in range(4):
                start = (which * groups + group) * 8
                values[which] = jnp.where(chosen, found[start : start + 8], values[which])
        for which in range(4):
            pair, side = divmod(which, 2)
            value = jnp.sum(values[which], axis=0, keepdims=True)
            coef_ref[pair : pair + 1, side * half_count + first : side * half_count + first + TILE] = value


def second_kernel(grid, plan, orbitals_ref, occ_ref, first_ref, weight_ref, places_ref, table_ref, *refs):
    outs, coef_ref, cube_ref = refs[:-2], refs[-2], refs[-1]
    rows, cols, groups, row_width, group_width = plan
    r, _ = own_place()
    picks = RADIX * KX_ROWS
    cube_ref[:picks, :] = first_ref[...]
    cube_ref[picks:, :] = spectrum_of(grid, orbitals_ref[0], occ_ref[0], table_ref)
    pick(cube_ref, places_ref, coef_ref)
    weight = weight_ref[:, :1]
    for k, out_ref in enumerate(outs):
        block = lax.rem(r + k, rows)
        group = lax.rem(block, groups)
        start = pl.multiple_of(block * row_width, LANES)
        out_ref[:, :row_width] = coef_ref[:, pl.ds(start, row_width)].astype(jnp.bfloat16)
        for c in range(cols):
            start = pl.multiple_of((c * groups + group) * group_width, LANES)
            part = weight * coef_ref[:, pl.ds(start, group_width)]
            out_ref[:, row_width + c * group_width : row_width + (c + 1) * group_width] = part.astype(jnp.bfloat16)


def cost(flops, data):
    return pl.CostEstimate(flops=flops, bytes_accessed=data, transcendentals=0)


def in_vmem(count):
    return [pl.BlockSpec(memory_space=pltpu.VMEM)] * count


def transform(cond_orbitals, occ_orbitals, occ_second, sphere_index, levels, plan):
    rows, cols, groups, row_width, group_width = plan
    grid = cond_orbitals.shape[1]
    table = jnp.asarray(packed_tables(grid))
    orbitals = jnp.concatenate([cond_orbitals, occ_orbitals], axis=0)
    picks = RADIX * KX_ROWS
    params = dict(
        compiler_params=pltpu.CompilerParams(vmem_limit_bytes=VMEM_LIMIT),
        cost_estimate=cost(2 * 10**9, 2 * 10**6),
    )
    handed = pl.pallas_call(
        functools.partial(first_kernel, grid),
        out_shape=[
            jax.ShapeDtypeStruct((picks, 2 * LANES), jnp.bfloat16),
            jax.ShapeDtypeStruct((STEPS, LANES), jnp.float32),
            jax.ShapeDtypeStruct((2, sphere_index.shape[1]), jnp.int32),
            jax.ShapeDtypeStruct(table.shape, table.dtype),
        ],
        in_specs=in_vmem(4),
        out_specs=in_vmem(4),
        name="first_pair",
        **params,
    )(orbitals, table, levels, sphere_index)
    message = jax.ShapeDtypeStruct((STEPS, row_width + cols * group_width), jnp.bfloat16)
    return pl.pallas_call(
        functools.partial(second_kernel, grid, plan),
        out_shape=[message] * rows,
        in_specs=in_vmem(6),
        out_specs=in_vmem(rows),
        scratch_shapes=[
            pltpu.VMEM((STEPS, 2 * sphere_index.shape[1]), jnp.float32),
            pltpu.VMEM((STEPS * picks, 2 * LANES), jnp.bfloat16),
        ],
        name="second_pair",
        **params,
    )(orbitals, occ_second, *handed)


def pack_kernel(plan, *refs):
    rows, cols, groups, row_width, group_width = plan
    arrived, outs, staged_ref, mixed_ref = refs[:rows], refs[rows:-2], refs[-2], refs[-1]
    r, c = own_place()
    for k, ref in enumerate(arrived):
        staged_ref[lax.rem(r - k + rows, rows)] = ref[...].astype(jnp.float32)
    for block in range(rows):
        mixed_ref[STEPS * block : STEPS * (block + 1), :] = staged_ref[block]
    for k, out_ref in enumerate(outs):
        out_ref[:, :row_width] = mixed_ref[:, :row_width].astype(jnp.bfloat16)
        z = lax.rem(c // 2 + k, cols // 2)
        start = pl.multiple_of(row_width + z * (2 * group_width), LANES)
        out_ref[:, row_width:] = mixed_ref[:, pl.ds(start, 2 * group_width)].astype(jnp.bfloat16)


def pack(arrived, plan):
    rows, cols, groups, row_width, group_width = plan
    message = jax.ShapeDtypeStruct((rows * STEPS, row_width + 2 * group_width), jnp.bfloat16)
    width = arrived[0].shape[1]
    return pl.pallas_call(
        functools.partial(pack_kernel, plan),
        out_shape=[message] * (cols // 2),
        in_specs=in_vmem(rows),
        out_specs=in_vmem(cols // 2),
        scratch_shapes=[pltpu.VMEM((rows, STEPS, width), jnp.float32), pltpu.VMEM((rows * STEPS, width), jnp.float32)],
        compiler_params=pltpu.CompilerParams(vmem_limit_bytes=VMEM_LIMIT),
        cost_estimate=cost(10**9, 10**6),
        name="pack",
    )(*arrived)


def stacked(refs, lanes):
    return jnp.concatenate([ref[:, lanes].astype(jnp.float32) for ref in refs], axis=0).astype(jnp.bfloat16)


def column_kernel(plan, *refs):
    rows, cols, groups, row_width, group_width = plan
    messages, out_ref = refs[:-1], refs[-1]
    _, c = own_place()
    start = pl.multiple_of(row_width + (c & 1) * group_width, LANES)
    out_ref[...] = stacked(messages, pl.ds(start, group_width))


def own_columns(messages, plan):
    rows, cols, groups, row_width, group_width = plan
    return pl.pallas_call(
        functools.partial(column_kernel, plan),
        out_shape=jax.ShapeDtypeStruct((cols * rows * STEPS, group_width), jnp.bfloat16),
        in_specs=in_vmem(cols),
        out_specs=in_vmem(1)[0],
        compiler_params=pltpu.CompilerParams(vmem_limit_bytes=VMEM_LIMIT),
        cost_estimate=cost(10**6, 10**5),
        name="own_columns",
    )(*messages)


def write_products(left_ref, right, out_ref, held_ref, sems, places, block, slots, group_width):
    count = left_ref.shape[1] // block

    def copies(i, slot):
        rows = pl.ds(pl.multiple_of(i * block, block), block)
        return [
            pltpu.make_async_copy(
                held_ref.at[slot, :, pl.ds(j * group_width, group_width)],
                out_ref.at[rows, pl.ds(place, group_width)],
                sems.at[slot, j],
            )
            for j, place in enumerate(places)
        ]

    def step(i, carry):
        slot = lax.rem(i, slots)

        @pl.when(i >= slots)
        def _():
            for copy in copies(i - slots, slot):
                copy.wait()

        here = pl.ds(pl.multiple_of(i * block, block), block)
        held_ref[slot] = lax.dot_general(left_ref[:, here], right[...], (((0,), (0,)), ((), ())), preferred_element_type=jnp.float32)
        for copy in copies(i, slot):
            copy.start()
        return carry

    lax.fori_loop(0, count, step, 0)
    for i in range(max(0, count - slots), count):
        for copy in copies(i, i % slots):
            copy.wait()


def first_outer_kernel(plan, block, slots, *refs):
    rows, cols, groups, row_width, group_width = plan
    messages, (columns_ref, out_ref, left_ref, held_ref, sems) = refs[:cols], refs[cols:]
    r, _ = own_place()
    left_ref[...] = stacked(messages, slice(0, row_width))
    place = pl.multiple_of(lax.rem(r, groups) * group_width, LANES)
    write_products(left_ref, columns_ref, out_ref, held_ref, sems, [place], block, slots, group_width)


def second_outer_kernel(plan, block, slots, *refs):
    rows, cols, groups, row_width, group_width = plan
    arrived, (left_ref, _, out_ref, right_ref, held_ref, sems) = refs[: groups - 1], refs[groups - 1 :]
    r, _ = own_place()
    places = []
    for j, ref in enumerate(arrived):
        right_ref[:, j * group_width : (j + 1) * group_width] = ref[...]
        places.append(pl.multiple_of(lax.rem(lax.rem(r, groups) - j - 1 + groups, groups) * group_width, LANES))
    write_products(left_ref, right_ref, out_ref, held_ref, sems, places, block, slots, group_width)


def outer(messages, columns, arrived, plan):
    rows, cols, groups, row_width, group_width = plan
    depth = columns.shape[0]
    hbm = pl.BlockSpec(memory_space=pltpu.HBM)
    tile = jax.ShapeDtypeStruct((row_width, groups * group_width), jnp.float32)

    def shapes(block, width, copies):
        slots = min(4, row_width // block)
        return slots, [pltpu.VMEM((slots, block, width), jnp.float32), pltpu.SemaphoreType.DMA((slots, copies))]

    block = min(512, row_width)
    slots, scratch = shapes(block, group_width, 1)
    part, left = pl.pallas_call(
        functools.partial(first_outer_kernel, plan, block, slots),
        out_shape=[tile, jax.ShapeDtypeStruct((depth, row_width), jnp.bfloat16)],
        in_specs=in_vmem(cols + 1),
        out_specs=[hbm] + in_vmem(1),
        scratch_shapes=scratch,
        compiler_params=pltpu.CompilerParams(vmem_limit_bytes=VMEM_LIMIT),
        cost_estimate=cost(4 * 10**9, 10**7),
        name="own_outer",
    )(*messages, columns)
    block = min(256, row_width)
    width = (groups - 1) * group_width
    slots, scratch = shapes(block, width, groups - 1)
    return pl.pallas_call(
        functools.partial(second_outer_kernel, plan, block, slots),
        out_shape=tile,
        in_specs=in_vmem(groups) + [hbm],
        out_specs=hbm,
        input_output_aliases={groups: 0},
        scratch_shapes=[pltpu.VMEM((depth, width), jnp.bfloat16)] + scratch,
        compiler_params=pltpu.CompilerParams(vmem_limit_bytes=VMEM_LIMIT),
        cost_estimate=cost(10**10, 3 * 10**7),
        name="other_outer",
    )(*arrived, left, part)


def shifted(value, axis, by, within=None):
    devices = lax.axis_size(axis)
    within = within or devices
    return lax.ppermute(value, axis, [(i, i // within * within + (i + by) % within) for i in range(devices)])


def swapped(value, axis):
    devices = lax.axis_size(axis)
    return lax.ppermute(value, axis, [(i, i ^ 1) for i in range(devices)])


def on_device(cond_orbitals, occ_orbitals, cond_energy, occ_energy, occ_band, sphere_index):
    rows = lax.axis_size("row")
    cols = lax.axis_size("col")
    entries = 2 * sphere_index.shape[1]
    groups = rows
    while groups > 1 and (rows % groups or entries // cols % (groups * LANES)):
        groups -= 1
    plan = (rows, cols, groups, entries // rows, entries // cols // groups)
    occ_second = shifted(occ_orbitals, "row", 1)
    levels = jnp.stack([cond_energy, occ_energy, occ_band.astype(jnp.float32)])
    sent = transform(cond_orbitals, occ_orbitals, occ_second, sphere_index, levels, plan)
    packed = pack([sent[0]] + [shifted(sent[k], "row", k) for k in range(1, rows)], plan)
    messages = [packed[0]] + [shifted(packed[k], "col", 2 * k) for k in range(1, cols // 2)]
    messages += [swapped(value, "col") for value in messages]
    columns = own_columns(messages, plan)
    arrived = [shifted(columns, "row", k, groups) for k in range(1, groups)]
    return outer(messages, columns, arrived, plan)


def solution(mesh):
    placed = (P(("row", "col"), None, None), P(("row", "col"), None, None), P(), P(), P(), P())
    return jax.shard_map(
        on_device, mesh=mesh, in_specs=placed, out_specs=P("row", "col"), check_vma=False
    )
```

time: 314 us -> 47.5 us (0.15)
  local copies, waits for them, and re-layouts: 141 us -> 3.82 us
  other arithmetic: 95.5 us -> 1.34 us
  blocking collectives: 38.5 us -> 0 us
  matrix products: 22.5 us -> 0 us
  Pallas kernels: 0 us -> 16.9 us
  waiting for transfers between devices: 0.99 us -> 10.7 us
    unnamed x1 -> x0, other arithmetic: 91 us -> none
    gather x4 -> x0, local copies, waits for them, and re-layouts: 70.9 us -> none  [transform(): jnp.take(flat_parts, cube_index, axis=2).reshape(batch_size, -1)]
    all_gather x2 -> x0, blocking collectives: 38.5 us -> none  [the longest x1 25.1 us: on_device(): row_panel = lax.all_gather(row_blocks, 'col', axis=1, tiled=True)]
    dot_general x9 -> x0, matrix products: 22.5 us -> none  [the longest x1 14.1 us: on_device(): jnp.einsum('kpg,kph->gh', row_panel, col_panel, preferred_element_type=jn...]
    pallas_call x0 -> x6, Pallas kernels: none -> 16.9 us  [the longest x1 8.84 us: outer(): pl.pallas_call(functools.partial(second_outer_kernel, plan, block, slots)...]
    unnamed x23 -> x5, local copies, waits for them, and re-layouts: 19.6 us -> 2.87 us
    reshape x4 -> x0, local copies, waits for them, and re-layouts: 15.5 us -> none  [transform(): flat_parts = section_three.reshape(batch_size, 2, -1)]
    all_to_all x2 -> x0, local copies, waits for them, and re-layouts: 15.4 us -> none  [on_device(): lax.all_to_all(coefficients[None], 'row', split_axis=2, concat_axis=0, ti...]
  transfers between devices with their start and end apart: 3 -> 14, of which waited for: 1 -> 6; matrix products, arithmetic and copies ran while one was open for 27% -> 7% of each run, Pallas kernels for 0% -> 10%
where the time goes in v3:
time: 47.5 us; the launch traced here: 47.3 us
  Pallas kernels  16.9 us (36%)
  starting transfers between devices  14.3 us (30%)
  waiting for transfers between devices  10.7 us (23%)
  local copies, waits for them, and re-layouts  3.82 us (8%)
  other arithmetic  1.34 us (3%)
    ppermute x10, starting transfers between devices, shifted(): lax.ppermute(value, axis, [(i, i // within * within + (i + by) % within)...  10.7 us
    pallas_call x1, Pallas kernels, outer(): pl.pallas_call(functools.partial(second_outer_kernel, plan, block, slots)...  8.84 us
    ppermute x10, waiting for transfers between devices, shifted(): lax.ppermute(value, axis, [(i, i // within * within + (i + by) % within)...  6.54 us
    ppermute x4, waiting for transfers between devices, swapped(): return lax.ppermute(value, axis, [(i, i ^ 1) for i in range(devices)])  4.2 us
    pallas_call x1, Pallas kernels, outer(): pl.pallas_call(functools.partial(first_outer_kernel, plan, block, slots),...  3.68 us
    ppermute x4, starting transfers between devices, swapped(): return lax.ppermute(value, axis, [(i, i ^ 1) for i in range(devices)])  3.62 us
    pallas_call x1, Pallas kernels, transform(): pl.pallas_call(functools.partial(second_kernel, grid, plan), out_shape=[m...  3.41 us
    unnamed x5, local copies, waits for them, and re-layouts  2.87 us
  transfers between devices with their start and end apart: 14, of which 6 were waited for; matrix products, arithmetic and copies ran while one was open for 7% of the time, Pallas kernels for 10%

profile of v3, /device:TPU:1, one launch (start us, length us, event | category | flops | bytes accessed | tf_op | source)
XLA Modules:
  0.0 47.3 jit_solution(5427014900123226515)
XLA Ops:
  0.0 2.6 %collective-permute-start = (bf16[1,48,2304]{2,1,0:T(8,128)(2,1)}, bf16[1,48,2304]{2,1,0:T(8,128)(2,1)S(1)}, u32[]{:S(2)}, u32[]{:S(2)}) collective-permute-start(bf16[1,48,2304]{2,1,0:T(8,128)(2,1)} %param.8), channel_id=1, source_target_pairs={{0,8},{8,16},{16,24},{24,0},{1,9},{9,17},{17,25},{25,1},{2,10},{10... | collective-permute-start | bytes 663560 | tf_op jit(solution)/shard_map/ppermute | solution.py:417
  2.6 0.7 %convert_bitcast_fusion = f32[1,32]{1,0:T(1,128)S(1)} fusion(s32[32]{0:T(128)} %param.11), kind=kLoop, calls=%fused_computation.3 | loop fusion | flops 32 | bytes 256 | tf_op jit(solution)/shard_map/stack | solution.py:434
  3.3 0.9 %constant_dynamic-update-slice_fusion.1 = bf16[2,48,2304]{2,1,0:T(8,128)(2,1)S(1)} fusion(bf16[1,48,2304]{2,1,0:T(8,128)(2,1)} %param.7), kind=kLoop, calls=%fused_computation.1 | loop fusion | bytes 442368
  4.2 1.0 %constant_dynamic-update-slice_fusion.orbitals_ref = bf16[2,48,2304]{2,1,0:T(8,128)(2,1)S(1)} fusion(bf16[2,48,2304]{2,1,0:T(8,128)(2,1)S(1)} %constant_dynamic-update-slice_fusion.1, bf16[1,48,2304]{2,1,0:T(8,128)(2,1)} %param.8), kind=kLoop, calls=%fused_computation | loop fusion | bytes 442368 | tf_op jit(solution)/shard_map/concatenate | solution.py:232
  5.2 0.7 %pad_maximum_fusion.levels_ref = f32[3,32]{1,0:T(4,128)S(1)} fusion(f32[1,32]{1,0:T(1,128)S(1)} %convert_bitcast_fusion, f32[1,32]{1,0:T(1,128)} %bitcast.4, f32[1,32]{1,0:T(1,128)} %bitcast.5), kind=kLoop, calls=%fused_computation.2 | loop fusion | flops 192 | bytes 768 | tf_op jit(solution)/shard_map/stack | solution.py:434
  5.9 0.0 copy-start
  5.9 0.9 %copy-done = s32[3,8192]{1,0:T(4,128)S(1)} copy-done((s32[3,8192]{1,0:T(4,128)S(1)}, s32[3,8192]{1,0:T(4,128)}, u32[]{:S(2)}) %copy-start) | copy-done | bytes 98328
  6.8 0.0 copy-start.1
  6.8 1.0 %copy-done.1 = bf16[1760,128]{1,0:T(8,128)(2,1)S(1)} copy-done((bf16[1760,128]{1,0:T(8,128)(2,1)S(1)}, bf16[1760,128]{1,0:T(8,128)(2,1)}, u32[]{:S(2)}) %copy-start.1) | copy-done | bytes 450584
  7.8 0.9 %first_pair.1 = (bf16[240,256]{1,0:T(8,128)(2,1)S(1)}, f32[2,128]{1,0:T(2,128)S(1)}, s32[2,8192]{1,0:T(2,128)S(1)}, bf16[1760,128]{1,0:T(8,128)(2,1)S(1)}) custom-call(bf16[2,48,2304]{2,1,0:T(8,128)(2,1)S(1)} %constant_dynamic-update-slice_fusion.orbitals_ref, bf16[1760,128]{1,0:T(8,128)(2,1)S(1)} %copy-done.1, f32[3,32]{1,0:T(4,128)S(1)} %pad_maximum_fusion.levels_ref, ...), custom_call_target="tpu_custom_call" | custom-call | flops 2000000000 | bytes 2000000 | tf_op jit(solution)/shard_map/first_pair/pallas_call | solution.py:238
  8.7 0.0 collective-permute-done.occ_ref
  8.7 3.4 %second_pair.1 = (bf16[2,8192]{1,0:T(2,128)(2,1)S(1)}, bf16[2,8192]{1,0:T(2,128)(2,1)S(1)}, bf16[2,8192]{1,0:T(2,128)(2,1)S(1)}, bf16[2,8192]{1,0:T(2,128)(2,1)S(1)}) custom-call(bf16[2,48,2304]{2,1,0:T(8,128)(2,1)S(1)} %constant_dynamic-update-slice_fusion.orbitals_ref, bf16[1,48,2304]{2,1,0:T(8,128)(2,1)S(1)} %collective-permute-done.occ_ref, ...), custom_call_target="tpu_custom_call" | custom-call | flops 2000000000 | bytes 2000000 | tf_op jit(solution)/shard_map/second_pair/pallas_call | solution.py:252
  12.1 0.1 collective-permute-start.1
  12.2 0.1 collective-permute-start.2
  12.3 0.4 collective-permute-start.3
  12.7 0.7 %collective-permute-done.1.refs_1_ = bf16[2,8192]{1,0:T(2,128)(2,1)S(1)} collective-permute-done((bf16[2,8192]{1,0:T(2,128)(2,1)S(1)}, bf16[2,8192]{1,0:T(2,128)(2,1)S(1)}, u32[]{:S(2)}, u32[]{:S(2)}) %collective-permute-start.1) | collective-permute-done | bytes 32800 | tf_op jit(solution)/shard_map/ppermute | solution.py:417
  13.4 1.6 %collective-permute-done.2.refs_2_ = bf16[2,8192]{1,0:T(2,128)(2,1)S(1)} collective-permute-done((bf16[2,8192]{1,0:T(2,128)(2,1)S(1)}, bf16[2,8192]{1,0:T(2,128)(2,1)S(1)}, u32[]{:S(2)}, u32[]{:S(2)}) %collective-permute-start.2) | collective-permute-done | bytes 32800 | tf_op jit(solution)/shard_map/ppermute | solution.py:417
  15.0 1.2 %collective-permute-done.3.refs_3_ = bf16[2,8192]{1,0:T(2,128)(2,1)S(1)} collective-permute-done((bf16[2,8192]{1,0:T(2,128)(2,1)S(1)}, bf16[2,8192]{1,0:T(2,128)(2,1)S(1)}, u32[]{:S(2)}, u32[]{:S(2)}) %collective-permute-start.3) | collective-permute-done | bytes 32800 | tf_op jit(solution)/shard_map/ppermute | solution.py:417
  16.2 0.1 pack.1
  16.4 1.4 %collective-permute-start.4 = (bf16[8,5120]{1,0:T(8,128)(2,1)S(1)}, bf16[8,5120]{1,0:T(8,128)(2,1)S(1)}, u32[]{:S(2)}, u32[]{:S(2)}) collective-permute-start(bf16[8,5120]{1,0:T(8,128)(2,1)S(1)} %get-tuple-element.28), channel_id=1, source_target_pairs={{0,2},{1,3},{2,4},{3,5},{4,6},{5,7},{6,0},{7,1},{8,10},{9,11},{10,... | collective-permute-start | bytes 245768 | tf_op jit(solution)/shard_map/ppermute | solution.py:417
  17.7 2.3 %collective-permute-start.5 = (bf16[8,5120]{1,0:T(8,128)(2,1)S(1)}, bf16[8,5120]{1,0:T(8,128)(2,1)S(1)}, u32[]{:S(2)}, u32[]{:S(2)}) collective-permute-start(bf16[8,5120]{1,0:T(8,128)(2,1)S(1)} %get-tuple-element.29), channel_id=1, source_target_pairs={{0,4},{1,5},{2,6},{3,7},{4,0},{5,1},{6,2},{7,3},{8,12},{9,13},{10,... | collective-permute-start | bytes 245768 | tf_op jit(solution)/shard_map/ppermute | solution.py:417
  20.1 1.1 %collective-permute-start.6 = (bf16[8,5120]{1,0:T(8,128)(2,1)S(1)}, bf16[8,5120]{1,0:T(8,128)(2,1)S(1)}, u32[]{:S(2)}, u32[]{:S(2)}) collective-permute-start(bf16[8,5120]{1,0:T(8,128)(2,1)S(1)} %get-tuple-element.30), channel_id=1, source_target_pairs={{0,6},{1,7},{2,0},{3,1},{4,2},{5,3},{6,4},{7,5},{8,14},{9,15},{10,... | collective-permute-start | bytes 245768 | tf_op jit(solution)/shard_map/ppermute | solution.py:417
  21.1 1.2 %collective-permute-start.7 = (bf16[8,5120]{1,0:T(8,128)(2,1)S(1)}, bf16[8,5120]{1,0:T(8,128)(2,1)S(1)}, u32[]{:S(2)}, u32[]{:S(2)}) collective-permute-start(bf16[8,5120]{1,0:T(8,128)(2,1)S(1)} %get-tuple-element.27.refs_0_), channel_id=1, source_target_pairs={{0,1},{1,0},{2,3},{3,2},{4,5},{5,4},{6,7},{7,6},{8,9},{9,8},{10,11... | collective-permute-start | bytes 245768 | tf_op jit(solution)/shard_map/ppermute | solution.py:422
  22.3 0.0 collective-permute-done.4.refs_1_
  22.3 0.9 %collective-permute-start.8 = (bf16[8,5120]{1,0:T(8,128)(2,1)S(1)}, bf16[8,5120]{1,0:T(8,128)(2,1)S(1)}, u32[]{:S(2)}, u32[]{:S(2)}) collective-permute-start(bf16[8,5120]{1,0:T(8,128)(2,1)S(1)} %collective-permute-done.4.refs_1_), channel_id=1, source_target_pairs={{0,1},{1,0},{2,3},{3,2},{4,5},{5,4},{6,7},{7,6},{8,9},{9,8},{10,11... | collective-permute-start | bytes 245768 | tf_op jit(solution)/shard_map/ppermute | solution.py:422
  23.3 3.0 %collective-permute-done.5.refs_2_ = bf16[8,5120]{1,0:T(8,128)(2,1)S(1)} collective-permute-done((bf16[8,5120]{1,0:T(8,128)(2,1)S(1)}, bf16[8,5120]{1,0:T(8,128)(2,1)S(1)}, u32[]{:S(2)}, u32[]{:S(2)}) %collective-permute-start.5) | collective-permute-done | bytes 81952 | tf_op jit(solution)/shard_map/ppermute | solution.py:417
  26.2 1.2 %collective-permute-start.9 = (bf16[8,5120]{1,0:T(8,128)(2,1)S(1)}, bf16[8,5120]{1,0:T(8,128)(2,1)S(1)}, u32[]{:S(2)}, u32[]{:S(2)}) collective-permute-start(bf16[8,5120]{1,0:T(8,128)(2,1)S(1)} %collective-permute-done.5.refs_2_), channel_id=1, source_target_pairs={{0,1},{1,0},{2,3},{3,2},{4,5},{5,4},{6,7},{7,6},{8,9},{9,8},{10,11... | collective-permute-start | bytes 245768 | tf_op jit(solution)/shard_map/ppermute | solution.py:422
  27.4 0.0 collective-permute-done.6.refs_3_
  27.4 0.3 collective-permute-start.10
  27.7 0.0 collective-permute-done.7.refs_4_
  27.7 0.0 collective-permute-done.8.refs_5_
  27.7 1.8 %collective-permute-done.9.refs_6_ = bf16[8,5120]{1,0:T(8,128)(2,1)S(1)} collective-permute-done((bf16[8,5120]{1,0:T(8,128)(2,1)S(1)}, bf16[8,5120]{1,0:T(8,128)(2,1)S(1)}, u32[]{:S(2)}, u32[]{:S(2)}) %collective-permute-start.9) | collective-permute-done | bytes 81952 | tf_op jit(solution)/shard_map/ppermute | solution.py:422
  29.5 2.4 %collective-permute-done.10.refs_7_ = bf16[8,5120]{1,0:T(8,128)(2,1)S(1)} collective-permute-done((bf16[8,5120]{1,0:T(8,128)(2,1)S(1)}, bf16[8,5120]{1,0:T(8,128)(2,1)S(1)}, u32[]{:S(2)}, u32[]{:S(2)}) %collective-permute-start.10) | collective-permute-done | bytes 81952 | tf_op jit(solution)/shard_map/ppermute | solution.py:422
  31.9 1.1 %collective-permute-start.13 = (bf16[64,512]{1,0:T(8,128)(2,1)S(1)}, bf16[64,512]{1,0:T(8,128)(2,1)S(1)}, u32[]{:S(2)}, u32[]{:S(2)}) collective-permute-start(bf16[64,512]{1,0:T(8,128)(2,1)S(1)} %own_columns.1.refs_8_), channel_id=1, source_target_pairs={{0,24},{8,0},{16,8},{24,16},{1,25},{9,1},{17,9},{25,17},{2,26},{10... | collective-permute-start | bytes 196616 | tf_op jit(solution)/shard_map/ppermute | solution.py:417
  33.0 0.7 %collective-permute-start.12 = (bf16[64,512]{1,0:T(8,128)(2,1)S(1)}, bf16[64,512]{1,0:T(8,128)(2,1)S(1)}, u32[]{:S(2)}, u32[]{:S(2)}) collective-permute-start(bf16[64,512]{1,0:T(8,128)(2,1)S(1)} %own_columns.1.refs_8_), channel_id=1, source_target_pairs={{0,16},{8,24},{16,0},{24,8},{1,17},{9,25},{17,1},{25,9},{2,18},{10... | collective-permute-start | bytes 196616 | tf_op jit(solution)/shard_map/ppermute | solution.py:417
  33.7 1.0 %collective-permute-start.11 = (bf16[64,512]{1,0:T(8,128)(2,1)S(1)}, bf16[64,512]{1,0:T(8,128)(2,1)S(1)}, u32[]{:S(2)}, u32[]{:S(2)}) collective-permute-start(bf16[64,512]{1,0:T(8,128)(2,1)S(1)} %own_columns.1.refs_8_), channel_id=1, source_target_pairs={{0,8},{8,16},{16,24},{24,0},{1,9},{9,17},{17,25},{25,1},{2,10},{10... | collective-permute-start | bytes 196616 | tf_op jit(solution)/shard_map/ppermute | solution.py:417
  34.7 3.7 %own_outer.1 = (f32[4096,2048]{1,0:T(8,128)}, bf16[64,4096]{1,0:T(8,128)(2,1)S(1)}) custom-call(bf16[8,5120]{1,0:T(8,128)(2,1)S(1)} %get-tuple-element.27.refs_0_, bf16[8,5120]{1,0:T(8,128)(2,1)S(1)} %collective-permute-done.4.refs_1_, bf16[8,5120]{1,0:T(8,128)(2,1)S(1)} %collective-permute-done.5.refs_2_, ...), custom_call_target="tpu_custom_call" | custom-call | flops 4000000000 | bytes 10000000 | tf_op jit(solution)/shard_map/own_outer/pallas_call | solution.py:388
  38.4 0.0 collective-permute-done.13.refs_2_
  38.4 0.0 collective-permute-done.12.refs_1_
  38.4 0.0 collective-permute-done.11.refs_0_
  38.4 8.8 %other_outer.1 = f32[4096,2048]{1,0:T(8,128)} custom-call(bf16[64,512]{1,0:T(8,128)(2,1)S(1)} %collective-permute-done.11.refs_0_, bf16[64,512]{1,0:T(8,128)(2,1)S(1)} %collective-permute-done.12.refs_1_, bf16[64,512]{1,0:T(8,128)(2,1)S(1)} %collective-permute-done.13.refs_2_, ...), custom_call_target="tpu_custom_call", output_to_operand_aliasing={{}: (4, {})} | custom-call | flops 10000000000 | bytes 30000000 | tf_op jit(solution)/shard_map/other_outer/pallas_call | solution.py:401
  (1 shorter events, 0.0 us)
Async XLA Ops:
  0.0 8.7 %collective-permute-start = (bf16[1,48,2304]{2,1,0:T(8,128)(2,1)}, bf16[1,48,2304]{2,1,0:T(8,128)(2,1)S(1)}, u32[]{:S(2)}, u32[]{:S(2)}) collective-permute-start(bf16[1,48,2304]{2,1,0:T(8,128)(2,1)} %param.8), channel_id=1, source_target_pairs={{0,8},{8,16},{16,24},{24,0},{1,9},{9,17},{17,25},{25,1},{2,10},{10... | collective-permute-start | bytes 663560 | tf_op jit(solution)/shard_map/ppermute | solution.py:417
  5.9 0.9 %copy-start = (s32[3,8192]{1,0:T(4,128)S(1)}, s32[3,8192]{1,0:T(4,128)}, u32[]{:S(2)}) copy-start(s32[3,8192]{1,0:T(4,128)} %sphere_ref.1) | copy-start | bytes 294916
  6.8 1.0 %copy-start.1 = (bf16[1760,128]{1,0:T(8,128)(2,1)S(1)}, bf16[1760,128]{1,0:T(8,128)(2,1)}, u32[]{:S(2)}) copy-start(bf16[1760,128]{1,0:T(8,128)(2,1)} %constant.2.clone.table_ref) | copy-start | bytes 1351684
  12.1 1.3 %collective-permute-start.1 = (bf16[2,8192]{1,0:T(2,128)(2,1)S(1)}, bf16[2,8192]{1,0:T(2,128)(2,1)S(1)}, u32[]{:S(2)}, u32[]{:S(2)}) collective-permute-start(bf16[2,8192]{1,0:T(2,128)(2,1)S(1)} %get-tuple-element.24), channel_id=1, source_target_pairs={{0,8},{8,16},{16,24},{24,0},{1,9},{9,17},{17,25},{25,1},{2,10},{10... | collective-permute-start | bytes 98312 | tf_op jit(solution)/shard_map/ppermute | solution.py:417
  12.2 2.8 %collective-permute-start.2 = (bf16[2,8192]{1,0:T(2,128)(2,1)S(1)}, bf16[2,8192]{1,0:T(2,128)(2,1)S(1)}, u32[]{:S(2)}, u32[]{:S(2)}) collective-permute-start(bf16[2,8192]{1,0:T(2,128)(2,1)S(1)} %get-tuple-element.25), channel_id=1, source_target_pairs={{0,16},{8,24},{16,0},{24,8},{1,17},{9,25},{17,1},{25,9},{2,18},{10... | collective-permute-start | bytes 98312 | tf_op jit(solution)/shard_map/ppermute | solution.py:417
  12.3 4.0 %collective-permute-start.3 = (bf16[2,8192]{1,0:T(2,128)(2,1)S(1)}, bf16[2,8192]{1,0:T(2,128)(2,1)S(1)}, u32[]{:S(2)}, u32[]{:S(2)}) collective-permute-start(bf16[2,8192]{1,0:T(2,128)(2,1)S(1)} %get-tuple-element.26), channel_id=1, source_target_pairs={{0,24},{8,0},{16,8},{24,16},{1,25},{9,1},{17,9},{25,17},{2,26},{10... | collective-permute-start | bytes 98312 | tf_op jit(solution)/shard_map/ppermute | solution.py:417
  16.4 5.9 %collective-permute-start.4 = (bf16[8,5120]{1,0:T(8,128)(2,1)S(1)}, bf16[8,5120]{1,0:T(8,128)(2,1)S(1)}, u32[]{:S(2)}, u32[]{:S(2)}) collective-permute-start(bf16[8,5120]{1,0:T(8,128)(2,1)S(1)} %get-tuple-element.28), channel_id=1, source_target_pairs={{0,2},{1,3},{2,4},{3,5},{4,6},{5,7},{6,0},{7,1},{8,10},{9,11},{10,... | collective-permute-start | bytes 245768 | tf_op jit(solution)/shard_map/ppermute | solution.py:417
  17.7 8.5 %collective-permute-start.5 = (bf16[8,5120]{1,0:T(8,128)(2,1)S(1)}, bf16[8,5120]{1,0:T(8,128)(2,1)S(1)}, u32[]{:S(2)}, u32[]{:S(2)}) collective-permute-start(bf16[8,5120]{1,0:T(8,128)(2,1)S(1)} %get-tuple-element.29), channel_id=1, source_target_pairs={{0,4},{1,5},{2,6},{3,7},{4,0},{5,1},{6,2},{7,3},{8,12},{9,13},{10,... | collective-permute-start | bytes 245768 | tf_op jit(solution)/shard_map/ppermute | solution.py:417
  20.1 7.4 %collective-permute-start.6 = (bf16[8,5120]{1,0:T(8,128)(2,1)S(1)}, bf16[8,5120]{1,0:T(8,128)(2,1)S(1)}, u32[]{:S(2)}, u32[]{:S(2)}) collective-permute-start(bf16[8,5120]{1,0:T(8,128)(2,1)S(1)} %get-tuple-element.30), channel_id=1, source_target_pairs={{0,6},{1,7},{2,0},{3,1},{4,2},{5,3},{6,4},{7,5},{8,14},{9,15},{10,... | collective-permute-start | bytes 245768 | tf_op jit(solution)/shard_map/ppermute | solution.py:417
  21.1 6.6 %collective-permute-start.7 = (bf16[8,5120]{1,0:T(8,128)(2,1)S(1)}, bf16[8,5120]{1,0:T(8,128)(2,1)S(1)}, u32[]{:S(2)}, u32[]{:S(2)}) collective-permute-start(bf16[8,5120]{1,0:T(8,128)(2,1)S(1)} %get-tuple-element.27.refs_0_), channel_id=1, source_target_pairs={{0,1},{1,0},{2,3},{3,2},{4,5},{5,4},{6,7},{7,6},{8,9},{9,8},{10,11... | collective-permute-start | bytes 245768 | tf_op jit(solution)/shard_map/ppermute | solution.py:422
  22.3 5.4 %collective-permute-start.8 = (bf16[8,5120]{1,0:T(8,128)(2,1)S(1)}, bf16[8,5120]{1,0:T(8,128)(2,1)S(1)}, u32[]{:S(2)}, u32[]{:S(2)}) collective-permute-start(bf16[8,5120]{1,0:T(8,128)(2,1)S(1)} %collective-permute-done.4.refs_1_), channel_id=1, source_target_pairs={{0,1},{1,0},{2,3},{3,2},{4,5},{5,4},{6,7},{7,6},{8,9},{9,8},{10,11... | collective-permute-start | bytes 245768 | tf_op jit(solution)/shard_map/ppermute | solution.py:422
  26.2 3.3 %collective-permute-start.9 = (bf16[8,5120]{1,0:T(8,128)(2,1)S(1)}, bf16[8,5120]{1,0:T(8,128)(2,1)S(1)}, u32[]{:S(2)}, u32[]{:S(2)}) collective-permute-start(bf16[8,5120]{1,0:T(8,128)(2,1)S(1)} %collective-permute-done.5.refs_2_), channel_id=1, source_target_pairs={{0,1},{1,0},{2,3},{3,2},{4,5},{5,4},{6,7},{7,6},{8,9},{9,8},{10,11... | collective-permute-start | bytes 245768 | tf_op jit(solution)/shard_map/ppermute | solution.py:422
  27.4 4.5 %collective-permute-start.10 = (bf16[8,5120]{1,0:T(8,128)(2,1)S(1)}, bf16[8,5120]{1,0:T(8,128)(2,1)S(1)}, u32[]{:S(2)}, u32[]{:S(2)}) collective-permute-start(bf16[8,5120]{1,0:T(8,128)(2,1)S(1)} %collective-permute-done.6.refs_3_), channel_id=1, source_target_pairs={{0,1},{1,0},{2,3},{3,2},{4,5},{5,4},{6,7},{7,6},{8,9},{9,8},{10,11... | collective-permute-start | bytes 245768 | tf_op jit(solution)/shard_map/ppermute | solution.py:422
  31.9 6.5 %collective-permute-start.13 = (bf16[64,512]{1,0:T(8,128)(2,1)S(1)}, bf16[64,512]{1,0:T(8,128)(2,1)S(1)}, u32[]{:S(2)}, u32[]{:S(2)}) collective-permute-start(bf16[64,512]{1,0:T(8,128)(2,1)S(1)} %own_columns.1.refs_8_), channel_id=1, source_target_pairs={{0,24},{8,0},{16,8},{24,16},{1,25},{9,1},{17,9},{25,17},{2,26},{10... | collective-permute-start | bytes 196616 | tf_op jit(solution)/shard_map/ppermute | solution.py:417
  33.0 5.4 %collective-permute-start.12 = (bf16[64,512]{1,0:T(8,128)(2,1)S(1)}, bf16[64,512]{1,0:T(8,128)(2,1)S(1)}, u32[]{:S(2)}, u32[]{:S(2)}) collective-permute-start(bf16[64,512]{1,0:T(8,128)(2,1)S(1)} %own_columns.1.refs_8_), channel_id=1, source_target_pairs={{0,16},{8,24},{16,0},{24,8},{1,17},{9,25},{17,1},{25,9},{2,18},{10... | collective-permute-start | bytes 196616 | tf_op jit(solution)/shard_map/ppermute | solution.py:417
  33.7 4.7 %collective-permute-start.11 = (bf16[64,512]{1,0:T(8,128)(2,1)S(1)}, bf16[64,512]{1,0:T(8,128)(2,1)S(1)}, u32[]{:S(2)}, u32[]{:S(2)}) collective-permute-start(bf16[64,512]{1,0:T(8,128)(2,1)S(1)} %own_columns.1.refs_8_), channel_id=1, source_target_pairs={{0,8},{8,16},{16,24},{24,0},{1,9},{9,17},{17,25},{25,1},{2,10},{10... | collective-permute-start | bytes 196616 | tf_op jit(solution)/shard_map/ppermute | solution.py:417

commit v4 on v3

v4 whole, which is shorter than its diff:
```python
import functools
import math

import jax
import jax.numpy as jnp
import ml_dtypes
import numpy as np
from jax import lax
from jax.experimental import pallas as pl
from jax.experimental.pallas import tpu as pltpu
from jax.sharding import PartitionSpec as P

GMAX = 18
STEPS = 2
RADIX = 6
SPAN = 2 * GMAX + 1
KX_ROWS = 40
LANES = 128
OMEGA_SQUARED = 0.0625
TILE = 512
VMEM_LIMIT = 40 * 2**20


def split(values, count):
    parts = []
    for _ in range(count):
        parts.append(values.astype(ml_dtypes.bfloat16))
        values = values - parts[-1].astype(np.float64)
    return parts


def table_rows(grid):
    width = (grid // RADIX) * grid
    x_first = 4 * width
    twiddle_first = x_first + 2 * KX_ROWS
    return width, x_first, twiddle_first


def packed_tables(grid):
    turn = 2.0 * np.pi / grid
    width, _, _ = table_rows(grid)
    y_lo = np.arange(width) // grid
    z = np.arange(width) % grid

    column = np.arange((2 * GMAX // RADIX + 1) * GMAX)
    q = column // GMAX - GMAX // RADIX
    kz = column % GMAX + 1
    phase = (RADIX * q[None, :] * y_lo[:, None] + kz[None, :] * z[:, None]) % grid
    last = np.zeros((2 * width, LANES))
    last[:width, : column.size] = np.cos(turn * phase)
    last[width:, : column.size] = -np.sin(turn * phase)
    pieces = split(last, 2)

    kx = np.arange(SPAN) - GMAX
    angle = turn * (kx[:, None] * np.arange(grid)[None, :] % grid)
    x_table = np.zeros((2 * KX_ROWS, grid))
    x_table[:SPAN] = np.cos(angle)
    x_table[KX_ROWS : KX_ROWS + SPAN] = -np.sin(angle)
    x_table = np.concatenate(split(x_table, 2), axis=1)
    pieces.append(np.pad(x_table, ((0, 0), (0, LANES - 2 * grid))))

    angle = turn * (np.arange(RADIX)[:, None] * y_lo[None, :] % grid)
    twiddle = np.zeros((16, width))
    twiddle[:RADIX] = np.cos(angle)
    twiddle[RADIX : 2 * RADIX] = -np.sin(angle)
    for part in split(twiddle, 3):
        pieces += [part[:, first : first + LANES] for first in range(0, width, LANES)]
    return np.concatenate(pieces, axis=0)


def dft_six(re, im):
    half = 0.5
    root = math.sqrt(3.0) / 2.0
    s_re = [re[h] + re[h + 3] for h in range(3)]
    s_im = [im[h] + im[h + 3] for h in range(3)]
    d_re = [re[h] - re[h + 3] for h in range(3)]
    d_im = [im[h] - im[h + 3] for h in range(3)]
    out = [None] * 6
    sum_re, sum_im = s_re[1] + s_re[2], s_im[1] + s_im[2]
    dif_re, dif_im = (s_re[1] - s_re[2]) * root, (s_im[1] - s_im[2]) * root
    out[0] = (s_re[0] + sum_re, s_im[0] + sum_im)
    mid_re, mid_im = s_re[0] - half * sum_re, s_im[0] - half * sum_im
    out[2] = (mid_re + dif_im, mid_im - dif_re)
    out[4] = (mid_re - dif_im, mid_im + dif_re)
    sum_re, sum_im = (d_re[1] + d_re[2]) * root, (d_im[1] + d_im[2]) * root
    dif_re, dif_im = d_re[1] - d_re[2], d_im[1] - d_im[2]
    out[3] = (d_re[0] - dif_re, d_im[0] - dif_im)
    mid_re, mid_im = d_re[0] + half * dif_re, d_im[0] + half * dif_im
    out[1] = (mid_re + sum_im, mid_im - sum_re)
    out[5] = (mid_re - sum_im, mid_im + sum_re)
    return out


def dot(a, b):
    return jnp.dot(a, b, preferred_element_type=jnp.float32)


def own_place():
    return lax.axis_index("row"), lax.axis_index("col")


def spectrum_of(grid, cond, occ, table_ref):
    norm = np.float32(grid ** (-1.5))
    width, x_first, twiddle_first = table_rows(grid)
    density = (cond.astype(jnp.float32) * occ.astype(jnp.float32)).astype(jnp.bfloat16)
    x_table = table_ref[x_first:twiddle_first, : 2 * grid]
    section = dot(x_table, jnp.concatenate([density, density], axis=0))
    re = [section[:KX_ROWS, h * width : (h + 1) * width] for h in range(RADIX)]
    im = [section[KX_ROWS:, h * width : (h + 1) * width] for h in range(RADIX)]
    chunks = width // LANES
    twiddle = 0.0
    for part in range(3):
        first = twiddle_first + 16 * chunks * part
        whole = [table_ref[first + 16 * i : first + 16 * (i + 1), :].astype(jnp.float32) for i in range(chunks)]
        twiddle = twiddle + jnp.concatenate(whole, axis=1)
    rows = []
    for residue, (d_re, d_im) in enumerate(dft_six(re, im)):
        if residue > 0:
            t_re = twiddle[residue : residue + 1, :]
            t_im = twiddle[RADIX + residue : RADIX + residue + 1, :]
            d_re, d_im = d_re * t_re - d_im * t_im, d_re * t_im + d_im * t_re
        rows.append(jnp.concatenate([d_re, d_im], axis=1))
    whole = jnp.concatenate(rows, axis=0)
    whole_hi = whole.astype(jnp.bfloat16)
    whole_lo = (whole - whole_hi.astype(jnp.float32)).astype(jnp.bfloat16)

    def rotation(first):
        cos_part = table_ref[first : first + width, :]
        sin_part = table_ref[first + width : first + 2 * width, :]
        upper = jnp.concatenate([cos_part, sin_part], axis=1)
        return jnp.concatenate([upper, jnp.concatenate([-sin_part, cos_part], axis=1)], axis=0)

    upper, lower = rotation(0), rotation(2 * width)
    spectrum = (dot(whole_hi, upper) + dot(whole_lo, upper) + dot(whole_hi, lower)) * norm
    parts = []
    for side in range(2):
        own = spectrum[:, side * LANES : (side + 1) * LANES]
        for group in range(RADIX // 2):
            first = 2 * group * KX_ROWS
            parts.append(jnp.concatenate([own[first : first + KX_ROWS], own[first + KX_ROWS : first + 2 * KX_ROWS]], axis=1))
    return jnp.concatenate(parts, axis=0).astype(jnp.bfloat16)


def pair_weights(sources, levels_ref):
    rows, cols = lax.axis_size("row"), lax.axis_size("col")
    r, _ = own_place()
    devices = rows * cols
    pairs = STEPS * len(sources)
    line = lax.broadcasted_iota(jnp.int32, (pairs, 1), 0)
    band = jnp.zeros((pairs, 1), jnp.int32)
    slot = jnp.zeros((pairs, 1), jnp.int32)
    for j, source in enumerate(sources):
        place = r * cols + source
        for step in range(STEPS):
            here = line == STEPS * j + step
            band = jnp.where(here, place, band)
            slot = jnp.where(here, lax.rem(place - step * cols + devices, devices), slot)
    lane = lax.broadcasted_iota(jnp.int32, (pairs, levels_ref.shape[1]), 1)

    def at(which, chosen):
        return jnp.sum(jnp.where(lane == chosen, levels_ref[which : which + 1, :], 0.0), axis=1, keepdims=True)

    gap = at(0, band) - at(1, at(2, slot).astype(jnp.int32))
    return -4.0 * gap / (gap * gap + OMEGA_SQUARED) / (devices * STEPS)


def first_kernel(grid, orbitals_ref, table_ref, sphere_ref, cube_ref, places_ref, table_out):
    half = grid // 2
    sx, sy, kz = sphere_ref[0:1, :], sphere_ref[1:2, :], sphere_ref[2:3, :]
    kx = jnp.where(sx >= half, sx - grid, sx) + GMAX
    ky = jnp.where(sy >= half, sy - grid, sy) + GMAX
    q = (ky * 43) >> 8
    residue = ky - q * RADIX
    places_ref[0:1, :] = (residue & 1) * LANES + q * GMAX + kz - 1
    places_ref[1:2, :] = (residue >> 1) * KX_ROWS + kx
    table_out[...] = table_ref[...]
    cube_ref[...] = spectrum_of(grid, orbitals_ref[0], orbitals_ref[1], table_ref)


def pick(cube_ref, places_ref, coef_ref):
    groups = RADIX // 2 * KX_ROWS // 8
    half_count = places_ref.shape[1]
    counted = lax.broadcasted_iota(jnp.int32, (2 * LANES, TILE), 0).astype(jnp.float32).astype(jnp.bfloat16)
    line = lax.broadcasted_iota(jnp.int32, (8, TILE), 0)
    for first in range(0, half_count, TILE):
        here = slice(first, first + TILE)
        lane = places_ref[0:1, here].astype(jnp.float32).astype(jnp.bfloat16)
        row = places_ref[1:2, here]
        one_hot = jnp.where(counted == lane, jnp.bfloat16(1), jnp.bfloat16(0))
        found = dot(cube_ref[...], one_hot)
        away = line - row
        values = [jnp.zeros((8, TILE), jnp.float32)] * 4
        for group in range(groups):
            chosen = away == -8 * group
            for which in range(4):
                start = (which * groups + group) * 8
                values[which] = jnp.where(chosen, found[start : start + 8], values[which])
        for which in range(4):
            pair, side = divmod(which, 2)
            value = jnp.sum(values[which], axis=0, keepdims=True)
            coef_ref[pair : pair + 1, side * half_count + first : side * half_count + first + TILE] = value.astype(jnp.bfloat16)


def second_kernel(grid, orbitals_ref, occ_ref, first_ref, places_ref, table_ref, coef_ref, cube_ref):
    picks = RADIX * KX_ROWS
    cube_ref[:picks, :] = first_ref[...]
    cube_ref[picks:, :] = spectrum_of(grid, orbitals_ref[0], occ_ref[0], table_ref)
    pick(cube_ref, places_ref, coef_ref)


def cost(flops, data):
    return pl.CostEstimate(flops=flops, bytes_accessed=data, transcendentals=0)


def in_vmem(count):
    return [pl.BlockSpec(memory_space=pltpu.VMEM)] * count


def transform(cond_orbitals, occ_orbitals, occ_second, sphere_index):
    grid = cond_orbitals.shape[1]
    half_count = sphere_index.shape[1]
    table = jnp.asarray(packed_tables(grid))
    orbitals = jnp.concatenate([cond_orbitals, occ_orbitals], axis=0)
    picks = RADIX * KX_ROWS
    params = dict(
        compiler_params=pltpu.CompilerParams(vmem_limit_bytes=VMEM_LIMIT),
        cost_estimate=cost(2 * 10**9, 2 * 10**6),
    )
    handed = pl.pallas_call(
        functools.partial(first_kernel, grid),
        out_shape=[
            jax.ShapeDtypeStruct((picks, 2 * LANES), jnp.bfloat16),
            jax.ShapeDtypeStruct((2, half_count), jnp.int32),
            jax.ShapeDtypeStruct(table.shape, table.dtype),
        ],
        in_specs=in_vmem(3),
        out_specs=in_vmem(3),
        name="first_pair",
        **params,
    )(orbitals, table, sphere_index)
    return pl.pallas_call(
        functools.partial(second_kernel, grid),
        out_shape=jax.ShapeDtypeStruct((STEPS, 2 * half_count), jnp.bfloat16),
        in_specs=in_vmem(5),
        out_specs=in_vmem(1)[0],
        scratch_shapes=[pltpu.VMEM((STEPS * picks, 2 * LANES), jnp.bfloat16)],
        name="second_pair",
        **params,
    )(orbitals, occ_second, *handed)


def pack_kernel(plan, targets, levels_ref, *refs):
    rows, cols, row_width, col_width = plan
    arrived, outs, mixed_ref = refs[: cols // 2], refs[cols // 2 : -1], refs[-1]
    r, c = own_place()
    for j, ref in enumerate(arrived):
        mixed_ref[STEPS * j : STEPS * (j + 1), :] = ref[...].astype(jnp.float32)
    weight = pair_weights([lax.rem(c - 2 * k + cols, cols) for k in range(cols // 2)], levels_ref)
    columns = []
    for side in range(2):
        start = pl.multiple_of((c ^ side) * col_width, LANES)
        columns.append((weight * mixed_ref[:, pl.ds(start, col_width)]).astype(jnp.bfloat16))
    for (step, side), out_ref in zip(targets, outs):
        start = pl.multiple_of(lax.rem(r + step, rows) * row_width, LANES)
        out_ref[:, :row_width] = mixed_ref[:, pl.ds(start, row_width)].astype(jnp.bfloat16)
        out_ref[:, row_width:] = columns[side]


def pack(arrived, levels, targets, plan):
    rows, cols, row_width, col_width = plan
    pairs = STEPS * len(arrived)
    return pl.pallas_call(
        functools.partial(pack_kernel, plan, targets),
        out_shape=[jax.ShapeDtypeStruct((pairs, row_width + col_width), jnp.bfloat16)] * len(targets),
        in_specs=in_vmem(1 + len(arrived)),
        out_specs=in_vmem(len(targets)),
        scratch_shapes=[pltpu.VMEM((pairs, arrived[0].shape[1]), jnp.float32)],
        compiler_params=pltpu.CompilerParams(vmem_limit_bytes=VMEM_LIMIT),
        cost_estimate=cost(10**9, 10**6),
        name="pack",
    )(levels, *arrived)


def outer_kernel(row_width, block, slots, *refs):
    messages, (out_ref, left_ref, right_ref, held_ref, sems) = refs[:-5], refs[-5:]
    depth = messages[0].shape[0]
    merge = max(1, 16 // depth)
    for j in range(0, len(messages), merge):
        whole = jnp.concatenate([ref[...].astype(jnp.float32) for ref in messages[j : j + merge]], axis=0).astype(jnp.bfloat16)
        left_ref[depth * j : depth * (j + merge), :] = whole[:, :row_width]
        right_ref[depth * j : depth * (j + merge), :] = whole[:, row_width:]
    count = row_width // block

    def copy_out(i, slot):
        rows = pl.ds(pl.multiple_of(i * block, block), block)
        return pltpu.make_async_copy(held_ref.at[slot], out_ref.at[rows], sems.at[slot])

    def step(i, carry):
        slot = lax.rem(i, slots)

        @pl.when(i >= slots)
        def _():
            copy_out(i - slots, slot).wait()

        here = pl.ds(pl.multiple_of(i * block, block), block)
        held_ref[slot] = lax.dot_general(
            left_ref[:, here], right_ref[...], (((0,), (0,)), ((), ())), preferred_element_type=jnp.float32
        )
        copy_out(i, slot).start()
        return carry

    lax.fori_loop(0, count, step, 0)
    for i in range(max(0, count - slots), count):
        copy_out(i, i % slots).wait()


def outer(messages, plan):
    rows, cols, row_width, col_width = plan
    depth = messages[0].shape[0]
    block = min(256, row_width)
    slots = min(4, row_width // block)
    return pl.pallas_call(
        functools.partial(outer_kernel, row_width, block, slots),
        out_shape=jax.ShapeDtypeStruct((row_width, col_width), jnp.float32),
        in_specs=in_vmem(len(messages)),
        out_specs=pl.BlockSpec(memory_space=pltpu.HBM),
        scratch_shapes=[
            pltpu.VMEM((depth * len(messages), row_width), jnp.bfloat16),
            pltpu.VMEM((depth * len(messages), col_width), jnp.bfloat16),
            pltpu.VMEM((slots, block, col_width), jnp.float32),
            pltpu.SemaphoreType.DMA((slots,)),
        ],
        compiler_params=pltpu.CompilerParams(vmem_limit_bytes=VMEM_LIMIT),
        cost_estimate=cost(10**10, 3 * 10**7),
        name="outer",
    )(*messages)


def shifted(value, axis, by):
    devices = lax.axis_size(axis)
    return lax.ppermute(value, axis, [(i, (i + by) % devices) for i in range(devices)])


def sent_to(value, step, side, rows, cols):
    moves = [(r * cols + c, (r + step) % rows * cols + (c ^ side)) for r in range(rows) for c in range(cols)]
    return lax.ppermute(value, ("row", "col"), moves)


def on_device(cond_orbitals, occ_orbitals, cond_energy, occ_energy, occ_band, sphere_index):
    rows = lax.axis_size("row")
    cols = lax.axis_size("col")
    entries = 2 * sphere_index.shape[1]
    plan = (rows, cols, entries // rows, entries // cols)
    occ_second = shifted(occ_orbitals, "row", 1)
    levels = jnp.stack([cond_energy, occ_energy, occ_band.astype(jnp.float32)])
    own = transform(cond_orbitals, occ_orbitals, occ_second, sphere_index)
    arrived = [own] + [shifted(own, "col", 2 * k) for k in range(1, cols // 2)]
    targets = [(step, side) for step in range(rows) for side in range(2)]
    packed = pack(arrived, levels, targets, plan)
    messages = [packed[0]] + [sent_to(value, *target, rows, cols) for value, target in zip(packed[1:], targets[1:])]
    return outer(messages, plan)


def solution(mesh):
    placed = (P(("row", "col"), None, None), P(("row", "col"), None, None), P(), P(), P(), P())
    return jax.shard_map(
        on_device, mesh=mesh, in_specs=placed, out_specs=P("row", "col"), check_vma=False
    )
```

time: 47.5 us -> 46 us (0.968)
  Pallas kernels: 16.9 us -> 16 us
  starting transfers between devices: 14.3 us -> 13.6 us
    pallas_call x5 -> x3, Pallas kernels: 16.1 us -> 15.1 us  [the longest x1 11.4 us: outer(): pl.pallas_call(functools.partial(outer_kernel, row_width, block, slots),...]
    ppermute x14 -> x11, starting transfers between devices: 14.3 us -> 13.6 us  [the longest x7 7.18 us: sent_to(): return lax.ppermute(value, ('row', 'col'), moves)]
    ppermute x14 -> x11, waiting for transfers between devices: 10.7 us -> 10.9 us  [the longest x7 5.5 us: sent_to(): return lax.ppermute(value, ('row', 'col'), moves)]
  transfers between devices with their start and end apart: 14 -> 11, of which waited for: 6 -> 5; matrix products, arithmetic and copies ran while one was open for 7% -> 7% of each run, Pallas kernels for 10% -> 2%
where the time goes in v4:
time: 46 us; the launch traced here: 45.7 us
  Pallas kernels  16 us (35%)
  starting transfers between devices  13.6 us (30%)
  waiting for transfers between devices  10.9 us (24%)
  local copies, waits for them, and re-layouts  3.82 us (8%)
  other arithmetic  1.34 us (3%)
    pallas_call x1, Pallas kernels, outer(): pl.pallas_call(functools.partial(outer_kernel, row_width, block, slots),...  11.4 us
    ppermute x7, starting transfers between devices, sent_to(): return lax.ppermute(value, ('row', 'col'), moves)  7.18 us
    ppermute x4, starting transfers between devices, shifted(): lax.ppermute(value, axis, [(i, (i + by) % devices) for i in range(devices)])  6.46 us
    ppermute x7, waiting for transfers between devices, sent_to(): return lax.ppermute(value, ('row', 'col'), moves)  5.5 us
    ppermute x4, waiting for transfers between devices, shifted(): lax.ppermute(value, axis, [(i, (i + by) % devices) for i in range(devices)])  5.41 us
    pallas_call x1, Pallas kernels, transform(): pl.pallas_call(functools.partial(second_kernel, grid), out_shape=jax.Shap...  3.38 us
    unnamed x5, local copies, waits for them, and re-layouts  2.86 us
    another operation x2, other arithmetic, on_device(): levels = jnp.stack([cond_energy, occ_energy, occ_band.astype(jnp.float32)])  1.34 us
  transfers between devices with their start and end apart: 11, of which 5 were waited for; matrix products, arithmetic and copies ran while one was open for 7% of the time, Pallas kernels for 2%

profile of v4, /device:TPU:1, one launch (start us, length us, event | category | flops | bytes accessed | tf_op | source)
XLA Modules:
  0.0 45.7 jit_solution(5056219090797629877)
XLA Ops:
  0.0 2.6 %collective-permute-start = (bf16[1,48,2304]{2,1,0:T(8,128)(2,1)}, bf16[1,48,2304]{2,1,0:T(8,128)(2,1)S(1)}, u32[]{:S(2)}, u32[]{:S(2)}) collective-permute-start(bf16[1,48,2304]{2,1,0:T(8,128)(2,1)} %param.8), channel_id=1, source_target_pairs={{0,8},{8,16},{16,24},{24,0},{1,9},{9,17},{17,25},{25,1},{2,10},{10... | collective-permute-start | bytes 663560 | tf_op jit(solution)/shard_map/ppermute | solution.py:341
  2.6 0.9 %constant_dynamic-update-slice_fusion.1 = bf16[2,48,2304]{2,1,0:T(8,128)(2,1)S(1)} fusion(bf16[1,48,2304]{2,1,0:T(8,128)(2,1)} %param.7), kind=kLoop, calls=%fused_computation.1 | loop fusion | bytes 442368
  3.6 1.0 %constant_dynamic-update-slice_fusion.orbitals_ref = bf16[2,48,2304]{2,1,0:T(8,128)(2,1)S(1)} fusion(bf16[2,48,2304]{2,1,0:T(8,128)(2,1)S(1)} %constant_dynamic-update-slice_fusion.1, bf16[1,48,2304]{2,1,0:T(8,128)(2,1)} %param.8), kind=kLoop, calls=%fused_computation | loop fusion | bytes 442368 | tf_op jit(solution)/shard_map/concatenate | solution.py:223
  4.5 0.0 copy-start
  4.6 0.9 %copy-done = s32[3,8192]{1,0:T(4,128)S(1)} copy-done((s32[3,8192]{1,0:T(4,128)S(1)}, s32[3,8192]{1,0:T(4,128)}, u32[]{:S(2)}) %copy-start) | copy-done | bytes 98328
  5.4 0.0 copy-start.1
  5.5 1.0 %copy-done.1 = bf16[1760,128]{1,0:T(8,128)(2,1)S(1)} copy-done((bf16[1760,128]{1,0:T(8,128)(2,1)S(1)}, bf16[1760,128]{1,0:T(8,128)(2,1)}, u32[]{:S(2)}) %copy-start.1) | copy-done | bytes 450584
  6.5 0.9 %first_pair.1 = (bf16[240,256]{1,0:T(8,128)(2,1)S(1)}, s32[2,8192]{1,0:T(2,128)S(1)}, bf16[1760,128]{1,0:T(8,128)(2,1)S(1)}) custom-call(bf16[2,48,2304]{2,1,0:T(8,128)(2,1)S(1)} %constant_dynamic-update-slice_fusion.orbitals_ref, bf16[1760,128]{1,0:T(8,128)(2,1)S(1)} %copy-done.1, s32[3,8192]{1,0:T(4,128)S(1)} %copy-done), custom_call_target="tpu_custom_call" | custom-call | flops 2000000000 | bytes 2000000 | tf_op jit(solution)/shard_map/first_pair/pallas_call | solution.py:229
  7.3 0.7 %convert_bitcast_fusion = f32[1,32]{1,0:T(1,128)S(1)} fusion(s32[32]{0:T(128)} %param.11), kind=kLoop, calls=%fused_computation.3 | loop fusion | flops 32 | bytes 256 | tf_op jit(solution)/shard_map/stack | solution.py:355
  8.0 0.0 collective-permute-done.occ_ref
  8.0 3.4 %second_pair.1.refs_0_ = bf16[2,16384]{1,0:T(2,128)(2,1)S(1)} custom-call(bf16[2,48,2304]{2,1,0:T(8,128)(2,1)S(1)} %constant_dynamic-update-slice_fusion.orbitals_ref, bf16[1,48,2304]{2,1,0:T(8,128)(2,1)S(1)} %collective-permute-done.occ_ref, bf16[240,256]{1,0:T(8,128)(2,1)S(1)} %get-tuple-element.16.first_ref, s32[2,8192]{1,0:T(2,128)S(1)} %get-tuple-element.17.places_ref, ...), custom_call_target="tpu_custom_call" | custom-call | flops 2000000000 | bytes 2000000 | tf_op jit(solution)/shard_map/second_pair/pallas_call | solution.py:241
  11.4 3.4 %collective-permute-start.3 = (bf16[2,16384]{1,0:T(2,128)(2,1)S(1)}, bf16[2,16384]{1,0:T(2,128)(2,1)S(1)}, u32[]{:S(2)}, u32[]{:S(2)}) collective-permute-start(bf16[2,16384]{1,0:T(2,128)(2,1)S(1)} %second_pair.1.refs_0_), channel_id=1, source_target_pairs={{0,6},{1,7},{2,0},{3,1},{4,2},{5,3},{6,4},{7,5},{8,14},{9,15},{10,... | collective-permute-start | bytes 196616 | tf_op jit(solution)/shard_map/ppermute | solution.py:341
  14.8 0.0 collective-permute-start.2
  14.8 0.5 collective-permute-start.1
  15.2 0.7 %pad_maximum_fusion.levels_ref = f32[3,32]{1,0:T(4,128)S(1)} fusion(f32[1,32]{1,0:T(1,128)S(1)} %convert_bitcast_fusion, f32[1,32]{1,0:T(1,128)} %bitcast.4, f32[1,32]{1,0:T(1,128)} %bitcast.5), kind=kLoop, calls=%fused_computation.2 | loop fusion | flops 192 | bytes 768 | tf_op jit(solution)/shard_map/stack | solution.py:355
  15.9 0.7 %collective-permute-done.3.refs_3_ = bf16[2,16384]{1,0:T(2,128)(2,1)S(1)} collective-permute-done((bf16[2,16384]{1,0:T(2,128)(2,1)S(1)}, bf16[2,16384]{1,0:T(2,128)(2,1)S(1)}, u32[]{:S(2)}, u32[]{:S(2)}) %collective-permute-start.3) | collective-permute-done | bytes 65568 | tf_op jit(solution)/shard_map/ppermute | solution.py:341
  16.6 4.7 %collective-permute-done.2.refs_2_ = bf16[2,16384]{1,0:T(2,128)(2,1)S(1)} collective-permute-done((bf16[2,16384]{1,0:T(2,128)(2,1)S(1)}, bf16[2,16384]{1,0:T(2,128)(2,1)S(1)}, u32[]{:S(2)}, u32[]{:S(2)}) %collective-permute-start.2) | collective-permute-done | bytes 65568 | tf_op jit(solution)/shard_map/ppermute | solution.py:341
  21.3 0.0 collective-permute-done.1.refs_1_
  21.3 0.3 pack.1
  21.6 1.3 %collective-permute-start.4 = (bf16[8,6144]{1,0:T(8,128)(2,1)S(1)}, bf16[8,6144]{1,0:T(8,128)(2,1)S(1)}, u32[]{:S(2)}, u32[]{:S(2)}) collective-permute-start(bf16[8,6144]{1,0:T(8,128)(2,1)S(1)} %get-tuple-element.20), channel_id=1, source_target_pairs={{0,1},{1,0},{2,3},{3,2},{4,5},{5,4},{6,7},{7,6},{8,9},{9,8},{10,11... | collective-permute-start | bytes 294920 | tf_op jit(solution)/shard_map/ppermute | solution.py:346
  22.9 1.3 %collective-permute-start.5 = (bf16[8,6144]{1,0:T(8,128)(2,1)S(1)}, bf16[8,6144]{1,0:T(8,128)(2,1)S(1)}, u32[]{:S(2)}, u32[]{:S(2)}) collective-permute-start(bf16[8,6144]{1,0:T(8,128)(2,1)S(1)} %get-tuple-element.21), channel_id=1, source_target_pairs={{0,8},{1,9},{2,10},{3,11},{4,12},{5,13},{6,14},{7,15},{8,16},{9,17... | collective-permute-start | bytes 294920 | tf_op jit(solution)/shard_map/ppermute | solution.py:346
  24.2 0.0 collective-permute-start.6
  24.2 0.7 %collective-permute-start.7 = (bf16[8,6144]{1,0:T(8,128)(2,1)S(1)}, bf16[8,6144]{1,0:T(8,128)(2,1)S(1)}, u32[]{:S(2)}, u32[]{:S(2)}) collective-permute-start(bf16[8,6144]{1,0:T(8,128)(2,1)S(1)} %get-tuple-element.23), channel_id=1, source_target_pairs={{0,16},{1,17},{2,18},{3,19},{4,20},{5,21},{6,22},{7,23},{8,24},{9,... | collective-permute-start | bytes 294920 | tf_op jit(solution)/shard_map/ppermute | solution.py:346
  24.9 1.6 %collective-permute-start.8 = (bf16[8,6144]{1,0:T(8,128)(2,1)S(1)}, bf16[8,6144]{1,0:T(8,128)(2,1)S(1)}, u32[]{:S(2)}, u32[]{:S(2)}) collective-permute-start(bf16[8,6144]{1,0:T(8,128)(2,1)S(1)} %get-tuple-element.24), channel_id=1, source_target_pairs={{0,17},{1,16},{2,19},{3,18},{4,21},{5,20},{6,23},{7,22},{8,25},{9,... | collective-permute-start | bytes 294920 | tf_op jit(solution)/shard_map/ppermute | solution.py:346
  26.6 0.0 collective-permute-done.4.refs_1_
  26.6 1.2 %collective-permute-start.9 = (bf16[8,6144]{1,0:T(8,128)(2,1)S(1)}, bf16[8,6144]{1,0:T(8,128)(2,1)S(1)}, u32[]{:S(2)}, u32[]{:S(2)}) collective-permute-start(bf16[8,6144]{1,0:T(8,128)(2,1)S(1)} %get-tuple-element.25), channel_id=1, source_target_pairs={{0,24},{1,25},{2,26},{3,27},{4,28},{5,29},{6,30},{7,31},{8,0},{9,1... | collective-permute-start | bytes 294920 | tf_op jit(solution)/shard_map/ppermute | solution.py:346
  27.8 0.0 collective-permute-done.5.refs_2_
  27.8 1.0 %collective-permute-start.10 = (bf16[8,6144]{1,0:T(8,128)(2,1)S(1)}, bf16[8,6144]{1,0:T(8,128)(2,1)S(1)}, u32[]{:S(2)}, u32[]{:S(2)}) collective-permute-start(bf16[8,6144]{1,0:T(8,128)(2,1)S(1)} %get-tuple-element.26), channel_id=1, source_target_pairs={{0,25},{1,24},{2,27},{3,26},{4,29},{5,28},{6,31},{7,30},{8,1},{9,0... | collective-permute-start | bytes 294920 | tf_op jit(solution)/shard_map/ppermute | solution.py:346
  28.8 0.6 %collective-permute-done.6.refs_3_ = bf16[8,6144]{1,0:T(8,128)(2,1)S(1)} collective-permute-done((bf16[8,6144]{1,0:T(8,128)(2,1)S(1)}, bf16[8,6144]{1,0:T(8,128)(2,1)S(1)}, u32[]{:S(2)}, u32[]{:S(2)}) %collective-permute-start.6) | collective-permute-done | bytes 98336 | tf_op jit(solution)/shard_map/ppermute | solution.py:346
  29.4 3.6 %collective-permute-done.7.refs_4_ = bf16[8,6144]{1,0:T(8,128)(2,1)S(1)} collective-permute-done((bf16[8,6144]{1,0:T(8,128)(2,1)S(1)}, bf16[8,6144]{1,0:T(8,128)(2,1)S(1)}, u32[]{:S(2)}, u32[]{:S(2)}) %collective-permute-start.7) | collective-permute-done | bytes 98336 | tf_op jit(solution)/shard_map/ppermute | solution.py:346
  33.0 0.0 collective-permute-done.8.refs_5_
  33.0 1.2 %collective-permute-done.9.refs_6_ = bf16[8,6144]{1,0:T(8,128)(2,1)S(1)} collective-permute-done((bf16[8,6144]{1,0:T(8,128)(2,1)S(1)}, bf16[8,6144]{1,0:T(8,128)(2,1)S(1)}, u32[]{:S(2)}, u32[]{:S(2)}) %collective-permute-start.9) | collective-permute-done | bytes 98336 | tf_op jit(solution)/shard_map/ppermute | solution.py:346
  34.3 0.0 collective-permute-done.10.refs_7_
  34.3 11.4 %outer.1 = f32[4096,2048]{1,0:T(8,128)} custom-call(bf16[8,6144]{1,0:T(8,128)(2,1)S(1)} %get-tuple-element.19.refs_0_, bf16[8,6144]{1,0:T(8,128)(2,1)S(1)} %collective-permute-done.4.refs_1_, bf16[8,6144]{1,0:T(8,128)(2,1)S(1)} %collective-permute-done.5.refs_2_, bf16[8,6144]{1,0:T(8,128)(2,1)S(1)} %collective-permute-done.6.refs_3_, ...), custom_call_target="tpu_custom_call" | custom-call | flops 10000000000 | bytes 30000000 | tf_op jit(solution)/shard_map/outer/pallas_call | solution.py:322
Async XLA Ops:
  0.0 8.0 %collective-permute-start = (bf16[1,48,2304]{2,1,0:T(8,128)(2,1)}, bf16[1,48,2304]{2,1,0:T(8,128)(2,1)S(1)}, u32[]{:S(2)}, u32[]{:S(2)}) collective-permute-start(bf16[1,48,2304]{2,1,0:T(8,128)(2,1)} %param.8), channel_id=1, source_target_pairs={{0,8},{8,16},{16,24},{24,0},{1,9},{9,17},{17,25},{25,1},{2,10},{10... | collective-permute-start | bytes 663560 | tf_op jit(solution)/shard_map/ppermute | solution.py:341
  4.5 0.9 %copy-start = (s32[3,8192]{1,0:T(4,128)S(1)}, s32[3,8192]{1,0:T(4,128)}, u32[]{:S(2)}) copy-start(s32[3,8192]{1,0:T(4,128)} %sphere_ref.1) | copy-start | bytes 294916
  5.4 1.0 %copy-start.1 = (bf16[1760,128]{1,0:T(8,128)(2,1)S(1)}, bf16[1760,128]{1,0:T(8,128)(2,1)}, u32[]{:S(2)}) copy-start(bf16[1760,128]{1,0:T(8,128)(2,1)} %constant.2.clone.table_ref) | copy-start | bytes 1351684
  11.4 5.3 %collective-permute-start.3 = (bf16[2,16384]{1,0:T(2,128)(2,1)S(1)}, bf16[2,16384]{1,0:T(2,128)(2,1)S(1)}, u32[]{:S(2)}, u32[]{:S(2)}) collective-permute-start(bf16[2,16384]{1,0:T(2,128)(2,1)S(1)} %second_pair.1.refs_0_), channel_id=1, source_target_pairs={{0,6},{1,7},{2,0},{3,1},{4,2},{5,3},{6,4},{7,5},{8,14},{9,15},{10,... | collective-permute-start | bytes 196616 | tf_op jit(solution)/shard_map/ppermute | solution.py:341
  14.8 6.5 %collective-permute-start.2 = (bf16[2,16384]{1,0:T(2,128)(2,1)S(1)}, bf16[2,16384]{1,0:T(2,128)(2,1)S(1)}, u32[]{:S(2)}, u32[]{:S(2)}) collective-permute-start(bf16[2,16384]{1,0:T(2,128)(2,1)S(1)} %second_pair.1.refs_0_), channel_id=1, source_target_pairs={{0,4},{1,5},{2,6},{3,7},{4,0},{5,1},{6,2},{7,3},{8,12},{9,13},{10,... | collective-permute-start | bytes 196616 | tf_op jit(solution)/shard_map/ppermute | solution.py:341
  14.8 6.5 %collective-permute-start.1 = (bf16[2,16384]{1,0:T(2,128)(2,1)S(1)}, bf16[2,16384]{1,0:T(2,128)(2,1)S(1)}, u32[]{:S(2)}, u32[]{:S(2)}) collective-permute-start(bf16[2,16384]{1,0:T(2,128)(2,1)S(1)} %second_pair.1.refs_0_), channel_id=1, source_target_pairs={{0,2},{1,3},{2,4},{3,5},{4,6},{5,7},{6,0},{7,1},{8,10},{9,11},{10,... | collective-permute-start | bytes 196616 | tf_op jit(solution)/shard_map/ppermute | solution.py:341
  21.6 4.9 %collective-permute-start.4 = (bf16[8,6144]{1,0:T(8,128)(2,1)S(1)}, bf16[8,6144]{1,0:T(8,128)(2,1)S(1)}, u32[]{:S(2)}, u32[]{:S(2)}) collective-permute-start(bf16[8,6144]{1,0:T(8,128)(2,1)S(1)} %get-tuple-element.20), channel_id=1, source_target_pairs={{0,1},{1,0},{2,3},{3,2},{4,5},{5,4},{6,7},{7,6},{8,9},{9,8},{10,11... | collective-permute-start | bytes 294920 | tf_op jit(solution)/shard_map/ppermute | solution.py:346
  22.9 4.9 %collective-permute-start.5 = (bf16[8,6144]{1,0:T(8,128)(2,1)S(1)}, bf16[8,6144]{1,0:T(8,128)(2,1)S(1)}, u32[]{:S(2)}, u32[]{:S(2)}) collective-permute-start(bf16[8,6144]{1,0:T(8,128)(2,1)S(1)} %get-tuple-element.21), channel_id=1, source_target_pairs={{0,8},{1,9},{2,10},{3,11},{4,12},{5,13},{6,14},{7,15},{8,16},{9,17... | collective-permute-start | bytes 294920 | tf_op jit(solution)/shard_map/ppermute | solution.py:346
  24.2 5.2 %collective-permute-start.6 = (bf16[8,6144]{1,0:T(8,128)(2,1)S(1)}, bf16[8,6144]{1,0:T(8,128)(2,1)S(1)}, u32[]{:S(2)}, u32[]{:S(2)}) collective-permute-start(bf16[8,6144]{1,0:T(8,128)(2,1)S(1)} %get-tuple-element.22), channel_id=1, source_target_pairs={{0,9},{1,8},{2,11},{3,10},{4,13},{5,12},{6,15},{7,14},{8,17},{9,16... | collective-permute-start | bytes 294920 | tf_op jit(solution)/shard_map/ppermute | solution.py:346
  24.2 8.9 %collective-permute-start.7 = (bf16[8,6144]{1,0:T(8,128)(2,1)S(1)}, bf16[8,6144]{1,0:T(8,128)(2,1)S(1)}, u32[]{:S(2)}, u32[]{:S(2)}) collective-permute-start(bf16[8,6144]{1,0:T(8,128)(2,1)S(1)} %get-tuple-element.23), channel_id=1, source_target_pairs={{0,16},{1,17},{2,18},{3,19},{4,20},{5,21},{6,22},{7,23},{8,24},{9,... | collective-permute-start | bytes 294920 | tf_op jit(solution)/shard_map/ppermute | solution.py:346
  24.9 8.1 %collective-permute-start.8 = (bf16[8,6144]{1,0:T(8,128)(2,1)S(1)}, bf16[8,6144]{1,0:T(8,128)(2,1)S(1)}, u32[]{:S(2)}, u32[]{:S(2)}) collective-permute-start(bf16[8,6144]{1,0:T(8,128)(2,1)S(1)} %get-tuple-element.24), channel_id=1, source_target_pairs={{0,17},{1,16},{2,19},{3,18},{4,21},{5,20},{6,23},{7,22},{8,25},{9,... | collective-permute-start | bytes 294920 | tf_op jit(solution)/shard_map/ppermute | solution.py:346
  26.6 7.7 %collective-permute-start.9 = (bf16[8,6144]{1,0:T(8,128)(2,1)S(1)}, bf16[8,6144]{1,0:T(8,128)(2,1)S(1)}, u32[]{:S(2)}, u32[]{:S(2)}) collective-permute-start(bf16[8,6144]{1,0:T(8,128)(2,1)S(1)} %get-tuple-element.25), channel_id=1, source_target_pairs={{0,24},{1,25},{2,26},{3,27},{4,28},{5,29},{6,30},{7,31},{8,0},{9,1... | collective-permute-start | bytes 294920 | tf_op jit(solution)/shard_map/ppermute | solution.py:346
  27.8 6.5 %collective-permute-start.10 = (bf16[8,6144]{1,0:T(8,128)(2,1)S(1)}, bf16[8,6144]{1,0:T(8,128)(2,1)S(1)}, u32[]{:S(2)}, u32[]{:S(2)}) collective-permute-start(bf16[8,6144]{1,0:T(8,128)(2,1)S(1)} %get-tuple-element.26), channel_id=1, source_target_pairs={{0,25},{1,24},{2,27},{3,26},{4,29},{5,28},{6,31},{7,30},{8,1},{9,0... | collective-permute-start | bytes 294920 | tf_op jit(solution)/shard_map/ppermute | solution.py:346

commit v5 on v4

--- a/solution.py
+++ b/solution.py
@@ -201,7 +201,8 @@
             coef_ref[pair : pair + 1, side * half_count + first : side * half_count + first + TILE] = value.astype(jnp.bfloat16)
 
 
-def second_kernel(grid, orbitals_ref, occ_ref, first_ref, places_ref, table_ref, coef_ref, cube_ref):
+def second_kernel(grid, orbitals_ref, occ_ref, first_ref, places_ref, table_ref, coef_ref, later_ref, cube_ref):
+    later_ref[...] = jnp.zeros_like(later_ref)
     picks = RADIX * KX_ROWS
     cube_ref[:picks, :] = first_ref[...]
     cube_ref[picks:, :] = spectrum_of(grid, orbitals_ref[0], occ_ref[0], table_ref)
@@ -216,7 +217,7 @@
     return [pl.BlockSpec(memory_space=pltpu.VMEM)] * count
 
 
-def transform(cond_orbitals, occ_orbitals, occ_second, sphere_index):
+def transform(cond_orbitals, occ_orbitals, occ_second, sphere_index, band_shape):
     grid = cond_orbitals.shape[1]
     half_count = sphere_index.shape[1]
     table = jnp.asarray(packed_tables(grid))
@@ -240,22 +241,25 @@
     )(orbitals, table, sphere_index)
     return pl.pallas_call(
         functools.partial(second_kernel, grid),
-        out_shape=jax.ShapeDtypeStruct((STEPS, 2 * half_count), jnp.bfloat16),
+        out_shape=[
+            jax.ShapeDtypeStruct((STEPS, 2 * half_count), jnp.bfloat16),
+            jax.ShapeDtypeStruct((1, *band_shape), jnp.int32),
+        ],
         in_specs=in_vmem(5),
-        out_specs=in_vmem(1)[0],
+        out_specs=in_vmem(2),
         scratch_shapes=[pltpu.VMEM((STEPS * picks, 2 * LANES), jnp.bfloat16)],
         name="second_pair",
         **params,
     )(orbitals, occ_second, *handed)
 
 
-def pack_kernel(plan, targets, levels_ref, *refs):
+def pack_kernel(plan, turns, targets, levels_ref, *refs):
     rows, cols, row_width, col_width = plan
     arrived, outs, mixed_ref = refs[: cols // 2], refs[cols // 2 : -1], refs[-1]
     r, c = own_place()
     for j, ref in enumerate(arrived):
         mixed_ref[STEPS * j : STEPS * (j + 1), :] = ref[...].astype(jnp.float32)
-    weight = pair_weights([lax.rem(c - 2 * k + cols, cols) for k in range(cols // 2)], levels_ref)
+    weight = pair_weights([c ^ turn for turn in turns], levels_ref)
     columns = []
     for side in range(2):
         start = pl.multiple_of((c ^ side) * col_width, LANES)
@@ -266,11 +270,11 @@
         out_ref[:, row_width:] = columns[side]
 
 
-def pack(arrived, levels, targets, plan):
+def pack(arrived, levels, turns, targets, plan):
     rows, cols, row_width, col_width = plan
     pairs = STEPS * len(arrived)
     return pl.pallas_call(
-        functools.partial(pack_kernel, plan, targets),
+        functools.partial(pack_kernel, plan, turns, targets),
         out_shape=[jax.ShapeDtypeStruct((pairs, row_width + col_width), jnp.bfloat16)] * len(targets),
         in_specs=in_vmem(1 + len(arrived)),
         out_specs=in_vmem(len(targets)),
@@ -341,6 +345,15 @@
     return lax.ppermute(value, axis, [(i, (i + by) % devices) for i in range(devices)])
 
 
+def turned(value, axis, turn):
+    devices = lax.axis_size(axis)
+    return lax.ppermute(value, axis, [(i, i ^ turn) for i in range(devices)])
+
+
+def far_first(turn):
+    return (-turn.bit_length(), turn)
+
+
 def sent_to(value, step, side, rows, cols):
     moves = [(r * cols + c, (r + step) % rows * cols + (c ^ side)) for r in range(rows) for c in range(cols)]
     return lax.ppermute(value, ("row", "col"), moves)
@@ -352,11 +365,12 @@
     entries = 2 * sphere_index.shape[1]
     plan = (rows, cols, entries // rows, entries // cols)
     occ_second = shifted(occ_orbitals, "row", 1)
-    levels = jnp.stack([cond_energy, occ_energy, occ_band.astype(jnp.float32)])
-    own = transform(cond_orbitals, occ_orbitals, occ_second, sphere_index)
-    arrived = [own] + [shifted(own, "col", 2 * k) for k in range(1, cols // 2)]
+    own, later = transform(cond_orbitals, occ_orbitals, occ_second, sphere_index, occ_band.shape)
+    levels = jnp.stack([cond_energy, occ_energy, (occ_band + later[0]).astype(jnp.float32)])
+    turns = [0] + sorted(range(2, cols, 2), key=far_first)
+    arrived = [own] + [turned(own, "col", turn) for turn in turns[1:]]
     targets = [(step, side) for step in range(rows) for side in range(2)]
-    packed = pack(arrived, levels, targets, plan)
+    packed = pack(arrived, levels, turns, targets, plan)
     messages = [packed[0]] + [sent_to(value, *target, rows, cols) for value, target in zip(packed[1:], targets[1:])]
     return outer(messages, plan)
 

time: 46 us -> 45.9 us (level)
    ppermute x0 -> x3, waiting for transfers between devices: none -> 5.47 us  [turned(): return lax.ppermute(value, axis, [(i, i ^ turn) for i in range(devices)])]
    ppermute x4 -> x1, waiting for transfers between devices: 5.41 us -> 0.01 us  [shifted(): lax.ppermute(value, axis, [(i, (i + by) % devices) for i in range(devices)])]
    ppermute x4 -> x1, starting transfers between devices: 6.46 us -> 2.63 us  [shifted(): lax.ppermute(value, axis, [(i, (i + by) % devices) for i in range(devices)])]
    ppermute x0 -> x3, starting transfers between devices: none -> 3.68 us  [turned(): return lax.ppermute(value, axis, [(i, i ^ turn) for i in range(devices)])]
where the time goes in v5:
time: 45.9 us; the launch traced here: 45.7 us
  Pallas kernels  16 us (35%)
  starting transfers between devices  13.5 us (29%)
  waiting for transfers between devices  10.9 us (24%)
  local copies, waits for them, and re-layouts  3.82 us (8%)
  other arithmetic  1.34 us (3%)
    pallas_call x1, Pallas kernels, outer(): pl.pallas_call(functools.partial(outer_kernel, row_width, block, slots),...  11.4 us
    ppermute x7, starting transfers between devices, sent_to(): return lax.ppermute(value, ('row', 'col'), moves)  7.2 us
    ppermute x7, waiting for transfers between devices, sent_to(): return lax.ppermute(value, ('row', 'col'), moves)  5.47 us
    ppermute x3, waiting for transfers between devices, turned(): return lax.ppermute(value, axis, [(i, i ^ turn) for i in range(devices)])  5.47 us
    ppermute x3, starting transfers between devices, turned(): return lax.ppermute(value, axis, [(i, i ^ turn) for i in range(devices)])  3.68 us
    pallas_call x1, Pallas kernels, transform(): pl.pallas_call(functools.partial(second_kernel, grid), out_shape=[jax.Sha...  3.38 us
    unnamed x5, local copies, waits for them, and re-layouts  2.86 us
    ppermute x1, starting transfers between devices, shifted(): lax.ppermute(value, axis, [(i, (i + by) % devices) for i in range(devices)])  2.63 us
  transfers between devices with their start and end apart: 11, of which 5 were waited for; matrix products, arithmetic and copies ran while one was open for 7% of the time, Pallas kernels for 2%

profile of v5, /device:TPU:1, one launch (start us, length us, event | category | flops | bytes accessed | tf_op | source)
XLA Modules:
  0.0 45.7 jit_solution(8293469478445185141)
XLA Ops:
  0.0 2.6 %collective-permute-start = (bf16[1,48,2304]{2,1,0:T(8,128)(2,1)}, bf16[1,48,2304]{2,1,0:T(8,128)(2,1)S(1)}, u32[]{:S(2)}, u32[]{:S(2)}) collective-permute-start(bf16[1,48,2304]{2,1,0:T(8,128)(2,1)} %param.8), channel_id=1, source_target_pairs={{0,8},{8,16},{16,24},{24,0},{1,9},{9,17},{17,25},{25,1},{2,10},{10... | collective-permute-start | bytes 663560 | tf_op jit(solution)/shard_map/ppermute | solution.py:345
  2.6 0.9 %constant_dynamic-update-slice_fusion.1 = bf16[2,48,2304]{2,1,0:T(8,128)(2,1)S(1)} fusion(bf16[1,48,2304]{2,1,0:T(8,128)(2,1)} %param.7), kind=kLoop, calls=%fused_computation.1 | loop fusion | bytes 442368
  3.6 1.0 %constant_dynamic-update-slice_fusion.orbitals_ref = bf16[2,48,2304]{2,1,0:T(8,128)(2,1)S(1)} fusion(bf16[2,48,2304]{2,1,0:T(8,128)(2,1)S(1)} %constant_dynamic-update-slice_fusion.1, bf16[1,48,2304]{2,1,0:T(8,128)(2,1)} %param.8), kind=kLoop, calls=%fused_computation | loop fusion | bytes 442368 | tf_op jit(solution)/shard_map/concatenate | solution.py:224
  4.5 0.0 copy-start
  4.6 0.9 %copy-done = s32[3,8192]{1,0:T(4,128)S(1)} copy-done((s32[3,8192]{1,0:T(4,128)S(1)}, s32[3,8192]{1,0:T(4,128)}, u32[]{:S(2)}) %copy-start) | copy-done | bytes 98328
  5.4 0.0 copy-start.1
  5.5 1.0 %copy-done.1 = bf16[1760,128]{1,0:T(8,128)(2,1)S(1)} copy-done((bf16[1760,128]{1,0:T(8,128)(2,1)S(1)}, bf16[1760,128]{1,0:T(8,128)(2,1)}, u32[]{:S(2)}) %copy-start.1) | copy-done | bytes 450584
  6.5 0.9 %first_pair.1 = (bf16[240,256]{1,0:T(8,128)(2,1)S(1)}, s32[2,8192]{1,0:T(2,128)S(1)}, bf16[1760,128]{1,0:T(8,128)(2,1)S(1)}) custom-call(bf16[2,48,2304]{2,1,0:T(8,128)(2,1)S(1)} %constant_dynamic-update-slice_fusion.orbitals_ref, bf16[1760,128]{1,0:T(8,128)(2,1)S(1)} %copy-done.1, s32[3,8192]{1,0:T(4,128)S(1)} %copy-done), custom_call_target="tpu_custom_call" | custom-call | flops 2000000000 | bytes 2000000 | tf_op jit(solution)/shard_map/first_pair/pallas_call | solution.py:230
  7.3 0.0 collective-permute-done.occ_ref
  7.4 3.4 %second_pair.1 = (bf16[2,16384]{1,0:T(2,128)(2,1)S(1)}, s32[1,32]{1,0:T(1,128)S(1)}) custom-call(bf16[2,48,2304]{2,1,0:T(8,128)(2,1)S(1)} %constant_dynamic-update-slice_fusion.orbitals_ref, bf16[1,48,2304]{2,1,0:T(8,128)(2,1)S(1)} %collective-permute-done.occ_ref, bf16[240,256]{1,0:T(8,128)(2,1)S(1)} %get-tuple-element.18.first_ref, ...), custom_call_target="tpu_custom_call" | custom-call | flops 2000000000 | bytes 2000000 | tf_op jit(solution)/shard_map/second_pair/pallas_call | solution.py:242
  10.7 1.4 %collective-permute-start.3 = (bf16[2,16384]{1,0:T(2,128)(2,1)S(1)}, bf16[2,16384]{1,0:T(2,128)(2,1)S(1)}, u32[]{:S(2)}, u32[]{:S(2)}) collective-permute-start(bf16[2,16384]{1,0:T(2,128)(2,1)S(1)} %get-tuple-element.22.refs_0_), channel_id=1, source_target_pairs={{0,2},{1,3},{2,0},{3,1},{4,6},{5,7},{6,4},{7,5},{8,10},{9,11},{10,... | collective-permute-start | bytes 196616 | tf_op jit(solution)/shard_map/ppermute | solution.py:350
  12.1 2.2 %collective-permute-start.2 = (bf16[2,16384]{1,0:T(2,128)(2,1)S(1)}, bf16[2,16384]{1,0:T(2,128)(2,1)S(1)}, u32[]{:S(2)}, u32[]{:S(2)}) collective-permute-start(bf16[2,16384]{1,0:T(2,128)(2,1)S(1)} %get-tuple-element.22.refs_0_), channel_id=1, source_target_pairs={{0,6},{1,7},{2,4},{3,5},{4,2},{5,3},{6,0},{7,1},{8,14},{9,15},{10,... | collective-permute-start | bytes 196616 | tf_op jit(solution)/shard_map/ppermute | solution.py:350
  14.3 0.1 collective-permute-start.1
  14.4 0.7 %fusion.1 = f32[1,32]{1,0:T(1,128)S(1)} fusion(s32[32]{0:T(128)} %param.11, s32[1,32]{1,0:T(1,128)S(1)} %get-tuple-element.21), kind=kLoop, calls=%fused_computation.5 | loop fusion | flops 64 | bytes 384 | tf_op jit(solution)/shard_map/stack | solution.py:369
  15.1 0.7 %pad_maximum_fusion.levels_ref = f32[3,32]{1,0:T(4,128)S(1)} fusion(f32[1,32]{1,0:T(1,128)S(1)} %fusion.1, f32[1,32]{1,0:T(1,128)} %bitcast.10, f32[1,32]{1,0:T(1,128)} %bitcast.11), kind=kLoop, calls=%fused_computation.2 | loop fusion | flops 192 | bytes 768 | tf_op jit(solution)/shard_map/stack | solution.py:369
  15.8 0.0 collective-permute-done.3.refs_3_
  15.8 2.5 %collective-permute-done.2.refs_2_ = bf16[2,16384]{1,0:T(2,128)(2,1)S(1)} collective-permute-done((bf16[2,16384]{1,0:T(2,128)(2,1)S(1)}, bf16[2,16384]{1,0:T(2,128)(2,1)S(1)}, u32[]{:S(2)}, u32[]{:S(2)}) %collective-permute-start.2) | collective-permute-done | bytes 65568 | tf_op jit(solution)/shard_map/ppermute | solution.py:350
  18.2 3.0 %collective-permute-done.1.refs_1_ = bf16[2,16384]{1,0:T(2,128)(2,1)S(1)} collective-permute-done((bf16[2,16384]{1,0:T(2,128)(2,1)S(1)}, bf16[2,16384]{1,0:T(2,128)(2,1)S(1)}, u32[]{:S(2)}, u32[]{:S(2)}) %collective-permute-start.1) | collective-permute-done | bytes 65568 | tf_op jit(solution)/shard_map/ppermute | solution.py:350
  21.2 0.3 pack.1
  21.5 1.3 %collective-permute-start.4 = (bf16[8,6144]{1,0:T(8,128)(2,1)S(1)}, bf16[8,6144]{1,0:T(8,128)(2,1)S(1)}, u32[]{:S(2)}, u32[]{:S(2)}) collective-permute-start(bf16[8,6144]{1,0:T(8,128)(2,1)S(1)} %get-tuple-element.24), channel_id=1, source_target_pairs={{0,1},{1,0},{2,3},{3,2},{4,5},{5,4},{6,7},{7,6},{8,9},{9,8},{10,11... | collective-permute-start | bytes 294920 | tf_op jit(solution)/shard_map/ppermute | solution.py:359
  22.8 1.1 %collective-permute-start.5 = (bf16[8,6144]{1,0:T(8,128)(2,1)S(1)}, bf16[8,6144]{1,0:T(8,128)(2,1)S(1)}, u32[]{:S(2)}, u32[]{:S(2)}) collective-permute-start(bf16[8,6144]{1,0:T(8,128)(2,1)S(1)} %get-tuple-element.25), channel_id=1, source_target_pairs={{0,8},{1,9},{2,10},{3,11},{4,12},{5,13},{6,14},{7,15},{8,16},{9,17... | collective-permute-start | bytes 294920 | tf_op jit(solution)/shard_map/ppermute | solution.py:359
  24.0 0.0 collective-permute-start.6
  24.0 0.9 %collective-permute-start.7 = (bf16[8,6144]{1,0:T(8,128)(2,1)S(1)}, bf16[8,6144]{1,0:T(8,128)(2,1)S(1)}, u32[]{:S(2)}, u32[]{:S(2)}) collective-permute-start(bf16[8,6144]{1,0:T(8,128)(2,1)S(1)} %get-tuple-element.27), channel_id=1, source_target_pairs={{0,16},{1,17},{2,18},{3,19},{4,20},{5,21},{6,22},{7,23},{8,24},{9,... | collective-permute-start | bytes 294920 | tf_op jit(solution)/shard_map/ppermute | solution.py:359
  24.8 1.5 %collective-permute-start.8 = (bf16[8,6144]{1,0:T(8,128)(2,1)S(1)}, bf16[8,6144]{1,0:T(8,128)(2,1)S(1)}, u32[]{:S(2)}, u32[]{:S(2)}) collective-permute-start(bf16[8,6144]{1,0:T(8,128)(2,1)S(1)} %get-tuple-element.28), channel_id=1, source_target_pairs={{0,17},{1,16},{2,19},{3,18},{4,21},{5,20},{6,23},{7,22},{8,25},{9,... | collective-permute-start | bytes 294920 | tf_op jit(solution)/shard_map/ppermute | solution.py:359
  26.3 0.0 collective-permute-done.4.refs_1_
  26.3 1.2 %collective-permute-start.9 = (bf16[8,6144]{1,0:T(8,128)(2,1)S(1)}, bf16[8,6144]{1,0:T(8,128)(2,1)S(1)}, u32[]{:S(2)}, u32[]{:S(2)}) collective-permute-start(bf16[8,6144]{1,0:T(8,128)(2,1)S(1)} %get-tuple-element.29), channel_id=1, source_target_pairs={{0,24},{1,25},{2,26},{3,27},{4,28},{5,29},{6,30},{7,31},{8,0},{9,1... | collective-permute-start | bytes 294920 | tf_op jit(solution)/shard_map/ppermute | solution.py:359
  27.6 0.0 collective-permute-done.5.refs_2_
  27.6 1.2 %collective-permute-start.10 = (bf16[8,6144]{1,0:T(8,128)(2,1)S(1)}, bf16[8,6144]{1,0:T(8,128)(2,1)S(1)}, u32[]{:S(2)}, u32[]{:S(2)}) collective-permute-start(bf16[8,6144]{1,0:T(8,128)(2,1)S(1)} %get-tuple-element.30), channel_id=1, source_target_pairs={{0,25},{1,24},{2,27},{3,26},{4,29},{5,28},{6,31},{7,30},{8,1},{9,0... | collective-permute-start | bytes 294920 | tf_op jit(solution)/shard_map/ppermute | solution.py:359
  28.7 0.5 %collective-permute-done.6.refs_3_ = bf16[8,6144]{1,0:T(8,128)(2,1)S(1)} collective-permute-done((bf16[8,6144]{1,0:T(8,128)(2,1)S(1)}, bf16[8,6144]{1,0:T(8,128)(2,1)S(1)}, u32[]{:S(2)}, u32[]{:S(2)}) %collective-permute-start.6) | collective-permute-done | bytes 98336 | tf_op jit(solution)/shard_map/ppermute | solution.py:359
  29.2 3.8 %collective-permute-done.7.refs_4_ = bf16[8,6144]{1,0:T(8,128)(2,1)S(1)} collective-permute-done((bf16[8,6144]{1,0:T(8,128)(2,1)S(1)}, bf16[8,6144]{1,0:T(8,128)(2,1)S(1)}, u32[]{:S(2)}, u32[]{:S(2)}) %collective-permute-start.7) | collective-permute-done | bytes 98336 | tf_op jit(solution)/shard_map/ppermute | solution.py:359
  33.1 0.0 collective-permute-done.8.refs_5_
  33.1 1.1 %collective-permute-done.9.refs_6_ = bf16[8,6144]{1,0:T(8,128)(2,1)S(1)} collective-permute-done((bf16[8,6144]{1,0:T(8,128)(2,1)S(1)}, bf16[8,6144]{1,0:T(8,128)(2,1)S(1)}, u32[]{:S(2)}, u32[]{:S(2)}) %collective-permute-start.9) | collective-permute-done | bytes 98336 | tf_op jit(solution)/shard_map/ppermute | solution.py:359
  34.2 0.0 collective-permute-done.10.refs_7_
  34.2 11.4 %outer.1 = f32[4096,2048]{1,0:T(8,128)} custom-call(bf16[8,6144]{1,0:T(8,128)(2,1)S(1)} %get-tuple-element.23.refs_0_, bf16[8,6144]{1,0:T(8,128)(2,1)S(1)} %collective-permute-done.4.refs_1_, bf16[8,6144]{1,0:T(8,128)(2,1)S(1)} %collective-permute-done.5.refs_2_, bf16[8,6144]{1,0:T(8,128)(2,1)S(1)} %collective-permute-done.6.refs_3_, ...), custom_call_target="tpu_custom_call" | custom-call | flops 10000000000 | bytes 30000000 | tf_op jit(solution)/shard_map/outer/pallas_call | solution.py:326
Async XLA Ops:
  0.0 7.3 %collective-permute-start = (bf16[1,48,2304]{2,1,0:T(8,128)(2,1)}, bf16[1,48,2304]{2,1,0:T(8,128)(2,1)S(1)}, u32[]{:S(2)}, u32[]{:S(2)}) collective-permute-start(bf16[1,48,2304]{2,1,0:T(8,128)(2,1)} %param.8), channel_id=1, source_target_pairs={{0,8},{8,16},{16,24},{24,0},{1,9},{9,17},{17,25},{25,1},{2,10},{10... | collective-permute-start | bytes 663560 | tf_op jit(solution)/shard_map/ppermute | solution.py:345
  4.5 0.9 %copy-start = (s32[3,8192]{1,0:T(4,128)S(1)}, s32[3,8192]{1,0:T(4,128)}, u32[]{:S(2)}) copy-start(s32[3,8192]{1,0:T(4,128)} %sphere_ref.1) | copy-start | bytes 294916
  5.4 1.0 %copy-start.1 = (bf16[1760,128]{1,0:T(8,128)(2,1)S(1)}, bf16[1760,128]{1,0:T(8,128)(2,1)}, u32[]{:S(2)}) copy-start(bf16[1760,128]{1,0:T(8,128)(2,1)} %constant.2.clone.table_ref) | copy-start | bytes 1351684
  10.7 5.0 %collective-permute-start.3 = (bf16[2,16384]{1,0:T(2,128)(2,1)S(1)}, bf16[2,16384]{1,0:T(2,128)(2,1)S(1)}, u32[]{:S(2)}, u32[]{:S(2)}) collective-permute-start(bf16[2,16384]{1,0:T(2,128)(2,1)S(1)} %get-tuple-element.22.refs_0_), channel_id=1, source_target_pairs={{0,2},{1,3},{2,0},{3,1},{4,6},{5,7},{6,4},{7,5},{8,10},{9,11},{10,... | collective-permute-start | bytes 196616 | tf_op jit(solution)/shard_map/ppermute | solution.py:350
  12.1 6.1 %collective-permute-start.2 = (bf16[2,16384]{1,0:T(2,128)(2,1)S(1)}, bf16[2,16384]{1,0:T(2,128)(2,1)S(1)}, u32[]{:S(2)}, u32[]{:S(2)}) collective-permute-start(bf16[2,16384]{1,0:T(2,128)(2,1)S(1)} %get-tuple-element.22.refs_0_), channel_id=1, source_target_pairs={{0,6},{1,7},{2,4},{3,5},{4,2},{5,3},{6,0},{7,1},{8,14},{9,15},{10,... | collective-permute-start | bytes 196616 | tf_op jit(solution)/shard_map/ppermute | solution.py:350
  14.3 6.9 %collective-permute-start.1 = (bf16[2,16384]{1,0:T(2,128)(2,1)S(1)}, bf16[2,16384]{1,0:T(2,128)(2,1)S(1)}, u32[]{:S(2)}, u32[]{:S(2)}) collective-permute-start(bf16[2,16384]{1,0:T(2,128)(2,1)S(1)} %get-tuple-element.22.refs_0_), channel_id=1, source_target_pairs={{0,4},{1,5},{2,6},{3,7},{4,0},{5,1},{6,2},{7,3},{8,12},{9,13},{10,... | collective-permute-start | bytes 196616 | tf_op jit(solution)/shard_map/ppermute | solution.py:350
  21.5 4.8 %collective-permute-start.4 = (bf16[8,6144]{1,0:T(8,128)(2,1)S(1)}, bf16[8,6144]{1,0:T(8,128)(2,1)S(1)}, u32[]{:S(2)}, u32[]{:S(2)}) collective-permute-start(bf16[8,6144]{1,0:T(8,128)(2,1)S(1)} %get-tuple-element.24), channel_id=1, source_target_pairs={{0,1},{1,0},{2,3},{3,2},{4,5},{5,4},{6,7},{7,6},{8,9},{9,8},{10,11... | collective-permute-start | bytes 294920 | tf_op jit(solution)/shard_map/ppermute | solution.py:359
  22.8 4.8 %collective-permute-start.5 = (bf16[8,6144]{1,0:T(8,128)(2,1)S(1)}, bf16[8,6144]{1,0:T(8,128)(2,1)S(1)}, u32[]{:S(2)}, u32[]{:S(2)}) collective-permute-start(bf16[8,6144]{1,0:T(8,128)(2,1)S(1)} %get-tuple-element.25), channel_id=1, source_target_pairs={{0,8},{1,9},{2,10},{3,11},{4,12},{5,13},{6,14},{7,15},{8,16},{9,17... | collective-permute-start | bytes 294920 | tf_op jit(solution)/shard_map/ppermute | solution.py:359
  24.0 5.3 %collective-permute-start.6 = (bf16[8,6144]{1,0:T(8,128)(2,1)S(1)}, bf16[8,6144]{1,0:T(8,128)(2,1)S(1)}, u32[]{:S(2)}, u32[]{:S(2)}) collective-permute-start(bf16[8,6144]{1,0:T(8,128)(2,1)S(1)} %get-tuple-element.26), channel_id=1, source_target_pairs={{0,9},{1,8},{2,11},{3,10},{4,13},{5,12},{6,15},{7,14},{8,17},{9,16... | collective-permute-start | bytes 294920 | tf_op jit(solution)/shard_map/ppermute | solution.py:359
  24.0 9.1 %collective-permute-start.7 = (bf16[8,6144]{1,0:T(8,128)(2,1)S(1)}, bf16[8,6144]{1,0:T(8,128)(2,1)S(1)}, u32[]{:S(2)}, u32[]{:S(2)}) collective-permute-start(bf16[8,6144]{1,0:T(8,128)(2,1)S(1)} %get-tuple-element.27), channel_id=1, source_target_pairs={{0,16},{1,17},{2,18},{3,19},{4,20},{5,21},{6,22},{7,23},{8,24},{9,... | collective-permute-start | bytes 294920 | tf_op jit(solution)/shard_map/ppermute | solution.py:359
  24.8 8.3 %collective-permute-start.8 = (bf16[8,6144]{1,0:T(8,128)(2,1)S(1)}, bf16[8,6144]{1,0:T(8,128)(2,1)S(1)}, u32[]{:S(2)}, u32[]{:S(2)}) collective-permute-start(bf16[8,6144]{1,0:T(8,128)(2,1)S(1)} %get-tuple-element.28), channel_id=1, source_target_pairs={{0,17},{1,16},{2,19},{3,18},{4,21},{5,20},{6,23},{7,22},{8,25},{9,... | collective-permute-start | bytes 294920 | tf_op jit(solution)/shard_map/ppermute | solution.py:359
  26.3 7.9 %collective-permute-start.9 = (bf16[8,6144]{1,0:T(8,128)(2,1)S(1)}, bf16[8,6144]{1,0:T(8,128)(2,1)S(1)}, u32[]{:S(2)}, u32[]{:S(2)}) collective-permute-start(bf16[8,6144]{1,0:T(8,128)(2,1)S(1)} %get-tuple-element.29), channel_id=1, source_target_pairs={{0,24},{1,25},{2,26},{3,27},{4,28},{5,29},{6,30},{7,31},{8,0},{9,1... | collective-permute-start | bytes 294920 | tf_op jit(solution)/shard_map/ppermute | solution.py:359
  27.6 6.6 %collective-permute-start.10 = (bf16[8,6144]{1,0:T(8,128)(2,1)S(1)}, bf16[8,6144]{1,0:T(8,128)(2,1)S(1)}, u32[]{:S(2)}, u32[]{:S(2)}) collective-permute-start(bf16[8,6144]{1,0:T(8,128)(2,1)S(1)} %get-tuple-element.30), channel_id=1, source_target_pairs={{0,25},{1,24},{2,27},{3,26},{4,29},{5,28},{6,31},{7,30},{8,1},{9,0... | collective-permute-start | bytes 294920 | tf_op jit(solution)/shard_map/ppermute | solution.py:359

commit v6 on v5

--- a/solution.py
+++ b/solution.py
@@ -264,10 +264,10 @@
     for side in range(2):
         start = pl.multiple_of((c ^ side) * col_width, LANES)
         columns.append((weight * mixed_ref[:, pl.ds(start, col_width)]).astype(jnp.bfloat16))
-    for (step, side), out_ref in zip(targets, outs):
-        start = pl.multiple_of(lax.rem(r + step, rows) * row_width, LANES)
-        out_ref[:, :row_width] = mixed_ref[:, pl.ds(start, row_width)].astype(jnp.bfloat16)
-        out_ref[:, row_width:] = columns[side]
+    for (turn, side), out_ref in zip(targets, outs):
+        start = pl.multiple_of((r ^ turn) // 2 * (2 * row_width), LANES)
+        out_ref[:, : 2 * row_width] = mixed_ref[:, pl.ds(start, 2 * row_width)].astype(jnp.bfloat16)
+        out_ref[:, 2 * row_width :] = columns[side]
 
 
 def pack(arrived, levels, turns, targets, plan):
@@ -275,7 +275,7 @@
     pairs = STEPS * len(arrived)
     return pl.pallas_call(
         functools.partial(pack_kernel, plan, turns, targets),
-        out_shape=[jax.ShapeDtypeStruct((pairs, row_width + col_width), jnp.bfloat16)] * len(targets),
+        out_shape=[jax.ShapeDtypeStruct((pairs, 2 * row_width + col_width), jnp.bfloat16)] * len(targets),
         in_specs=in_vmem(1 + len(arrived)),
         out_specs=in_vmem(len(targets)),
         scratch_shapes=[pltpu.VMEM((pairs, arrived[0].shape[1]), jnp.float32)],
@@ -285,14 +285,21 @@
     )(levels, *arrived)
 
 
+def stacked(refs, lanes):
+    return jnp.concatenate([ref[:, lanes].astype(jnp.float32) for ref in refs], axis=0).astype(jnp.bfloat16)
+
+
 def outer_kernel(row_width, block, slots, *refs):
     messages, (out_ref, left_ref, right_ref, held_ref, sems) = refs[:-5], refs[-5:]
     depth = messages[0].shape[0]
     merge = max(1, 16 // depth)
+    r, _ = own_place()
+    own_rows = pl.ds(pl.multiple_of((r & 1) * row_width, LANES), row_width)
+    columns = slice(2 * row_width, None)
     for j in range(0, len(messages), merge):
-        whole = jnp.concatenate([ref[...].astype(jnp.float32) for ref in messages[j : j + merge]], axis=0).astype(jnp.bfloat16)
-        left_ref[depth * j : depth * (j + merge), :] = whole[:, :row_width]
-        right_ref[depth * j : depth * (j + merge), :] = whole[:, row_width:]
+        here = slice(depth * j, depth * (j + merge))
+        left_ref[here, :] = stacked(messages[j : j + merge], own_rows)
+        right_ref[here, :] = stacked(messages[j : j + merge], columns)
     count = row_width // block
 
     def copy_out(i, slot):
@@ -350,12 +357,8 @@
     return lax.ppermute(value, axis, [(i, i ^ turn) for i in range(devices)])
 
 
-def far_first(turn):
-    return (-turn.bit_length(), turn)
-
-
-def sent_to(value, step, side, rows, cols):
-    moves = [(r * cols + c, (r + step) % rows * cols + (c ^ side)) for r in range(rows) for c in range(cols)]
+def sent_across(value, turn, side, rows, cols):
+    moves = [(r * cols + c, (r ^ turn) * cols + (c ^ side)) for r in range(rows) for c in range(cols)]
     return lax.ppermute(value, ("row", "col"), moves)
 
 
@@ -367,12 +370,12 @@
     occ_second = shifted(occ_orbitals, "row", 1)
     own, later = transform(cond_orbitals, occ_orbitals, occ_second, sphere_index, occ_band.shape)
     levels = jnp.stack([cond_energy, occ_energy, (occ_band + later[0]).astype(jnp.float32)])
-    turns = [0] + sorted(range(2, cols, 2), key=far_first)
+    turns = [0, 2, *range(cols - 2, 2, -2)]
     arrived = [own] + [turned(own, "col", turn) for turn in turns[1:]]
-    targets = [(step, side) for step in range(rows) for side in range(2)]
-    packed = pack(arrived, levels, turns, targets, plan)
-    messages = [packed[0]] + [sent_to(value, *target, rows, cols) for value, target in zip(packed[1:], targets[1:])]
-    return outer(messages, plan)
+    targets = [(turn, side) for turn in range(0, rows, 2) for side in range(2)]
+    packed = list(pack(arrived, levels, turns, targets, plan))
+    straight = packed[:1] + [sent_across(value, *target, rows, cols) for value, target in zip(packed[1:], targets[1:])]
+    return outer(straight + [turned(value, "row", 1) for value in straight], plan)
 
 
 def solution(mesh):

time: 45.9 us -> 44.6 us (0.972)
  waiting for transfers between devices: 10.9 us -> 7.81 us
  starting transfers between devices: 13.5 us -> 15.2 us
    ppermute x3 -> x7, starting transfers between devices: 3.68 us -> 9.57 us  [turned(): return lax.ppermute(value, axis, [(i, i ^ turn) for i in range(devices)])]
    ppermute x7 -> x3, starting transfers between devices: 7.2 us -> 2.96 us  [sent_across(): return lax.ppermute(value, ('row', 'col'), moves)]
    ppermute x7 -> x3, waiting for transfers between devices: 5.47 us -> 2.97 us  [sent_across(): return lax.ppermute(value, ('row', 'col'), moves)]
    ppermute x3 -> x7, waiting for transfers between devices: 5.47 us -> 4.84 us  [turned(): return lax.ppermute(value, axis, [(i, i ^ turn) for i in range(devices)])]
  transfers between devices with their start and end apart: 11 -> 11, of which waited for: 5 -> 7; matrix products, arithmetic and copies ran while one was open for 7% -> 7% of each run, Pallas kernels for 2% -> 2%
where the time goes in v6:
time: 44.6 us; the launch traced here: 44.2 us
  Pallas kernels  16 us (36%)
  starting transfers between devices  15.2 us (34%)
  waiting for transfers between devices  7.81 us (18%)
  local copies, waits for them, and re-layouts  3.82 us (9%)
  other arithmetic  1.34 us (3%)
    pallas_call x1, Pallas kernels, outer(): pl.pallas_call(functools.partial(outer_kernel, row_width, block, slots),...  11.4 us
    ppermute x7, starting transfers between devices, turned(): return lax.ppermute(value, axis, [(i, i ^ turn) for i in range(devices)])  9.57 us
    ppermute x7, waiting for transfers between devices, turned(): return lax.ppermute(value, axis, [(i, i ^ turn) for i in range(devices)])  4.84 us
    pallas_call x1, Pallas kernels, transform(): pl.pallas_call(functools.partial(second_kernel, grid), out_shape=[jax.Sha...  3.39 us
    ppermute x3, waiting for transfers between devices, sent_across(): return lax.ppermute(value, ('row', 'col'), moves)  2.97 us
    ppermute x3, starting transfers between devices, sent_across(): return lax.ppermute(value, ('row', 'col'), moves)  2.96 us
    unnamed x5, local copies, waits for them, and re-layouts  2.86 us
    ppermute x1, starting transfers between devices, shifted(): lax.ppermute(value, axis, [(i, (i + by) % devices) for i in range(devices)])  2.63 us
  transfers between devices with their start and end apart: 11, of which 7 were waited for; matrix products, arithmetic and copies ran while one was open for 7% of the time, Pallas kernels for 2%

profile of v6, /device:TPU:1, one launch (start us, length us, event | category | flops | bytes accessed | tf_op | source)
XLA Modules:
  0.0 44.2 jit_solution(13251005137867975497)
XLA Ops:
  0.0 2.6 %collective-permute-start = (bf16[1,48,2304]{2,1,0:T(8,128)(2,1)}, bf16[1,48,2304]{2,1,0:T(8,128)(2,1)S(1)}, u32[]{:S(2)}, u32[]{:S(2)}) collective-permute-start(bf16[1,48,2304]{2,1,0:T(8,128)(2,1)} %param.8), channel_id=1, source_target_pairs={{0,8},{8,16},{16,24},{24,0},{1,9},{9,17},{17,25},{25,1},{2,10},{10... | collective-permute-start | bytes 663560 | tf_op jit(solution)/shard_map/ppermute | solution.py:352
  2.6 0.9 %constant_dynamic-update-slice_fusion.1 = bf16[2,48,2304]{2,1,0:T(8,128)(2,1)S(1)} fusion(bf16[1,48,2304]{2,1,0:T(8,128)(2,1)} %param.7), kind=kLoop, calls=%fused_computation.1 | loop fusion | bytes 442368
  3.6 1.0 %constant_dynamic-update-slice_fusion.orbitals_ref = bf16[2,48,2304]{2,1,0:T(8,128)(2,1)S(1)} fusion(bf16[2,48,2304]{2,1,0:T(8,128)(2,1)S(1)} %constant_dynamic-update-slice_fusion.1, bf16[1,48,2304]{2,1,0:T(8,128)(2,1)} %param.8), kind=kLoop, calls=%fused_computation | loop fusion | bytes 442368 | tf_op jit(solution)/shard_map/concatenate | solution.py:224
  4.5 0.0 copy-start
  4.6 0.9 %copy-done = s32[3,8192]{1,0:T(4,128)S(1)} copy-done((s32[3,8192]{1,0:T(4,128)S(1)}, s32[3,8192]{1,0:T(4,128)}, u32[]{:S(2)}) %copy-start) | copy-done | bytes 98328
  5.4 0.0 copy-start.1
  5.5 1.0 %copy-done.1 = bf16[1760,128]{1,0:T(8,128)(2,1)S(1)} copy-done((bf16[1760,128]{1,0:T(8,128)(2,1)S(1)}, bf16[1760,128]{1,0:T(8,128)(2,1)}, u32[]{:S(2)}) %copy-start.1) | copy-done | bytes 450584
  6.5 0.9 %first_pair.1 = (bf16[240,256]{1,0:T(8,128)(2,1)S(1)}, s32[2,8192]{1,0:T(2,128)S(1)}, bf16[1760,128]{1,0:T(8,128)(2,1)S(1)}) custom-call(bf16[2,48,2304]{2,1,0:T(8,128)(2,1)S(1)} %constant_dynamic-update-slice_fusion.orbitals_ref, bf16[1760,128]{1,0:T(8,128)(2,1)S(1)} %copy-done.1, s32[3,8192]{1,0:T(4,128)S(1)} %copy-done), custom_call_target="tpu_custom_call" | custom-call | flops 2000000000 | bytes 2000000 | tf_op jit(solution)/shard_map/first_pair/pallas_call | solution.py:230
  7.3 0.0 collective-permute-done.occ_ref
  7.4 3.4 %second_pair.1 = (bf16[2,16384]{1,0:T(2,128)(2,1)S(1)}, s32[1,32]{1,0:T(1,128)S(1)}) custom-call(bf16[2,48,2304]{2,1,0:T(8,128)(2,1)S(1)} %constant_dynamic-update-slice_fusion.orbitals_ref, bf16[1,48,2304]{2,1,0:T(8,128)(2,1)S(1)} %collective-permute-done.occ_ref, bf16[240,256]{1,0:T(8,128)(2,1)S(1)} %get-tuple-element.14.first_ref, ...), custom_call_target="tpu_custom_call" | custom-call | flops 2000000000 | bytes 2000000 | tf_op jit(solution)/shard_map/second_pair/pallas_call | solution.py:242
  10.7 2.4 %collective-permute-start.3 = (bf16[2,16384]{1,0:T(2,128)(2,1)S(1)}, bf16[2,16384]{1,0:T(2,128)(2,1)S(1)}, u32[]{:S(2)}, u32[]{:S(2)}) collective-permute-start(bf16[2,16384]{1,0:T(2,128)(2,1)S(1)} %get-tuple-element.18.refs_0_), channel_id=1, source_target_pairs={{0,4},{1,5},{2,6},{3,7},{4,0},{5,1},{6,2},{7,3},{8,12},{9,13},{10,... | collective-permute-start | bytes 196616 | tf_op jit(solution)/shard_map/ppermute | solution.py:357
  13.1 1.1 %collective-permute-start.2 = (bf16[2,16384]{1,0:T(2,128)(2,1)S(1)}, bf16[2,16384]{1,0:T(2,128)(2,1)S(1)}, u32[]{:S(2)}, u32[]{:S(2)}) collective-permute-start(bf16[2,16384]{1,0:T(2,128)(2,1)S(1)} %get-tuple-element.18.refs_0_), channel_id=1, source_target_pairs={{0,6},{1,7},{2,4},{3,5},{4,2},{5,3},{6,0},{7,1},{8,14},{9,15},{10,... | collective-permute-start | bytes 196616 | tf_op jit(solution)/shard_map/ppermute | solution.py:357
  14.2 0.2 collective-permute-start.1
  14.4 0.7 %fusion.1 = f32[1,32]{1,0:T(1,128)S(1)} fusion(s32[32]{0:T(128)} %param.11, s32[1,32]{1,0:T(1,128)S(1)} %get-tuple-element.17), kind=kLoop, calls=%fused_computation.5 | loop fusion | flops 64 | bytes 384 | tf_op jit(solution)/shard_map/stack | solution.py:372
  15.1 0.7 %pad_maximum_fusion.levels_ref = f32[3,32]{1,0:T(4,128)S(1)} fusion(f32[1,32]{1,0:T(1,128)S(1)} %fusion.1, f32[1,32]{1,0:T(1,128)} %bitcast.10, f32[1,32]{1,0:T(1,128)} %bitcast.11), kind=kLoop, calls=%fused_computation.2 | loop fusion | flops 192 | bytes 768 | tf_op jit(solution)/shard_map/stack | solution.py:372
  15.8 1.1 %collective-permute-done.3.refs_3_ = bf16[2,16384]{1,0:T(2,128)(2,1)S(1)} collective-permute-done((bf16[2,16384]{1,0:T(2,128)(2,1)S(1)}, bf16[2,16384]{1,0:T(2,128)(2,1)S(1)}, u32[]{:S(2)}, u32[]{:S(2)}) %collective-permute-start.3) | collective-permute-done | bytes 65568 | tf_op jit(solution)/shard_map/ppermute | solution.py:357
  16.9 1.8 %collective-permute-done.2.refs_2_ = bf16[2,16384]{1,0:T(2,128)(2,1)S(1)} collective-permute-done((bf16[2,16384]{1,0:T(2,128)(2,1)S(1)}, bf16[2,16384]{1,0:T(2,128)(2,1)S(1)}, u32[]{:S(2)}, u32[]{:S(2)}) %collective-permute-start.2) | collective-permute-done | bytes 65568 | tf_op jit(solution)/shard_map/ppermute | solution.py:357
  18.7 0.5 %collective-permute-done.1.refs_1_ = bf16[2,16384]{1,0:T(2,128)(2,1)S(1)} collective-permute-done((bf16[2,16384]{1,0:T(2,128)(2,1)S(1)}, bf16[2,16384]{1,0:T(2,128)(2,1)S(1)}, u32[]{:S(2)}, u32[]{:S(2)}) %collective-permute-start.1) | collective-permute-done | bytes 65568 | tf_op jit(solution)/shard_map/ppermute | solution.py:357
  19.2 0.3 pack.1
  19.5 1.7 %collective-permute-start.4 = (bf16[8,10240]{1,0:T(8,128)(2,1)S(1)}, bf16[8,10240]{1,0:T(8,128)(2,1)S(1)}, u32[]{:S(2)}, u32[]{:S(2)}) collective-permute-start(bf16[8,10240]{1,0:T(8,128)(2,1)S(1)} %get-tuple-element.20), channel_id=1, source_target_pairs={{0,1},{1,0},{2,3},{3,2},{4,5},{5,4},{6,7},{7,6},{8,9},{9,8},{10,11... | collective-permute-start | bytes 491528 | tf_op jit(solution)/shard_map/ppermute | solution.py:362
  21.2 0.0 collective-permute-start.5
  21.2 1.3 %collective-permute-start.6 = (bf16[8,10240]{1,0:T(8,128)(2,1)S(1)}, bf16[8,10240]{1,0:T(8,128)(2,1)S(1)}, u32[]{:S(2)}, u32[]{:S(2)}) collective-permute-start(bf16[8,10240]{1,0:T(8,128)(2,1)S(1)} %get-tuple-element.22), channel_id=1, source_target_pairs={{0,17},{1,16},{2,19},{3,18},{4,21},{5,20},{6,23},{7,22},{8,25},{9,... | collective-permute-start | bytes 491528 | tf_op jit(solution)/shard_map/ppermute | solution.py:362
  22.5 1.6 %collective-permute-start.7 = (bf16[8,10240]{1,0:T(8,128)(2,1)S(1)}, bf16[8,10240]{1,0:T(8,128)(2,1)S(1)}, u32[]{:S(2)}, u32[]{:S(2)}) collective-permute-start(bf16[8,10240]{1,0:T(8,128)(2,1)S(1)} %get-tuple-element.19.refs_0_), channel_id=1, source_target_pairs={{0,8},{8,0},{16,24},{24,16},{1,9},{9,1},{17,25},{25,17},{2,10},{10... | collective-permute-start | bytes 491528 | tf_op jit(solution)/shard_map/ppermute | solution.py:357
  24.1 0.5 %collective-permute-done.4.refs_1_ = bf16[8,10240]{1,0:T(8,128)(2,1)S(1)} collective-permute-done((bf16[8,10240]{1,0:T(8,128)(2,1)S(1)}, bf16[8,10240]{1,0:T(8,128)(2,1)S(1)}, u32[]{:S(2)}, u32[]{:S(2)}) %collective-permute-start.4) | collective-permute-done | bytes 163872 | tf_op jit(solution)/shard_map/ppermute | solution.py:362
  24.6 2.6 %collective-permute-start.8 = (bf16[8,10240]{1,0:T(8,128)(2,1)S(1)}, bf16[8,10240]{1,0:T(8,128)(2,1)S(1)}, u32[]{:S(2)}, u32[]{:S(2)}) collective-permute-start(bf16[8,10240]{1,0:T(8,128)(2,1)S(1)} %collective-permute-done.4.refs_1_), channel_id=1, source_target_pairs={{0,8},{8,0},{16,24},{24,16},{1,9},{9,1},{17,25},{25,17},{2,10},{10... | collective-permute-start | bytes 491528 | tf_op jit(solution)/shard_map/ppermute | solution.py:357
  27.2 2.5 %collective-permute-done.5.refs_2_ = bf16[8,10240]{1,0:T(8,128)(2,1)S(1)} collective-permute-done((bf16[8,10240]{1,0:T(8,128)(2,1)S(1)}, bf16[8,10240]{1,0:T(8,128)(2,1)S(1)}, u32[]{:S(2)}, u32[]{:S(2)}) %collective-permute-start.5) | collective-permute-done | bytes 163872 | tf_op jit(solution)/shard_map/ppermute | solution.py:362
  29.7 1.7 %collective-permute-start.9 = (bf16[8,10240]{1,0:T(8,128)(2,1)S(1)}, bf16[8,10240]{1,0:T(8,128)(2,1)S(1)}, u32[]{:S(2)}, u32[]{:S(2)}) collective-permute-start(bf16[8,10240]{1,0:T(8,128)(2,1)S(1)} %collective-permute-done.5.refs_2_), channel_id=1, source_target_pairs={{0,8},{8,0},{16,24},{24,16},{1,9},{9,1},{17,25},{25,17},{2,10},{10... | collective-permute-start | bytes 491528 | tf_op jit(solution)/shard_map/ppermute | solution.py:357
  31.3 0.0 collective-permute-done.6.refs_3_
  31.3 0.0 collective-permute-start.10
  31.4 0.0 collective-permute-done.7.refs_4_
  31.4 0.0 collective-permute-done.8.refs_5_
  31.4 1.0 %collective-permute-done.9.refs_6_ = bf16[8,10240]{1,0:T(8,128)(2,1)S(1)} collective-permute-done((bf16[8,10240]{1,0:T(8,128)(2,1)S(1)}, bf16[8,10240]{1,0:T(8,128)(2,1)S(1)}, u32[]{:S(2)}, u32[]{:S(2)}) %collective-permute-start.9) | collective-permute-done | bytes 163872 | tf_op jit(solution)/shard_map/ppermute | solution.py:357
  32.4 0.4 collective-permute-done.10.refs_7_
  32.7 11.4 %outer.1 = f32[4096,2048]{1,0:T(8,128)} custom-call(bf16[8,10240]{1,0:T(8,128)(2,1)S(1)} %get-tuple-element.19.refs_0_, bf16[8,10240]{1,0:T(8,128)(2,1)S(1)} %collective-permute-done.4.refs_1_, bf16[8,10240]{1,0:T(8,128)(2,1)S(1)} %collective-permute-done.5.refs_2_, bf16[8,10240]{1,0:T(8,128)(2,1)S(1)} %collective-permute-done.6.refs_3_, ...), custom_call_target="tpu_custom_call" | custom-call | flops 10000000000 | bytes 30000000 | tf_op jit(solution)/shard_map/outer/pallas_call | solution.py:333
Async XLA Ops:
  0.0 7.3 %collective-permute-start = (bf16[1,48,2304]{2,1,0:T(8,128)(2,1)}, bf16[1,48,2304]{2,1,0:T(8,128)(2,1)S(1)}, u32[]{:S(2)}, u32[]{:S(2)}) collective-permute-start(bf16[1,48,2304]{2,1,0:T(8,128)(2,1)} %param.8), channel_id=1, source_target_pairs={{0,8},{8,16},{16,24},{24,0},{1,9},{9,17},{17,25},{25,1},{2,10},{10... | collective-permute-start | bytes 663560 | tf_op jit(solution)/shard_map/ppermute | solution.py:352
  4.5 0.9 %copy-start = (s32[3,8192]{1,0:T(4,128)S(1)}, s32[3,8192]{1,0:T(4,128)}, u32[]{:S(2)}) copy-start(s32[3,8192]{1,0:T(4,128)} %sphere_ref.1) | copy-start | bytes 294916
  5.4 1.0 %copy-start.1 = (bf16[1760,128]{1,0:T(8,128)(2,1)S(1)}, bf16[1760,128]{1,0:T(8,128)(2,1)}, u32[]{:S(2)}) copy-start(bf16[1760,128]{1,0:T(8,128)(2,1)} %constant.2.clone.table_ref) | copy-start | bytes 1351684
  10.7 6.1 %collective-permute-start.3 = (bf16[2,16384]{1,0:T(2,128)(2,1)S(1)}, bf16[2,16384]{1,0:T(2,128)(2,1)S(1)}, u32[]{:S(2)}, u32[]{:S(2)}) collective-permute-start(bf16[2,16384]{1,0:T(2,128)(2,1)S(1)} %get-tuple-element.18.refs_0_), channel_id=1, source_target_pairs={{0,4},{1,5},{2,6},{3,7},{4,0},{5,1},{6,2},{7,3},{8,12},{9,13},{10,... | collective-permute-start | bytes 196616 | tf_op jit(solution)/shard_map/ppermute | solution.py:357
  13.1 5.6 %collective-permute-start.2 = (bf16[2,16384]{1,0:T(2,128)(2,1)S(1)}, bf16[2,16384]{1,0:T(2,128)(2,1)S(1)}, u32[]{:S(2)}, u32[]{:S(2)}) collective-permute-start(bf16[2,16384]{1,0:T(2,128)(2,1)S(1)} %get-tuple-element.18.refs_0_), channel_id=1, source_target_pairs={{0,6},{1,7},{2,4},{3,5},{4,2},{5,3},{6,0},{7,1},{8,14},{9,15},{10,... | collective-permute-start | bytes 196616 | tf_op jit(solution)/shard_map/ppermute | solution.py:357
  14.2 5.0 %collective-permute-start.1 = (bf16[2,16384]{1,0:T(2,128)(2,1)S(1)}, bf16[2,16384]{1,0:T(2,128)(2,1)S(1)}, u32[]{:S(2)}, u32[]{:S(2)}) collective-permute-start(bf16[2,16384]{1,0:T(2,128)(2,1)S(1)} %get-tuple-element.18.refs_0_), channel_id=1, source_target_pairs={{0,2},{1,3},{2,0},{3,1},{4,6},{5,7},{6,4},{7,5},{8,10},{9,11},{10,... | collective-permute-start | bytes 196616 | tf_op jit(solution)/shard_map/ppermute | solution.py:357
  19.5 5.1 %collective-permute-start.4 = (bf16[8,10240]{1,0:T(8,128)(2,1)S(1)}, bf16[8,10240]{1,0:T(8,128)(2,1)S(1)}, u32[]{:S(2)}, u32[]{:S(2)}) collective-permute-start(bf16[8,10240]{1,0:T(8,128)(2,1)S(1)} %get-tuple-element.20), channel_id=1, source_target_pairs={{0,1},{1,0},{2,3},{3,2},{4,5},{5,4},{6,7},{7,6},{8,9},{9,8},{10,11... | collective-permute-start | bytes 491528 | tf_op jit(solution)/shard_map/ppermute | solution.py:362
  21.2 8.5 %collective-permute-start.5 = (bf16[8,10240]{1,0:T(8,128)(2,1)S(1)}, bf16[8,10240]{1,0:T(8,128)(2,1)S(1)}, u32[]{:S(2)}, u32[]{:S(2)}) collective-permute-start(bf16[8,10240]{1,0:T(8,128)(2,1)S(1)} %get-tuple-element.21), channel_id=1, source_target_pairs={{0,16},{1,17},{2,18},{3,19},{4,20},{5,21},{6,22},{7,23},{8,24},{9,... | collective-permute-start | bytes 491528 | tf_op jit(solution)/shard_map/ppermute | solution.py:362
  21.2 10.1 %collective-permute-start.6 = (bf16[8,10240]{1,0:T(8,128)(2,1)S(1)}, bf16[8,10240]{1,0:T(8,128)(2,1)S(1)}, u32[]{:S(2)}, u32[]{:S(2)}) collective-permute-start(bf16[8,10240]{1,0:T(8,128)(2,1)S(1)} %get-tuple-element.22), channel_id=1, source_target_pairs={{0,17},{1,16},{2,19},{3,18},{4,21},{5,20},{6,23},{7,22},{8,25},{9,... | collective-permute-start | bytes 491528 | tf_op jit(solution)/shard_map/ppermute | solution.py:362
  22.5 8.9 %collective-permute-start.7 = (bf16[8,10240]{1,0:T(8,128)(2,1)S(1)}, bf16[8,10240]{1,0:T(8,128)(2,1)S(1)}, u32[]{:S(2)}, u32[]{:S(2)}) collective-permute-start(bf16[8,10240]{1,0:T(8,128)(2,1)S(1)} %get-tuple-element.19.refs_0_), channel_id=1, source_target_pairs={{0,8},{8,0},{16,24},{24,16},{1,9},{9,1},{17,25},{25,17},{2,10},{10... | collective-permute-start | bytes 491528 | tf_op jit(solution)/shard_map/ppermute | solution.py:357
  24.6 6.8 %collective-permute-start.8 = (bf16[8,10240]{1,0:T(8,128)(2,1)S(1)}, bf16[8,10240]{1,0:T(8,128)(2,1)S(1)}, u32[]{:S(2)}, u32[]{:S(2)}) collective-permute-start(bf16[8,10240]{1,0:T(8,128)(2,1)S(1)} %collective-permute-done.4.refs_1_), channel_id=1, source_target_pairs={{0,8},{8,0},{16,24},{24,16},{1,9},{9,1},{17,25},{25,17},{2,10},{10... | collective-permute-start | bytes 491528 | tf_op jit(solution)/shard_map/ppermute | solution.py:357
  29.7 2.7 %collective-permute-start.9 = (bf16[8,10240]{1,0:T(8,128)(2,1)S(1)}, bf16[8,10240]{1,0:T(8,128)(2,1)S(1)}, u32[]{:S(2)}, u32[]{:S(2)}) collective-permute-start(bf16[8,10240]{1,0:T(8,128)(2,1)S(1)} %collective-permute-done.5.refs_2_), channel_id=1, source_target_pairs={{0,8},{8,0},{16,24},{24,16},{1,9},{9,1},{17,25},{25,17},{2,10},{10... | collective-permute-start | bytes 491528 | tf_op jit(solution)/shard_map/ppermute | solution.py:357
  31.3 1.4 %collective-permute-start.10 = (bf16[8,10240]{1,0:T(8,128)(2,1)S(1)}, bf16[8,10240]{1,0:T(8,128)(2,1)S(1)}, u32[]{:S(2)}, u32[]{:S(2)}) collective-permute-start(bf16[8,10240]{1,0:T(8,128)(2,1)S(1)} %collective-permute-done.6.refs_3_), channel_id=1, source_target_pairs={{0,8},{8,0},{16,24},{24,16},{1,9},{9,1},{17,25},{25,17},{2,10},{10... | collective-permute-start | bytes 491528 | tf_op jit(solution)/shard_map/ppermute | solution.py:357

commit v7 on v6

--- a/solution.py
+++ b/solution.py
@@ -255,7 +255,7 @@
 
 def pack_kernel(plan, turns, targets, levels_ref, *refs):
     rows, cols, row_width, col_width = plan
-    arrived, outs, mixed_ref = refs[: cols // 2], refs[cols // 2 : -1], refs[-1]
+    arrived, outs, mixed_ref = refs[: len(turns)], refs[len(turns) : -1], refs[-1]
     r, c = own_place()
     for j, ref in enumerate(arrived):
         mixed_ref[STEPS * j : STEPS * (j + 1), :] = ref[...].astype(jnp.float32)
@@ -370,12 +370,14 @@
     occ_second = shifted(occ_orbitals, "row", 1)
     own, later = transform(cond_orbitals, occ_orbitals, occ_second, sphere_index, occ_band.shape)
     levels = jnp.stack([cond_energy, occ_energy, (occ_band + later[0]).astype(jnp.float32)])
-    turns = [0, 2, *range(cols - 2, 2, -2)]
-    arrived = [own] + [turned(own, "col", turn) for turn in turns[1:]]
+    arrived = {turn: turned(own, "col", turn) if turn else own for turn in range(0, cols, 2)}
     targets = [(turn, side) for turn in range(0, rows, 2) for side in range(2)]
-    packed = list(pack(arrived, levels, turns, targets, plan))
-    straight = packed[:1] + [sent_across(value, *target, rows, cols) for value, target in zip(packed[1:], targets[1:])]
-    return outer(straight + [turned(value, "row", 1) for value in straight], plan)
+    messages = []
+    for turns in (range(0, cols // 2, 2), range(cols // 2, cols, 2)):
+        packed = list(pack([arrived[turn] for turn in turns], levels, turns, targets, plan))
+        straight = packed[:1] + [sent_across(value, *target, rows, cols) for value, target in zip(packed[1:], targets[1:])]
+        messages += straight + [turned(value, "row", 1) for value in straight]
+    return outer(messages, plan)
 
 
 def solution(mesh):

time: 44.6 us -> 44.8 us (level)
  waiting for transfers between devices: 7.81 us -> 3.84 us
  starting transfers between devices: 15.2 us -> 19 us
    ppermute x3 -> x6, waiting for transfers between devices: 2.97 us -> 0.02 us  [sent_across(): return lax.ppermute(value, ('row', 'col'), moves)]
    ppermute x3 -> x6, starting transfers between devices: 2.96 us -> 5.43 us  [sent_across(): return lax.ppermute(value, ('row', 'col'), moves)]
    ppermute x7 -> x11, starting transfers between devices: 9.57 us -> 11 us  [turned(): return lax.ppermute(value, axis, [(i, i ^ turn) for i in range(devices)])]
    ppermute x7 -> x11, waiting for transfers between devices: 4.84 us -> 3.82 us  [turned(): return lax.ppermute(value, axis, [(i, i ^ turn) for i in range(devices)])]
  transfers between devices with their start and end apart: 11 -> 18, of which waited for: 7 -> 4; matrix products, arithmetic and copies ran while one was open for 7% -> 7% of each run, Pallas kernels for 2% -> 3%
where the time goes in v7:
time: 44.8 us; the launch traced here: 44.3 us
  starting transfers between devices  19 us (42%)
  Pallas kernels  16.2 us (36%)
  waiting for transfers between devices  3.84 us (9%)
  local copies, waits for them, and re-layouts  3.82 us (9%)
  other arithmetic  1.34 us (3%)
    pallas_call x1, Pallas kernels, outer(): pl.pallas_call(functools.partial(outer_kernel, row_width, block, slots),...  11.6 us
    ppermute x11, starting transfers between devices, turned(): return lax.ppermute(value, axis, [(i, i ^ turn) for i in range(devices)])  11 us
    ppermute x6, starting transfers between devices, sent_across(): return lax.ppermute(value, ('row', 'col'), moves)  5.43 us
    ppermute x11, waiting for transfers between devices, turned(): return lax.ppermute(value, axis, [(i, i ^ turn) for i in range(devices)])  3.82 us
    pallas_call x1, Pallas kernels, transform(): pl.pallas_call(functools.partial(second_kernel, grid), out_shape=[jax.Sha...  3.39 us
    unnamed x5, local copies, waits for them, and re-layouts  2.86 us
    ppermute x1, starting transfers between devices, shifted(): lax.ppermute(value, axis, [(i, (i + by) % devices) for i in range(devices)])  2.63 us
    another operation x2, other arithmetic, on_device(): jnp.stack([cond_energy, occ_energy, (occ_band + later[0]).astype(jnp.floa...  1.34 us
  transfers between devices with their start and end apart: 18, of which 4 were waited for; matrix products, arithmetic and copies ran while one was open for 7% of the time, Pallas kernels for 3%

profile of v7, /device:TPU:1, one launch (start us, length us, event | category | flops | bytes accessed | tf_op | source)
XLA Modules:
  0.0 44.3 jit_solution(7420856801235637781)
XLA Ops:
  0.0 2.6 %collective-permute-start = (bf16[1,48,2304]{2,1,0:T(8,128)(2,1)}, bf16[1,48,2304]{2,1,0:T(8,128)(2,1)S(1)}, u32[]{:S(2)}, u32[]{:S(2)}) collective-permute-start(bf16[1,48,2304]{2,1,0:T(8,128)(2,1)} %param.8), channel_id=1, source_target_pairs={{0,8},{8,16},{16,24},{24,0},{1,9},{9,17},{17,25},{25,1},{2,10},{10... | collective-permute-start | bytes 663560 | tf_op jit(solution)/shard_map/ppermute | solution.py:352
  2.6 0.9 %constant_dynamic-update-slice_fusion.1 = bf16[2,48,2304]{2,1,0:T(8,128)(2,1)S(1)} fusion(bf16[1,48,2304]{2,1,0:T(8,128)(2,1)} %param.7), kind=kLoop, calls=%fused_computation.1 | loop fusion | bytes 442368
  3.6 1.0 %constant_dynamic-update-slice_fusion.orbitals_ref = bf16[2,48,2304]{2,1,0:T(8,128)(2,1)S(1)} fusion(bf16[2,48,2304]{2,1,0:T(8,128)(2,1)S(1)} %constant_dynamic-update-slice_fusion.1, bf16[1,48,2304]{2,1,0:T(8,128)(2,1)} %param.8), kind=kLoop, calls=%fused_computation | loop fusion | bytes 442368 | tf_op jit(solution)/shard_map/concatenate | solution.py:224
  4.5 0.0 copy-start
  4.6 0.9 %copy-done = s32[3,8192]{1,0:T(4,128)S(1)} copy-done((s32[3,8192]{1,0:T(4,128)S(1)}, s32[3,8192]{1,0:T(4,128)}, u32[]{:S(2)}) %copy-start) | copy-done | bytes 98328
  5.4 0.0 copy-start.1
  5.5 1.0 %copy-done.1 = bf16[1760,128]{1,0:T(8,128)(2,1)S(1)} copy-done((bf16[1760,128]{1,0:T(8,128)(2,1)S(1)}, bf16[1760,128]{1,0:T(8,128)(2,1)}, u32[]{:S(2)}) %copy-start.1) | copy-done | bytes 450584
  6.5 0.9 %first_pair.1 = (bf16[240,256]{1,0:T(8,128)(2,1)S(1)}, s32[2,8192]{1,0:T(2,128)S(1)}, bf16[1760,128]{1,0:T(8,128)(2,1)S(1)}) custom-call(bf16[2,48,2304]{2,1,0:T(8,128)(2,1)S(1)} %constant_dynamic-update-slice_fusion.orbitals_ref, bf16[1760,128]{1,0:T(8,128)(2,1)S(1)} %copy-done.1, s32[3,8192]{1,0:T(4,128)S(1)} %copy-done), custom_call_target="tpu_custom_call" | custom-call | flops 2000000000 | bytes 2000000 | tf_op jit(solution)/shard_map/first_pair/pallas_call | solution.py:230
  7.3 0.0 collective-permute-done.occ_ref
  7.4 3.4 %second_pair.1 = (bf16[2,16384]{1,0:T(2,128)(2,1)S(1)}, s32[1,32]{1,0:T(1,128)S(1)}) custom-call(bf16[2,48,2304]{2,1,0:T(8,128)(2,1)S(1)} %constant_dynamic-update-slice_fusion.orbitals_ref, bf16[1,48,2304]{2,1,0:T(8,128)(2,1)S(1)} %collective-permute-done.occ_ref, bf16[240,256]{1,0:T(8,128)(2,1)S(1)} %get-tuple-element.18.first_ref, ...), custom_call_target="tpu_custom_call" | custom-call | flops 2000000000 | bytes 2000000 | tf_op jit(solution)/shard_map/second_pair/pallas_call | solution.py:242
  10.7 3.4 %collective-permute-start.10 = (bf16[2,16384]{1,0:T(2,128)(2,1)S(1)}, bf16[2,16384]{1,0:T(2,128)(2,1)S(1)}, u32[]{:S(2)}, u32[]{:S(2)}) collective-permute-start(bf16[2,16384]{1,0:T(2,128)(2,1)S(1)} %get-tuple-element.22.refs_0_), channel_id=1, source_target_pairs={{0,6},{1,7},{2,4},{3,5},{4,2},{5,3},{6,0},{7,1},{8,14},{9,15},{10,... | collective-permute-start | bytes 196616 | tf_op jit(solution)/shard_map/ppermute | solution.py:357
  14.1 0.0 collective-permute-start.9
  14.1 0.4 collective-permute-start.1
  14.5 0.7 %fusion.1 = f32[1,32]{1,0:T(1,128)S(1)} fusion(s32[32]{0:T(128)} %param.11, s32[1,32]{1,0:T(1,128)S(1)} %get-tuple-element.21), kind=kLoop, calls=%fused_computation.5 | loop fusion | flops 64 | bytes 384 | tf_op jit(solution)/shard_map/stack | solution.py:372
  15.2 0.7 %pad_maximum_fusion.levels_ref = f32[3,32]{1,0:T(4,128)S(1)} fusion(f32[1,32]{1,0:T(1,128)S(1)} %fusion.1, f32[1,32]{1,0:T(1,128)} %bitcast.10, f32[1,32]{1,0:T(1,128)} %bitcast.11), kind=kLoop, calls=%fused_computation.2 | loop fusion | flops 192 | bytes 768 | tf_op jit(solution)/shard_map/stack | solution.py:372
  15.8 2.9 %collective-permute-done.1.refs_1_ = bf16[2,16384]{1,0:T(2,128)(2,1)S(1)} collective-permute-done((bf16[2,16384]{1,0:T(2,128)(2,1)S(1)}, bf16[2,16384]{1,0:T(2,128)(2,1)S(1)}, u32[]{:S(2)}, u32[]{:S(2)}) %collective-permute-start.1) | collective-permute-done | bytes 65568 | tf_op jit(solution)/shard_map/ppermute | solution.py:357
  18.7 0.2 pack.2
  18.9 1.3 %collective-permute-start.2 = (bf16[4,10240]{1,0:T(4,128)(2,1)S(1)}, bf16[4,10240]{1,0:T(4,128)(2,1)S(1)}, u32[]{:S(2)}, u32[]{:S(2)}) collective-permute-start(bf16[4,10240]{1,0:T(4,128)(2,1)S(1)} %get-tuple-element.24), channel_id=1, source_target_pairs={{0,1},{1,0},{2,3},{3,2},{4,5},{5,4},{6,7},{7,6},{8,9},{9,8},{10,11... | collective-permute-start | bytes 245768 | tf_op jit(solution)/shard_map/ppermute | solution.py:362
  20.2 0.0 collective-permute-start.3
  20.2 1.4 %collective-permute-start.4 = (bf16[4,10240]{1,0:T(4,128)(2,1)S(1)}, bf16[4,10240]{1,0:T(4,128)(2,1)S(1)}, u32[]{:S(2)}, u32[]{:S(2)}) collective-permute-start(bf16[4,10240]{1,0:T(4,128)(2,1)S(1)} %get-tuple-element.26), channel_id=1, source_target_pairs={{0,17},{1,16},{2,19},{3,18},{4,21},{5,20},{6,23},{7,22},{8,25},{9,... | collective-permute-start | bytes 245768 | tf_op jit(solution)/shard_map/ppermute | solution.py:362
  21.6 0.0 collective-permute-done.10.refs_1_
  21.6 1.4 %collective-permute-start.5 = (bf16[4,10240]{1,0:T(4,128)(2,1)S(1)}, bf16[4,10240]{1,0:T(4,128)(2,1)S(1)}, u32[]{:S(2)}, u32[]{:S(2)}) collective-permute-start(bf16[4,10240]{1,0:T(4,128)(2,1)S(1)} %get-tuple-element.23.refs_0_), channel_id=1, source_target_pairs={{0,8},{8,0},{16,24},{24,16},{1,9},{9,1},{17,25},{25,17},{2,10},{10... | collective-permute-start | bytes 245768 | tf_op jit(solution)/shard_map/ppermute | solution.py:357
  23.1 0.0 collective-permute-done.9.refs_0_
  23.1 0.2 pack.3
  23.3 1.3 %collective-permute-start.11 = (bf16[4,10240]{1,0:T(4,128)(2,1)S(1)}, bf16[4,10240]{1,0:T(4,128)(2,1)S(1)}, u32[]{:S(2)}, u32[]{:S(2)}) collective-permute-start(bf16[4,10240]{1,0:T(4,128)(2,1)S(1)} %get-tuple-element.28), channel_id=1, source_target_pairs={{0,1},{1,0},{2,3},{3,2},{4,5},{5,4},{6,7},{7,6},{8,9},{9,8},{10,11... | collective-permute-start | bytes 245768 | tf_op jit(solution)/shard_map/ppermute | solution.py:362
  24.5 0.0 collective-permute-done.2.refs_1_
  24.5 0.4 collective-permute-start.12
  25.0 0.0 collective-permute-done.3.refs_2_
  25.0 1.0 %collective-permute-start.13 = (bf16[4,10240]{1,0:T(4,128)(2,1)S(1)}, bf16[4,10240]{1,0:T(4,128)(2,1)S(1)}, u32[]{:S(2)}, u32[]{:S(2)}) collective-permute-start(bf16[4,10240]{1,0:T(4,128)(2,1)S(1)} %get-tuple-element.30), channel_id=1, source_target_pairs={{0,17},{1,16},{2,19},{3,18},{4,21},{5,20},{6,23},{7,22},{8,25},{9,... | collective-permute-start | bytes 245768 | tf_op jit(solution)/shard_map/ppermute | solution.py:362
  26.0 0.0 collective-permute-done.4.refs_3_
  26.0 1.7 %collective-permute-start.14 = (bf16[4,10240]{1,0:T(4,128)(2,1)S(1)}, bf16[4,10240]{1,0:T(4,128)(2,1)S(1)}, u32[]{:S(2)}, u32[]{:S(2)}) collective-permute-start(bf16[4,10240]{1,0:T(4,128)(2,1)S(1)} %get-tuple-element.27.refs_8_), channel_id=1, source_target_pairs={{0,8},{8,0},{16,24},{24,16},{1,9},{9,1},{17,25},{25,17},{2,10},{10... | collective-permute-start | bytes 245768 | tf_op jit(solution)/shard_map/ppermute | solution.py:357
  27.7 0.0 collective-permute-done.5.refs_4_
  27.7 0.0 collective-permute-start.6
  27.7 0.0 collective-permute-done.11.refs_9_
  27.7 1.0 %collective-permute-start.7 = (bf16[4,10240]{1,0:T(4,128)(2,1)S(1)}, bf16[4,10240]{1,0:T(4,128)(2,1)S(1)}, u32[]{:S(2)}, u32[]{:S(2)}) collective-permute-start(bf16[4,10240]{1,0:T(4,128)(2,1)S(1)} %collective-permute-done.3.refs_2_), channel_id=1, source_target_pairs={{0,8},{8,0},{16,24},{24,16},{1,9},{9,1},{17,25},{25,17},{2,10},{10... | collective-permute-start | bytes 245768 | tf_op jit(solution)/shard_map/ppermute | solution.py:357
  28.7 0.0 collective-permute-done.12.refs_10_
  28.7 1.6 %collective-permute-start.8 = (bf16[4,10240]{1,0:T(4,128)(2,1)S(1)}, bf16[4,10240]{1,0:T(4,128)(2,1)S(1)}, u32[]{:S(2)}, u32[]{:S(2)}) collective-permute-start(bf16[4,10240]{1,0:T(4,128)(2,1)S(1)} %collective-permute-done.4.refs_3_), channel_id=1, source_target_pairs={{0,8},{8,0},{16,24},{24,16},{1,9},{9,1},{17,25},{25,17},{2,10},{10... | collective-permute-start | bytes 245768 | tf_op jit(solution)/shard_map/ppermute | solution.py:357
  30.3 0.0 collective-permute-done.13.refs_11_
  30.3 1.0 %collective-permute-start.15 = (bf16[4,10240]{1,0:T(4,128)(2,1)S(1)}, bf16[4,10240]{1,0:T(4,128)(2,1)S(1)}, u32[]{:S(2)}, u32[]{:S(2)}) collective-permute-start(bf16[4,10240]{1,0:T(4,128)(2,1)S(1)} %collective-permute-done.11.refs_9_), channel_id=1, source_target_pairs={{0,8},{8,0},{16,24},{24,16},{1,9},{9,1},{17,25},{25,17},{2,10},{10... | collective-permute-start | bytes 245768 | tf_op jit(solution)/shard_map/ppermute | solution.py:357
  31.3 0.0 collective-permute-done.14.refs_12_
  31.3 0.0 collective-permute-start.16
  31.3 0.0 collective-permute-done.6.refs_5_
  31.3 0.5 %collective-permute-start.17 = (bf16[4,10240]{1,0:T(4,128)(2,1)S(1)}, bf16[4,10240]{1,0:T(4,128)(2,1)S(1)}, u32[]{:S(2)}, u32[]{:S(2)}) collective-permute-start(bf16[4,10240]{1,0:T(4,128)(2,1)S(1)} %collective-permute-done.13.refs_11_), channel_id=1, source_target_pairs={{0,8},{8,0},{16,24},{24,16},{1,9},{9,1},{17,25},{25,17},{2,10},{10... | collective-permute-start | bytes 245768 | tf_op jit(solution)/shard_map/ppermute | solution.py:357
  31.8 0.0 collective-permute-done.7.refs_6_
  31.8 0.0 collective-permute-done.8.refs_7_
  31.8 0.4 collective-permute-done.15.refs_13_
  32.2 0.4 collective-permute-done.16.refs_14_
  32.6 0.2 collective-permute-done.17.refs_15_
  32.7 11.6 %outer.1 = f32[4096,2048]{1,0:T(8,128)} custom-call(bf16[4,10240]{1,0:T(4,128)(2,1)S(1)} %get-tuple-element.23.refs_0_, bf16[4,10240]{1,0:T(4,128)(2,1)S(1)} %collective-permute-done.2.refs_1_, bf16[4,10240]{1,0:T(4,128)(2,1)S(1)} %collective-permute-done.3.refs_2_, bf16[4,10240]{1,0:T(4,128)(2,1)S(1)} %collective-permute-done.4.refs_3_, ...), custom_call_target="tpu_custom_call" | custom-call | flops 10000000000 | bytes 30000000 | tf_op jit(solution)/shard_map/outer/pallas_call | solution.py:333
Async XLA Ops:
  0.0 7.3 %collective-permute-start = (bf16[1,48,2304]{2,1,0:T(8,128)(2,1)}, bf16[1,48,2304]{2,1,0:T(8,128)(2,1)S(1)}, u32[]{:S(2)}, u32[]{:S(2)}) collective-permute-start(bf16[1,48,2304]{2,1,0:T(8,128)(2,1)} %param.8), channel_id=1, source_target_pairs={{0,8},{8,16},{16,24},{24,0},{1,9},{9,17},{17,25},{25,1},{2,10},{10... | collective-permute-start | bytes 663560 | tf_op jit(solution)/shard_map/ppermute | solution.py:352
  4.5 0.9 %copy-start = (s32[3,8192]{1,0:T(4,128)S(1)}, s32[3,8192]{1,0:T(4,128)}, u32[]{:S(2)}) copy-start(s32[3,8192]{1,0:T(4,128)} %sphere_ref.1) | copy-start | bytes 294916
  5.4 1.0 %copy-start.1 = (bf16[1760,128]{1,0:T(8,128)(2,1)S(1)}, bf16[1760,128]{1,0:T(8,128)(2,1)}, u32[]{:S(2)}) copy-start(bf16[1760,128]{1,0:T(8,128)(2,1)} %constant.2.clone.table_ref) | copy-start | bytes 1351684
  10.7 10.9 %collective-permute-start.10 = (bf16[2,16384]{1,0:T(2,128)(2,1)S(1)}, bf16[2,16384]{1,0:T(2,128)(2,1)S(1)}, u32[]{:S(2)}, u32[]{:S(2)}) collective-permute-start(bf16[2,16384]{1,0:T(2,128)(2,1)S(1)} %get-tuple-element.22.refs_0_), channel_id=1, source_target_pairs={{0,6},{1,7},{2,4},{3,5},{4,2},{5,3},{6,0},{7,1},{8,14},{9,15},{10,... | collective-permute-start | bytes 196616 | tf_op jit(solution)/shard_map/ppermute | solution.py:357
  14.1 8.9 %collective-permute-start.9 = (bf16[2,16384]{1,0:T(2,128)(2,1)S(1)}, bf16[2,16384]{1,0:T(2,128)(2,1)S(1)}, u32[]{:S(2)}, u32[]{:S(2)}) collective-permute-start(bf16[2,16384]{1,0:T(2,128)(2,1)S(1)} %get-tuple-element.22.refs_0_), channel_id=1, source_target_pairs={{0,4},{1,5},{2,6},{3,7},{4,0},{5,1},{6,2},{7,3},{8,12},{9,13},{10,... | collective-permute-start | bytes 196616 | tf_op jit(solution)/shard_map/ppermute | solution.py:357
  14.1 4.6 %collective-permute-start.1 = (bf16[2,16384]{1,0:T(2,128)(2,1)S(1)}, bf16[2,16384]{1,0:T(2,128)(2,1)S(1)}, u32[]{:S(2)}, u32[]{:S(2)}) collective-permute-start(bf16[2,16384]{1,0:T(2,128)(2,1)S(1)} %get-tuple-element.22.refs_0_), channel_id=1, source_target_pairs={{0,2},{1,3},{2,0},{3,1},{4,6},{5,7},{6,4},{7,5},{8,10},{9,11},{10,... | collective-permute-start | bytes 196616 | tf_op jit(solution)/shard_map/ppermute | solution.py:357
  18.9 5.6 %collective-permute-start.2 = (bf16[4,10240]{1,0:T(4,128)(2,1)S(1)}, bf16[4,10240]{1,0:T(4,128)(2,1)S(1)}, u32[]{:S(2)}, u32[]{:S(2)}) collective-permute-start(bf16[4,10240]{1,0:T(4,128)(2,1)S(1)} %get-tuple-element.24), channel_id=1, source_target_pairs={{0,1},{1,0},{2,3},{3,2},{4,5},{5,4},{6,7},{7,6},{8,9},{9,8},{10,11... | collective-permute-start | bytes 245768 | tf_op jit(solution)/shard_map/ppermute | solution.py:362
  20.2 4.8 %collective-permute-start.3 = (bf16[4,10240]{1,0:T(4,128)(2,1)S(1)}, bf16[4,10240]{1,0:T(4,128)(2,1)S(1)}, u32[]{:S(2)}, u32[]{:S(2)}) collective-permute-start(bf16[4,10240]{1,0:T(4,128)(2,1)S(1)} %get-tuple-element.25), channel_id=1, source_target_pairs={{0,16},{1,17},{2,18},{3,19},{4,20},{5,21},{6,22},{7,23},{8,24},{9,... | collective-permute-start | bytes 245768 | tf_op jit(solution)/shard_map/ppermute | solution.py:362
  20.2 5.8 %collective-permute-start.4 = (bf16[4,10240]{1,0:T(4,128)(2,1)S(1)}, bf16[4,10240]{1,0:T(4,128)(2,1)S(1)}, u32[]{:S(2)}, u32[]{:S(2)}) collective-permute-start(bf16[4,10240]{1,0:T(4,128)(2,1)S(1)} %get-tuple-element.26), channel_id=1, source_target_pairs={{0,17},{1,16},{2,19},{3,18},{4,21},{5,20},{6,23},{7,22},{8,25},{9,... | collective-permute-start | bytes 245768 | tf_op jit(solution)/shard_map/ppermute | solution.py:362
  21.6 6.1 %collective-permute-start.5 = (bf16[4,10240]{1,0:T(4,128)(2,1)S(1)}, bf16[4,10240]{1,0:T(4,128)(2,1)S(1)}, u32[]{:S(2)}, u32[]{:S(2)}) collective-permute-start(bf16[4,10240]{1,0:T(4,128)(2,1)S(1)} %get-tuple-element.23.refs_0_), channel_id=1, source_target_pairs={{0,8},{8,0},{16,24},{24,16},{1,9},{9,1},{17,25},{25,17},{2,10},{10... | collective-permute-start | bytes 245768 | tf_op jit(solution)/shard_map/ppermute | solution.py:357
  23.3 4.5 %collective-permute-start.11 = (bf16[4,10240]{1,0:T(4,128)(2,1)S(1)}, bf16[4,10240]{1,0:T(4,128)(2,1)S(1)}, u32[]{:S(2)}, u32[]{:S(2)}) collective-permute-start(bf16[4,10240]{1,0:T(4,128)(2,1)S(1)} %get-tuple-element.28), channel_id=1, source_target_pairs={{0,1},{1,0},{2,3},{3,2},{4,5},{5,4},{6,7},{7,6},{8,9},{9,8},{10,11... | collective-permute-start | bytes 245768 | tf_op jit(solution)/shard_map/ppermute | solution.py:362
  24.5 4.2 %collective-permute-start.12 = (bf16[4,10240]{1,0:T(4,128)(2,1)S(1)}, bf16[4,10240]{1,0:T(4,128)(2,1)S(1)}, u32[]{:S(2)}, u32[]{:S(2)}) collective-permute-start(bf16[4,10240]{1,0:T(4,128)(2,1)S(1)} %get-tuple-element.29), channel_id=1, source_target_pairs={{0,16},{1,17},{2,18},{3,19},{4,20},{5,21},{6,22},{7,23},{8,24},{9,... | collective-permute-start | bytes 245768 | tf_op jit(solution)/shard_map/ppermute | solution.py:362
  25.0 5.3 %collective-permute-start.13 = (bf16[4,10240]{1,0:T(4,128)(2,1)S(1)}, bf16[4,10240]{1,0:T(4,128)(2,1)S(1)}, u32[]{:S(2)}, u32[]{:S(2)}) collective-permute-start(bf16[4,10240]{1,0:T(4,128)(2,1)S(1)} %get-tuple-element.30), channel_id=1, source_target_pairs={{0,17},{1,16},{2,19},{3,18},{4,21},{5,20},{6,23},{7,22},{8,25},{9,... | collective-permute-start | bytes 245768 | tf_op jit(solution)/shard_map/ppermute | solution.py:362
  26.0 5.3 %collective-permute-start.14 = (bf16[4,10240]{1,0:T(4,128)(2,1)S(1)}, bf16[4,10240]{1,0:T(4,128)(2,1)S(1)}, u32[]{:S(2)}, u32[]{:S(2)}) collective-permute-start(bf16[4,10240]{1,0:T(4,128)(2,1)S(1)} %get-tuple-element.27.refs_8_), channel_id=1, source_target_pairs={{0,8},{8,0},{16,24},{24,16},{1,9},{9,1},{17,25},{25,17},{2,10},{10... | collective-permute-start | bytes 245768 | tf_op jit(solution)/shard_map/ppermute | solution.py:357
  27.7 3.6 %collective-permute-start.6 = (bf16[4,10240]{1,0:T(4,128)(2,1)S(1)}, bf16[4,10240]{1,0:T(4,128)(2,1)S(1)}, u32[]{:S(2)}, u32[]{:S(2)}) collective-permute-start(bf16[4,10240]{1,0:T(4,128)(2,1)S(1)} %collective-permute-done.2.refs_1_), channel_id=1, source_target_pairs={{0,8},{8,0},{16,24},{24,16},{1,9},{9,1},{17,25},{25,17},{2,10},{10... | collective-permute-start | bytes 245768 | tf_op jit(solution)/shard_map/ppermute | solution.py:357
  27.7 4.1 %collective-permute-start.7 = (bf16[4,10240]{1,0:T(4,128)(2,1)S(1)}, bf16[4,10240]{1,0:T(4,128)(2,1)S(1)}, u32[]{:S(2)}, u32[]{:S(2)}) collective-permute-start(bf16[4,10240]{1,0:T(4,128)(2,1)S(1)} %collective-permute-done.3.refs_2_), channel_id=1, source_target_pairs={{0,8},{8,0},{16,24},{24,16},{1,9},{9,1},{17,25},{25,17},{2,10},{10... | collective-permute-start | bytes 245768 | tf_op jit(solution)/shard_map/ppermute | solution.py:357
  28.7 3.1 %collective-permute-start.8 = (bf16[4,10240]{1,0:T(4,128)(2,1)S(1)}, bf16[4,10240]{1,0:T(4,128)(2,1)S(1)}, u32[]{:S(2)}, u32[]{:S(2)}) collective-permute-start(bf16[4,10240]{1,0:T(4,128)(2,1)S(1)} %collective-permute-done.4.refs_3_), channel_id=1, source_target_pairs={{0,8},{8,0},{16,24},{24,16},{1,9},{9,1},{17,25},{25,17},{2,10},{10... | collective-permute-start | bytes 245768 | tf_op jit(solution)/shard_map/ppermute | solution.py:357
  30.3 1.9 %collective-permute-start.15 = (bf16[4,10240]{1,0:T(4,128)(2,1)S(1)}, bf16[4,10240]{1,0:T(4,128)(2,1)S(1)}, u32[]{:S(2)}, u32[]{:S(2)}) collective-permute-start(bf16[4,10240]{1,0:T(4,128)(2,1)S(1)} %collective-permute-done.11.refs_9_), channel_id=1, source_target_pairs={{0,8},{8,0},{16,24},{24,16},{1,9},{9,1},{17,25},{25,17},{2,10},{10... | collective-permute-start | bytes 245768 | tf_op jit(solution)/shard_map/ppermute | solution.py:357
  31.3 1.3 %collective-permute-start.16 = (bf16[4,10240]{1,0:T(4,128)(2,1)S(1)}, bf16[4,10240]{1,0:T(4,128)(2,1)S(1)}, u32[]{:S(2)}, u32[]{:S(2)}) collective-permute-start(bf16[4,10240]{1,0:T(4,128)(2,1)S(1)} %collective-permute-done.12.refs_10_), channel_id=1, source_target_pairs={{0,8},{8,0},{16,24},{24,16},{1,9},{9,1},{17,25},{25,17},{2,10},{10... | collective-permute-start | bytes 245768 | tf_op jit(solution)/shard_map/ppermute | solution.py:357
  31.3 1.4 %collective-permute-start.17 = (bf16[4,10240]{1,0:T(4,128)(2,1)S(1)}, bf16[4,10240]{1,0:T(4,128)(2,1)S(1)}, u32[]{:S(2)}, u32[]{:S(2)}) collective-permute-start(bf16[4,10240]{1,0:T(4,128)(2,1)S(1)} %collective-permute-done.13.refs_11_), channel_id=1, source_target_pairs={{0,8},{8,0},{16,24},{24,16},{1,9},{9,1},{17,25},{25,17},{2,10},{10... | collective-permute-start | bytes 245768 | tf_op jit(solution)/shard_map/ppermute | solution.py:357

commit v8 on v7

--- a/solution.py
+++ b/solution.py
@@ -253,12 +253,17 @@
     )(orbitals, occ_second, *handed)
 
 
-def pack_kernel(plan, turns, targets, levels_ref, *refs):
+def pack_kernel(plan, turns, targets, merged, levels_ref, *refs):
     rows, cols, row_width, col_width = plan
-    arrived, outs, mixed_ref = refs[: len(turns)], refs[len(turns) : -1], refs[-1]
+    count = len(refs) - len(targets) - 1 - merged
+    arrived, outs, mixed_ref = refs[:count], refs[count:-1], refs[-1]
     r, c = own_place()
-    for j, ref in enumerate(arrived):
-        mixed_ref[STEPS * j : STEPS * (j + 1), :] = ref[...].astype(jnp.float32)
+    first = 0
+    for ref in arrived:
+        mixed_ref[first : first + ref.shape[0], :] = ref[...].astype(jnp.float32)
+        first += ref.shape[0]
+    if merged:
+        outs[-1][...] = mixed_ref[...].astype(jnp.bfloat16)
     weight = pair_weights([c ^ turn for turn in turns], levels_ref)
     columns = []
     for side in range(2):
@@ -270,15 +275,17 @@
         out_ref[:, 2 * row_width :] = columns[side]
 
 
-def pack(arrived, levels, turns, targets, plan):
+def pack(arrived, levels, turns, targets, merged, plan):
     rows, cols, row_width, col_width = plan
-    pairs = STEPS * len(arrived)
+    pairs = STEPS * len(turns)
+    entries = arrived[0].shape[1]
+    shapes = [(pairs, 2 * row_width + col_width)] * len(targets) + [(pairs, entries)] * merged
     return pl.pallas_call(
-        functools.partial(pack_kernel, plan, turns, targets),
-        out_shape=[jax.ShapeDtypeStruct((pairs, 2 * row_width + col_width), jnp.bfloat16)] * len(targets),
+        functools.partial(pack_kernel, plan, turns, targets, merged),
+        out_shape=[jax.ShapeDtypeStruct(shape, jnp.bfloat16) for shape in shapes],
         in_specs=in_vmem(1 + len(arrived)),
-        out_specs=in_vmem(len(targets)),
-        scratch_shapes=[pltpu.VMEM((pairs, arrived[0].shape[1]), jnp.float32)],
+        out_specs=in_vmem(len(shapes)),
+        scratch_shapes=[pltpu.VMEM((pairs, entries), jnp.float32)],
         compiler_params=pltpu.CompilerParams(vmem_limit_bytes=VMEM_LIMIT),
         cost_estimate=cost(10**9, 10**6),
         name="pack",
@@ -370,13 +377,23 @@
     occ_second = shifted(occ_orbitals, "row", 1)
     own, later = transform(cond_orbitals, occ_orbitals, occ_second, sphere_index, occ_band.shape)
     levels = jnp.stack([cond_energy, occ_energy, (occ_band + later[0]).astype(jnp.float32)])
-    arrived = {turn: turned(own, "col", turn) if turn else own for turn in range(0, cols, 2)}
     targets = [(turn, side) for turn in range(0, rows, 2) for side in range(2)]
-    messages = []
-    for turns in (range(0, cols // 2, 2), range(cols // 2, cols, 2)):
-        packed = list(pack([arrived[turn] for turn in turns], levels, turns, targets, plan))
-        straight = packed[:1] + [sent_across(value, *target, rows, cols) for value, target in zip(packed[1:], targets[1:])]
-        messages += straight + [turned(value, "row", 1) for value in straight]
+
+    def sent(packed):
+        straight = [packed[0]] + [sent_across(value, *target, rows, cols) for value, target in zip(packed[1:], targets[1:])]
+        return straight + [turned(value, "row", 1) for value in straight]
+
+    held, turns, bit = [own], [0], cols // 2
+    while bit > 2:
+        if len(held) > 1:
+            held = [jnp.concatenate(held, axis=0)]
+        held.append(turned(held[0], "col", bit))
+        turns += [turn + bit for turn in turns]
+        bit //= 2
+    *packed, merged = pack(held, levels, turns, targets, 1, plan)
+    messages = sent(packed)
+    far = turned(merged, "col", bit)
+    messages += sent(pack([far], levels, [turn + bit for turn in turns], targets, 0, plan))
     return outer(messages, plan)
 
 

time: 44.8 us -> 46.4 us (1.036)
  starting transfers between devices: 19 us -> 20.1 us
  waiting for transfers between devices: 3.84 us -> 4.42 us
    ppermute x11 -> x10, starting transfers between devices: 11 us -> 12.1 us  [turned(): return lax.ppermute(value, axis, [(i, i ^ turn) for i in range(devices)])]
    ppermute x6, waiting for transfers between devices: 0.02 us -> 0.83 us  [sent_across(): return lax.ppermute(value, ('row', 'col'), moves)]
    ppermute x11 -> x10, waiting for transfers between devices: 3.82 us -> 3.58 us  [turned(): return lax.ppermute(value, axis, [(i, i ^ turn) for i in range(devices)])]
  transfers between devices with their start and end apart: 18 -> 17, of which waited for: 4 -> 5; matrix products, arithmetic and copies ran while one was open for 7% -> 7% of each run, Pallas kernels for 3% -> 2%
where the time goes in v8:
time: 46.4 us; the launch traced here: 46 us
  starting transfers between devices  20.1 us (43%)
  Pallas kernels  16.2 us (35%)
  waiting for transfers between devices  4.42 us (10%)
  local copies, waits for them, and re-layouts  3.82 us (8%)
  other arithmetic  1.34 us (3%)
    ppermute x10, starting transfers between devices, turned(): return lax.ppermute(value, axis, [(i, i ^ turn) for i in range(devices)])  12.1 us
    pallas_call x1, Pallas kernels, outer(): pl.pallas_call(functools.partial(outer_kernel, row_width, block, slots),...  11.6 us
    ppermute x6, starting transfers between devices, sent_across(): return lax.ppermute(value, ('row', 'col'), moves)  5.39 us
    ppermute x10, waiting for transfers between devices, turned(): return lax.ppermute(value, axis, [(i, i ^ turn) for i in range(devices)])  3.58 us
    pallas_call x1, Pallas kernels, transform(): pl.pallas_call(functools.partial(second_kernel, grid), out_shape=[jax.Sha...  3.39 us
    unnamed x5, local copies, waits for them, and re-layouts  2.86 us
    ppermute x1, starting transfers between devices, shifted(): lax.ppermute(value, axis, [(i, (i + by) % devices) for i in range(devices)])  2.63 us
    another operation x2, other arithmetic, on_device(): jnp.stack([cond_energy, occ_energy, (occ_band + later[0]).astype(jnp.floa...  1.34 us
  transfers between devices with their start and end apart: 17, of which 5 were waited for; matrix products, arithmetic and copies ran while one was open for 7% of the time, Pallas kernels for 2%

profile of v8, /device:TPU:1, one launch (start us, length us, event | category | flops | bytes accessed | tf_op | source)
XLA Modules:
  0.0 46.0 jit_solution(14379115617776398973)
XLA Ops:
  0.0 2.6 %collective-permute-start = (bf16[1,48,2304]{2,1,0:T(8,128)(2,1)}, bf16[1,48,2304]{2,1,0:T(8,128)(2,1)S(1)}, u32[]{:S(2)}, u32[]{:S(2)}) collective-permute-start(bf16[1,48,2304]{2,1,0:T(8,128)(2,1)} %param.8), channel_id=1, source_target_pairs={{0,8},{8,16},{16,24},{24,0},{1,9},{9,17},{17,25},{25,1},{2,10},{10... | collective-permute-start | bytes 663560 | tf_op jit(solution)/shard_map/ppermute | solution.py:359
  2.6 0.9 %constant_dynamic-update-slice_fusion.1 = bf16[2,48,2304]{2,1,0:T(8,128)(2,1)S(1)} fusion(bf16[1,48,2304]{2,1,0:T(8,128)(2,1)} %param.7), kind=kLoop, calls=%fused_computation.1 | loop fusion | bytes 442368
  3.6 1.0 %constant_dynamic-update-slice_fusion.orbitals_ref = bf16[2,48,2304]{2,1,0:T(8,128)(2,1)S(1)} fusion(bf16[2,48,2304]{2,1,0:T(8,128)(2,1)S(1)} %constant_dynamic-update-slice_fusion.1, bf16[1,48,2304]{2,1,0:T(8,128)(2,1)} %param.8), kind=kLoop, calls=%fused_computation | loop fusion | bytes 442368 | tf_op jit(solution)/shard_map/concatenate | solution.py:224
  4.5 0.0 copy-start
  4.6 0.9 %copy-done = s32[3,8192]{1,0:T(4,128)S(1)} copy-done((s32[3,8192]{1,0:T(4,128)S(1)}, s32[3,8192]{1,0:T(4,128)}, u32[]{:S(2)}) %copy-start) | copy-done | bytes 98328
  5.4 0.0 copy-start.1
  5.5 1.0 %copy-done.1 = bf16[1760,128]{1,0:T(8,128)(2,1)S(1)} copy-done((bf16[1760,128]{1,0:T(8,128)(2,1)S(1)}, bf16[1760,128]{1,0:T(8,128)(2,1)}, u32[]{:S(2)}) %copy-start.1) | copy-done | bytes 450584
  6.5 0.9 %first_pair.1 = (bf16[240,256]{1,0:T(8,128)(2,1)S(1)}, s32[2,8192]{1,0:T(2,128)S(1)}, bf16[1760,128]{1,0:T(8,128)(2,1)S(1)}) custom-call(bf16[2,48,2304]{2,1,0:T(8,128)(2,1)S(1)} %constant_dynamic-update-slice_fusion.orbitals_ref, bf16[1760,128]{1,0:T(8,128)(2,1)S(1)} %copy-done.1, s32[3,8192]{1,0:T(4,128)S(1)} %copy-done), custom_call_target="tpu_custom_call" | custom-call | flops 2000000000 | bytes 2000000 | tf_op jit(solution)/shard_map/first_pair/pallas_call | solution.py:230
  7.3 0.0 collective-permute-done.occ_ref
  7.4 3.4 %second_pair.1 = (bf16[2,16384]{1,0:T(2,128)(2,1)S(1)}, s32[1,32]{1,0:T(1,128)S(1)}) custom-call(bf16[2,48,2304]{2,1,0:T(8,128)(2,1)S(1)} %constant_dynamic-update-slice_fusion.orbitals_ref, bf16[1,48,2304]{2,1,0:T(8,128)(2,1)S(1)} %collective-permute-done.occ_ref, bf16[240,256]{1,0:T(8,128)(2,1)S(1)} %get-tuple-element.19.first_ref, ...), custom_call_target="tpu_custom_call" | custom-call | flops 2000000000 | bytes 2000000 | tf_op jit(solution)/shard_map/second_pair/pallas_call | solution.py:242
  10.7 2.4 %collective-permute-start.1 = (bf16[2,16384]{1,0:T(2,128)(2,1)S(1)}, bf16[2,16384]{1,0:T(2,128)(2,1)S(1)}, u32[]{:S(2)}, u32[]{:S(2)}) collective-permute-start(bf16[2,16384]{1,0:T(2,128)(2,1)S(1)} %get-tuple-element.23.refs_0_), channel_id=1, source_target_pairs={{0,4},{1,5},{2,6},{3,7},{4,0},{5,1},{6,2},{7,3},{8,12},{9,13},{10,... | collective-permute-start | bytes 196616 | tf_op jit(solution)/shard_map/ppermute | solution.py:364
  13.1 0.7 %fusion.1 = f32[1,32]{1,0:T(1,128)S(1)} fusion(s32[32]{0:T(128)} %param.11, s32[1,32]{1,0:T(1,128)S(1)} %get-tuple-element.22), kind=kLoop, calls=%fused_computation.5 | loop fusion | flops 64 | bytes 384 | tf_op jit(solution)/shard_map/stack | solution.py:379
  13.8 0.7 %pad_maximum_fusion.levels_ref = f32[3,32]{1,0:T(4,128)S(1)} fusion(f32[1,32]{1,0:T(1,128)S(1)} %fusion.1, f32[1,32]{1,0:T(1,128)} %bitcast.10, f32[1,32]{1,0:T(1,128)} %bitcast.11), kind=kLoop, calls=%fused_computation.2 | loop fusion | flops 192 | bytes 768 | tf_op jit(solution)/shard_map/stack | solution.py:379
  14.5 2.3 %collective-permute-done.1.refs_1_ = bf16[2,16384]{1,0:T(2,128)(2,1)S(1)} collective-permute-done((bf16[2,16384]{1,0:T(2,128)(2,1)S(1)}, bf16[2,16384]{1,0:T(2,128)(2,1)S(1)}, u32[]{:S(2)}, u32[]{:S(2)}) %collective-permute-start.1) | collective-permute-done | bytes 65568 | tf_op jit(solution)/shard_map/ppermute | solution.py:364
  16.8 0.2 pack.2
  17.0 0.9 %collective-permute-start.9 = (bf16[4,16384]{1,0:T(4,128)(2,1)S(1)}, bf16[4,16384]{1,0:T(4,128)(2,1)S(1)}, u32[]{:S(2)}, u32[]{:S(2)}) collective-permute-start(bf16[4,16384]{1,0:T(4,128)(2,1)S(1)} %get-tuple-element.28), channel_id=1, source_target_pairs={{0,2},{1,3},{2,0},{3,1},{4,6},{5,7},{6,4},{7,5},{8,10},{9,11},{10,... | collective-permute-start | bytes 393224 | tf_op jit(solution)/shard_map/ppermute | solution.py:364
  17.9 1.2 %collective-permute-start.2 = (bf16[4,10240]{1,0:T(4,128)(2,1)S(1)}, bf16[4,10240]{1,0:T(4,128)(2,1)S(1)}, u32[]{:S(2)}, u32[]{:S(2)}) collective-permute-start(bf16[4,10240]{1,0:T(4,128)(2,1)S(1)} %get-tuple-element.25), channel_id=1, source_target_pairs={{0,1},{1,0},{2,3},{3,2},{4,5},{5,4},{6,7},{7,6},{8,9},{9,8},{10,11... | collective-permute-start | bytes 245768 | tf_op jit(solution)/shard_map/ppermute | solution.py:369
  19.1 0.0 collective-permute-start.3
  19.1 1.4 %collective-permute-start.4 = (bf16[4,10240]{1,0:T(4,128)(2,1)S(1)}, bf16[4,10240]{1,0:T(4,128)(2,1)S(1)}, u32[]{:S(2)}, u32[]{:S(2)}) collective-permute-start(bf16[4,10240]{1,0:T(4,128)(2,1)S(1)} %get-tuple-element.27), channel_id=1, source_target_pairs={{0,17},{1,16},{2,19},{3,18},{4,21},{5,20},{6,23},{7,22},{8,25},{9,... | collective-permute-start | bytes 245768 | tf_op jit(solution)/shard_map/ppermute | solution.py:369
  20.5 1.5 %collective-permute-start.5 = (bf16[4,10240]{1,0:T(4,128)(2,1)S(1)}, bf16[4,10240]{1,0:T(4,128)(2,1)S(1)}, u32[]{:S(2)}, u32[]{:S(2)}) collective-permute-start(bf16[4,10240]{1,0:T(4,128)(2,1)S(1)} %get-tuple-element.24.refs_0_), channel_id=1, source_target_pairs={{0,8},{8,0},{16,24},{24,16},{1,9},{9,1},{17,25},{25,17},{2,10},{10... | collective-permute-start | bytes 245768 | tf_op jit(solution)/shard_map/ppermute | solution.py:364
  22.1 0.0 collective-permute-done.2.refs_1_
  22.1 0.9 %collective-permute-start.6 = (bf16[4,10240]{1,0:T(4,128)(2,1)S(1)}, bf16[4,10240]{1,0:T(4,128)(2,1)S(1)}, u32[]{:S(2)}, u32[]{:S(2)}) collective-permute-start(bf16[4,10240]{1,0:T(4,128)(2,1)S(1)} %collective-permute-done.2.refs_1_), channel_id=1, source_target_pairs={{0,8},{8,0},{16,24},{24,16},{1,9},{9,1},{17,25},{25,17},{2,10},{10... | collective-permute-start | bytes 245768 | tf_op jit(solution)/shard_map/ppermute | solution.py:364
  23.0 0.0 collective-permute-done.3.refs_2_
  23.0 1.8 %collective-permute-start.7 = (bf16[4,10240]{1,0:T(4,128)(2,1)S(1)}, bf16[4,10240]{1,0:T(4,128)(2,1)S(1)}, u32[]{:S(2)}, u32[]{:S(2)}) collective-permute-start(bf16[4,10240]{1,0:T(4,128)(2,1)S(1)} %collective-permute-done.3.refs_2_), channel_id=1, source_target_pairs={{0,8},{8,0},{16,24},{24,16},{1,9},{9,1},{17,25},{25,17},{2,10},{10... | collective-permute-start | bytes 245768 | tf_op jit(solution)/shard_map/ppermute | solution.py:364
  24.9 0.0 collective-permute-done.9.refs_0_
  24.9 0.2 pack.3
  25.1 1.5 %collective-permute-start.10 = (bf16[4,10240]{1,0:T(4,128)(2,1)S(1)}, bf16[4,10240]{1,0:T(4,128)(2,1)S(1)}, u32[]{:S(2)}, u32[]{:S(2)}) collective-permute-start(bf16[4,10240]{1,0:T(4,128)(2,1)S(1)} %get-tuple-element.30), channel_id=1, source_target_pairs={{0,1},{1,0},{2,3},{3,2},{4,5},{5,4},{6,7},{7,6},{8,9},{9,8},{10,11... | collective-permute-start | bytes 245768 | tf_op jit(solution)/shard_map/ppermute | solution.py:369
  26.5 0.0 collective-permute-done.4.refs_3_
  26.6 0.0 collective-permute-start.11
  26.6 0.0 collective-permute-done.5.refs_4_
  26.6 1.3 %collective-permute-start.12 = (bf16[4,10240]{1,0:T(4,128)(2,1)S(1)}, bf16[4,10240]{1,0:T(4,128)(2,1)S(1)}, u32[]{:S(2)}, u32[]{:S(2)}) collective-permute-start(bf16[4,10240]{1,0:T(4,128)(2,1)S(1)} %get-tuple-element.32), channel_id=1, source_target_pairs={{0,17},{1,16},{2,19},{3,18},{4,21},{5,20},{6,23},{7,22},{8,25},{9,... | collective-permute-start | bytes 245768 | tf_op jit(solution)/shard_map/ppermute | solution.py:369
  27.8 0.0 collective-permute-done.6.refs_5_
  27.8 0.8 %collective-permute-start.8 = (bf16[4,10240]{1,0:T(4,128)(2,1)S(1)}, bf16[4,10240]{1,0:T(4,128)(2,1)S(1)}, u32[]{:S(2)}, u32[]{:S(2)}) collective-permute-start(bf16[4,10240]{1,0:T(4,128)(2,1)S(1)} %collective-permute-done.4.refs_3_), channel_id=1, source_target_pairs={{0,8},{8,0},{16,24},{24,16},{1,9},{9,1},{17,25},{25,17},{2,10},{10... | collective-permute-start | bytes 245768 | tf_op jit(solution)/shard_map/ppermute | solution.py:364
  28.6 0.0 collective-permute-done.7.refs_6_
  28.6 0.1 collective-permute-start.13
  28.7 0.5 %collective-permute-done.10.refs_9_ = bf16[4,10240]{1,0:T(4,128)(2,1)S(1)} collective-permute-done((bf16[4,10240]{1,0:T(4,128)(2,1)S(1)}, bf16[4,10240]{1,0:T(4,128)(2,1)S(1)}, u32[]{:S(2)}, u32[]{:S(2)}) %collective-permute-start.10) | collective-permute-done | bytes 81952 | tf_op jit(solution)/shard_map/ppermute | solution.py:369
  29.2 0.8 %collective-permute-start.14 = (bf16[4,10240]{1,0:T(4,128)(2,1)S(1)}, bf16[4,10240]{1,0:T(4,128)(2,1)S(1)}, u32[]{:S(2)}, u32[]{:S(2)}) collective-permute-start(bf16[4,10240]{1,0:T(4,128)(2,1)S(1)} %collective-permute-done.10.refs_9_), channel_id=1, source_target_pairs={{0,8},{8,0},{16,24},{24,16},{1,9},{9,1},{17,25},{25,17},{2,10},{10... | collective-permute-start | bytes 245768 | tf_op jit(solution)/shard_map/ppermute | solution.py:364
  30.0 0.3 collective-permute-done.11.refs_10_
  30.3 2.8 %collective-permute-start.15 = (bf16[4,10240]{1,0:T(4,128)(2,1)S(1)}, bf16[4,10240]{1,0:T(4,128)(2,1)S(1)}, u32[]{:S(2)}, u32[]{:S(2)}) collective-permute-start(bf16[4,10240]{1,0:T(4,128)(2,1)S(1)} %collective-permute-done.11.refs_10_), channel_id=1, source_target_pairs={{0,8},{8,0},{16,24},{24,16},{1,9},{9,1},{17,25},{25,17},{2,10},{10... | collective-permute-start | bytes 245768 | tf_op jit(solution)/shard_map/ppermute | solution.py:364
  33.2 0.0 collective-permute-done.12.refs_11_
  33.2 0.0 collective-permute-start.16
  33.2 0.0 collective-permute-done.8.refs_7_
  33.2 0.0 collective-permute-done.13.refs_12_
  33.2 0.0 collective-permute-done.14.refs_13_
  33.2 0.9 %collective-permute-done.15.refs_14_ = bf16[4,10240]{1,0:T(4,128)(2,1)S(1)} collective-permute-done((bf16[4,10240]{1,0:T(4,128)(2,1)S(1)}, bf16[4,10240]{1,0:T(4,128)(2,1)S(1)}, u32[]{:S(2)}, u32[]{:S(2)}) %collective-permute-start.15) | collective-permute-done | bytes 81952 | tf_op jit(solution)/shard_map/ppermute | solution.py:364
  34.1 0.4 collective-permute-done.16.refs_15_
  34.5 11.6 %outer.1 = f32[4096,2048]{1,0:T(8,128)} custom-call(bf16[4,10240]{1,0:T(4,128)(2,1)S(1)} %get-tuple-element.24.refs_0_, bf16[4,10240]{1,0:T(4,128)(2,1)S(1)} %collective-permute-done.2.refs_1_, bf16[4,10240]{1,0:T(4,128)(2,1)S(1)} %collective-permute-done.3.refs_2_, bf16[4,10240]{1,0:T(4,128)(2,1)S(1)} %collective-permute-done.4.refs_3_, ...), custom_call_target="tpu_custom_call" | custom-call | flops 10000000000 | bytes 30000000 | tf_op jit(solution)/shard_map/outer/pallas_call | solution.py:340
Async XLA Ops:
  0.0 7.3 %collective-permute-start = (bf16[1,48,2304]{2,1,0:T(8,128)(2,1)}, bf16[1,48,2304]{2,1,0:T(8,128)(2,1)S(1)}, u32[]{:S(2)}, u32[]{:S(2)}) collective-permute-start(bf16[1,48,2304]{2,1,0:T(8,128)(2,1)} %param.8), channel_id=1, source_target_pairs={{0,8},{8,16},{16,24},{24,0},{1,9},{9,17},{17,25},{25,1},{2,10},{10... | collective-permute-start | bytes 663560 | tf_op jit(solution)/shard_map/ppermute | solution.py:359
  4.5 0.9 %copy-start = (s32[3,8192]{1,0:T(4,128)S(1)}, s32[3,8192]{1,0:T(4,128)}, u32[]{:S(2)}) copy-start(s32[3,8192]{1,0:T(4,128)} %sphere_ref.1) | copy-start | bytes 294916
  5.4 1.0 %copy-start.1 = (bf16[1760,128]{1,0:T(8,128)(2,1)S(1)}, bf16[1760,128]{1,0:T(8,128)(2,1)}, u32[]{:S(2)}) copy-start(bf16[1760,128]{1,0:T(8,128)(2,1)} %constant.2.clone.table_ref) | copy-start | bytes 1351684
  10.7 6.0 %collective-permute-start.1 = (bf16[2,16384]{1,0:T(2,128)(2,1)S(1)}, bf16[2,16384]{1,0:T(2,128)(2,1)S(1)}, u32[]{:S(2)}, u32[]{:S(2)}) collective-permute-start(bf16[2,16384]{1,0:T(2,128)(2,1)S(1)} %get-tuple-element.23.refs_0_), channel_id=1, source_target_pairs={{0,4},{1,5},{2,6},{3,7},{4,0},{5,1},{6,2},{7,3},{8,12},{9,13},{10,... | collective-permute-start | bytes 196616 | tf_op jit(solution)/shard_map/ppermute | solution.py:364
  17.0 7.9 %collective-permute-start.9 = (bf16[4,16384]{1,0:T(4,128)(2,1)S(1)}, bf16[4,16384]{1,0:T(4,128)(2,1)S(1)}, u32[]{:S(2)}, u32[]{:S(2)}) collective-permute-start(bf16[4,16384]{1,0:T(4,128)(2,1)S(1)} %get-tuple-element.28), channel_id=1, source_target_pairs={{0,2},{1,3},{2,0},{3,1},{4,6},{5,7},{6,4},{7,5},{8,10},{9,11},{10,... | collective-permute-start | bytes 393224 | tf_op jit(solution)/shard_map/ppermute | solution.py:364
  17.9 4.2 %collective-permute-start.2 = (bf16[4,10240]{1,0:T(4,128)(2,1)S(1)}, bf16[4,10240]{1,0:T(4,128)(2,1)S(1)}, u32[]{:S(2)}, u32[]{:S(2)}) collective-permute-start(bf16[4,10240]{1,0:T(4,128)(2,1)S(1)} %get-tuple-element.25), channel_id=1, source_target_pairs={{0,1},{1,0},{2,3},{3,2},{4,5},{5,4},{6,7},{7,6},{8,9},{9,8},{10,11... | collective-permute-start | bytes 245768 | tf_op jit(solution)/shard_map/ppermute | solution.py:369
  19.1 3.9 %collective-permute-start.3 = (bf16[4,10240]{1,0:T(4,128)(2,1)S(1)}, bf16[4,10240]{1,0:T(4,128)(2,1)S(1)}, u32[]{:S(2)}, u32[]{:S(2)}) collective-permute-start(bf16[4,10240]{1,0:T(4,128)(2,1)S(1)} %get-tuple-element.26), channel_id=1, source_target_pairs={{0,16},{1,17},{2,18},{3,19},{4,20},{5,21},{6,22},{7,23},{8,24},{9,... | collective-permute-start | bytes 245768 | tf_op jit(solution)/shard_map/ppermute | solution.py:369
  19.1 7.4 %collective-permute-start.4 = (bf16[4,10240]{1,0:T(4,128)(2,1)S(1)}, bf16[4,10240]{1,0:T(4,128)(2,1)S(1)}, u32[]{:S(2)}, u32[]{:S(2)}) collective-permute-start(bf16[4,10240]{1,0:T(4,128)(2,1)S(1)} %get-tuple-element.27), channel_id=1, source_target_pairs={{0,17},{1,16},{2,19},{3,18},{4,21},{5,20},{6,23},{7,22},{8,25},{9,... | collective-permute-start | bytes 245768 | tf_op jit(solution)/shard_map/ppermute | solution.py:369
  20.5 6.0 %collective-permute-start.5 = (bf16[4,10240]{1,0:T(4,128)(2,1)S(1)}, bf16[4,10240]{1,0:T(4,128)(2,1)S(1)}, u32[]{:S(2)}, u32[]{:S(2)}) collective-permute-start(bf16[4,10240]{1,0:T(4,128)(2,1)S(1)} %get-tuple-element.24.refs_0_), channel_id=1, source_target_pairs={{0,8},{8,0},{16,24},{24,16},{1,9},{9,1},{17,25},{25,17},{2,10},{10... | collective-permute-start | bytes 245768 | tf_op jit(solution)/shard_map/ppermute | solution.py:364
  22.1 5.7 %collective-permute-start.6 = (bf16[4,10240]{1,0:T(4,128)(2,1)S(1)}, bf16[4,10240]{1,0:T(4,128)(2,1)S(1)}, u32[]{:S(2)}, u32[]{:S(2)}) collective-permute-start(bf16[4,10240]{1,0:T(4,128)(2,1)S(1)} %collective-permute-done.2.refs_1_), channel_id=1, source_target_pairs={{0,8},{8,0},{16,24},{24,16},{1,9},{9,1},{17,25},{25,17},{2,10},{10... | collective-permute-start | bytes 245768 | tf_op jit(solution)/shard_map/ppermute | solution.py:364
  23.0 5.6 %collective-permute-start.7 = (bf16[4,10240]{1,0:T(4,128)(2,1)S(1)}, bf16[4,10240]{1,0:T(4,128)(2,1)S(1)}, u32[]{:S(2)}, u32[]{:S(2)}) collective-permute-start(bf16[4,10240]{1,0:T(4,128)(2,1)S(1)} %collective-permute-done.3.refs_2_), channel_id=1, source_target_pairs={{0,8},{8,0},{16,24},{24,16},{1,9},{9,1},{17,25},{25,17},{2,10},{10... | collective-permute-start | bytes 245768 | tf_op jit(solution)/shard_map/ppermute | solution.py:364
  25.1 4.1 %collective-permute-start.10 = (bf16[4,10240]{1,0:T(4,128)(2,1)S(1)}, bf16[4,10240]{1,0:T(4,128)(2,1)S(1)}, u32[]{:S(2)}, u32[]{:S(2)}) collective-permute-start(bf16[4,10240]{1,0:T(4,128)(2,1)S(1)} %get-tuple-element.30), channel_id=1, source_target_pairs={{0,1},{1,0},{2,3},{3,2},{4,5},{5,4},{6,7},{7,6},{8,9},{9,8},{10,11... | collective-permute-start | bytes 245768 | tf_op jit(solution)/shard_map/ppermute | solution.py:369
  26.6 3.8 %collective-permute-start.11 = (bf16[4,10240]{1,0:T(4,128)(2,1)S(1)}, bf16[4,10240]{1,0:T(4,128)(2,1)S(1)}, u32[]{:S(2)}, u32[]{:S(2)}) collective-permute-start(bf16[4,10240]{1,0:T(4,128)(2,1)S(1)} %get-tuple-element.31), channel_id=1, source_target_pairs={{0,16},{1,17},{2,18},{3,19},{4,20},{5,21},{6,22},{7,23},{8,24},{9,... | collective-permute-start | bytes 245768 | tf_op jit(solution)/shard_map/ppermute | solution.py:369
  26.6 6.6 %collective-permute-start.12 = (bf16[4,10240]{1,0:T(4,128)(2,1)S(1)}, bf16[4,10240]{1,0:T(4,128)(2,1)S(1)}, u32[]{:S(2)}, u32[]{:S(2)}) collective-permute-start(bf16[4,10240]{1,0:T(4,128)(2,1)S(1)} %get-tuple-element.32), channel_id=1, source_target_pairs={{0,17},{1,16},{2,19},{3,18},{4,21},{5,20},{6,23},{7,22},{8,25},{9,... | collective-permute-start | bytes 245768 | tf_op jit(solution)/shard_map/ppermute | solution.py:369
  27.8 5.4 %collective-permute-start.8 = (bf16[4,10240]{1,0:T(4,128)(2,1)S(1)}, bf16[4,10240]{1,0:T(4,128)(2,1)S(1)}, u32[]{:S(2)}, u32[]{:S(2)}) collective-permute-start(bf16[4,10240]{1,0:T(4,128)(2,1)S(1)} %collective-permute-done.4.refs_3_), channel_id=1, source_target_pairs={{0,8},{8,0},{16,24},{24,16},{1,9},{9,1},{17,25},{25,17},{2,10},{10... | collective-permute-start | bytes 245768 | tf_op jit(solution)/shard_map/ppermute | solution.py:364
  28.6 4.5 %collective-permute-start.13 = (bf16[4,10240]{1,0:T(4,128)(2,1)S(1)}, bf16[4,10240]{1,0:T(4,128)(2,1)S(1)}, u32[]{:S(2)}, u32[]{:S(2)}) collective-permute-start(bf16[4,10240]{1,0:T(4,128)(2,1)S(1)} %get-tuple-element.29.refs_8_), channel_id=1, source_target_pairs={{0,8},{8,0},{16,24},{24,16},{1,9},{9,1},{17,25},{25,17},{2,10},{10... | collective-permute-start | bytes 245768 | tf_op jit(solution)/shard_map/ppermute | solution.py:364
  29.2 4.0 %collective-permute-start.14 = (bf16[4,10240]{1,0:T(4,128)(2,1)S(1)}, bf16[4,10240]{1,0:T(4,128)(2,1)S(1)}, u32[]{:S(2)}, u32[]{:S(2)}) collective-permute-start(bf16[4,10240]{1,0:T(4,128)(2,1)S(1)} %collective-permute-done.10.refs_9_), channel_id=1, source_target_pairs={{0,8},{8,0},{16,24},{24,16},{1,9},{9,1},{17,25},{25,17},{2,10},{10... | collective-permute-start | bytes 245768 | tf_op jit(solution)/shard_map/ppermute | solution.py:364
  30.3 3.8 %collective-permute-start.15 = (bf16[4,10240]{1,0:T(4,128)(2,1)S(1)}, bf16[4,10240]{1,0:T(4,128)(2,1)S(1)}, u32[]{:S(2)}, u32[]{:S(2)}) collective-permute-start(bf16[4,10240]{1,0:T(4,128)(2,1)S(1)} %collective-permute-done.11.refs_10_), channel_id=1, source_target_pairs={{0,8},{8,0},{16,24},{24,16},{1,9},{9,1},{17,25},{25,17},{2,10},{10... | collective-permute-start | bytes 245768 | tf_op jit(solution)/shard_map/ppermute | solution.py:364
  33.2 1.3 %collective-permute-start.16 = (bf16[4,10240]{1,0:T(4,128)(2,1)S(1)}, bf16[4,10240]{1,0:T(4,128)(2,1)S(1)}, u32[]{:S(2)}, u32[]{:S(2)}) collective-permute-start(bf16[4,10240]{1,0:T(4,128)(2,1)S(1)} %collective-permute-done.12.refs_11_), channel_id=1, source_target_pairs={{0,8},{8,0},{16,24},{24,16},{1,9},{9,1},{17,25},{25,17},{2,10},{10... | collective-permute-start | bytes 245768 | tf_op jit(solution)/shard_map/ppermute | solution.py:364

commit v9 on v8

--- a/solution.py
+++ b/solution.py
@@ -296,17 +296,40 @@
     return jnp.concatenate([ref[:, lanes].astype(jnp.float32) for ref in refs], axis=0).astype(jnp.bfloat16)
 
 
+def join_kernel(row_width, *refs):
+    messages, outs = refs[:-2], refs[-2:]
+    depth = messages[0].shape[0]
+    merge = max(1, 16 // depth)
+    r, _ = own_place()
+    for j in range(0, len(messages), merge):
+        here = slice(depth * j, depth * (j + merge))
+        columns = stacked(messages[j : j + merge], slice(2 * row_width, None))
+        for side, out_ref in enumerate(outs):
+            lanes = pl.ds(pl.multiple_of((r & 1 ^ side) * row_width, LANES), row_width)
+            out_ref[here, :row_width] = stacked(messages[j : j + merge], lanes)
+            out_ref[here, row_width:] = columns
+
+
+def join(messages, plan):
+    rows, cols, row_width, col_width = plan
+    depth = messages[0].shape[0]
+    return pl.pallas_call(
+        functools.partial(join_kernel, row_width),
+        out_shape=[jax.ShapeDtypeStruct((depth * len(messages), row_width + col_width), jnp.bfloat16)] * 2,
+        in_specs=in_vmem(len(messages)),
+        out_specs=in_vmem(2),
+        compiler_params=pltpu.CompilerParams(vmem_limit_bytes=VMEM_LIMIT),
+        cost_estimate=cost(10**9, 10**6),
+        name="join",
+    )(*messages)
+
+
 def outer_kernel(row_width, block, slots, *refs):
     messages, (out_ref, left_ref, right_ref, held_ref, sems) = refs[:-5], refs[-5:]
     depth = messages[0].shape[0]
-    merge = max(1, 16 // depth)
-    r, _ = own_place()
-    own_rows = pl.ds(pl.multiple_of((r & 1) * row_width, LANES), row_width)
-    columns = slice(2 * row_width, None)
-    for j in range(0, len(messages), merge):
-        here = slice(depth * j, depth * (j + merge))
-        left_ref[here, :] = stacked(messages[j : j + merge], own_rows)
-        right_ref[here, :] = stacked(messages[j : j + merge], columns)
+    for j, ref in enumerate(messages):
+        left_ref[depth * j : depth * (j + 1), :] = ref[:, :row_width]
+        right_ref[depth * j : depth * (j + 1), :] = ref[:, row_width:]
     count = row_width // block
 
     def copy_out(i, slot):
@@ -380,8 +403,7 @@
     targets = [(turn, side) for turn in range(0, rows, 2) for side in range(2)]
 
     def sent(packed):
-        straight = [packed[0]] + [sent_across(value, *target, rows, cols) for value, target in zip(packed[1:], targets[1:])]
-        return straight + [turned(value, "row", 1) for value in straight]
+        return [packed[0]] + [sent_across(value, *target, rows, cols) for value, target in zip(packed[1:], targets[1:])]
 
     held, turns, bit = [own], [0], cols // 2
     while bit > 2:
@@ -394,7 +416,8 @@
     messages = sent(packed)
     far = turned(merged, "col", bit)
     messages += sent(pack([far], levels, [turn + bit for turn in turns], targets, 0, plan))
-    return outer(messages, plan)
+    kept, passed = join(messages, plan)
+    return outer([kept, turned(passed, "row", 1)], plan)
 
 
 def solution(mesh):

time: 46.4 us -> 44.4 us (0.957)
  starting transfers between devices: 20.1 us -> 14.1 us
  waiting for transfers between devices: 4.42 us -> 8.25 us
    ppermute x10 -> x3, starting transfers between devices: 12.1 us -> 6.09 us  [turned(): return lax.ppermute(value, axis, [(i, i ^ turn) for i in range(devices)])]
    ppermute x10 -> x3, waiting for transfers between devices: 3.58 us -> 5.68 us  [turned(): return lax.ppermute(value, axis, [(i, i ^ turn) for i in range(devices)])]
    ppermute x6, waiting for transfers between devices: 0.83 us -> 2.57 us  [sent_across(): return lax.ppermute(value, ('row', 'col'), moves)]
  transfers between devices with their start and end apart: 17 -> 10, of which waited for: 5 -> 6; matrix products, arithmetic and copies ran while one was open for 7% -> 7% of each run, Pallas kernels for 2% -> 2%
where the time goes in v9:
time: 44.4 us; the launch traced here: 43.8 us
  Pallas kernels  16.3 us (37%)
  starting transfers between devices  14.1 us (32%)
  waiting for transfers between devices  8.25 us (19%)
  local copies, waits for them, and re-layouts  3.82 us (9%)
  other arithmetic  1.34 us (3%)
    pallas_call x1, Pallas kernels, outer(): pl.pallas_call(functools.partial(outer_kernel, row_width, block, slots),...  11.4 us
    ppermute x3, starting transfers between devices, turned(): return lax.ppermute(value, axis, [(i, i ^ turn) for i in range(devices)])  6.09 us
    ppermute x3, waiting for transfers between devices, turned(): return lax.ppermute(value, axis, [(i, i ^ turn) for i in range(devices)])  5.68 us
    ppermute x6, starting transfers between devices, sent_across(): return lax.ppermute(value, ('row', 'col'), moves)  5.36 us
    pallas_call x1, Pallas kernels, transform(): pl.pallas_call(functools.partial(second_kernel, grid), out_shape=[jax.Sha...  3.39 us
    unnamed x5, local copies, waits for them, and re-layouts  2.86 us
    ppermute x1, starting transfers between devices, shifted(): lax.ppermute(value, axis, [(i, (i + by) % devices) for i in range(devices)])  2.63 us
    ppermute x6, waiting for transfers between devices, sent_across(): return lax.ppermute(value, ('row', 'col'), moves)  2.57 us
  transfers between devices with their start and end apart: 10, of which 6 were waited for; matrix products, arithmetic and copies ran while one was open for 7% of the time, Pallas kernels for 2%

profile of v9, /device:TPU:1, one launch (start us, length us, event | category | flops | bytes accessed | tf_op | source)
XLA Modules:
  0.0 43.8 jit_solution(11096653354992439290)
XLA Ops:
  0.0 2.6 %collective-permute-start = (bf16[1,48,2304]{2,1,0:T(8,128)(2,1)}, bf16[1,48,2304]{2,1,0:T(8,128)(2,1)S(1)}, u32[]{:S(2)}, u32[]{:S(2)}) collective-permute-start(bf16[1,48,2304]{2,1,0:T(8,128)(2,1)} %param.8), channel_id=1, source_target_pairs={{0,8},{8,16},{16,24},{24,0},{1,9},{9,17},{17,25},{25,1},{2,10},{10... | collective-permute-start | bytes 663560 | tf_op jit(solution)/shard_map/ppermute | solution.py:382
  2.6 0.9 %constant_dynamic-update-slice_fusion.1 = bf16[2,48,2304]{2,1,0:T(8,128)(2,1)S(1)} fusion(bf16[1,48,2304]{2,1,0:T(8,128)(2,1)} %param.7), kind=kLoop, calls=%fused_computation.1 | loop fusion | bytes 442368
  3.6 1.0 %constant_dynamic-update-slice_fusion.orbitals_ref = bf16[2,48,2304]{2,1,0:T(8,128)(2,1)S(1)} fusion(bf16[2,48,2304]{2,1,0:T(8,128)(2,1)S(1)} %constant_dynamic-update-slice_fusion.1, bf16[1,48,2304]{2,1,0:T(8,128)(2,1)} %param.8), kind=kLoop, calls=%fused_computation | loop fusion | bytes 442368 | tf_op jit(solution)/shard_map/concatenate | solution.py:224
  4.5 0.0 copy-start
  4.6 0.9 %copy-done = s32[3,8192]{1,0:T(4,128)S(1)} copy-done((s32[3,8192]{1,0:T(4,128)S(1)}, s32[3,8192]{1,0:T(4,128)}, u32[]{:S(2)}) %copy-start) | copy-done | bytes 98328
  5.4 0.0 copy-start.1
  5.5 1.0 %copy-done.1 = bf16[1760,128]{1,0:T(8,128)(2,1)S(1)} copy-done((bf16[1760,128]{1,0:T(8,128)(2,1)S(1)}, bf16[1760,128]{1,0:T(8,128)(2,1)}, u32[]{:S(2)}) %copy-start.1) | copy-done | bytes 450584
  6.5 0.9 %first_pair.1 = (bf16[240,256]{1,0:T(8,128)(2,1)S(1)}, s32[2,8192]{1,0:T(2,128)S(1)}, bf16[1760,128]{1,0:T(8,128)(2,1)S(1)}) custom-call(bf16[2,48,2304]{2,1,0:T(8,128)(2,1)S(1)} %constant_dynamic-update-slice_fusion.orbitals_ref, bf16[1760,128]{1,0:T(8,128)(2,1)S(1)} %copy-done.1, s32[3,8192]{1,0:T(4,128)S(1)} %copy-done), custom_call_target="tpu_custom_call" | custom-call | flops 2000000000 | bytes 2000000 | tf_op jit(solution)/shard_map/first_pair/pallas_call | solution.py:230
  7.3 0.0 collective-permute-done.occ_ref
  7.4 3.4 %second_pair.1 = (bf16[2,16384]{1,0:T(2,128)(2,1)S(1)}, s32[1,32]{1,0:T(1,128)S(1)}) custom-call(bf16[2,48,2304]{2,1,0:T(8,128)(2,1)S(1)} %constant_dynamic-update-slice_fusion.orbitals_ref, bf16[1,48,2304]{2,1,0:T(8,128)(2,1)S(1)} %collective-permute-done.occ_ref, bf16[240,256]{1,0:T(8,128)(2,1)S(1)} %get-tuple-element.21.first_ref, ...), custom_call_target="tpu_custom_call" | custom-call | flops 2000000000 | bytes 2000000 | tf_op jit(solution)/shard_map/second_pair/pallas_call | solution.py:242
  10.7 2.4 %collective-permute-start.1 = (bf16[2,16384]{1,0:T(2,128)(2,1)S(1)}, bf16[2,16384]{1,0:T(2,128)(2,1)S(1)}, u32[]{:S(2)}, u32[]{:S(2)}) collective-permute-start(bf16[2,16384]{1,0:T(2,128)(2,1)S(1)} %get-tuple-element.25.refs_0_), channel_id=1, source_target_pairs={{0,4},{1,5},{2,6},{3,7},{4,0},{5,1},{6,2},{7,3},{8,12},{9,13},{10,... | collective-permute-start | bytes 196616 | tf_op jit(solution)/shard_map/ppermute | solution.py:387
  13.1 0.7 %fusion.1 = f32[1,32]{1,0:T(1,128)S(1)} fusion(s32[32]{0:T(128)} %param.11, s32[1,32]{1,0:T(1,128)S(1)} %get-tuple-element.24), kind=kLoop, calls=%fused_computation.5 | loop fusion | flops 64 | bytes 384 | tf_op jit(solution)/shard_map/stack | solution.py:402
  13.8 0.7 %pad_maximum_fusion.levels_ref = f32[3,32]{1,0:T(4,128)S(1)} fusion(f32[1,32]{1,0:T(1,128)S(1)} %fusion.1, f32[1,32]{1,0:T(1,128)} %bitcast.10, f32[1,32]{1,0:T(1,128)} %bitcast.11), kind=kLoop, calls=%fused_computation.2 | loop fusion | flops 192 | bytes 768 | tf_op jit(solution)/shard_map/stack | solution.py:402
  14.5 2.3 %collective-permute-done.1.refs_1_ = bf16[2,16384]{1,0:T(2,128)(2,1)S(1)} collective-permute-done((bf16[2,16384]{1,0:T(2,128)(2,1)S(1)}, bf16[2,16384]{1,0:T(2,128)(2,1)S(1)}, u32[]{:S(2)}, u32[]{:S(2)}) %collective-permute-start.1) | collective-permute-done | bytes 65568 | tf_op jit(solution)/shard_map/ppermute | solution.py:387
  16.8 0.2 pack.2
  17.0 0.9 %collective-permute-start.5 = (bf16[4,16384]{1,0:T(4,128)(2,1)S(1)}, bf16[4,16384]{1,0:T(4,128)(2,1)S(1)}, u32[]{:S(2)}, u32[]{:S(2)}) collective-permute-start(bf16[4,16384]{1,0:T(4,128)(2,1)S(1)} %get-tuple-element.30), channel_id=1, source_target_pairs={{0,2},{1,3},{2,0},{3,1},{4,6},{5,7},{6,4},{7,5},{8,10},{9,11},{10,... | collective-permute-start | bytes 393224 | tf_op jit(solution)/shard_map/ppermute | solution.py:387
  17.9 1.2 %collective-permute-start.2 = (bf16[4,10240]{1,0:T(4,128)(2,1)S(1)}, bf16[4,10240]{1,0:T(4,128)(2,1)S(1)}, u32[]{:S(2)}, u32[]{:S(2)}) collective-permute-start(bf16[4,10240]{1,0:T(4,128)(2,1)S(1)} %get-tuple-element.27), channel_id=1, source_target_pairs={{0,1},{1,0},{2,3},{3,2},{4,5},{5,4},{6,7},{7,6},{8,9},{9,8},{10,11... | collective-permute-start | bytes 245768 | tf_op jit(solution)/shard_map/ppermute | solution.py:392
  19.1 0.0 collective-permute-start.3
  19.1 1.4 %collective-permute-start.4 = (bf16[4,10240]{1,0:T(4,128)(2,1)S(1)}, bf16[4,10240]{1,0:T(4,128)(2,1)S(1)}, u32[]{:S(2)}, u32[]{:S(2)}) collective-permute-start(bf16[4,10240]{1,0:T(4,128)(2,1)S(1)} %get-tuple-element.29), channel_id=1, source_target_pairs={{0,17},{1,16},{2,19},{3,18},{4,21},{5,20},{6,23},{7,22},{8,25},{9,... | collective-permute-start | bytes 245768 | tf_op jit(solution)/shard_map/ppermute | solution.py:392
  20.5 2.0 %collective-permute-done.5.refs_0_ = bf16[4,16384]{1,0:T(4,128)(2,1)S(1)} collective-permute-done((bf16[4,16384]{1,0:T(4,128)(2,1)S(1)}, bf16[4,16384]{1,0:T(4,128)(2,1)S(1)}, u32[]{:S(2)}, u32[]{:S(2)}) %collective-permute-start.5) | collective-permute-done | bytes 131104 | tf_op jit(solution)/shard_map/ppermute | solution.py:387
  22.5 0.2 pack.3
  22.8 0.5 %collective-permute-start.6 = (bf16[4,10240]{1,0:T(4,128)(2,1)S(1)}, bf16[4,10240]{1,0:T(4,128)(2,1)S(1)}, u32[]{:S(2)}, u32[]{:S(2)}) collective-permute-start(bf16[4,10240]{1,0:T(4,128)(2,1)S(1)} %get-tuple-element.32), channel_id=1, source_target_pairs={{0,1},{1,0},{2,3},{3,2},{4,5},{5,4},{6,7},{7,6},{8,9},{9,8},{10,11... | collective-permute-start | bytes 245768 | tf_op jit(solution)/shard_map/ppermute | solution.py:392
  23.3 0.0 collective-permute-start.7
  23.3 0.0 collective-permute-done.2.refs_1_
  23.3 2.2 %collective-permute-start.8 = (bf16[4,10240]{1,0:T(4,128)(2,1)S(1)}, bf16[4,10240]{1,0:T(4,128)(2,1)S(1)}, u32[]{:S(2)}, u32[]{:S(2)}) collective-permute-start(bf16[4,10240]{1,0:T(4,128)(2,1)S(1)} %get-tuple-element.34), channel_id=1, source_target_pairs={{0,17},{1,16},{2,19},{3,18},{4,21},{5,20},{6,23},{7,22},{8,25},{9,... | collective-permute-start | bytes 245768 | tf_op jit(solution)/shard_map/ppermute | solution.py:392
  25.5 0.0 collective-permute-done.3.refs_2_
  25.5 0.0 collective-permute-done.4.refs_3_
  25.5 1.1 %collective-permute-done.6.refs_5_ = bf16[4,10240]{1,0:T(4,128)(2,1)S(1)} collective-permute-done((bf16[4,10240]{1,0:T(4,128)(2,1)S(1)}, bf16[4,10240]{1,0:T(4,128)(2,1)S(1)}, u32[]{:S(2)}, u32[]{:S(2)}) %collective-permute-start.6) | collective-permute-done | bytes 81952 | tf_op jit(solution)/shard_map/ppermute | solution.py:392
  26.6 0.2 collective-permute-done.7.refs_6_
  26.9 1.2 %collective-permute-done.8.refs_7_ = bf16[4,10240]{1,0:T(4,128)(2,1)S(1)} collective-permute-done((bf16[4,10240]{1,0:T(4,128)(2,1)S(1)}, bf16[4,10240]{1,0:T(4,128)(2,1)S(1)}, u32[]{:S(2)}, u32[]{:S(2)}) %collective-permute-start.8) | collective-permute-done | bytes 81952 | tf_op jit(solution)/shard_map/ppermute | solution.py:392
  28.0 0.2 join.1
  28.2 2.8 %collective-permute-start.9 = (bf16[32,6144]{1,0:T(8,128)(2,1)S(1)}, bf16[32,6144]{1,0:T(8,128)(2,1)S(1)}, u32[]{:S(2)}, u32[]{:S(2)}) collective-permute-start(bf16[32,6144]{1,0:T(8,128)(2,1)S(1)} %get-tuple-element.36), channel_id=1, source_target_pairs={{0,8},{8,0},{16,24},{24,16},{1,9},{9,1},{17,25},{25,17},{2,10},{10... | collective-permute-start | bytes 1179656 | tf_op jit(solution)/shard_map/ppermute | solution.py:387
  31.0 1.3 %collective-permute-done.9.refs_1_ = bf16[32,6144]{1,0:T(8,128)(2,1)S(1)} collective-permute-done((bf16[32,6144]{1,0:T(8,128)(2,1)S(1)}, bf16[32,6144]{1,0:T(8,128)(2,1)S(1)}, u32[]{:S(2)}, u32[]{:S(2)}) %collective-permute-start.9) | collective-permute-done | bytes 393248 | tf_op jit(solution)/shard_map/ppermute | solution.py:387
  32.4 11.4 %outer.1 = f32[4096,2048]{1,0:T(8,128)} custom-call(bf16[32,6144]{1,0:T(8,128)(2,1)S(1)} %get-tuple-element.35.refs_0_, bf16[32,6144]{1,0:T(8,128)(2,1)S(1)} %collective-permute-done.9.refs_1_), custom_call_target="tpu_custom_call" | custom-call | flops 10000000000 | bytes 30000000 | tf_op jit(solution)/shard_map/outer/pallas_call | solution.py:363
Async XLA Ops:
  0.0 7.3 %collective-permute-start = (bf16[1,48,2304]{2,1,0:T(8,128)(2,1)}, bf16[1,48,2304]{2,1,0:T(8,128)(2,1)S(1)}, u32[]{:S(2)}, u32[]{:S(2)}) collective-permute-start(bf16[1,48,2304]{2,1,0:T(8,128)(2,1)} %param.8), channel_id=1, source_target_pairs={{0,8},{8,16},{16,24},{24,0},{1,9},{9,17},{17,25},{25,1},{2,10},{10... | collective-permute-start | bytes 663560 | tf_op jit(solution)/shard_map/ppermute | solution.py:382
  4.5 0.9 %copy-start = (s32[3,8192]{1,0:T(4,128)S(1)}, s32[3,8192]{1,0:T(4,128)}, u32[]{:S(2)}) copy-start(s32[3,8192]{1,0:T(4,128)} %sphere_ref.1) | copy-start | bytes 294916
  5.4 1.0 %copy-start.1 = (bf16[1760,128]{1,0:T(8,128)(2,1)S(1)}, bf16[1760,128]{1,0:T(8,128)(2,1)}, u32[]{:S(2)}) copy-start(bf16[1760,128]{1,0:T(8,128)(2,1)} %constant.2.clone.table_ref) | copy-start | bytes 1351684
  10.7 6.0 %collective-permute-start.1 = (bf16[2,16384]{1,0:T(2,128)(2,1)S(1)}, bf16[2,16384]{1,0:T(2,128)(2,1)S(1)}, u32[]{:S(2)}, u32[]{:S(2)}) collective-permute-start(bf16[2,16384]{1,0:T(2,128)(2,1)S(1)} %get-tuple-element.25.refs_0_), channel_id=1, source_target_pairs={{0,4},{1,5},{2,6},{3,7},{4,0},{5,1},{6,2},{7,3},{8,12},{9,13},{10,... | collective-permute-start | bytes 196616 | tf_op jit(solution)/shard_map/ppermute | solution.py:387
  17.0 5.5 %collective-permute-start.5 = (bf16[4,16384]{1,0:T(4,128)(2,1)S(1)}, bf16[4,16384]{1,0:T(4,128)(2,1)S(1)}, u32[]{:S(2)}, u32[]{:S(2)}) collective-permute-start(bf16[4,16384]{1,0:T(4,128)(2,1)S(1)} %get-tuple-element.30), channel_id=1, source_target_pairs={{0,2},{1,3},{2,0},{3,1},{4,6},{5,7},{6,4},{7,5},{8,10},{9,11},{10,... | collective-permute-start | bytes 393224 | tf_op jit(solution)/shard_map/ppermute | solution.py:387
  17.9 5.4 %collective-permute-start.2 = (bf16[4,10240]{1,0:T(4,128)(2,1)S(1)}, bf16[4,10240]{1,0:T(4,128)(2,1)S(1)}, u32[]{:S(2)}, u32[]{:S(2)}) collective-permute-start(bf16[4,10240]{1,0:T(4,128)(2,1)S(1)} %get-tuple-element.27), channel_id=1, source_target_pairs={{0,1},{1,0},{2,3},{3,2},{4,5},{5,4},{6,7},{7,6},{8,9},{9,8},{10,11... | collective-permute-start | bytes 245768 | tf_op jit(solution)/shard_map/ppermute | solution.py:392
  19.1 6.4 %collective-permute-start.3 = (bf16[4,10240]{1,0:T(4,128)(2,1)S(1)}, bf16[4,10240]{1,0:T(4,128)(2,1)S(1)}, u32[]{:S(2)}, u32[]{:S(2)}) collective-permute-start(bf16[4,10240]{1,0:T(4,128)(2,1)S(1)} %get-tuple-element.28), channel_id=1, source_target_pairs={{0,16},{1,17},{2,18},{3,19},{4,20},{5,21},{6,22},{7,23},{8,24},{9,... | collective-permute-start | bytes 245768 | tf_op jit(solution)/shard_map/ppermute | solution.py:392
  19.1 6.4 %collective-permute-start.4 = (bf16[4,10240]{1,0:T(4,128)(2,1)S(1)}, bf16[4,10240]{1,0:T(4,128)(2,1)S(1)}, u32[]{:S(2)}, u32[]{:S(2)}) collective-permute-start(bf16[4,10240]{1,0:T(4,128)(2,1)S(1)} %get-tuple-element.29), channel_id=1, source_target_pairs={{0,17},{1,16},{2,19},{3,18},{4,21},{5,20},{6,23},{7,22},{8,25},{9,... | collective-permute-start | bytes 245768 | tf_op jit(solution)/shard_map/ppermute | solution.py:392
  22.8 3.9 %collective-permute-start.6 = (bf16[4,10240]{1,0:T(4,128)(2,1)S(1)}, bf16[4,10240]{1,0:T(4,128)(2,1)S(1)}, u32[]{:S(2)}, u32[]{:S(2)}) collective-permute-start(bf16[4,10240]{1,0:T(4,128)(2,1)S(1)} %get-tuple-element.32), channel_id=1, source_target_pairs={{0,1},{1,0},{2,3},{3,2},{4,5},{5,4},{6,7},{7,6},{8,9},{9,8},{10,11... | collective-permute-start | bytes 245768 | tf_op jit(solution)/shard_map/ppermute | solution.py:392
  23.3 3.6 %collective-permute-start.7 = (bf16[4,10240]{1,0:T(4,128)(2,1)S(1)}, bf16[4,10240]{1,0:T(4,128)(2,1)S(1)}, u32[]{:S(2)}, u32[]{:S(2)}) collective-permute-start(bf16[4,10240]{1,0:T(4,128)(2,1)S(1)} %get-tuple-element.33), channel_id=1, source_target_pairs={{0,16},{1,17},{2,18},{3,19},{4,20},{5,21},{6,22},{7,23},{8,24},{9,... | collective-permute-start | bytes 245768 | tf_op jit(solution)/shard_map/ppermute | solution.py:392
  23.3 4.8 %collective-permute-start.8 = (bf16[4,10240]{1,0:T(4,128)(2,1)S(1)}, bf16[4,10240]{1,0:T(4,128)(2,1)S(1)}, u32[]{:S(2)}, u32[]{:S(2)}) collective-permute-start(bf16[4,10240]{1,0:T(4,128)(2,1)S(1)} %get-tuple-element.34), channel_id=1, source_target_pairs={{0,17},{1,16},{2,19},{3,18},{4,21},{5,20},{6,23},{7,22},{8,25},{9,... | collective-permute-start | bytes 245768 | tf_op jit(solution)/shard_map/ppermute | solution.py:392
  28.2 4.2 %collective-permute-start.9 = (bf16[32,6144]{1,0:T(8,128)(2,1)S(1)}, bf16[32,6144]{1,0:T(8,128)(2,1)S(1)}, u32[]{:S(2)}, u32[]{:S(2)}) collective-permute-start(bf16[32,6144]{1,0:T(8,128)(2,1)S(1)} %get-tuple-element.36), channel_id=1, source_target_pairs={{0,8},{8,0},{16,24},{24,16},{1,9},{9,1},{17,25},{25,17},{2,10},{10... | collective-permute-start | bytes 1179656 | tf_op jit(solution)/shard_map/ppermute | solution.py:387

commit v10 on v9

--- a/solution.py
+++ b/solution.py
@@ -325,10 +325,9 @@
 
 
 def outer_kernel(row_width, block, slots, *refs):
-    messages, (out_ref, left_ref, right_ref, held_ref, sems) = refs[:-5], refs[-5:]
+    messages, (out_ref, right_ref, held_ref, sems) = refs[:-4], refs[-4:]
     depth = messages[0].shape[0]
     for j, ref in enumerate(messages):
-        left_ref[depth * j : depth * (j + 1), :] = ref[:, :row_width]
         right_ref[depth * j : depth * (j + 1), :] = ref[:, row_width:]
     count = row_width // block
 
@@ -344,9 +343,8 @@
             copy_out(i - slots, slot).wait()
 
         here = pl.ds(pl.multiple_of(i * block, block), block)
-        held_ref[slot] = lax.dot_general(
-            left_ref[:, here], right_ref[...], (((0,), (0,)), ((), ())), preferred_element_type=jnp.float32
-        )
+        left = jnp.concatenate([ref[:, here] for ref in messages], axis=0)
+        held_ref[slot] = lax.dot_general(left, right_ref[...], (((0,), (0,)), ((), ())), preferred_element_type=jnp.float32)
         copy_out(i, slot).start()
         return carry
 
@@ -366,7 +364,6 @@
         in_specs=in_vmem(len(messages)),
         out_specs=pl.BlockSpec(memory_space=pltpu.HBM),
         scratch_shapes=[
-            pltpu.VMEM((depth * len(messages), row_width), jnp.bfloat16),
             pltpu.VMEM((depth * len(messages), col_width), jnp.bfloat16),
             pltpu.VMEM((slots, block, col_width), jnp.float32),
             pltpu.SemaphoreType.DMA((slots,)),
@@ -400,7 +397,8 @@
     occ_second = shifted(occ_orbitals, "row", 1)
     own, later = transform(cond_orbitals, occ_orbitals, occ_second, sphere_index, occ_band.shape)
     levels = jnp.stack([cond_energy, occ_energy, (occ_band + later[0]).astype(jnp.float32)])
-    targets = [(turn, side) for turn in range(0, rows, 2) for side in range(2)]
+    targets = [(0, 0)] + [(turn, side) for side in (1, 0) for turn in range(rows - 2, -2, -2) if turn or side]
+    targets.append(targets.pop(rows // 2))
 
     def sent(packed):
         return [packed[0]] + [sent_across(value, *target, rows, cols) for value, target in zip(packed[1:], targets[1:])]

time: 44.4 us -> 44.5 us (level)
  no operation moved by 1% of the time
where the time goes in v10:
time: 44.5 us; the launch traced here: 43.9 us
  Pallas kernels  16.2 us (36%)
  starting transfers between devices  13.9 us (31%)
  waiting for transfers between devices  8.53 us (19%)
  local copies, waits for them, and re-layouts  3.82 us (9%)
  other arithmetic  1.34 us (3%)
    pallas_call x1, Pallas kernels, outer(): pl.pallas_call(functools.partial(outer_kernel, row_width, block, slots),...  11.4 us
    ppermute x3, starting transfers between devices, turned(): return lax.ppermute(value, axis, [(i, i ^ turn) for i in range(devices)])  5.91 us
    ppermute x3, waiting for transfers between devices, turned(): return lax.ppermute(value, axis, [(i, i ^ turn) for i in range(devices)])  5.64 us
    ppermute x6, starting transfers between devices, sent_across(): return lax.ppermute(value, ('row', 'col'), moves)  5.36 us
    pallas_call x1, Pallas kernels, transform(): pl.pallas_call(functools.partial(second_kernel, grid), out_shape=[jax.Sha...  3.39 us
    ppermute x6, waiting for transfers between devices, sent_across(): return lax.ppermute(value, ('row', 'col'), moves)  2.89 us
    unnamed x5, local copies, waits for them, and re-layouts  2.86 us
    ppermute x1, starting transfers between devices, shifted(): lax.ppermute(value, axis, [(i, (i + by) % devices) for i in range(devices)])  2.63 us
  transfers between devices with their start and end apart: 10, of which 6 were waited for; matrix products, arithmetic and copies ran while one was open for 7% of the time, Pallas kernels for 2%

profile of v10, /device:TPU:1, one launch (start us, length us, event | category | flops | bytes accessed | tf_op | source)
XLA Modules:
  0.0 43.9 jit_solution(3032531625919881329)
XLA Ops:
  0.0 2.6 %collective-permute-start = (bf16[1,48,2304]{2,1,0:T(8,128)(2,1)}, bf16[1,48,2304]{2,1,0:T(8,128)(2,1)S(1)}, u32[]{:S(2)}, u32[]{:S(2)}) collective-permute-start(bf16[1,48,2304]{2,1,0:T(8,128)(2,1)} %param.8), channel_id=1, source_target_pairs={{0,8},{8,16},{16,24},{24,0},{1,9},{9,17},{17,25},{25,1},{2,10},{10... | collective-permute-start | bytes 663560 | tf_op jit(solution)/shard_map/ppermute | solution.py:379
  2.6 0.9 %constant_dynamic-update-slice_fusion.1 = bf16[2,48,2304]{2,1,0:T(8,128)(2,1)S(1)} fusion(bf16[1,48,2304]{2,1,0:T(8,128)(2,1)} %param.7), kind=kLoop, calls=%fused_computation.1 | loop fusion | bytes 442368
  3.6 1.0 %constant_dynamic-update-slice_fusion.orbitals_ref = bf16[2,48,2304]{2,1,0:T(8,128)(2,1)S(1)} fusion(bf16[2,48,2304]{2,1,0:T(8,128)(2,1)S(1)} %constant_dynamic-update-slice_fusion.1, bf16[1,48,2304]{2,1,0:T(8,128)(2,1)} %param.8), kind=kLoop, calls=%fused_computation | loop fusion | bytes 442368 | tf_op jit(solution)/shard_map/concatenate | solution.py:224
  4.5 0.0 copy-start
  4.6 0.9 %copy-done = s32[3,8192]{1,0:T(4,128)S(1)} copy-done((s32[3,8192]{1,0:T(4,128)S(1)}, s32[3,8192]{1,0:T(4,128)}, u32[]{:S(2)}) %copy-start) | copy-done | bytes 98328
  5.4 0.0 copy-start.1
  5.5 1.0 %copy-done.1 = bf16[1760,128]{1,0:T(8,128)(2,1)S(1)} copy-done((bf16[1760,128]{1,0:T(8,128)(2,1)S(1)}, bf16[1760,128]{1,0:T(8,128)(2,1)}, u32[]{:S(2)}) %copy-start.1) | copy-done | bytes 450584
  6.5 0.9 %first_pair.1 = (bf16[240,256]{1,0:T(8,128)(2,1)S(1)}, s32[2,8192]{1,0:T(2,128)S(1)}, bf16[1760,128]{1,0:T(8,128)(2,1)S(1)}) custom-call(bf16[2,48,2304]{2,1,0:T(8,128)(2,1)S(1)} %constant_dynamic-update-slice_fusion.orbitals_ref, bf16[1760,128]{1,0:T(8,128)(2,1)S(1)} %copy-done.1, s32[3,8192]{1,0:T(4,128)S(1)} %copy-done), custom_call_target="tpu_custom_call" | custom-call | flops 2000000000 | bytes 2000000 | tf_op jit(solution)/shard_map/first_pair/pallas_call | solution.py:230
  7.3 0.0 collective-permute-done.occ_ref
  7.4 3.4 %second_pair.1 = (bf16[2,16384]{1,0:T(2,128)(2,1)S(1)}, s32[1,32]{1,0:T(1,128)S(1)}) custom-call(bf16[2,48,2304]{2,1,0:T(8,128)(2,1)S(1)} %constant_dynamic-update-slice_fusion.orbitals_ref, bf16[1,48,2304]{2,1,0:T(8,128)(2,1)S(1)} %collective-permute-done.occ_ref, bf16[240,256]{1,0:T(8,128)(2,1)S(1)} %get-tuple-element.21.first_ref, ...), custom_call_target="tpu_custom_call" | custom-call | flops 2000000000 | bytes 2000000 | tf_op jit(solution)/shard_map/second_pair/pallas_call | solution.py:242
  10.7 2.4 %collective-permute-start.1 = (bf16[2,16384]{1,0:T(2,128)(2,1)S(1)}, bf16[2,16384]{1,0:T(2,128)(2,1)S(1)}, u32[]{:S(2)}, u32[]{:S(2)}) collective-permute-start(bf16[2,16384]{1,0:T(2,128)(2,1)S(1)} %get-tuple-element.25.refs_0_), channel_id=1, source_target_pairs={{0,4},{1,5},{2,6},{3,7},{4,0},{5,1},{6,2},{7,3},{8,12},{9,13},{10,... | collective-permute-start | bytes 196616 | tf_op jit(solution)/shard_map/ppermute | solution.py:384
  13.1 0.7 %fusion.1 = f32[1,32]{1,0:T(1,128)S(1)} fusion(s32[32]{0:T(128)} %param.11, s32[1,32]{1,0:T(1,128)S(1)} %get-tuple-element.24), kind=kLoop, calls=%fused_computation.5 | loop fusion | flops 64 | bytes 384 | tf_op jit(solution)/shard_map/stack | solution.py:399
  13.8 0.7 %pad_maximum_fusion.levels_ref = f32[3,32]{1,0:T(4,128)S(1)} fusion(f32[1,32]{1,0:T(1,128)S(1)} %fusion.1, f32[1,32]{1,0:T(1,128)} %bitcast.10, f32[1,32]{1,0:T(1,128)} %bitcast.11), kind=kLoop, calls=%fused_computation.2 | loop fusion | flops 192 | bytes 768 | tf_op jit(solution)/shard_map/stack | solution.py:399
  14.5 2.3 %collective-permute-done.1.refs_1_ = bf16[2,16384]{1,0:T(2,128)(2,1)S(1)} collective-permute-done((bf16[2,16384]{1,0:T(2,128)(2,1)S(1)}, bf16[2,16384]{1,0:T(2,128)(2,1)S(1)}, u32[]{:S(2)}, u32[]{:S(2)}) %collective-permute-start.1) | collective-permute-done | bytes 65568 | tf_op jit(solution)/shard_map/ppermute | solution.py:384
  16.8 0.2 pack.2
  17.0 0.9 %collective-permute-start.5 = (bf16[4,16384]{1,0:T(4,128)(2,1)S(1)}, bf16[4,16384]{1,0:T(4,128)(2,1)S(1)}, u32[]{:S(2)}, u32[]{:S(2)}) collective-permute-start(bf16[4,16384]{1,0:T(4,128)(2,1)S(1)} %get-tuple-element.30), channel_id=1, source_target_pairs={{0,2},{1,3},{2,0},{3,1},{4,6},{5,7},{6,4},{7,5},{8,10},{9,11},{10,... | collective-permute-start | bytes 393224 | tf_op jit(solution)/shard_map/ppermute | solution.py:384
  17.9 0.0 collective-permute-start.2
  17.9 2.4 %collective-permute-start.3 = (bf16[4,10240]{1,0:T(4,128)(2,1)S(1)}, bf16[4,10240]{1,0:T(4,128)(2,1)S(1)}, u32[]{:S(2)}, u32[]{:S(2)}) collective-permute-start(bf16[4,10240]{1,0:T(4,128)(2,1)S(1)} %get-tuple-element.28), channel_id=1, source_target_pairs={{0,16},{1,17},{2,18},{3,19},{4,20},{5,21},{6,22},{7,23},{8,24},{9,... | collective-permute-start | bytes 245768 | tf_op jit(solution)/shard_map/ppermute | solution.py:389
  20.3 0.3 collective-permute-start.4
  20.6 2.0 %collective-permute-done.5.refs_0_ = bf16[4,16384]{1,0:T(4,128)(2,1)S(1)} collective-permute-done((bf16[4,16384]{1,0:T(4,128)(2,1)S(1)}, bf16[4,16384]{1,0:T(4,128)(2,1)S(1)}, u32[]{:S(2)}, u32[]{:S(2)}) %collective-permute-start.5) | collective-permute-done | bytes 131104 | tf_op jit(solution)/shard_map/ppermute | solution.py:384
  22.5 0.2 pack.3
  22.7 0.1 collective-permute-start.6
  22.8 1.7 %collective-permute-start.7 = (bf16[4,10240]{1,0:T(4,128)(2,1)S(1)}, bf16[4,10240]{1,0:T(4,128)(2,1)S(1)}, u32[]{:S(2)}, u32[]{:S(2)}) collective-permute-start(bf16[4,10240]{1,0:T(4,128)(2,1)S(1)} %get-tuple-element.33), channel_id=1, source_target_pairs={{0,16},{1,17},{2,18},{3,19},{4,20},{5,21},{6,22},{7,23},{8,24},{9,... | collective-permute-start | bytes 245768 | tf_op jit(solution)/shard_map/ppermute | solution.py:389
  24.5 0.0 collective-permute-done.2.refs_1_
  24.5 1.0 %collective-permute-start.8 = (bf16[4,10240]{1,0:T(4,128)(2,1)S(1)}, bf16[4,10240]{1,0:T(4,128)(2,1)S(1)}, u32[]{:S(2)}, u32[]{:S(2)}) collective-permute-start(bf16[4,10240]{1,0:T(4,128)(2,1)S(1)} %get-tuple-element.34), channel_id=1, source_target_pairs={{0,1},{1,0},{2,3},{3,2},{4,5},{5,4},{6,7},{7,6},{8,9},{9,8},{10,11... | collective-permute-start | bytes 245768 | tf_op jit(solution)/shard_map/ppermute | solution.py:389
  25.4 0.0 collective-permute-done.3.refs_2_
  25.4 0.0 collective-permute-done.4.refs_3_
  25.5 1.9 %collective-permute-done.6.refs_5_ = bf16[4,10240]{1,0:T(4,128)(2,1)S(1)} collective-permute-done((bf16[4,10240]{1,0:T(4,128)(2,1)S(1)}, bf16[4,10240]{1,0:T(4,128)(2,1)S(1)}, u32[]{:S(2)}, u32[]{:S(2)}) %collective-permute-start.6) | collective-permute-done | bytes 81952 | tf_op jit(solution)/shard_map/ppermute | solution.py:389
  27.3 0.4 collective-permute-done.7.refs_6_
  27.7 0.6 %collective-permute-done.8.refs_7_ = bf16[4,10240]{1,0:T(4,128)(2,1)S(1)} collective-permute-done((bf16[4,10240]{1,0:T(4,128)(2,1)S(1)}, bf16[4,10240]{1,0:T(4,128)(2,1)S(1)}, u32[]{:S(2)}, u32[]{:S(2)}) %collective-permute-start.8) | collective-permute-done | bytes 81952 | tf_op jit(solution)/shard_map/ppermute | solution.py:389
  28.3 0.2 join.1
  28.5 2.6 %collective-permute-start.9 = (bf16[32,6144]{1,0:T(8,128)(2,1)S(1)}, bf16[32,6144]{1,0:T(8,128)(2,1)S(1)}, u32[]{:S(2)}, u32[]{:S(2)}) collective-permute-start(bf16[32,6144]{1,0:T(8,128)(2,1)S(1)} %get-tuple-element.36), channel_id=1, source_target_pairs={{0,8},{8,0},{16,24},{24,16},{1,9},{9,1},{17,25},{25,17},{2,10},{10... | collective-permute-start | bytes 1179656 | tf_op jit(solution)/shard_map/ppermute | solution.py:384
  31.1 1.3 %collective-permute-done.9.refs_1_ = bf16[32,6144]{1,0:T(8,128)(2,1)S(1)} collective-permute-done((bf16[32,6144]{1,0:T(8,128)(2,1)S(1)}, bf16[32,6144]{1,0:T(8,128)(2,1)S(1)}, u32[]{:S(2)}, u32[]{:S(2)}) %collective-permute-start.9) | collective-permute-done | bytes 393248 | tf_op jit(solution)/shard_map/ppermute | solution.py:384
  32.5 11.4 %outer.1 = f32[4096,2048]{1,0:T(8,128)} custom-call(bf16[32,6144]{1,0:T(8,128)(2,1)S(1)} %get-tuple-element.35.refs_0_, bf16[32,6144]{1,0:T(8,128)(2,1)S(1)} %collective-permute-done.9.refs_1_), custom_call_target="tpu_custom_call" | custom-call | flops 10000000000 | bytes 30000000 | tf_op jit(solution)/shard_map/outer/pallas_call | solution.py:361
Async XLA Ops:
  0.0 7.3 %collective-permute-start = (bf16[1,48,2304]{2,1,0:T(8,128)(2,1)}, bf16[1,48,2304]{2,1,0:T(8,128)(2,1)S(1)}, u32[]{:S(2)}, u32[]{:S(2)}) collective-permute-start(bf16[1,48,2304]{2,1,0:T(8,128)(2,1)} %param.8), channel_id=1, source_target_pairs={{0,8},{8,16},{16,24},{24,0},{1,9},{9,17},{17,25},{25,1},{2,10},{10... | collective-permute-start | bytes 663560 | tf_op jit(solution)/shard_map/ppermute | solution.py:379
  4.5 0.9 %copy-start = (s32[3,8192]{1,0:T(4,128)S(1)}, s32[3,8192]{1,0:T(4,128)}, u32[]{:S(2)}) copy-start(s32[3,8192]{1,0:T(4,128)} %sphere_ref.1) | copy-start | bytes 294916
  5.4 1.0 %copy-start.1 = (bf16[1760,128]{1,0:T(8,128)(2,1)S(1)}, bf16[1760,128]{1,0:T(8,128)(2,1)}, u32[]{:S(2)}) copy-start(bf16[1760,128]{1,0:T(8,128)(2,1)} %constant.2.clone.table_ref) | copy-start | bytes 1351684
  10.7 6.0 %collective-permute-start.1 = (bf16[2,16384]{1,0:T(2,128)(2,1)S(1)}, bf16[2,16384]{1,0:T(2,128)(2,1)S(1)}, u32[]{:S(2)}, u32[]{:S(2)}) collective-permute-start(bf16[2,16384]{1,0:T(2,128)(2,1)S(1)} %get-tuple-element.25.refs_0_), channel_id=1, source_target_pairs={{0,4},{1,5},{2,6},{3,7},{4,0},{5,1},{6,2},{7,3},{8,12},{9,13},{10,... | collective-permute-start | bytes 196616 | tf_op jit(solution)/shard_map/ppermute | solution.py:384
  17.0 5.5 %collective-permute-start.5 = (bf16[4,16384]{1,0:T(4,128)(2,1)S(1)}, bf16[4,16384]{1,0:T(4,128)(2,1)S(1)}, u32[]{:S(2)}, u32[]{:S(2)}) collective-permute-start(bf16[4,16384]{1,0:T(4,128)(2,1)S(1)} %get-tuple-element.30), channel_id=1, source_target_pairs={{0,2},{1,3},{2,0},{3,1},{4,6},{5,7},{6,4},{7,5},{8,10},{9,11},{10,... | collective-permute-start | bytes 393224 | tf_op jit(solution)/shard_map/ppermute | solution.py:384
  17.9 6.6 %collective-permute-start.2 = (bf16[4,10240]{1,0:T(4,128)(2,1)S(1)}, bf16[4,10240]{1,0:T(4,128)(2,1)S(1)}, u32[]{:S(2)}, u32[]{:S(2)}) collective-permute-start(bf16[4,10240]{1,0:T(4,128)(2,1)S(1)} %get-tuple-element.27), channel_id=1, source_target_pairs={{0,17},{1,16},{2,19},{3,18},{4,21},{5,20},{6,23},{7,22},{8,25},{9,... | collective-permute-start | bytes 245768 | tf_op jit(solution)/shard_map/ppermute | solution.py:389
  17.9 7.5 %collective-permute-start.3 = (bf16[4,10240]{1,0:T(4,128)(2,1)S(1)}, bf16[4,10240]{1,0:T(4,128)(2,1)S(1)}, u32[]{:S(2)}, u32[]{:S(2)}) collective-permute-start(bf16[4,10240]{1,0:T(4,128)(2,1)S(1)} %get-tuple-element.28), channel_id=1, source_target_pairs={{0,16},{1,17},{2,18},{3,19},{4,20},{5,21},{6,22},{7,23},{8,24},{9,... | collective-permute-start | bytes 245768 | tf_op jit(solution)/shard_map/ppermute | solution.py:389
  20.3 5.2 %collective-permute-start.4 = (bf16[4,10240]{1,0:T(4,128)(2,1)S(1)}, bf16[4,10240]{1,0:T(4,128)(2,1)S(1)}, u32[]{:S(2)}, u32[]{:S(2)}) collective-permute-start(bf16[4,10240]{1,0:T(4,128)(2,1)S(1)} %get-tuple-element.29), channel_id=1, source_target_pairs={{0,1},{1,0},{2,3},{3,2},{4,5},{5,4},{6,7},{7,6},{8,9},{9,8},{10,11... | collective-permute-start | bytes 245768 | tf_op jit(solution)/shard_map/ppermute | solution.py:389
  22.7 4.6 %collective-permute-start.6 = (bf16[4,10240]{1,0:T(4,128)(2,1)S(1)}, bf16[4,10240]{1,0:T(4,128)(2,1)S(1)}, u32[]{:S(2)}, u32[]{:S(2)}) collective-permute-start(bf16[4,10240]{1,0:T(4,128)(2,1)S(1)} %get-tuple-element.32), channel_id=1, source_target_pairs={{0,17},{1,16},{2,19},{3,18},{4,21},{5,20},{6,23},{7,22},{8,25},{9,... | collective-permute-start | bytes 245768 | tf_op jit(solution)/shard_map/ppermute | solution.py:389
  22.8 4.9 %collective-permute-start.7 = (bf16[4,10240]{1,0:T(4,128)(2,1)S(1)}, bf16[4,10240]{1,0:T(4,128)(2,1)S(1)}, u32[]{:S(2)}, u32[]{:S(2)}) collective-permute-start(bf16[4,10240]{1,0:T(4,128)(2,1)S(1)} %get-tuple-element.33), channel_id=1, source_target_pairs={{0,16},{1,17},{2,18},{3,19},{4,20},{5,21},{6,22},{7,23},{8,24},{9,... | collective-permute-start | bytes 245768 | tf_op jit(solution)/shard_map/ppermute | solution.py:389
  24.5 3.9 %collective-permute-start.8 = (bf16[4,10240]{1,0:T(4,128)(2,1)S(1)}, bf16[4,10240]{1,0:T(4,128)(2,1)S(1)}, u32[]{:S(2)}, u32[]{:S(2)}) collective-permute-start(bf16[4,10240]{1,0:T(4,128)(2,1)S(1)} %get-tuple-element.34), channel_id=1, source_target_pairs={{0,1},{1,0},{2,3},{3,2},{4,5},{5,4},{6,7},{7,6},{8,9},{9,8},{10,11... | collective-permute-start | bytes 245768 | tf_op jit(solution)/shard_map/ppermute | solution.py:389
  28.5 4.0 %collective-permute-start.9 = (bf16[32,6144]{1,0:T(8,128)(2,1)S(1)}, bf16[32,6144]{1,0:T(8,128)(2,1)S(1)}, u32[]{:S(2)}, u32[]{:S(2)}) collective-permute-start(bf16[32,6144]{1,0:T(8,128)(2,1)S(1)} %get-tuple-element.36), channel_id=1, source_target_pairs={{0,8},{8,0},{16,24},{24,16},{1,9},{9,1},{17,25},{25,17},{2,10},{10... | collective-permute-start | bytes 1179656 | tf_op jit(solution)/shard_map/ppermute | solution.py:384

commit v11 on v10

--- a/solution.py
+++ b/solution.py
@@ -143,14 +143,12 @@
 
 def pair_weights(sources, levels_ref):
     rows, cols = lax.axis_size("row"), lax.axis_size("col")
-    r, _ = own_place()
     devices = rows * cols
     pairs = STEPS * len(sources)
     line = lax.broadcasted_iota(jnp.int32, (pairs, 1), 0)
     band = jnp.zeros((pairs, 1), jnp.int32)
     slot = jnp.zeros((pairs, 1), jnp.int32)
-    for j, source in enumerate(sources):
-        place = r * cols + source
+    for j, place in enumerate(sources):
         for step in range(STEPS):
             here = line == STEPS * j + step
             band = jnp.where(here, place, band)
@@ -201,12 +199,25 @@
             coef_ref[pair : pair + 1, side * half_count + first : side * half_count + first + TILE] = value.astype(jnp.bfloat16)
 
 
-def second_kernel(grid, orbitals_ref, occ_ref, first_ref, places_ref, table_ref, coef_ref, later_ref, cube_ref):
+def fill_message(plan, target, coefficients_ref, out_ref):
+    rows, cols, row_width, col_width = plan
+    r, c = own_place()
+    turn, side = target
+    start = pl.multiple_of((r ^ turn) // 2 * (2 * row_width), LANES)
+    out_ref[:, : 2 * row_width] = coefficients_ref[:, pl.ds(start, 2 * row_width)].astype(jnp.bfloat16)
+    start = pl.multiple_of((c ^ side) * col_width, LANES)
+    out_ref[:, 2 * row_width :] = coefficients_ref[:, pl.ds(start, col_width)].astype(jnp.bfloat16)
+
+
+def second_kernel(grid, plan, targets, orbitals_ref, occ_ref, first_ref, places_ref, table_ref, coef_ref, later_ref, *refs):
+    outs, cube_ref = refs[:-1], refs[-1]
     later_ref[...] = jnp.zeros_like(later_ref)
     picks = RADIX * KX_ROWS
     cube_ref[:picks, :] = first_ref[...]
     cube_ref[picks:, :] = spectrum_of(grid, orbitals_ref[0], occ_ref[0], table_ref)
     pick(cube_ref, places_ref, coef_ref)
+    for target, out_ref in zip(targets, outs):
+        fill_message(plan, target, coef_ref, out_ref)
 
 
 def cost(flops, data):
@@ -217,7 +228,7 @@
     return [pl.BlockSpec(memory_space=pltpu.VMEM)] * count
 
 
-def transform(cond_orbitals, occ_orbitals, occ_second, sphere_index, band_shape):
+def transform(cond_orbitals, occ_orbitals, occ_second, sphere_index, band_shape, targets, plan):
     grid = cond_orbitals.shape[1]
     half_count = sphere_index.shape[1]
     table = jnp.asarray(packed_tables(grid))
@@ -240,88 +251,86 @@
         **params,
     )(orbitals, table, sphere_index)
     return pl.pallas_call(
-        functools.partial(second_kernel, grid),
+        functools.partial(second_kernel, grid, plan, targets),
         out_shape=[
             jax.ShapeDtypeStruct((STEPS, 2 * half_count), jnp.bfloat16),
             jax.ShapeDtypeStruct((1, *band_shape), jnp.int32),
+            *[message_shape(STEPS, plan)] * len(targets),
         ],
         in_specs=in_vmem(5),
-        out_specs=in_vmem(2),
+        out_specs=in_vmem(2 + len(targets)),
         scratch_shapes=[pltpu.VMEM((STEPS * picks, 2 * LANES), jnp.bfloat16)],
         name="second_pair",
         **params,
     )(orbitals, occ_second, *handed)
 
 
-def pack_kernel(plan, turns, targets, merged, levels_ref, *refs):
+def message_shape(pairs, plan):
     rows, cols, row_width, col_width = plan
-    count = len(refs) - len(targets) - 1 - merged
-    arrived, outs, mixed_ref = refs[:count], refs[count:-1], refs[-1]
-    r, c = own_place()
+    return jax.ShapeDtypeStruct((pairs, 2 * row_width + col_width), jnp.bfloat16)
+
+
+def pack_kernel(plan, targets, count, *refs):
+    arrived, outs, mixed_ref = refs[:count], refs[-1 - len(targets) : -1], refs[-1]
     first = 0
     for ref in arrived:
         mixed_ref[first : first + ref.shape[0], :] = ref[...].astype(jnp.float32)
         first += ref.shape[0]
-    if merged:
-        outs[-1][...] = mixed_ref[...].astype(jnp.bfloat16)
-    weight = pair_weights([c ^ turn for turn in turns], levels_ref)
-    columns = []
-    for side in range(2):
-        start = pl.multiple_of((c ^ side) * col_width, LANES)
-        columns.append((weight * mixed_ref[:, pl.ds(start, col_width)]).astype(jnp.bfloat16))
-    for (turn, side), out_ref in zip(targets, outs):
-        start = pl.multiple_of((r ^ turn) // 2 * (2 * row_width), LANES)
-        out_ref[:, : 2 * row_width] = mixed_ref[:, pl.ds(start, 2 * row_width)].astype(jnp.bfloat16)
-        out_ref[:, 2 * row_width :] = columns[side]
-
-
-def pack(arrived, levels, turns, targets, merged, plan):
-    rows, cols, row_width, col_width = plan
-    pairs = STEPS * len(turns)
-    entries = arrived[0].shape[1]
-    shapes = [(pairs, 2 * row_width + col_width)] * len(targets) + [(pairs, entries)] * merged
+    for target, out_ref in zip(targets, outs):
+        fill_message(plan, target, mixed_ref, out_ref)
+
+
+def pack(arrived, behind, targets, plan):
+    pairs = sum(value.shape[0] for value in arrived)
     return pl.pallas_call(
-        functools.partial(pack_kernel, plan, turns, targets, merged),
-        out_shape=[jax.ShapeDtypeStruct(shape, jnp.bfloat16) for shape in shapes],
-        in_specs=in_vmem(1 + len(arrived)),
-        out_specs=in_vmem(len(shapes)),
-        scratch_shapes=[pltpu.VMEM((pairs, entries), jnp.float32)],
+        functools.partial(pack_kernel, plan, targets, len(arrived)),
+        out_shape=[message_shape(pairs, plan)] * len(targets),
+        in_specs=in_vmem(len(arrived) + len(behind)),
+        out_specs=in_vmem(len(targets)),
+        scratch_shapes=[pltpu.VMEM((pairs, arrived[0].shape[1]), jnp.float32)],
         compiler_params=pltpu.CompilerParams(vmem_limit_bytes=VMEM_LIMIT),
         cost_estimate=cost(10**9, 10**6),
         name="pack",
-    )(levels, *arrived)
+    )(*arrived, *behind)
 
 
 def stacked(refs, lanes):
     return jnp.concatenate([ref[:, lanes].astype(jnp.float32) for ref in refs], axis=0).astype(jnp.bfloat16)
 
 
-def join_kernel(row_width, *refs):
+def join_kernel(plan, turns, levels_ref, *refs):
+    rows, cols, row_width, col_width = plan
     messages, outs = refs[:-2], refs[-2:]
-    depth = messages[0].shape[0]
-    merge = max(1, 16 // depth)
-    r, _ = own_place()
-    for j in range(0, len(messages), merge):
-        here = slice(depth * j, depth * (j + merge))
-        columns = stacked(messages[j : j + merge], slice(2 * row_width, None))
+    r, c = own_place()
+    weights = pair_weights([(r ^ row_turn) * cols + (c ^ col_turn) for part in turns for row_turn, col_turn in part], levels_ref)
+    first, group = 0, []
+    for ref in messages:
+        group.append(ref)
+        depth = sum(part.shape[0] for part in group)
+        if depth % 16 and ref is not messages[-1]:
+            continue
+        here = slice(first, first + depth)
+        columns = stacked(group, slice(2 * row_width, None)).astype(jnp.float32)
+        columns = (weights[here] * columns).astype(jnp.bfloat16)
         for side, out_ref in enumerate(outs):
             lanes = pl.ds(pl.multiple_of((r & 1 ^ side) * row_width, LANES), row_width)
-            out_ref[here, :row_width] = stacked(messages[j : j + merge], lanes)
+            out_ref[here, :row_width] = stacked(group, lanes)
             out_ref[here, row_width:] = columns
-
-
-def join(messages, plan):
+        first, group = first + depth, []
+
+
+def join(messages, turns, levels, plan):
     rows, cols, row_width, col_width = plan
-    depth = messages[0].shape[0]
+    depth = sum(message.shape[0] for message in messages)
     return pl.pallas_call(
-        functools.partial(join_kernel, row_width),
-        out_shape=[jax.ShapeDtypeStruct((depth * len(messages), row_width + col_width), jnp.bfloat16)] * 2,
-        in_specs=in_vmem(len(messages)),
+        functools.partial(join_kernel, plan, turns),
+        out_shape=[jax.ShapeDtypeStruct((depth, row_width + col_width), jnp.bfloat16)] * 2,
+        in_specs=in_vmem(1 + len(messages)),
         out_specs=in_vmem(2),
         compiler_params=pltpu.CompilerParams(vmem_limit_bytes=VMEM_LIMIT),
         cost_estimate=cost(10**9, 10**6),
         name="join",
-    )(*messages)
+    )(levels, *messages)
 
 
 def outer_kernel(row_width, block, slots, *refs):
@@ -395,26 +404,33 @@
     entries = 2 * sphere_index.shape[1]
     plan = (rows, cols, entries // rows, entries // cols)
     occ_second = shifted(occ_orbitals, "row", 1)
-    own, later = transform(cond_orbitals, occ_orbitals, occ_second, sphere_index, occ_band.shape)
-    levels = jnp.stack([cond_energy, occ_energy, (occ_band + later[0]).astype(jnp.float32)])
     targets = [(0, 0)] + [(turn, side) for side in (1, 0) for turn in range(rows - 2, -2, -2) if turn or side]
     targets.append(targets.pop(rows // 2))
 
     def sent(packed):
         return [packed[0]] + [sent_across(value, *target, rows, cols) for value, target in zip(packed[1:], targets[1:])]
 
-    held, turns, bit = [own], [0], cols // 2
+    own, later, *packed = transform(cond_orbitals, occ_orbitals, occ_second, sphere_index, occ_band.shape, targets, plan)
+    levels = jnp.stack([cond_energy, occ_energy, (occ_band + later[0]).astype(jnp.float32)])
+    others, other_turns, bit = [], [], cols // 2
     while bit > 2:
-        if len(held) > 1:
-            held = [jnp.concatenate(held, axis=0)]
-        held.append(turned(held[0], "col", bit))
-        turns += [turn + bit for turn in turns]
+        held = jnp.concatenate([own, *others], axis=0) if others else own
+        others.append(turned(held, "col", bit))
+        other_turns += [turn + bit for turn in [0, *other_turns]]
         bit //= 2
-    *packed, merged = pack(held, levels, turns, targets, 1, plan)
-    messages = sent(packed)
-    far = turned(merged, "col", bit)
-    messages += sent(pack([far], levels, [turn + bit for turn in turns], targets, 0, plan))
-    kept, passed = join(messages, plan)
+    beside = turned(own, "col", bit)
+    relayed = turned(jnp.concatenate(others, axis=0) if len(others) > 1 else others[0], "col", bit)
+    first = sent(packed)
+    middle = sent(pack([*others, beside], first[1:], targets, plan))
+    last = sent(pack([relayed], [], targets, plan))
+
+    def turns_of(target, turns):
+        return [(target[0], target[1] ^ turn) for turn in turns]
+
+    turns = [turns_of(target, [*other_turns, bit]) for target in targets]
+    turns += [turns_of(target, [0, *[turn + bit for turn in other_turns]]) for target in targets]
+    messages = middle + [message for pair in zip(first, last) for message in pair]
+    kept, passed = join(messages, turns, levels, plan)
     return outer([kept, turned(passed, "row", 1)], plan)
 
 

time: 44.5 us -> 45.7 us (1.027)
  starting transfers between devices: 13.9 us -> 18.8 us
  waiting for transfers between devices: 8.53 us -> 4.71 us
    ppermute x3 -> x4, waiting for transfers between devices: 5.64 us -> 1.36 us  [turned(): return lax.ppermute(value, axis, [(i, i ^ turn) for i in range(devices)])]
    ppermute x6 -> x9, starting transfers between devices: 5.36 us -> 8.08 us  [sent_across(): return lax.ppermute(value, ('row', 'col'), moves)]
    ppermute x3 -> x4, starting transfers between devices: 5.91 us -> 8.09 us  [turned(): return lax.ppermute(value, axis, [(i, i ^ turn) for i in range(devices)])]
    ppermute x6 -> x9, waiting for transfers between devices: 2.89 us -> 3.35 us  [sent_across(): return lax.ppermute(value, ('row', 'col'), moves)]
  transfers between devices with their start and end apart: 10 -> 14, of which waited for: 6 -> 6; matrix products, arithmetic and copies ran while one was open for 7% -> 7% of each run, Pallas kernels for 2% -> 2%
where the time goes in v11:
time: 45.7 us; the launch traced here: 45.2 us
  starting transfers between devices  18.8 us (41%)
  Pallas kernels  16.4 us (36%)
  waiting for transfers between devices  4.71 us (10%)
  local copies, waits for them, and re-layouts  3.82 us (8%)
  other arithmetic  1.34 us (3%)
    pallas_call x1, Pallas kernels, outer(): pl.pallas_call(functools.partial(outer_kernel, row_width, block, slots),...  11.4 us
    ppermute x4, starting transfers between devices, turned(): return lax.ppermute(value, axis, [(i, i ^ turn) for i in range(devices)])  8.09 us
    ppermute x9, starting transfers between devices, sent_across(): return lax.ppermute(value, ('row', 'col'), moves)  8.08 us
    pallas_call x1, Pallas kernels, transform(): pl.pallas_call(functools.partial(second_kernel, grid, plan, targets), out...  3.41 us
    ppermute x9, waiting for transfers between devices, sent_across(): return lax.ppermute(value, ('row', 'col'), moves)  3.35 us
    unnamed x5, local copies, waits for them, and re-layouts  2.86 us
    ppermute x1, starting transfers between devices, shifted(): lax.ppermute(value, axis, [(i, (i + by) % devices) for i in range(devices)])  2.63 us
    ppermute x4, waiting for transfers between devices, turned(): return lax.ppermute(value, axis, [(i, i ^ turn) for i in range(devices)])  1.36 us
  transfers between devices with their start and end apart: 14, of which 6 were waited for; matrix products, arithmetic and copies ran while one was open for 7% of the time, Pallas kernels for 2%

profile of v11, /device:TPU:1, one launch (start us, length us, event | category | flops | bytes accessed | tf_op | source)
XLA Modules:
  0.0 45.2 jit_solution(16610737818720444436)
XLA Ops:
  0.0 2.6 %collective-permute-start = (bf16[1,48,2304]{2,1,0:T(8,128)(2,1)}, bf16[1,48,2304]{2,1,0:T(8,128)(2,1)S(1)}, u32[]{:S(2)}, u32[]{:S(2)}) collective-permute-start(bf16[1,48,2304]{2,1,0:T(8,128)(2,1)} %param.8), channel_id=1, source_target_pairs={{0,8},{8,16},{16,24},{24,0},{1,9},{9,17},{17,25},{25,1},{2,10},{10... | collective-permute-start | bytes 663560 | tf_op jit(solution)/shard_map/ppermute | solution.py:388
  2.6 0.9 %constant_dynamic-update-slice_fusion.1 = bf16[2,48,2304]{2,1,0:T(8,128)(2,1)S(1)} fusion(bf16[1,48,2304]{2,1,0:T(8,128)(2,1)} %param.7), kind=kLoop, calls=%fused_computation.1 | loop fusion | bytes 442368
  3.6 1.0 %constant_dynamic-update-slice_fusion.orbitals_ref = bf16[2,48,2304]{2,1,0:T(8,128)(2,1)S(1)} fusion(bf16[2,48,2304]{2,1,0:T(8,128)(2,1)S(1)} %constant_dynamic-update-slice_fusion.1, bf16[1,48,2304]{2,1,0:T(8,128)(2,1)} %param.8), kind=kLoop, calls=%fused_computation | loop fusion | bytes 442368 | tf_op jit(solution)/shard_map/concatenate | solution.py:235
  4.5 0.0 copy-start
  4.6 0.9 %copy-done = s32[3,8192]{1,0:T(4,128)S(1)} copy-done((s32[3,8192]{1,0:T(4,128)S(1)}, s32[3,8192]{1,0:T(4,128)}, u32[]{:S(2)}) %copy-start) | copy-done | bytes 98328
  5.4 0.0 copy-start.1
  5.5 1.0 %copy-done.1 = bf16[1760,128]{1,0:T(8,128)(2,1)S(1)} copy-done((bf16[1760,128]{1,0:T(8,128)(2,1)S(1)}, bf16[1760,128]{1,0:T(8,128)(2,1)}, u32[]{:S(2)}) %copy-start.1) | copy-done | bytes 450584
  6.5 0.9 %first_pair.1 = (bf16[240,256]{1,0:T(8,128)(2,1)S(1)}, s32[2,8192]{1,0:T(2,128)S(1)}, bf16[1760,128]{1,0:T(8,128)(2,1)S(1)}) custom-call(bf16[2,48,2304]{2,1,0:T(8,128)(2,1)S(1)} %constant_dynamic-update-slice_fusion.orbitals_ref, bf16[1760,128]{1,0:T(8,128)(2,1)S(1)} %copy-done.1, s32[3,8192]{1,0:T(4,128)S(1)} %copy-done), custom_call_target="tpu_custom_call" | custom-call | flops 2000000000 | bytes 2000000 | tf_op jit(solution)/shard_map/first_pair/pallas_call | solution.py:241
  7.3 0.0 collective-permute-done.occ_ref
  7.4 3.4 %second_pair.1 = (bf16[2,16384]{1,0:T(2,128)(2,1)S(1)}, s32[1,32]{1,0:T(1,128)S(1)}, bf16[2,10240]{1,0:T(2,128)(2,1)S(1)}, bf16[2,10240]{1,0:T(2,128)(2,1)S(1)},...) custom-call(bf16[2,48,2304]{2,1,0:T(8,128)(2,1)S(1)} %constant_dynamic-update-slice_fusion.orbitals_ref, ...), custom_call_target="tpu_custom_call" | custom-call | flops 2000000000 | bytes 2000000 | tf_op jit(solution)/shard_map/second_pair/pallas_call | solution.py:253
  10.8 1.4 %collective-permute-start.2 = (bf16[2,16384]{1,0:T(2,128)(2,1)S(1)}, bf16[2,16384]{1,0:T(2,128)(2,1)S(1)}, u32[]{:S(2)}, u32[]{:S(2)}) collective-permute-start(bf16[2,16384]{1,0:T(2,128)(2,1)S(1)} %get-tuple-element.28), channel_id=1, source_target_pairs={{0,2},{1,3},{2,0},{3,1},{4,6},{5,7},{6,4},{7,5},{8,10},{9,11},{10,... | collective-permute-start | bytes 196616 | tf_op jit(solution)/shard_map/ppermute | solution.py:393
  12.1 2.3 %collective-permute-start.1 = (bf16[2,16384]{1,0:T(2,128)(2,1)S(1)}, bf16[2,16384]{1,0:T(2,128)(2,1)S(1)}, u32[]{:S(2)}, u32[]{:S(2)}) collective-permute-start(bf16[2,16384]{1,0:T(2,128)(2,1)S(1)} %get-tuple-element.28), channel_id=1, source_target_pairs={{0,4},{1,5},{2,6},{3,7},{4,0},{5,1},{6,2},{7,3},{8,12},{9,13},{10,... | collective-permute-start | bytes 196616 | tf_op jit(solution)/shard_map/ppermute | solution.py:393
  14.4 1.2 %collective-permute-start.3 = (bf16[2,10240]{1,0:T(2,128)(2,1)S(1)}, bf16[2,10240]{1,0:T(2,128)(2,1)S(1)}, u32[]{:S(2)}, u32[]{:S(2)}) collective-permute-start(bf16[2,10240]{1,0:T(2,128)(2,1)S(1)} %get-tuple-element.29), channel_id=1, source_target_pairs={{0,17},{1,16},{2,19},{3,18},{4,21},{5,20},{6,23},{7,22},{8,25},{9,... | collective-permute-start | bytes 122888 | tf_op jit(solution)/shard_map/ppermute | solution.py:398
  15.6 1.2 %collective-permute-start.4 = (bf16[2,10240]{1,0:T(2,128)(2,1)S(1)}, bf16[2,10240]{1,0:T(2,128)(2,1)S(1)}, u32[]{:S(2)}, u32[]{:S(2)}) collective-permute-start(bf16[2,10240]{1,0:T(2,128)(2,1)S(1)} %get-tuple-element.30), channel_id=1, source_target_pairs={{0,16},{1,17},{2,18},{3,19},{4,20},{5,21},{6,22},{7,23},{8,24},{9,... | collective-permute-start | bytes 122888 | tf_op jit(solution)/shard_map/ppermute | solution.py:398
  16.8 0.3 collective-permute-start.5
  17.1 0.7 %fusion.1 = f32[1,32]{1,0:T(1,128)S(1)} fusion(s32[32]{0:T(128)} %param.11, s32[1,32]{1,0:T(1,128)S(1)} %get-tuple-element.27), kind=kLoop, calls=%fused_computation.5 | loop fusion | flops 64 | bytes 384 | tf_op jit(solution)/shard_map/stack | solution.py:414
  17.8 0.0 collective-permute-done.1.refs_0_
  17.8 0.8 %collective-permute-start.9 = (bf16[2,16384]{1,0:T(2,128)(2,1)S(1)}, bf16[2,16384]{1,0:T(2,128)(2,1)S(1)}, u32[]{:S(2)}, u32[]{:S(2)}) collective-permute-start(bf16[2,16384]{1,0:T(2,128)(2,1)S(1)} %collective-permute-done.1.refs_0_), channel_id=1, source_target_pairs={{0,2},{1,3},{2,0},{3,1},{4,6},{5,7},{6,4},{7,5},{8,10},{9,11},{10,... | collective-permute-start | bytes 196616 | tf_op jit(solution)/shard_map/ppermute | solution.py:393
  18.5 0.0 collective-permute-done.3.refs_2_.refs_6_
  18.5 0.7 %collective-permute-done.4.refs_3_.refs_8_ = bf16[2,10240]{1,0:T(2,128)(2,1)S(1)} collective-permute-done((bf16[2,10240]{1,0:T(2,128)(2,1)S(1)}, bf16[2,10240]{1,0:T(2,128)(2,1)S(1)}, u32[]{:S(2)}, u32[]{:S(2)}) %collective-permute-start.4) | collective-permute-done | bytes 40992 | tf_op jit(solution)/shard_map/ppermute | solution.py:398
  19.2 0.5 %collective-permute-done.5.refs_4_.refs_10_ = bf16[2,10240]{1,0:T(2,128)(2,1)S(1)} collective-permute-done((bf16[2,10240]{1,0:T(2,128)(2,1)S(1)}, bf16[2,10240]{1,0:T(2,128)(2,1)S(1)}, u32[]{:S(2)}, u32[]{:S(2)}) %collective-permute-start.5) | collective-permute-done | bytes 40992 | tf_op jit(solution)/shard_map/ppermute | solution.py:398
  19.7 0.0 collective-permute-done.2.refs_1_
  19.7 0.1 pack.2
  19.8 0.5 %collective-permute-start.6 = (bf16[4,10240]{1,0:T(4,128)(2,1)S(1)}, bf16[4,10240]{1,0:T(4,128)(2,1)S(1)}, u32[]{:S(2)}, u32[]{:S(2)}) collective-permute-start(bf16[4,10240]{1,0:T(4,128)(2,1)S(1)} %get-tuple-element.33), channel_id=1, source_target_pairs={{0,17},{1,16},{2,19},{3,18},{4,21},{5,20},{6,23},{7,22},{8,25},{9,... | collective-permute-start | bytes 245768 | tf_op jit(solution)/shard_map/ppermute | solution.py:398
  20.3 1.5 %collective-permute-start.7 = (bf16[4,10240]{1,0:T(4,128)(2,1)S(1)}, bf16[4,10240]{1,0:T(4,128)(2,1)S(1)}, u32[]{:S(2)}, u32[]{:S(2)}) collective-permute-start(bf16[4,10240]{1,0:T(4,128)(2,1)S(1)} %get-tuple-element.34), channel_id=1, source_target_pairs={{0,16},{1,17},{2,18},{3,19},{4,20},{5,21},{6,22},{7,23},{8,24},{9,... | collective-permute-start | bytes 245768 | tf_op jit(solution)/shard_map/ppermute | solution.py:398
  21.8 0.7 %collective-permute-start.8 = (bf16[4,10240]{1,0:T(4,128)(2,1)S(1)}, bf16[4,10240]{1,0:T(4,128)(2,1)S(1)}, u32[]{:S(2)}, u32[]{:S(2)}) collective-permute-start(bf16[4,10240]{1,0:T(4,128)(2,1)S(1)} %get-tuple-element.35), channel_id=1, source_target_pairs={{0,1},{1,0},{2,3},{3,2},{4,5},{5,4},{6,7},{7,6},{8,9},{9,8},{10,11... | collective-permute-start | bytes 245768 | tf_op jit(solution)/shard_map/ppermute | solution.py:398
  22.5 0.0 collective-permute-done.9.refs_0_
  22.5 0.1 pack.3
  22.7 0.5 %collective-permute-start.10 = (bf16[2,10240]{1,0:T(2,128)(2,1)S(1)}, bf16[2,10240]{1,0:T(2,128)(2,1)S(1)}, u32[]{:S(2)}, u32[]{:S(2)}) collective-permute-start(bf16[2,10240]{1,0:T(2,128)(2,1)S(1)} %get-tuple-element.38), channel_id=1, source_target_pairs={{0,17},{1,16},{2,19},{3,18},{4,21},{5,20},{6,23},{7,22},{8,25},{9,... | collective-permute-start | bytes 122888 | tf_op jit(solution)/shard_map/ppermute | solution.py:398
  23.2 1.5 %collective-permute-start.11 = (bf16[2,10240]{1,0:T(2,128)(2,1)S(1)}, bf16[2,10240]{1,0:T(2,128)(2,1)S(1)}, u32[]{:S(2)}, u32[]{:S(2)}) collective-permute-start(bf16[2,10240]{1,0:T(2,128)(2,1)S(1)} %get-tuple-element.39), channel_id=1, source_target_pairs={{0,16},{1,17},{2,18},{3,19},{4,20},{5,21},{6,22},{7,23},{8,24},{9,... | collective-permute-start | bytes 122888 | tf_op jit(solution)/shard_map/ppermute | solution.py:398
  24.6 0.0 collective-permute-done.6.refs_1_
  24.6 0.7 %collective-permute-start.12 = (bf16[2,10240]{1,0:T(2,128)(2,1)S(1)}, bf16[2,10240]{1,0:T(2,128)(2,1)S(1)}, u32[]{:S(2)}, u32[]{:S(2)}) collective-permute-start(bf16[2,10240]{1,0:T(2,128)(2,1)S(1)} %get-tuple-element.40), channel_id=1, source_target_pairs={{0,1},{1,0},{2,3},{3,2},{4,5},{5,4},{6,7},{7,6},{8,9},{9,8},{10,11... | collective-permute-start | bytes 122888 | tf_op jit(solution)/shard_map/ppermute | solution.py:398
  25.4 0.7 %pad_maximum_fusion.levels_ref = f32[3,32]{1,0:T(4,128)S(1)} fusion(f32[1,32]{1,0:T(1,128)S(1)} %fusion.1, f32[1,32]{1,0:T(1,128)} %bitcast.10, f32[1,32]{1,0:T(1,128)} %bitcast.11), kind=kLoop, calls=%fused_computation.2 | loop fusion | flops 192 | bytes 768 | tf_op jit(solution)/shard_map/stack | solution.py:414
  26.1 0.0 collective-permute-done.7.refs_2_
  26.1 0.0 collective-permute-done.8.refs_3_
  26.1 1.1 %collective-permute-done.10.refs_7_ = bf16[2,10240]{1,0:T(2,128)(2,1)S(1)} collective-permute-done((bf16[2,10240]{1,0:T(2,128)(2,1)S(1)}, bf16[2,10240]{1,0:T(2,128)(2,1)S(1)}, u32[]{:S(2)}, u32[]{:S(2)}) %collective-permute-start.10) | collective-permute-done | bytes 40992 | tf_op jit(solution)/shard_map/ppermute | solution.py:398
  27.2 0.7 %collective-permute-done.11.refs_9_ = bf16[2,10240]{1,0:T(2,128)(2,1)S(1)} collective-permute-done((bf16[2,10240]{1,0:T(2,128)(2,1)S(1)}, bf16[2,10240]{1,0:T(2,128)(2,1)S(1)}, u32[]{:S(2)}, u32[]{:S(2)}) %collective-permute-start.11) | collective-permute-done | bytes 40992 | tf_op jit(solution)/shard_map/ppermute | solution.py:398
  27.9 0.4 collective-permute-done.12.refs_11_
  28.3 0.5 %join.1 = (bf16[32,6144]{1,0:T(8,128)(2,1)S(1)}, bf16[32,6144]{1,0:T(8,128)(2,1)S(1)}) custom-call(f32[3,32]{1,0:T(4,128)S(1)} %pad_maximum_fusion.levels_ref, bf16[4,10240]{1,0:T(4,128)(2,1)S(1)} %get-tuple-element.32.refs_0_, bf16[4,10240]{1,0:T(4,128)(2,1)S(1)} %collective-permute-done.6.refs_1_, bf16[4,10240]{1,0:T(4,128)(2,1)S(1)} %collective-permute-done.7.refs_2_, ...), custom_call_target="tpu_custom_call" | custom-call | flops 1000000000 | bytes 1000000 | tf_op jit(solution)/shard_map/join/pallas_call | solution.py:325
  28.8 3.6 %collective-permute-start.13 = (bf16[32,6144]{1,0:T(8,128)(2,1)S(1)}, bf16[32,6144]{1,0:T(8,128)(2,1)S(1)}, u32[]{:S(2)}, u32[]{:S(2)}) collective-permute-start(bf16[32,6144]{1,0:T(8,128)(2,1)S(1)} %get-tuple-element.42), channel_id=1, source_target_pairs={{0,8},{8,0},{16,24},{24,16},{1,9},{9,1},{17,25},{25,17},{2,10},{10... | collective-permute-start | bytes 1179656 | tf_op jit(solution)/shard_map/ppermute | solution.py:393
  32.4 1.3 %collective-permute-done.13.refs_1_ = bf16[32,6144]{1,0:T(8,128)(2,1)S(1)} collective-permute-done((bf16[32,6144]{1,0:T(8,128)(2,1)S(1)}, bf16[32,6144]{1,0:T(8,128)(2,1)S(1)}, u32[]{:S(2)}, u32[]{:S(2)}) %collective-permute-start.13) | collective-permute-done | bytes 393248 | tf_op jit(solution)/shard_map/ppermute | solution.py:393
  33.8 11.4 %outer.1 = f32[4096,2048]{1,0:T(8,128)} custom-call(bf16[32,6144]{1,0:T(8,128)(2,1)S(1)} %get-tuple-element.41.refs_0_, bf16[32,6144]{1,0:T(8,128)(2,1)S(1)} %collective-permute-done.13.refs_1_), custom_call_target="tpu_custom_call" | custom-call | flops 10000000000 | bytes 30000000 | tf_op jit(solution)/shard_map/outer/pallas_call | solution.py:370
Async XLA Ops:
  0.0 7.3 %collective-permute-start = (bf16[1,48,2304]{2,1,0:T(8,128)(2,1)}, bf16[1,48,2304]{2,1,0:T(8,128)(2,1)S(1)}, u32[]{:S(2)}, u32[]{:S(2)}) collective-permute-start(bf16[1,48,2304]{2,1,0:T(8,128)(2,1)} %param.8), channel_id=1, source_target_pairs={{0,8},{8,16},{16,24},{24,0},{1,9},{9,17},{17,25},{25,1},{2,10},{10... | collective-permute-start | bytes 663560 | tf_op jit(solution)/shard_map/ppermute | solution.py:388
  4.5 0.9 %copy-start = (s32[3,8192]{1,0:T(4,128)S(1)}, s32[3,8192]{1,0:T(4,128)}, u32[]{:S(2)}) copy-start(s32[3,8192]{1,0:T(4,128)} %sphere_ref.1) | copy-start | bytes 294916
  5.4 1.0 %copy-start.1 = (bf16[1760,128]{1,0:T(8,128)(2,1)S(1)}, bf16[1760,128]{1,0:T(8,128)(2,1)}, u32[]{:S(2)}) copy-start(bf16[1760,128]{1,0:T(8,128)(2,1)} %constant.2.clone.table_ref) | copy-start | bytes 1351684
  10.8 8.9 %collective-permute-start.2 = (bf16[2,16384]{1,0:T(2,128)(2,1)S(1)}, bf16[2,16384]{1,0:T(2,128)(2,1)S(1)}, u32[]{:S(2)}, u32[]{:S(2)}) collective-permute-start(bf16[2,16384]{1,0:T(2,128)(2,1)S(1)} %get-tuple-element.28), channel_id=1, source_target_pairs={{0,2},{1,3},{2,0},{3,1},{4,6},{5,7},{6,4},{7,5},{8,10},{9,11},{10,... | collective-permute-start | bytes 196616 | tf_op jit(solution)/shard_map/ppermute | solution.py:393
  12.1 5.6 %collective-permute-start.1 = (bf16[2,16384]{1,0:T(2,128)(2,1)S(1)}, bf16[2,16384]{1,0:T(2,128)(2,1)S(1)}, u32[]{:S(2)}, u32[]{:S(2)}) collective-permute-start(bf16[2,16384]{1,0:T(2,128)(2,1)S(1)} %get-tuple-element.28), channel_id=1, source_target_pairs={{0,4},{1,5},{2,6},{3,7},{4,0},{5,1},{6,2},{7,3},{8,12},{9,13},{10,... | collective-permute-start | bytes 196616 | tf_op jit(solution)/shard_map/ppermute | solution.py:393
  14.4 4.1 %collective-permute-start.3 = (bf16[2,10240]{1,0:T(2,128)(2,1)S(1)}, bf16[2,10240]{1,0:T(2,128)(2,1)S(1)}, u32[]{:S(2)}, u32[]{:S(2)}) collective-permute-start(bf16[2,10240]{1,0:T(2,128)(2,1)S(1)} %get-tuple-element.29), channel_id=1, source_target_pairs={{0,17},{1,16},{2,19},{3,18},{4,21},{5,20},{6,23},{7,22},{8,25},{9,... | collective-permute-start | bytes 122888 | tf_op jit(solution)/shard_map/ppermute | solution.py:398
  15.6 3.6 %collective-permute-start.4 = (bf16[2,10240]{1,0:T(2,128)(2,1)S(1)}, bf16[2,10240]{1,0:T(2,128)(2,1)S(1)}, u32[]{:S(2)}, u32[]{:S(2)}) collective-permute-start(bf16[2,10240]{1,0:T(2,128)(2,1)S(1)} %get-tuple-element.30), channel_id=1, source_target_pairs={{0,16},{1,17},{2,18},{3,19},{4,20},{5,21},{6,22},{7,23},{8,24},{9,... | collective-permute-start | bytes 122888 | tf_op jit(solution)/shard_map/ppermute | solution.py:398
  16.8 2.9 %collective-permute-start.5 = (bf16[2,10240]{1,0:T(2,128)(2,1)S(1)}, bf16[2,10240]{1,0:T(2,128)(2,1)S(1)}, u32[]{:S(2)}, u32[]{:S(2)}) collective-permute-start(bf16[2,10240]{1,0:T(2,128)(2,1)S(1)} %get-tuple-element.31), channel_id=1, source_target_pairs={{0,1},{1,0},{2,3},{3,2},{4,5},{5,4},{6,7},{7,6},{8,9},{9,8},{10,11... | collective-permute-start | bytes 122888 | tf_op jit(solution)/shard_map/ppermute | solution.py:398
  17.8 4.8 %collective-permute-start.9 = (bf16[2,16384]{1,0:T(2,128)(2,1)S(1)}, bf16[2,16384]{1,0:T(2,128)(2,1)S(1)}, u32[]{:S(2)}, u32[]{:S(2)}) collective-permute-start(bf16[2,16384]{1,0:T(2,128)(2,1)S(1)} %collective-permute-done.1.refs_0_), channel_id=1, source_target_pairs={{0,2},{1,3},{2,0},{3,1},{4,6},{5,7},{6,4},{7,5},{8,10},{9,11},{10,... | collective-permute-start | bytes 196616 | tf_op jit(solution)/shard_map/ppermute | solution.py:393
  19.8 4.8 %collective-permute-start.6 = (bf16[4,10240]{1,0:T(4,128)(2,1)S(1)}, bf16[4,10240]{1,0:T(4,128)(2,1)S(1)}, u32[]{:S(2)}, u32[]{:S(2)}) collective-permute-start(bf16[4,10240]{1,0:T(4,128)(2,1)S(1)} %get-tuple-element.33), channel_id=1, source_target_pairs={{0,17},{1,16},{2,19},{3,18},{4,21},{5,20},{6,23},{7,22},{8,25},{9,... | collective-permute-start | bytes 245768 | tf_op jit(solution)/shard_map/ppermute | solution.py:398
  20.3 5.8 %collective-permute-start.7 = (bf16[4,10240]{1,0:T(4,128)(2,1)S(1)}, bf16[4,10240]{1,0:T(4,128)(2,1)S(1)}, u32[]{:S(2)}, u32[]{:S(2)}) collective-permute-start(bf16[4,10240]{1,0:T(4,128)(2,1)S(1)} %get-tuple-element.34), channel_id=1, source_target_pairs={{0,16},{1,17},{2,18},{3,19},{4,20},{5,21},{6,22},{7,23},{8,24},{9,... | collective-permute-start | bytes 245768 | tf_op jit(solution)/shard_map/ppermute | solution.py:398
  21.8 4.3 %collective-permute-start.8 = (bf16[4,10240]{1,0:T(4,128)(2,1)S(1)}, bf16[4,10240]{1,0:T(4,128)(2,1)S(1)}, u32[]{:S(2)}, u32[]{:S(2)}) collective-permute-start(bf16[4,10240]{1,0:T(4,128)(2,1)S(1)} %get-tuple-element.35), channel_id=1, source_target_pairs={{0,1},{1,0},{2,3},{3,2},{4,5},{5,4},{6,7},{7,6},{8,9},{9,8},{10,11... | collective-permute-start | bytes 245768 | tf_op jit(solution)/shard_map/ppermute | solution.py:398
  22.7 4.5 %collective-permute-start.10 = (bf16[2,10240]{1,0:T(2,128)(2,1)S(1)}, bf16[2,10240]{1,0:T(2,128)(2,1)S(1)}, u32[]{:S(2)}, u32[]{:S(2)}) collective-permute-start(bf16[2,10240]{1,0:T(2,128)(2,1)S(1)} %get-tuple-element.38), channel_id=1, source_target_pairs={{0,17},{1,16},{2,19},{3,18},{4,21},{5,20},{6,23},{7,22},{8,25},{9,... | collective-permute-start | bytes 122888 | tf_op jit(solution)/shard_map/ppermute | solution.py:398
  23.2 4.7 %collective-permute-start.11 = (bf16[2,10240]{1,0:T(2,128)(2,1)S(1)}, bf16[2,10240]{1,0:T(2,128)(2,1)S(1)}, u32[]{:S(2)}, u32[]{:S(2)}) collective-permute-start(bf16[2,10240]{1,0:T(2,128)(2,1)S(1)} %get-tuple-element.39), channel_id=1, source_target_pairs={{0,16},{1,17},{2,18},{3,19},{4,20},{5,21},{6,22},{7,23},{8,24},{9,... | collective-permute-start | bytes 122888 | tf_op jit(solution)/shard_map/ppermute | solution.py:398
  24.6 3.6 %collective-permute-start.12 = (bf16[2,10240]{1,0:T(2,128)(2,1)S(1)}, bf16[2,10240]{1,0:T(2,128)(2,1)S(1)}, u32[]{:S(2)}, u32[]{:S(2)}) collective-permute-start(bf16[2,10240]{1,0:T(2,128)(2,1)S(1)} %get-tuple-element.40), channel_id=1, source_target_pairs={{0,1},{1,0},{2,3},{3,2},{4,5},{5,4},{6,7},{7,6},{8,9},{9,8},{10,11... | collective-permute-start | bytes 122888 | tf_op jit(solution)/shard_map/ppermute | solution.py:398
  28.8 5.0 %collective-permute-start.13 = (bf16[32,6144]{1,0:T(8,128)(2,1)S(1)}, bf16[32,6144]{1,0:T(8,128)(2,1)S(1)}, u32[]{:S(2)}, u32[]{:S(2)}) collective-permute-start(bf16[32,6144]{1,0:T(8,128)(2,1)S(1)} %get-tuple-element.42), channel_id=1, source_target_pairs={{0,8},{8,0},{16,24},{24,16},{1,9},{9,1},{17,25},{25,17},{2,10},{10... | collective-permute-start | bytes 1179656 | tf_op jit(solution)/shard_map/ppermute | solution.py:393

commit v12 on v10

--- a/solution.py
+++ b/solution.py
@@ -3,7 +3,6 @@
 
 import jax
 import jax.numpy as jnp
-import ml_dtypes
 import numpy as np
 from jax import lax
 from jax.experimental import pallas as pl
@@ -21,51 +20,65 @@
 VMEM_LIMIT = 40 * 2**20
 
 
-def split(values, count):
-    parts = []
-    for _ in range(count):
-        parts.append(values.astype(ml_dtypes.bfloat16))
-        values = values - parts[-1].astype(np.float64)
-    return parts
+COSINE_TERMS = 10
 
 
 def table_rows(grid):
     width = (grid // RADIX) * grid
     x_first = 4 * width
-    twiddle_first = x_first + 2 * KX_ROWS
-    return width, x_first, twiddle_first
-
-
-def packed_tables(grid):
-    turn = 2.0 * np.pi / grid
-    width, _, _ = table_rows(grid)
-    y_lo = np.arange(width) // grid
-    z = np.arange(width) % grid
-
-    column = np.arange((2 * GMAX // RADIX + 1) * GMAX)
-    q = column // GMAX - GMAX // RADIX
-    kz = column % GMAX + 1
-    phase = (RADIX * q[None, :] * y_lo[:, None] + kz[None, :] * z[:, None]) % grid
-    last = np.zeros((2 * width, LANES))
-    last[:width, : column.size] = np.cos(turn * phase)
-    last[width:, : column.size] = -np.sin(turn * phase)
-    pieces = split(last, 2)
-
-    kx = np.arange(SPAN) - GMAX
-    angle = turn * (kx[:, None] * np.arange(grid)[None, :] % grid)
-    x_table = np.zeros((2 * KX_ROWS, grid))
-    x_table[:SPAN] = np.cos(angle)
-    x_table[KX_ROWS : KX_ROWS + SPAN] = -np.sin(angle)
-    x_table = np.concatenate(split(x_table, 2), axis=1)
-    pieces.append(np.pad(x_table, ((0, 0), (0, LANES - 2 * grid))))
-
-    angle = turn * (np.arange(RADIX)[:, None] * y_lo[None, :] % grid)
-    twiddle = np.zeros((16, width))
-    twiddle[:RADIX] = np.cos(angle)
-    twiddle[RADIX : 2 * RADIX] = -np.sin(angle)
-    for part in split(twiddle, 3):
-        pieces += [part[:, first : first + LANES] for first in range(0, width, LANES)]
-    return np.concatenate(pieces, axis=0)
+    return width, x_first, x_first + 2 * KX_ROWS
+
+
+def cosine(phase, grid):
+    phase = phase - (phase * 43691 >> 21) * 48
+    angle = (phase - grid // 2).astype(jnp.float32) * np.float32(2.0 * math.pi / grid)
+    square = angle * angle
+    value = jnp.zeros_like(angle)
+    for term in reversed(range(COSINE_TERMS)):
+        value = value * square - np.float32((-1.0) ** term / math.factorial(2 * term))
+    return value
+
+
+def in_two(values):
+    upper = values.astype(jnp.bfloat16)
+    return upper, (values - upper.astype(jnp.float32)).astype(jnp.bfloat16)
+
+
+def write_tables(grid, table_ref, twiddle_ref):
+    width, x_first, x_end = table_rows(grid)
+    quarter = grid // 4
+
+    def counted(shape, dimension):
+        return lax.broadcasted_iota(jnp.int32, shape, dimension)
+
+    row, lane = counted((2 * KX_ROWS, LANES), 0), counted((2 * KX_ROWS, LANES), 1)
+    below = (row >= KX_ROWS).astype(jnp.int32)
+    place = jnp.where(lane >= grid, lane - grid, lane)
+    place = jnp.where(place >= grid, 0, place)
+    frequency = row - KX_ROWS * below + (grid - GMAX)
+    upper, lower = in_two(cosine(frequency * place + quarter * below, grid))
+    mixed = jnp.where(lane < grid, upper.astype(jnp.float32), lower.astype(jnp.float32))
+    table_ref[x_first:x_end, :] = mixed.astype(jnp.bfloat16)
+
+    row, lane = counted((16, width), 0), counted((16, width), 1)
+    below = (row >= RADIX).astype(jnp.int32)
+    residue = jnp.where(row >= 2 * RADIX, 0, row - RADIX * below)
+    twiddle_ref[...] = cosine(residue * (lane * 43691 >> 21) + quarter * below, grid)
+
+    lane = counted((1, LANES), 1)
+    q = lane * 57 >> 10
+    kz = lane - q * GMAX + 1
+    y_phase = RADIX * (q + (grid // RADIX - GMAX // RADIX)) * counted((grid // RADIX, LANES), 0)
+    z_phase = kz * counted((grid, LANES), 0)
+    cos_y, sin_y = cosine(y_phase, grid), cosine(y_phase + 3 * quarter, grid)
+    cos_z, sin_z = cosine(z_phase, grid), cosine(z_phase + 3 * quarter, grid)
+    for y in range(grid // RADIX):
+        cos_here, sin_here = cos_y[y : y + 1], sin_y[y : y + 1]
+        whole = (cos_here * cos_z - sin_here * sin_z, -(sin_here * cos_z + cos_here * sin_z))
+        for part, values in enumerate(whole):
+            for level, piece in enumerate(in_two(values)):
+                first = (2 * level + part) * width + y * grid
+                table_ref[first : first + grid, :] = piece
 
 
 def dft_six(re, im):
@@ -99,25 +112,19 @@
     return lax.axis_index("row"), lax.axis_index("col")
 
 
-def spectrum_of(grid, cond, occ, table_ref):
+def spectrum_of(grid, cond, occ, table_ref, twiddle_ref):
     norm = np.float32(grid ** (-1.5))
-    width, x_first, twiddle_first = table_rows(grid)
+    width, x_first, x_end = table_rows(grid)
     density = (cond.astype(jnp.float32) * occ.astype(jnp.float32)).astype(jnp.bfloat16)
-    x_table = table_ref[x_first:twiddle_first, : 2 * grid]
+    x_table = table_ref[x_first:x_end, : 2 * grid]
     section = dot(x_table, jnp.concatenate([density, density], axis=0))
     re = [section[:KX_ROWS, h * width : (h + 1) * width] for h in range(RADIX)]
     im = [section[KX_ROWS:, h * width : (h + 1) * width] for h in range(RADIX)]
-    chunks = width // LANES
-    twiddle = 0.0
-    for part in range(3):
-        first = twiddle_first + 16 * chunks * part
-        whole = [table_ref[first + 16 * i : first + 16 * (i + 1), :].astype(jnp.float32) for i in range(chunks)]
-        twiddle = twiddle + jnp.concatenate(whole, axis=1)
     rows = []
     for residue, (d_re, d_im) in enumerate(dft_six(re, im)):
         if residue > 0:
-            t_re = twiddle[residue : residue + 1, :]
-            t_im = twiddle[RADIX + residue : RADIX + residue + 1, :]
+            t_re = twiddle_ref[residue : residue + 1, :]
+            t_im = twiddle_ref[RADIX + residue : RADIX + residue + 1, :]
             d_re, d_im = d_re * t_re - d_im * t_im, d_re * t_im + d_im * t_re
         rows.append(jnp.concatenate([d_re, d_im], axis=1))
     whole = jnp.concatenate(rows, axis=0)
@@ -164,7 +171,7 @@
     return -4.0 * gap / (gap * gap + OMEGA_SQUARED) / (devices * STEPS)
 
 
-def first_kernel(grid, orbitals_ref, table_ref, sphere_ref, cube_ref, places_ref, table_out):
+def first_kernel(grid, orbitals_ref, sphere_ref, cube_ref, places_ref, table_ref, twiddle_ref):
     half = grid // 2
     sx, sy, kz = sphere_ref[0:1, :], sphere_ref[1:2, :], sphere_ref[2:3, :]
     kx = jnp.where(sx >= half, sx - grid, sx) + GMAX
@@ -173,8 +180,8 @@
     residue = ky - q * RADIX
     places_ref[0:1, :] = (residue & 1) * LANES + q * GMAX + kz - 1
     places_ref[1:2, :] = (residue >> 1) * KX_ROWS + kx
-    table_out[...] = table_ref[...]
-    cube_ref[...] = spectrum_of(grid, orbitals_ref[0], orbitals_ref[1], table_ref)
+    write_tables(grid, table_ref, twiddle_ref)
+    cube_ref[...] = spectrum_of(grid, orbitals_ref[0], orbitals_ref[1], table_ref, twiddle_ref)
 
 
 def pick(cube_ref, places_ref, coef_ref):
@@ -201,11 +208,11 @@
             coef_ref[pair : pair + 1, side * half_count + first : side * half_count + first + TILE] = value.astype(jnp.bfloat16)
 
 
-def second_kernel(grid, orbitals_ref, occ_ref, first_ref, places_ref, table_ref, coef_ref, later_ref, cube_ref):
+def second_kernel(grid, orbitals_ref, occ_ref, first_ref, places_ref, table_ref, twiddle_ref, coef_ref, later_ref, cube_ref):
     later_ref[...] = jnp.zeros_like(later_ref)
     picks = RADIX * KX_ROWS
     cube_ref[:picks, :] = first_ref[...]
-    cube_ref[picks:, :] = spectrum_of(grid, orbitals_ref[0], occ_ref[0], table_ref)
+    cube_ref[picks:, :] = spectrum_of(grid, orbitals_ref[0], occ_ref[0], table_ref, twiddle_ref)
     pick(cube_ref, places_ref, coef_ref)
 
 
@@ -220,7 +227,7 @@
 def transform(cond_orbitals, occ_orbitals, occ_second, sphere_index, band_shape):
     grid = cond_orbitals.shape[1]
     half_count = sphere_index.shape[1]
-    table = jnp.asarray(packed_tables(grid))
+    width, _, table_count = table_rows(grid)
     orbitals = jnp.concatenate([cond_orbitals, occ_orbitals], axis=0)
     picks = RADIX * KX_ROWS
     params = dict(
@@ -232,20 +239,21 @@
         out_shape=[
             jax.ShapeDtypeStruct((picks, 2 * LANES), jnp.bfloat16),
             jax.ShapeDtypeStruct((2, half_count), jnp.int32),
-            jax.ShapeDtypeStruct(table.shape, table.dtype),
+            jax.ShapeDtypeStruct((table_count, LANES), jnp.bfloat16),
+            jax.ShapeDtypeStruct((16, width), jnp.float32),
         ],
-        in_specs=in_vmem(3),
-        out_specs=in_vmem(3),
+        in_specs=in_vmem(2),
+        out_specs=in_vmem(4),
         name="first_pair",
         **params,
-    )(orbitals, table, sphere_index)
+    )(orbitals, sphere_index)
     return pl.pallas_call(
         functools.partial(second_kernel, grid),
         out_shape=[
             jax.ShapeDtypeStruct((STEPS, 2 * half_count), jnp.bfloat16),
             jax.ShapeDtypeStruct((1, *band_shape), jnp.int32),
         ],
-        in_specs=in_vmem(5),
+        in_specs=in_vmem(6),
         out_specs=in_vmem(2),
         scratch_shapes=[pltpu.VMEM((STEPS * picks, 2 * LANES), jnp.bfloat16)],
         name="second_pair",

time: 44.5 us -> 43.5 us (0.978)
  waiting for transfers between devices: 8.53 us -> 6.3 us
  starting transfers between devices: 13.9 us -> 16.1 us
  local copies, waits for them, and re-layouts: 3.82 us -> 2.8 us
    ppermute x3, waiting for transfers between devices: 5.64 us -> 2.1 us  [turned(): return lax.ppermute(value, axis, [(i, i ^ turn) for i in range(devices)])]
    ppermute x3, starting transfers between devices: 5.91 us -> 8.08 us  [turned(): return lax.ppermute(value, axis, [(i, i ^ turn) for i in range(devices)])]
    ppermute x6, waiting for transfers between devices: 2.89 us -> 4.19 us  [sent_across(): return lax.ppermute(value, ('row', 'col'), moves)]
    unnamed x5 -> x3, local copies, waits for them, and re-layouts: 2.86 us -> 1.85 us
  transfers between devices with their start and end apart: 10 -> 10, of which waited for: 6 -> 7; matrix products, arithmetic and copies ran while one was open for 7% -> 8% of each run, Pallas kernels for 2% -> 3%
where the time goes in v12:
time: 43.5 us; the launch traced here: 43 us
  Pallas kernels  16.4 us (38%)
  starting transfers between devices  16.1 us (37%)
  waiting for transfers between devices  6.3 us (14%)
  local copies, waits for them, and re-layouts  2.8 us (6%)
  other arithmetic  1.34 us (3%)
    pallas_call x1, Pallas kernels, outer(): pl.pallas_call(functools.partial(outer_kernel, row_width, block, slots),...  11.4 us
    ppermute x3, starting transfers between devices, turned(): return lax.ppermute(value, axis, [(i, i ^ turn) for i in range(devices)])  8.08 us
    ppermute x6, starting transfers between devices, sent_across(): return lax.ppermute(value, ('row', 'col'), moves)  5.36 us
    ppermute x6, waiting for transfers between devices, sent_across(): return lax.ppermute(value, ('row', 'col'), moves)  4.19 us
    pallas_call x1, Pallas kernels, transform(): pl.pallas_call(functools.partial(second_kernel, grid), out_shape=[jax.Sha...  3.38 us
    ppermute x1, starting transfers between devices, shifted(): lax.ppermute(value, axis, [(i, (i + by) % devices) for i in range(devices)])  2.63 us
    ppermute x3, waiting for transfers between devices, turned(): return lax.ppermute(value, axis, [(i, i ^ turn) for i in range(devices)])  2.1 us
    unnamed x3, local copies, waits for them, and re-layouts  1.85 us
  transfers between devices with their start and end apart: 10, of which 7 were waited for; matrix products, arithmetic and copies ran while one was open for 8% of the time, Pallas kernels for 3%

profile of v12, /device:TPU:1, one launch (start us, length us, event | category | flops | bytes accessed | tf_op | source)
XLA Modules:
  0.0 43.0 jit_solution(14421514070524752580)
XLA Ops:
  0.0 2.6 %collective-permute-start = (bf16[1,48,2304]{2,1,0:T(8,128)(2,1)}, bf16[1,48,2304]{2,1,0:T(8,128)(2,1)S(1)}, u32[]{:S(2)}, u32[]{:S(2)}) collective-permute-start(bf16[1,48,2304]{2,1,0:T(8,128)(2,1)} %param.7), channel_id=1, source_target_pairs={{0,8},{8,16},{16,24},{24,0},{1,9},{9,17},{17,25},{25,1},{2,10},{10... | collective-permute-start | bytes 663560 | tf_op jit(solution)/shard_map/ppermute | solution.py:387
  2.6 0.9 %constant_dynamic-update-slice_fusion.1 = bf16[2,48,2304]{2,1,0:T(8,128)(2,1)S(1)} fusion(bf16[1,48,2304]{2,1,0:T(8,128)(2,1)} %param.6), kind=kLoop, calls=%fused_computation.1 | loop fusion | bytes 442368
  3.6 1.0 %constant_dynamic-update-slice_fusion.orbitals_ref = bf16[2,48,2304]{2,1,0:T(8,128)(2,1)S(1)} fusion(bf16[2,48,2304]{2,1,0:T(8,128)(2,1)S(1)} %constant_dynamic-update-slice_fusion.1, bf16[1,48,2304]{2,1,0:T(8,128)(2,1)} %param.7), kind=kLoop, calls=%fused_computation | loop fusion | bytes 442368 | tf_op jit(solution)/shard_map/concatenate | solution.py:231
  4.5 0.0 copy-start
  4.6 0.9 %copy-done = s32[3,8192]{1,0:T(4,128)S(1)} copy-done((s32[3,8192]{1,0:T(4,128)S(1)}, s32[3,8192]{1,0:T(4,128)}, u32[]{:S(2)}) %copy-start) | copy-done | bytes 98328
  5.4 1.1 %first_pair.1 = (bf16[240,256]{1,0:T(8,128)(2,1)S(1)}, s32[2,8192]{1,0:T(2,128)S(1)}, bf16[1616,128]{1,0:T(8,128)(2,1)S(1)}, f32[16,384]{1,0:T(8,128)S(1)}) custom-call(bf16[2,48,2304]{2,1,0:T(8,128)(2,1)S(1)} %constant_dynamic-update-slice_fusion.orbitals_ref, s32[3,8192]{1,0:T(4,128)S(1)} %copy-done), custom_call_target="tpu_custom_call" | custom-call | flops 2000000000 | bytes 2000000 | tf_op jit(solution)/shard_map/first_pair/pallas_call | solution.py:237
  6.5 0.0 collective-permute-done.occ_ref
  6.5 3.4 %second_pair.1 = (bf16[2,16384]{1,0:T(2,128)(2,1)S(1)}, s32[1,32]{1,0:T(1,128)S(1)}) custom-call(bf16[2,48,2304]{2,1,0:T(8,128)(2,1)S(1)} %constant_dynamic-update-slice_fusion.orbitals_ref, bf16[1,48,2304]{2,1,0:T(8,128)(2,1)S(1)} %collective-permute-done.occ_ref, bf16[240,256]{1,0:T(8,128)(2,1)S(1)} %get-tuple-element.22.first_ref, ...), custom_call_target="tpu_custom_call" | custom-call | flops 2000000000 | bytes 2000000 | tf_op jit(solution)/shard_map/second_pair/pallas_call | solution.py:250
  9.9 2.4 %collective-permute-start.1 = (bf16[2,16384]{1,0:T(2,128)(2,1)S(1)}, bf16[2,16384]{1,0:T(2,128)(2,1)S(1)}, u32[]{:S(2)}, u32[]{:S(2)}) collective-permute-start(bf16[2,16384]{1,0:T(2,128)(2,1)S(1)} %get-tuple-element.27.refs_0_), channel_id=1, source_target_pairs={{0,4},{1,5},{2,6},{3,7},{4,0},{5,1},{6,2},{7,3},{8,12},{9,13},{10,... | collective-permute-start | bytes 196616 | tf_op jit(solution)/shard_map/ppermute | solution.py:392
  12.3 0.7 %fusion.1 = f32[1,32]{1,0:T(1,128)S(1)} fusion(s32[32]{0:T(128)} %param.10, s32[1,32]{1,0:T(1,128)S(1)} %get-tuple-element.26), kind=kLoop, calls=%fused_computation.5 | loop fusion | flops 64 | bytes 384 | tf_op jit(solution)/shard_map/stack | solution.py:407
  13.0 0.7 %pad_maximum_fusion.levels_ref = f32[3,32]{1,0:T(4,128)S(1)} fusion(f32[1,32]{1,0:T(1,128)S(1)} %fusion.1, f32[1,32]{1,0:T(1,128)} %bitcast.10, f32[1,32]{1,0:T(1,128)} %bitcast.11), kind=kLoop, calls=%fused_computation.2 | loop fusion | flops 192 | bytes 768 | tf_op jit(solution)/shard_map/stack | solution.py:407
  13.6 0.7 %collective-permute-done.1.refs_1_ = bf16[2,16384]{1,0:T(2,128)(2,1)S(1)} collective-permute-done((bf16[2,16384]{1,0:T(2,128)(2,1)S(1)}, bf16[2,16384]{1,0:T(2,128)(2,1)S(1)}, u32[]{:S(2)}, u32[]{:S(2)}) %collective-permute-start.1) | collective-permute-done | bytes 65568 | tf_op jit(solution)/shard_map/ppermute | solution.py:392
  14.4 0.2 pack.2
  14.6 2.2 %collective-permute-start.5 = (bf16[4,16384]{1,0:T(4,128)(2,1)S(1)}, bf16[4,16384]{1,0:T(4,128)(2,1)S(1)}, u32[]{:S(2)}, u32[]{:S(2)}) collective-permute-start(bf16[4,16384]{1,0:T(4,128)(2,1)S(1)} %get-tuple-element.32), channel_id=1, source_target_pairs={{0,2},{1,3},{2,0},{3,1},{4,6},{5,7},{6,4},{7,5},{8,10},{9,11},{10,... | collective-permute-start | bytes 393224 | tf_op jit(solution)/shard_map/ppermute | solution.py:392
  16.8 0.0 collective-permute-start.2
  16.9 2.3 %collective-permute-start.3 = (bf16[4,10240]{1,0:T(4,128)(2,1)S(1)}, bf16[4,10240]{1,0:T(4,128)(2,1)S(1)}, u32[]{:S(2)}, u32[]{:S(2)}) collective-permute-start(bf16[4,10240]{1,0:T(4,128)(2,1)S(1)} %get-tuple-element.30), channel_id=1, source_target_pairs={{0,16},{1,17},{2,18},{3,19},{4,20},{5,21},{6,22},{7,23},{8,24},{9,... | collective-permute-start | bytes 245768 | tf_op jit(solution)/shard_map/ppermute | solution.py:397
  19.2 0.3 collective-permute-start.4
  19.5 0.0 collective-permute-done.5.refs_0_
  19.5 0.2 pack.3
  19.7 1.0 %collective-permute-start.6 = (bf16[4,10240]{1,0:T(4,128)(2,1)S(1)}, bf16[4,10240]{1,0:T(4,128)(2,1)S(1)}, u32[]{:S(2)}, u32[]{:S(2)}) collective-permute-start(bf16[4,10240]{1,0:T(4,128)(2,1)S(1)} %get-tuple-element.34), channel_id=1, source_target_pairs={{0,17},{1,16},{2,19},{3,18},{4,21},{5,20},{6,23},{7,22},{8,25},{9,... | collective-permute-start | bytes 245768 | tf_op jit(solution)/shard_map/ppermute | solution.py:397
  20.7 1.5 %collective-permute-start.7 = (bf16[4,10240]{1,0:T(4,128)(2,1)S(1)}, bf16[4,10240]{1,0:T(4,128)(2,1)S(1)}, u32[]{:S(2)}, u32[]{:S(2)}) collective-permute-start(bf16[4,10240]{1,0:T(4,128)(2,1)S(1)} %get-tuple-element.35), channel_id=1, source_target_pairs={{0,16},{1,17},{2,18},{3,19},{4,20},{5,21},{6,22},{7,23},{8,24},{9,... | collective-permute-start | bytes 245768 | tf_op jit(solution)/shard_map/ppermute | solution.py:397
  22.1 0.0 collective-permute-done.2.refs_1_
  22.1 0.3 collective-permute-start.8
  22.4 0.1 collective-permute-done.3.refs_2_
  22.5 1.0 %collective-permute-done.4.refs_3_ = bf16[4,10240]{1,0:T(4,128)(2,1)S(1)} collective-permute-done((bf16[4,10240]{1,0:T(4,128)(2,1)S(1)}, bf16[4,10240]{1,0:T(4,128)(2,1)S(1)}, u32[]{:S(2)}, u32[]{:S(2)}) %collective-permute-start.4) | collective-permute-done | bytes 81952 | tf_op jit(solution)/shard_map/ppermute | solution.py:397
  23.5 0.6 %collective-permute-done.6.refs_5_ = bf16[4,10240]{1,0:T(4,128)(2,1)S(1)} collective-permute-done((bf16[4,10240]{1,0:T(4,128)(2,1)S(1)}, bf16[4,10240]{1,0:T(4,128)(2,1)S(1)}, u32[]{:S(2)}, u32[]{:S(2)}) %collective-permute-start.6) | collective-permute-done | bytes 81952 | tf_op jit(solution)/shard_map/ppermute | solution.py:397
  24.1 1.9 %collective-permute-done.7.refs_6_ = bf16[4,10240]{1,0:T(4,128)(2,1)S(1)} collective-permute-done((bf16[4,10240]{1,0:T(4,128)(2,1)S(1)}, bf16[4,10240]{1,0:T(4,128)(2,1)S(1)}, u32[]{:S(2)}, u32[]{:S(2)}) %collective-permute-start.7) | collective-permute-done | bytes 81952 | tf_op jit(solution)/shard_map/ppermute | solution.py:397
  26.0 0.6 %collective-permute-done.8.refs_7_ = bf16[4,10240]{1,0:T(4,128)(2,1)S(1)} collective-permute-done((bf16[4,10240]{1,0:T(4,128)(2,1)S(1)}, bf16[4,10240]{1,0:T(4,128)(2,1)S(1)}, u32[]{:S(2)}, u32[]{:S(2)}) %collective-permute-start.8) | collective-permute-done | bytes 81952 | tf_op jit(solution)/shard_map/ppermute | solution.py:397
  26.6 0.2 join.1
  26.7 3.5 %collective-permute-start.9 = (bf16[32,6144]{1,0:T(8,128)(2,1)S(1)}, bf16[32,6144]{1,0:T(8,128)(2,1)S(1)}, u32[]{:S(2)}, u32[]{:S(2)}) collective-permute-start(bf16[32,6144]{1,0:T(8,128)(2,1)S(1)} %get-tuple-element.38), channel_id=1, source_target_pairs={{0,8},{8,0},{16,24},{24,16},{1,9},{9,1},{17,25},{25,17},{2,10},{10... | collective-permute-start | bytes 1179656 | tf_op jit(solution)/shard_map/ppermute | solution.py:392
  30.3 1.3 %collective-permute-done.9.refs_1_ = bf16[32,6144]{1,0:T(8,128)(2,1)S(1)} collective-permute-done((bf16[32,6144]{1,0:T(8,128)(2,1)S(1)}, bf16[32,6144]{1,0:T(8,128)(2,1)S(1)}, u32[]{:S(2)}, u32[]{:S(2)}) %collective-permute-start.9) | collective-permute-done | bytes 393248 | tf_op jit(solution)/shard_map/ppermute | solution.py:392
  31.6 11.4 %outer.1 = f32[4096,2048]{1,0:T(8,128)} custom-call(bf16[32,6144]{1,0:T(8,128)(2,1)S(1)} %get-tuple-element.37.refs_0_, bf16[32,6144]{1,0:T(8,128)(2,1)S(1)} %collective-permute-done.9.refs_1_), custom_call_target="tpu_custom_call" | custom-call | flops 10000000000 | bytes 30000000 | tf_op jit(solution)/shard_map/outer/pallas_call | solution.py:369
Async XLA Ops:
  0.0 6.5 %collective-permute-start = (bf16[1,48,2304]{2,1,0:T(8,128)(2,1)}, bf16[1,48,2304]{2,1,0:T(8,128)(2,1)S(1)}, u32[]{:S(2)}, u32[]{:S(2)}) collective-permute-start(bf16[1,48,2304]{2,1,0:T(8,128)(2,1)} %param.7), channel_id=1, source_target_pairs={{0,8},{8,16},{16,24},{24,0},{1,9},{9,17},{17,25},{25,1},{2,10},{10... | collective-permute-start | bytes 663560 | tf_op jit(solution)/shard_map/ppermute | solution.py:387
  4.5 0.9 %copy-start = (s32[3,8192]{1,0:T(4,128)S(1)}, s32[3,8192]{1,0:T(4,128)}, u32[]{:S(2)}) copy-start(s32[3,8192]{1,0:T(4,128)} %sphere_ref.1) | copy-start | bytes 294916
  9.9 4.5 %collective-permute-start.1 = (bf16[2,16384]{1,0:T(2,128)(2,1)S(1)}, bf16[2,16384]{1,0:T(2,128)(2,1)S(1)}, u32[]{:S(2)}, u32[]{:S(2)}) collective-permute-start(bf16[2,16384]{1,0:T(2,128)(2,1)S(1)} %get-tuple-element.27.refs_0_), channel_id=1, source_target_pairs={{0,4},{1,5},{2,6},{3,7},{4,0},{5,1},{6,2},{7,3},{8,12},{9,13},{10,... | collective-permute-start | bytes 196616 | tf_op jit(solution)/shard_map/ppermute | solution.py:392
  14.6 4.8 %collective-permute-start.5 = (bf16[4,16384]{1,0:T(4,128)(2,1)S(1)}, bf16[4,16384]{1,0:T(4,128)(2,1)S(1)}, u32[]{:S(2)}, u32[]{:S(2)}) collective-permute-start(bf16[4,16384]{1,0:T(4,128)(2,1)S(1)} %get-tuple-element.32), channel_id=1, source_target_pairs={{0,2},{1,3},{2,0},{3,1},{4,6},{5,7},{6,4},{7,5},{8,10},{9,11},{10,... | collective-permute-start | bytes 393224 | tf_op jit(solution)/shard_map/ppermute | solution.py:392
  16.8 5.3 %collective-permute-start.2 = (bf16[4,10240]{1,0:T(4,128)(2,1)S(1)}, bf16[4,10240]{1,0:T(4,128)(2,1)S(1)}, u32[]{:S(2)}, u32[]{:S(2)}) collective-permute-start(bf16[4,10240]{1,0:T(4,128)(2,1)S(1)} %get-tuple-element.29), channel_id=1, source_target_pairs={{0,17},{1,16},{2,19},{3,18},{4,21},{5,20},{6,23},{7,22},{8,25},{9,... | collective-permute-start | bytes 245768 | tf_op jit(solution)/shard_map/ppermute | solution.py:397
  16.9 5.6 %collective-permute-start.3 = (bf16[4,10240]{1,0:T(4,128)(2,1)S(1)}, bf16[4,10240]{1,0:T(4,128)(2,1)S(1)}, u32[]{:S(2)}, u32[]{:S(2)}) collective-permute-start(bf16[4,10240]{1,0:T(4,128)(2,1)S(1)} %get-tuple-element.30), channel_id=1, source_target_pairs={{0,16},{1,17},{2,18},{3,19},{4,20},{5,21},{6,22},{7,23},{8,24},{9,... | collective-permute-start | bytes 245768 | tf_op jit(solution)/shard_map/ppermute | solution.py:397
  19.2 4.2 %collective-permute-start.4 = (bf16[4,10240]{1,0:T(4,128)(2,1)S(1)}, bf16[4,10240]{1,0:T(4,128)(2,1)S(1)}, u32[]{:S(2)}, u32[]{:S(2)}) collective-permute-start(bf16[4,10240]{1,0:T(4,128)(2,1)S(1)} %get-tuple-element.31), channel_id=1, source_target_pairs={{0,1},{1,0},{2,3},{3,2},{4,5},{5,4},{6,7},{7,6},{8,9},{9,8},{10,11... | collective-permute-start | bytes 245768 | tf_op jit(solution)/shard_map/ppermute | solution.py:397
  19.7 4.4 %collective-permute-start.6 = (bf16[4,10240]{1,0:T(4,128)(2,1)S(1)}, bf16[4,10240]{1,0:T(4,128)(2,1)S(1)}, u32[]{:S(2)}, u32[]{:S(2)}) collective-permute-start(bf16[4,10240]{1,0:T(4,128)(2,1)S(1)} %get-tuple-element.34), channel_id=1, source_target_pairs={{0,17},{1,16},{2,19},{3,18},{4,21},{5,20},{6,23},{7,22},{8,25},{9,... | collective-permute-start | bytes 245768 | tf_op jit(solution)/shard_map/ppermute | solution.py:397
  20.7 5.3 %collective-permute-start.7 = (bf16[4,10240]{1,0:T(4,128)(2,1)S(1)}, bf16[4,10240]{1,0:T(4,128)(2,1)S(1)}, u32[]{:S(2)}, u32[]{:S(2)}) collective-permute-start(bf16[4,10240]{1,0:T(4,128)(2,1)S(1)} %get-tuple-element.35), channel_id=1, source_target_pairs={{0,16},{1,17},{2,18},{3,19},{4,20},{5,21},{6,22},{7,23},{8,24},{9,... | collective-permute-start | bytes 245768 | tf_op jit(solution)/shard_map/ppermute | solution.py:397
  22.1 4.4 %collective-permute-start.8 = (bf16[4,10240]{1,0:T(4,128)(2,1)S(1)}, bf16[4,10240]{1,0:T(4,128)(2,1)S(1)}, u32[]{:S(2)}, u32[]{:S(2)}) collective-permute-start(bf16[4,10240]{1,0:T(4,128)(2,1)S(1)} %get-tuple-element.36), channel_id=1, source_target_pairs={{0,1},{1,0},{2,3},{3,2},{4,5},{5,4},{6,7},{7,6},{8,9},{9,8},{10,11... | collective-permute-start | bytes 245768 | tf_op jit(solution)/shard_map/ppermute | solution.py:397
  26.7 4.9 %collective-permute-start.9 = (bf16[32,6144]{1,0:T(8,128)(2,1)S(1)}, bf16[32,6144]{1,0:T(8,128)(2,1)S(1)}, u32[]{:S(2)}, u32[]{:S(2)}) collective-permute-start(bf16[32,6144]{1,0:T(8,128)(2,1)S(1)} %get-tuple-element.38), channel_id=1, source_target_pairs={{0,8},{8,0},{16,24},{24,16},{1,9},{9,1},{17,25},{25,17},{2,10},{10... | collective-permute-start | bytes 1179656 | tf_op jit(solution)/shard_map/ppermute | solution.py:392

commit v13 on v12

--- a/solution.py
+++ b/solution.py
@@ -171,7 +171,7 @@
     return -4.0 * gap / (gap * gap + OMEGA_SQUARED) / (devices * STEPS)
 
 
-def first_kernel(grid, orbitals_ref, sphere_ref, cube_ref, places_ref, table_ref, twiddle_ref):
+def first_kernel(grid, orbitals_ref, sphere_ref, coef_ref, places_ref, table_ref, twiddle_ref, cube_ref):
     half = grid // 2
     sx, sy, kz = sphere_ref[0:1, :], sphere_ref[1:2, :], sphere_ref[2:3, :]
     kx = jnp.where(sx >= half, sx - grid, sx) + GMAX
@@ -182,9 +182,10 @@
     places_ref[1:2, :] = (residue >> 1) * KX_ROWS + kx
     write_tables(grid, table_ref, twiddle_ref)
     cube_ref[...] = spectrum_of(grid, orbitals_ref[0], orbitals_ref[1], table_ref, twiddle_ref)
-
-
-def pick(cube_ref, places_ref, coef_ref):
+    pick(cube_ref, places_ref, coef_ref, 0)
+
+
+def pick(cube_ref, places_ref, coef_ref, pair):
     groups = RADIX // 2 * KX_ROWS // 8
     half_count = places_ref.shape[1]
     counted = lax.broadcasted_iota(jnp.int32, (2 * LANES, TILE), 0).astype(jnp.float32).astype(jnp.bfloat16)
@@ -192,28 +193,25 @@
     for first in range(0, half_count, TILE):
         here = slice(first, first + TILE)
         lane = places_ref[0:1, here].astype(jnp.float32).astype(jnp.bfloat16)
-        row = places_ref[1:2, here]
         one_hot = jnp.where(counted == lane, jnp.bfloat16(1), jnp.bfloat16(0))
         found = dot(cube_ref[...], one_hot)
-        away = line - row
-        values = [jnp.zeros((8, TILE), jnp.float32)] * 4
+        away = line - places_ref[1:2, here]
+        values = [jnp.zeros((8, TILE), jnp.float32)] * 2
         for group in range(groups):
             chosen = away == -8 * group
-            for which in range(4):
-                start = (which * groups + group) * 8
-                values[which] = jnp.where(chosen, found[start : start + 8], values[which])
-        for which in range(4):
-            pair, side = divmod(which, 2)
-            value = jnp.sum(values[which], axis=0, keepdims=True)
-            coef_ref[pair : pair + 1, side * half_count + first : side * half_count + first + TILE] = value.astype(jnp.bfloat16)
+            for side in range(2):
+                start = (side * groups + group) * 8
+                values[side] = jnp.where(chosen, found[start : start + 8], values[side])
+        for side in range(2):
+            value = jnp.sum(values[side], axis=0, keepdims=True).astype(jnp.bfloat16)
+            coef_ref[pair : pair + 1, side * half_count + first : side * half_count + first + TILE] = value
 
 
 def second_kernel(grid, orbitals_ref, occ_ref, first_ref, places_ref, table_ref, twiddle_ref, coef_ref, later_ref, cube_ref):
     later_ref[...] = jnp.zeros_like(later_ref)
-    picks = RADIX * KX_ROWS
-    cube_ref[:picks, :] = first_ref[...]
-    cube_ref[picks:, :] = spectrum_of(grid, orbitals_ref[0], occ_ref[0], table_ref, twiddle_ref)
-    pick(cube_ref, places_ref, coef_ref)
+    coef_ref[0:1, :] = first_ref[...]
+    cube_ref[...] = spectrum_of(grid, orbitals_ref[0], occ_ref[0], table_ref, twiddle_ref)
+    pick(cube_ref, places_ref, coef_ref, 1)
 
 
 def cost(flops, data):
@@ -229,15 +227,16 @@
     half_count = sphere_index.shape[1]
     width, _, table_count = table_rows(grid)
     orbitals = jnp.concatenate([cond_orbitals, occ_orbitals], axis=0)
-    picks = RADIX * KX_ROWS
+    cube = pltpu.VMEM((RADIX * KX_ROWS, 2 * LANES), jnp.bfloat16)
     params = dict(
+        scratch_shapes=[cube],
         compiler_params=pltpu.CompilerParams(vmem_limit_bytes=VMEM_LIMIT),
         cost_estimate=cost(2 * 10**9, 2 * 10**6),
     )
     handed = pl.pallas_call(
         functools.partial(first_kernel, grid),
         out_shape=[
-            jax.ShapeDtypeStruct((picks, 2 * LANES), jnp.bfloat16),
+            jax.ShapeDtypeStruct((1, 2 * half_count), jnp.bfloat16),
             jax.ShapeDtypeStruct((2, half_count), jnp.int32),
             jax.ShapeDtypeStruct((table_count, LANES), jnp.bfloat16),
             jax.ShapeDtypeStruct((16, width), jnp.float32),
@@ -255,7 +254,6 @@
         ],
         in_specs=in_vmem(6),
         out_specs=in_vmem(2),
-        scratch_shapes=[pltpu.VMEM((STEPS * picks, 2 * LANES), jnp.bfloat16)],
         name="second_pair",
         **params,
     )(orbitals, occ_second, *handed)

time: 43.5 us -> 43 us (0.989)
  starting transfers between devices: 16.1 us -> 12.7 us
  waiting for transfers between devices: 6.3 us -> 8.55 us
  Pallas kernels: 16.4 us -> 17.1 us
    ppermute x3, starting transfers between devices: 8.08 us -> 4.73 us  [turned(): return lax.ppermute(value, axis, [(i, i ^ turn) for i in range(devices)])]
    ppermute x3, waiting for transfers between devices: 2.1 us -> 4.88 us  [turned(): return lax.ppermute(value, axis, [(i, i ^ turn) for i in range(devices)])]
    pallas_call x1, Pallas kernels: 1.08 us -> 2.62 us  [transform(): pl.pallas_call(functools.partial(first_kernel, grid), out_shape=[jax.Shap...]
    pallas_call x1, Pallas kernels: 3.38 us -> 2.45 us  [transform(): pl.pallas_call(functools.partial(second_kernel, grid), out_shape=[jax.Sha...]
    ppermute x6, waiting for transfers between devices: 4.19 us -> 3.66 us  [sent_across(): return lax.ppermute(value, ('row', 'col'), moves)]
  transfers between devices with their start and end apart: 10 -> 10, of which waited for: 7 -> 5; matrix products, arithmetic and copies ran while one was open for 8% -> 8% of each run, Pallas kernels for 3% -> 7%
where the time goes in v13:
time: 43 us; the launch traced here: 42.5 us
  Pallas kernels  17.1 us (40%)
  starting transfers between devices  12.7 us (30%)
  waiting for transfers between devices  8.55 us (20%)
  local copies, waits for them, and re-layouts  2.8 us (7%)
  other arithmetic  1.34 us (3%)
    pallas_call x1, Pallas kernels, outer(): pl.pallas_call(functools.partial(outer_kernel, row_width, block, slots),...  11.4 us
    ppermute x6, starting transfers between devices, sent_across(): return lax.ppermute(value, ('row', 'col'), moves)  5.36 us
    ppermute x3, waiting for transfers between devices, turned(): return lax.ppermute(value, axis, [(i, i ^ turn) for i in range(devices)])  4.88 us
    ppermute x3, starting transfers between devices, turned(): return lax.ppermute(value, axis, [(i, i ^ turn) for i in range(devices)])  4.73 us
    ppermute x6, waiting for transfers between devices, sent_across(): return lax.ppermute(value, ('row', 'col'), moves)  3.66 us
    ppermute x1, starting transfers between devices, shifted(): lax.ppermute(value, axis, [(i, (i + by) % devices) for i in range(devices)])  2.63 us
    pallas_call x1, Pallas kernels, transform(): pl.pallas_call(functools.partial(first_kernel, grid), out_shape=[jax.Shap...  2.62 us
    pallas_call x1, Pallas kernels, transform(): pl.pallas_call(functools.partial(second_kernel, grid), out_shape=[jax.Sha...  2.45 us
  transfers between devices with their start and end apart: 10, of which 5 were waited for; matrix products, arithmetic and copies ran while one was open for 8% of the time, Pallas kernels for 7%

profile of v13, /device:TPU:1, one launch (start us, length us, event | category | flops | bytes accessed | tf_op | source)
XLA Modules:
  0.0 42.5 jit_solution(7650956829479862768)
XLA Ops:
  0.0 2.6 %collective-permute-start = (bf16[1,48,2304]{2,1,0:T(8,128)(2,1)}, bf16[1,48,2304]{2,1,0:T(8,128)(2,1)S(1)}, u32[]{:S(2)}, u32[]{:S(2)}) collective-permute-start(bf16[1,48,2304]{2,1,0:T(8,128)(2,1)} %param.7), channel_id=1, source_target_pairs={{0,8},{8,16},{16,24},{24,0},{1,9},{9,17},{17,25},{25,1},{2,10},{10... | collective-permute-start | bytes 663560 | tf_op jit(solution)/shard_map/ppermute | solution.py:385
  2.6 0.9 %constant_dynamic-update-slice_fusion.1 = bf16[2,48,2304]{2,1,0:T(8,128)(2,1)S(1)} fusion(bf16[1,48,2304]{2,1,0:T(8,128)(2,1)} %param.6), kind=kLoop, calls=%fused_computation.1 | loop fusion | bytes 442368
  3.6 1.0 %constant_dynamic-update-slice_fusion.orbitals_ref = bf16[2,48,2304]{2,1,0:T(8,128)(2,1)S(1)} fusion(bf16[2,48,2304]{2,1,0:T(8,128)(2,1)S(1)} %constant_dynamic-update-slice_fusion.1, bf16[1,48,2304]{2,1,0:T(8,128)(2,1)} %param.7), kind=kLoop, calls=%fused_computation | loop fusion | bytes 442368 | tf_op jit(solution)/shard_map/concatenate | solution.py:229
  4.5 0.0 copy-start
  4.6 0.9 %copy-done = s32[3,8192]{1,0:T(4,128)S(1)} copy-done((s32[3,8192]{1,0:T(4,128)S(1)}, s32[3,8192]{1,0:T(4,128)}, u32[]{:S(2)}) %copy-start) | copy-done | bytes 98328
  5.4 2.6 %first_pair.1 = (bf16[1,16384]{1,0:T(2,128)(2,1)S(1)}, s32[2,8192]{1,0:T(2,128)S(1)}, bf16[1616,128]{1,0:T(8,128)(2,1)S(1)}, f32[16,384]{1,0:T(8,128)S(1)}) custom-call(bf16[2,48,2304]{2,1,0:T(8,128)(2,1)S(1)} %constant_dynamic-update-slice_fusion.orbitals_ref, s32[3,8192]{1,0:T(4,128)S(1)} %copy-done), custom_call_target="tpu_custom_call" | custom-call | flops 2000000000 | bytes 2000000 | tf_op jit(solution)/shard_map/first_pair/pallas_call | solution.py:236
  8.1 0.0 collective-permute-done.occ_ref
  8.1 2.4 %second_pair.1 = (bf16[2,16384]{1,0:T(2,128)(2,1)S(1)}, s32[1,32]{1,0:T(1,128)S(1)}) custom-call(bf16[2,48,2304]{2,1,0:T(8,128)(2,1)S(1)} %constant_dynamic-update-slice_fusion.orbitals_ref, bf16[1,48,2304]{2,1,0:T(8,128)(2,1)S(1)} %collective-permute-done.occ_ref, bf16[1,16384]{1,0:T(2,128)(2,1)S(1)} %get-tuple-element.22.first_ref, ...), custom_call_target="tpu_custom_call" | custom-call | flops 2000000000 | bytes 2000000 | tf_op jit(solution)/shard_map/second_pair/pallas_call | solution.py:249
  10.5 2.4 %collective-permute-start.1 = (bf16[2,16384]{1,0:T(2,128)(2,1)S(1)}, bf16[2,16384]{1,0:T(2,128)(2,1)S(1)}, u32[]{:S(2)}, u32[]{:S(2)}) collective-permute-start(bf16[2,16384]{1,0:T(2,128)(2,1)S(1)} %get-tuple-element.27.refs_0_), channel_id=1, source_target_pairs={{0,4},{1,5},{2,6},{3,7},{4,0},{5,1},{6,2},{7,3},{8,12},{9,13},{10,... | collective-permute-start | bytes 196616 | tf_op jit(solution)/shard_map/ppermute | solution.py:390
  12.9 0.7 %fusion.1 = f32[1,32]{1,0:T(1,128)S(1)} fusion(s32[32]{0:T(128)} %param.10, s32[1,32]{1,0:T(1,128)S(1)} %get-tuple-element.26), kind=kLoop, calls=%fused_computation.5 | loop fusion | flops 64 | bytes 384 | tf_op jit(solution)/shard_map/stack | solution.py:405
  13.6 0.7 %pad_maximum_fusion.levels_ref = f32[3,32]{1,0:T(4,128)S(1)} fusion(f32[1,32]{1,0:T(1,128)S(1)} %fusion.1, f32[1,32]{1,0:T(1,128)} %bitcast.10, f32[1,32]{1,0:T(1,128)} %bitcast.11), kind=kLoop, calls=%fused_computation.2 | loop fusion | flops 192 | bytes 768 | tf_op jit(solution)/shard_map/stack | solution.py:405
  14.3 1.8 %collective-permute-done.1.refs_1_ = bf16[2,16384]{1,0:T(2,128)(2,1)S(1)} collective-permute-done((bf16[2,16384]{1,0:T(2,128)(2,1)S(1)}, bf16[2,16384]{1,0:T(2,128)(2,1)S(1)}, u32[]{:S(2)}, u32[]{:S(2)}) %collective-permute-start.1) | collective-permute-done | bytes 65568 | tf_op jit(solution)/shard_map/ppermute | solution.py:390
  16.0 0.2 pack.2
  16.3 0.9 %collective-permute-start.5 = (bf16[4,16384]{1,0:T(4,128)(2,1)S(1)}, bf16[4,16384]{1,0:T(4,128)(2,1)S(1)}, u32[]{:S(2)}, u32[]{:S(2)}) collective-permute-start(bf16[4,16384]{1,0:T(4,128)(2,1)S(1)} %get-tuple-element.32), channel_id=1, source_target_pairs={{0,2},{1,3},{2,0},{3,1},{4,6},{5,7},{6,4},{7,5},{8,10},{9,11},{10,... | collective-permute-start | bytes 393224 | tf_op jit(solution)/shard_map/ppermute | solution.py:390
  17.2 1.6 %collective-permute-start.2 = (bf16[4,10240]{1,0:T(4,128)(2,1)S(1)}, bf16[4,10240]{1,0:T(4,128)(2,1)S(1)}, u32[]{:S(2)}, u32[]{:S(2)}) collective-permute-start(bf16[4,10240]{1,0:T(4,128)(2,1)S(1)} %get-tuple-element.29), channel_id=1, source_target_pairs={{0,17},{1,16},{2,19},{3,18},{4,21},{5,20},{6,23},{7,22},{8,25},{9,... | collective-permute-start | bytes 245768 | tf_op jit(solution)/shard_map/ppermute | solution.py:395
  18.8 0.8 %collective-permute-start.3 = (bf16[4,10240]{1,0:T(4,128)(2,1)S(1)}, bf16[4,10240]{1,0:T(4,128)(2,1)S(1)}, u32[]{:S(2)}, u32[]{:S(2)}) collective-permute-start(bf16[4,10240]{1,0:T(4,128)(2,1)S(1)} %get-tuple-element.30), channel_id=1, source_target_pairs={{0,16},{1,17},{2,18},{3,19},{4,20},{5,21},{6,22},{7,23},{8,24},{9,... | collective-permute-start | bytes 245768 | tf_op jit(solution)/shard_map/ppermute | solution.py:395
  19.6 0.2 collective-permute-start.4
  19.9 1.8 %collective-permute-done.5.refs_0_ = bf16[4,16384]{1,0:T(4,128)(2,1)S(1)} collective-permute-done((bf16[4,16384]{1,0:T(4,128)(2,1)S(1)}, bf16[4,16384]{1,0:T(4,128)(2,1)S(1)}, u32[]{:S(2)}, u32[]{:S(2)}) %collective-permute-start.5) | collective-permute-done | bytes 131104 | tf_op jit(solution)/shard_map/ppermute | solution.py:390
  21.6 0.2 pack.3
  21.8 0.1 collective-permute-start.6
  21.9 2.2 %collective-permute-start.7 = (bf16[4,10240]{1,0:T(4,128)(2,1)S(1)}, bf16[4,10240]{1,0:T(4,128)(2,1)S(1)}, u32[]{:S(2)}, u32[]{:S(2)}) collective-permute-start(bf16[4,10240]{1,0:T(4,128)(2,1)S(1)} %get-tuple-element.35), channel_id=1, source_target_pairs={{0,16},{1,17},{2,18},{3,19},{4,20},{5,21},{6,22},{7,23},{8,24},{9,... | collective-permute-start | bytes 245768 | tf_op jit(solution)/shard_map/ppermute | solution.py:395
  24.2 0.0 collective-permute-done.2.refs_1_
  24.2 0.4 collective-permute-start.8
  24.5 0.0 collective-permute-done.3.refs_2_
  24.6 0.0 collective-permute-done.4.refs_3_
  24.6 1.9 %collective-permute-done.6.refs_5_ = bf16[4,10240]{1,0:T(4,128)(2,1)S(1)} collective-permute-done((bf16[4,10240]{1,0:T(4,128)(2,1)S(1)}, bf16[4,10240]{1,0:T(4,128)(2,1)S(1)}, u32[]{:S(2)}, u32[]{:S(2)}) %collective-permute-start.6) | collective-permute-done | bytes 81952 | tf_op jit(solution)/shard_map/ppermute | solution.py:395
  26.4 1.8 %collective-permute-done.7.refs_6_ = bf16[4,10240]{1,0:T(4,128)(2,1)S(1)} collective-permute-done((bf16[4,10240]{1,0:T(4,128)(2,1)S(1)}, bf16[4,10240]{1,0:T(4,128)(2,1)S(1)}, u32[]{:S(2)}, u32[]{:S(2)}) %collective-permute-start.7) | collective-permute-done | bytes 81952 | tf_op jit(solution)/shard_map/ppermute | solution.py:395
  28.2 0.0 collective-permute-done.8.refs_7_
  28.2 0.2 join.1
  28.4 1.4 %collective-permute-start.9 = (bf16[32,6144]{1,0:T(8,128)(2,1)S(1)}, bf16[32,6144]{1,0:T(8,128)(2,1)S(1)}, u32[]{:S(2)}, u32[]{:S(2)}) collective-permute-start(bf16[32,6144]{1,0:T(8,128)(2,1)S(1)} %get-tuple-element.38), channel_id=1, source_target_pairs={{0,8},{8,0},{16,24},{24,16},{1,9},{9,1},{17,25},{25,17},{2,10},{10... | collective-permute-start | bytes 1179656 | tf_op jit(solution)/shard_map/ppermute | solution.py:390
  29.8 1.3 %collective-permute-done.9.refs_1_ = bf16[32,6144]{1,0:T(8,128)(2,1)S(1)} collective-permute-done((bf16[32,6144]{1,0:T(8,128)(2,1)S(1)}, bf16[32,6144]{1,0:T(8,128)(2,1)S(1)}, u32[]{:S(2)}, u32[]{:S(2)}) %collective-permute-start.9) | collective-permute-done | bytes 393248 | tf_op jit(solution)/shard_map/ppermute | solution.py:390
  31.1 11.4 %outer.1 = f32[4096,2048]{1,0:T(8,128)} custom-call(bf16[32,6144]{1,0:T(8,128)(2,1)S(1)} %get-tuple-element.37.refs_0_, bf16[32,6144]{1,0:T(8,128)(2,1)S(1)} %collective-permute-done.9.refs_1_), custom_call_target="tpu_custom_call" | custom-call | flops 10000000000 | bytes 30000000 | tf_op jit(solution)/shard_map/outer/pallas_call | solution.py:367
Async XLA Ops:
  0.0 8.1 %collective-permute-start = (bf16[1,48,2304]{2,1,0:T(8,128)(2,1)}, bf16[1,48,2304]{2,1,0:T(8,128)(2,1)S(1)}, u32[]{:S(2)}, u32[]{:S(2)}) collective-permute-start(bf16[1,48,2304]{2,1,0:T(8,128)(2,1)} %param.7), channel_id=1, source_target_pairs={{0,8},{8,16},{16,24},{24,0},{1,9},{9,17},{17,25},{25,1},{2,10},{10... | collective-permute-start | bytes 663560 | tf_op jit(solution)/shard_map/ppermute | solution.py:385
  4.5 0.9 %copy-start = (s32[3,8192]{1,0:T(4,128)S(1)}, s32[3,8192]{1,0:T(4,128)}, u32[]{:S(2)}) copy-start(s32[3,8192]{1,0:T(4,128)} %sphere_ref.1) | copy-start | bytes 294916
  10.5 5.5 %collective-permute-start.1 = (bf16[2,16384]{1,0:T(2,128)(2,1)S(1)}, bf16[2,16384]{1,0:T(2,128)(2,1)S(1)}, u32[]{:S(2)}, u32[]{:S(2)}) collective-permute-start(bf16[2,16384]{1,0:T(2,128)(2,1)S(1)} %get-tuple-element.27.refs_0_), channel_id=1, source_target_pairs={{0,4},{1,5},{2,6},{3,7},{4,0},{5,1},{6,2},{7,3},{8,12},{9,13},{10,... | collective-permute-start | bytes 196616 | tf_op jit(solution)/shard_map/ppermute | solution.py:390
  16.3 5.4 %collective-permute-start.5 = (bf16[4,16384]{1,0:T(4,128)(2,1)S(1)}, bf16[4,16384]{1,0:T(4,128)(2,1)S(1)}, u32[]{:S(2)}, u32[]{:S(2)}) collective-permute-start(bf16[4,16384]{1,0:T(4,128)(2,1)S(1)} %get-tuple-element.32), channel_id=1, source_target_pairs={{0,2},{1,3},{2,0},{3,1},{4,6},{5,7},{6,4},{7,5},{8,10},{9,11},{10,... | collective-permute-start | bytes 393224 | tf_op jit(solution)/shard_map/ppermute | solution.py:390
  17.2 6.9 %collective-permute-start.2 = (bf16[4,10240]{1,0:T(4,128)(2,1)S(1)}, bf16[4,10240]{1,0:T(4,128)(2,1)S(1)}, u32[]{:S(2)}, u32[]{:S(2)}) collective-permute-start(bf16[4,10240]{1,0:T(4,128)(2,1)S(1)} %get-tuple-element.29), channel_id=1, source_target_pairs={{0,17},{1,16},{2,19},{3,18},{4,21},{5,20},{6,23},{7,22},{8,25},{9,... | collective-permute-start | bytes 245768 | tf_op jit(solution)/shard_map/ppermute | solution.py:395
  18.8 5.7 %collective-permute-start.3 = (bf16[4,10240]{1,0:T(4,128)(2,1)S(1)}, bf16[4,10240]{1,0:T(4,128)(2,1)S(1)}, u32[]{:S(2)}, u32[]{:S(2)}) collective-permute-start(bf16[4,10240]{1,0:T(4,128)(2,1)S(1)} %get-tuple-element.30), channel_id=1, source_target_pairs={{0,16},{1,17},{2,18},{3,19},{4,20},{5,21},{6,22},{7,23},{8,24},{9,... | collective-permute-start | bytes 245768 | tf_op jit(solution)/shard_map/ppermute | solution.py:395
  19.6 4.9 %collective-permute-start.4 = (bf16[4,10240]{1,0:T(4,128)(2,1)S(1)}, bf16[4,10240]{1,0:T(4,128)(2,1)S(1)}, u32[]{:S(2)}, u32[]{:S(2)}) collective-permute-start(bf16[4,10240]{1,0:T(4,128)(2,1)S(1)} %get-tuple-element.31), channel_id=1, source_target_pairs={{0,1},{1,0},{2,3},{3,2},{4,5},{5,4},{6,7},{7,6},{8,9},{9,8},{10,11... | collective-permute-start | bytes 245768 | tf_op jit(solution)/shard_map/ppermute | solution.py:395
  21.8 4.6 %collective-permute-start.6 = (bf16[4,10240]{1,0:T(4,128)(2,1)S(1)}, bf16[4,10240]{1,0:T(4,128)(2,1)S(1)}, u32[]{:S(2)}, u32[]{:S(2)}) collective-permute-start(bf16[4,10240]{1,0:T(4,128)(2,1)S(1)} %get-tuple-element.34), channel_id=1, source_target_pairs={{0,17},{1,16},{2,19},{3,18},{4,21},{5,20},{6,23},{7,22},{8,25},{9,... | collective-permute-start | bytes 245768 | tf_op jit(solution)/shard_map/ppermute | solution.py:395
  21.9 6.3 %collective-permute-start.7 = (bf16[4,10240]{1,0:T(4,128)(2,1)S(1)}, bf16[4,10240]{1,0:T(4,128)(2,1)S(1)}, u32[]{:S(2)}, u32[]{:S(2)}) collective-permute-start(bf16[4,10240]{1,0:T(4,128)(2,1)S(1)} %get-tuple-element.35), channel_id=1, source_target_pairs={{0,16},{1,17},{2,18},{3,19},{4,20},{5,21},{6,22},{7,23},{8,24},{9,... | collective-permute-start | bytes 245768 | tf_op jit(solution)/shard_map/ppermute | solution.py:395
  24.2 4.1 %collective-permute-start.8 = (bf16[4,10240]{1,0:T(4,128)(2,1)S(1)}, bf16[4,10240]{1,0:T(4,128)(2,1)S(1)}, u32[]{:S(2)}, u32[]{:S(2)}) collective-permute-start(bf16[4,10240]{1,0:T(4,128)(2,1)S(1)} %get-tuple-element.36), channel_id=1, source_target_pairs={{0,1},{1,0},{2,3},{3,2},{4,5},{5,4},{6,7},{7,6},{8,9},{9,8},{10,11... | collective-permute-start | bytes 245768 | tf_op jit(solution)/shard_map/ppermute | solution.py:395
  28.4 2.8 %collective-permute-start.9 = (bf16[32,6144]{1,0:T(8,128)(2,1)S(1)}, bf16[32,6144]{1,0:T(8,128)(2,1)S(1)}, u32[]{:S(2)}, u32[]{:S(2)}) collective-permute-start(bf16[32,6144]{1,0:T(8,128)(2,1)S(1)} %get-tuple-element.38), channel_id=1, source_target_pairs={{0,8},{8,0},{16,24},{24,16},{1,9},{9,1},{17,25},{25,17},{2,10},{10... | collective-permute-start | bytes 1179656 | tf_op jit(solution)/shard_map/ppermute | solution.py:390

commit v14 on v13

--- a/solution.py
+++ b/solution.py
@@ -182,36 +182,55 @@
     places_ref[1:2, :] = (residue >> 1) * KX_ROWS + kx
     write_tables(grid, table_ref, twiddle_ref)
     cube_ref[...] = spectrum_of(grid, orbitals_ref[0], orbitals_ref[1], table_ref, twiddle_ref)
-    pick(cube_ref, places_ref, coef_ref, 0)
-
-
-def pick(cube_ref, places_ref, coef_ref, pair):
+
+    @pl.when(on_even_core())
+    def _():
+        pick(cube_ref, places_ref, coef_ref, [0])
+
+
+def pick(cube_ref, places_ref, coef_ref, pairs):
     groups = RADIX // 2 * KX_ROWS // 8
     half_count = places_ref.shape[1]
     counted = lax.broadcasted_iota(jnp.int32, (2 * LANES, TILE), 0).astype(jnp.float32).astype(jnp.bfloat16)
     line = lax.broadcasted_iota(jnp.int32, (8, TILE), 0)
+    parts = [(pair, side) for pair in pairs for side in range(2)]
     for first in range(0, half_count, TILE):
         here = slice(first, first + TILE)
         lane = places_ref[0:1, here].astype(jnp.float32).astype(jnp.bfloat16)
         one_hot = jnp.where(counted == lane, jnp.bfloat16(1), jnp.bfloat16(0))
         found = dot(cube_ref[...], one_hot)
         away = line - places_ref[1:2, here]
-        values = [jnp.zeros((8, TILE), jnp.float32)] * 2
+        values = [jnp.zeros((8, TILE), jnp.float32)] * len(parts)
         for group in range(groups):
             chosen = away == -8 * group
-            for side in range(2):
-                start = (side * groups + group) * 8
-                values[side] = jnp.where(chosen, found[start : start + 8], values[side])
-        for side in range(2):
-            value = jnp.sum(values[side], axis=0, keepdims=True).astype(jnp.bfloat16)
+            for which in range(len(parts)):
+                start = (which * groups + group) * 8
+                values[which] = jnp.where(chosen, found[start : start + 8], values[which])
+        for (pair, side), value in zip(parts, values):
+            value = jnp.sum(value, axis=0, keepdims=True).astype(jnp.bfloat16)
             coef_ref[pair : pair + 1, side * half_count + first : side * half_count + first + TILE] = value
 
 
-def second_kernel(grid, orbitals_ref, occ_ref, first_ref, places_ref, table_ref, twiddle_ref, coef_ref, later_ref, cube_ref):
+def on_even_core():
+    return lax.rem(lax.axis_index("row"), 2) == 0
+
+
+def second_kernel(
+    grid, orbitals_ref, occ_ref, first_ref, places_ref, table_ref, twiddle_ref, first_cube_ref, coef_ref, later_ref, cube_ref
+):
+    picks = first_cube_ref.shape[0]
     later_ref[...] = jnp.zeros_like(later_ref)
-    coef_ref[0:1, :] = first_ref[...]
-    cube_ref[...] = spectrum_of(grid, orbitals_ref[0], occ_ref[0], table_ref, twiddle_ref)
-    pick(cube_ref, places_ref, coef_ref, 1)
+    cube_ref[picks:, :] = spectrum_of(grid, orbitals_ref[0], occ_ref[0], table_ref, twiddle_ref)
+
+    @pl.when(on_even_core())
+    def _():
+        coef_ref[0:1, :] = first_ref[...]
+        pick(cube_ref.at[picks:], places_ref, coef_ref, [1])
+
+    @pl.when(jnp.logical_not(on_even_core()))
+    def _():
+        cube_ref[:picks, :] = first_cube_ref[...]
+        pick(cube_ref, places_ref, coef_ref, [0, 1])
 
 
 def cost(flops, data):
@@ -227,9 +246,8 @@
     half_count = sphere_index.shape[1]
     width, _, table_count = table_rows(grid)
     orbitals = jnp.concatenate([cond_orbitals, occ_orbitals], axis=0)
-    cube = pltpu.VMEM((RADIX * KX_ROWS, 2 * LANES), jnp.bfloat16)
+    picks = RADIX * KX_ROWS
     params = dict(
-        scratch_shapes=[cube],
         compiler_params=pltpu.CompilerParams(vmem_limit_bytes=VMEM_LIMIT),
         cost_estimate=cost(2 * 10**9, 2 * 10**6),
     )
@@ -240,9 +258,10 @@
             jax.ShapeDtypeStruct((2, half_count), jnp.int32),
             jax.ShapeDtypeStruct((table_count, LANES), jnp.bfloat16),
             jax.ShapeDtypeStruct((16, width), jnp.float32),
+            jax.ShapeDtypeStruct((picks, 2 * LANES), jnp.bfloat16),
         ],
         in_specs=in_vmem(2),
-        out_specs=in_vmem(4),
+        out_specs=in_vmem(5),
         name="first_pair",
         **params,
     )(orbitals, sphere_index)
@@ -252,8 +271,9 @@
             jax.ShapeDtypeStruct((STEPS, 2 * half_count), jnp.bfloat16),
             jax.ShapeDtypeStruct((1, *band_shape), jnp.int32),
         ],
-        in_specs=in_vmem(6),
+        in_specs=in_vmem(7),
         out_specs=in_vmem(2),
+        scratch_shapes=[pltpu.VMEM((STEPS * picks, 2 * LANES), jnp.bfloat16)],
         name="second_pair",
         **params,
     )(orbitals, occ_second, *handed)

time: 43 us -> 43.4 us (level)
  starting transfers between devices: 12.7 us -> 16 us
  waiting for transfers between devices: 8.55 us -> 6.56 us
  Pallas kernels: 17.1 us -> 16.1 us
    ppermute x3, starting transfers between devices: 4.73 us -> 7.54 us  [turned(): return lax.ppermute(value, axis, [(i, i ^ turn) for i in range(devices)])]
    ppermute x3, waiting for transfers between devices: 4.88 us -> 2.98 us  [turned(): return lax.ppermute(value, axis, [(i, i ^ turn) for i in range(devices)])]
    pallas_call x1, Pallas kernels: 2.62 us -> 1.07 us  [transform(): pl.pallas_call(functools.partial(first_kernel, grid), out_shape=[jax.Shap...]
    pallas_call x1, Pallas kernels: 2.45 us -> 3.06 us  [transform(): pl.pallas_call(functools.partial(second_kernel, grid), out_shape=[jax.Sha...]
    ppermute x6, starting transfers between devices: 5.36 us -> 5.83 us  [sent_across(): return lax.ppermute(value, ('row', 'col'), moves)]
  transfers between devices with their start and end apart: 10 -> 10, of which waited for: 5 -> 6; matrix products, arithmetic and copies ran while one was open for 8% -> 8% of each run, Pallas kernels for 7% -> 3%
where the time goes in v14:
time: 43.4 us; the launch traced here: 42.9 us
  Pallas kernels  16.1 us (37%)
  starting transfers between devices  16 us (37%)
  waiting for transfers between devices  6.56 us (15%)
  local copies, waits for them, and re-layouts  2.8 us (6%)
  other arithmetic  1.34 us (3%)
    pallas_call x1, Pallas kernels, outer(): pl.pallas_call(functools.partial(outer_kernel, row_width, block, slots),...  11.4 us
    ppermute x3, starting transfers between devices, turned(): return lax.ppermute(value, axis, [(i, i ^ turn) for i in range(devices)])  7.54 us
    ppermute x6, starting transfers between devices, sent_across(): return lax.ppermute(value, ('row', 'col'), moves)  5.83 us
    ppermute x6, waiting for transfers between devices, sent_across(): return lax.ppermute(value, ('row', 'col'), moves)  3.57 us
    pallas_call x1, Pallas kernels, transform(): pl.pallas_call(functools.partial(second_kernel, grid), out_shape=[jax.Sha...  3.06 us
    ppermute x3, waiting for transfers between devices, turned(): return lax.ppermute(value, axis, [(i, i ^ turn) for i in range(devices)])  2.98 us
    ppermute x1, starting transfers between devices, shifted(): lax.ppermute(value, axis, [(i, (i + by) % devices) for i in range(devices)])  2.63 us
    unnamed x3, local copies, waits for them, and re-layouts  1.85 us
  transfers between devices with their start and end apart: 10, of which 6 were waited for; matrix products, arithmetic and copies ran while one was open for 8% of the time, Pallas kernels for 3%

profile of v14, /device:TPU:1, one launch (start us, length us, event | category | flops | bytes accessed | tf_op | source)
XLA Modules:
  0.0 42.9 jit_solution(13733130025238297161)
XLA Ops:
  0.0 2.6 %collective-permute-start = (bf16[1,48,2304]{2,1,0:T(8,128)(2,1)}, bf16[1,48,2304]{2,1,0:T(8,128)(2,1)S(1)}, u32[]{:S(2)}, u32[]{:S(2)}) collective-permute-start(bf16[1,48,2304]{2,1,0:T(8,128)(2,1)} %param.7), channel_id=1, source_target_pairs={{0,8},{8,16},{16,24},{24,0},{1,9},{9,17},{17,25},{25,1},{2,10},{10... | collective-permute-start | bytes 663560 | tf_op jit(solution)/shard_map/ppermute | solution.py:405
  2.6 0.9 %constant_dynamic-update-slice_fusion.1 = bf16[2,48,2304]{2,1,0:T(8,128)(2,1)S(1)} fusion(bf16[1,48,2304]{2,1,0:T(8,128)(2,1)} %param.6), kind=kLoop, calls=%fused_computation.1 | loop fusion | bytes 442368
  3.6 1.0 %constant_dynamic-update-slice_fusion.orbitals_ref = bf16[2,48,2304]{2,1,0:T(8,128)(2,1)S(1)} fusion(bf16[2,48,2304]{2,1,0:T(8,128)(2,1)S(1)} %constant_dynamic-update-slice_fusion.1, bf16[1,48,2304]{2,1,0:T(8,128)(2,1)} %param.7), kind=kLoop, calls=%fused_computation | loop fusion | bytes 442368 | tf_op jit(solution)/shard_map/concatenate | solution.py:248
  4.5 0.0 copy-start
  4.6 0.9 %copy-done = s32[3,8192]{1,0:T(4,128)S(1)} copy-done((s32[3,8192]{1,0:T(4,128)S(1)}, s32[3,8192]{1,0:T(4,128)}, u32[]{:S(2)}) %copy-start) | copy-done | bytes 98328
  5.4 1.1 %first_pair.1 = (bf16[1,16384]{1,0:T(2,128)(2,1)S(1)}, s32[2,8192]{1,0:T(2,128)S(1)}, bf16[1616,128]{1,0:T(8,128)(2,1)S(1)}, f32[16,384]{1,0:T(8,128)S(1)}, bf16[240,256]{1,0:T(8,128)(2,1)S(1)}) custom-call(bf16[2,48,2304]{2,1,0:T(8,128)(2,1)S(1)} %constant_dynamic-update-slice_fusion.orbitals_ref, s32[3,8192]{1,0:T(4,128)S(1)} %copy-done), custom_call_target="tpu_custom_call" | custom-call | flops 2000000000 | bytes 2000000 | tf_op jit(solution)/shard_map/first_pair/pallas_call | solution.py:254
  6.5 0.0 collective-permute-done.occ_ref
  6.5 3.1 %second_pair.1 = (bf16[2,16384]{1,0:T(2,128)(2,1)S(1)}, s32[1,32]{1,0:T(1,128)S(1)}) custom-call(bf16[2,48,2304]{2,1,0:T(8,128)(2,1)S(1)} %constant_dynamic-update-slice_fusion.orbitals_ref, bf16[1,48,2304]{2,1,0:T(8,128)(2,1)S(1)} %collective-permute-done.occ_ref, bf16[1,16384]{1,0:T(2,128)(2,1)S(1)} %get-tuple-element.23.first_ref, ...), custom_call_target="tpu_custom_call" | custom-call | flops 2000000000 | bytes 2000000 | tf_op jit(solution)/shard_map/second_pair/pallas_call | solution.py:268
  9.6 2.4 %collective-permute-start.1 = (bf16[2,16384]{1,0:T(2,128)(2,1)S(1)}, bf16[2,16384]{1,0:T(2,128)(2,1)S(1)}, u32[]{:S(2)}, u32[]{:S(2)}) collective-permute-start(bf16[2,16384]{1,0:T(2,128)(2,1)S(1)} %get-tuple-element.29.refs_0_), channel_id=1, source_target_pairs={{0,4},{1,5},{2,6},{3,7},{4,0},{5,1},{6,2},{7,3},{8,12},{9,13},{10,... | collective-permute-start | bytes 196616 | tf_op jit(solution)/shard_map/ppermute | solution.py:410
  12.0 0.7 %fusion.1 = f32[1,32]{1,0:T(1,128)S(1)} fusion(s32[32]{0:T(128)} %param.10, s32[1,32]{1,0:T(1,128)S(1)} %get-tuple-element.28), kind=kLoop, calls=%fused_computation.5 | loop fusion | flops 64 | bytes 384 | tf_op jit(solution)/shard_map/stack | solution.py:425
  12.6 0.7 %pad_maximum_fusion.levels_ref = f32[3,32]{1,0:T(4,128)S(1)} fusion(f32[1,32]{1,0:T(1,128)S(1)} %fusion.1, f32[1,32]{1,0:T(1,128)} %bitcast.10, f32[1,32]{1,0:T(1,128)} %bitcast.11), kind=kLoop, calls=%fused_computation.2 | loop fusion | flops 192 | bytes 768 | tf_op jit(solution)/shard_map/stack | solution.py:425
  13.3 0.7 %collective-permute-done.1.refs_1_ = bf16[2,16384]{1,0:T(2,128)(2,1)S(1)} collective-permute-done((bf16[2,16384]{1,0:T(2,128)(2,1)S(1)}, bf16[2,16384]{1,0:T(2,128)(2,1)S(1)}, u32[]{:S(2)}, u32[]{:S(2)}) %collective-permute-start.1) | collective-permute-done | bytes 65568 | tf_op jit(solution)/shard_map/ppermute | solution.py:410
  14.0 0.2 pack.2
  14.3 2.5 %collective-permute-start.5 = (bf16[4,16384]{1,0:T(4,128)(2,1)S(1)}, bf16[4,16384]{1,0:T(4,128)(2,1)S(1)}, u32[]{:S(2)}, u32[]{:S(2)}) collective-permute-start(bf16[4,16384]{1,0:T(4,128)(2,1)S(1)} %get-tuple-element.34), channel_id=1, source_target_pairs={{0,2},{1,3},{2,0},{3,1},{4,6},{5,7},{6,4},{7,5},{8,10},{9,11},{10,... | collective-permute-start | bytes 393224 | tf_op jit(solution)/shard_map/ppermute | solution.py:410
  16.7 0.9 %collective-permute-start.2 = (bf16[4,10240]{1,0:T(4,128)(2,1)S(1)}, bf16[4,10240]{1,0:T(4,128)(2,1)S(1)}, u32[]{:S(2)}, u32[]{:S(2)}) collective-permute-start(bf16[4,10240]{1,0:T(4,128)(2,1)S(1)} %get-tuple-element.31), channel_id=1, source_target_pairs={{0,17},{1,16},{2,19},{3,18},{4,21},{5,20},{6,23},{7,22},{8,25},{9,... | collective-permute-start | bytes 245768 | tf_op jit(solution)/shard_map/ppermute | solution.py:415
  17.6 1.5 %collective-permute-start.3 = (bf16[4,10240]{1,0:T(4,128)(2,1)S(1)}, bf16[4,10240]{1,0:T(4,128)(2,1)S(1)}, u32[]{:S(2)}, u32[]{:S(2)}) collective-permute-start(bf16[4,10240]{1,0:T(4,128)(2,1)S(1)} %get-tuple-element.32), channel_id=1, source_target_pairs={{0,16},{1,17},{2,18},{3,19},{4,20},{5,21},{6,22},{7,23},{8,24},{9,... | collective-permute-start | bytes 245768 | tf_op jit(solution)/shard_map/ppermute | solution.py:415
  19.1 0.3 collective-permute-start.4
  19.4 0.9 %collective-permute-done.5.refs_0_ = bf16[4,16384]{1,0:T(4,128)(2,1)S(1)} collective-permute-done((bf16[4,16384]{1,0:T(4,128)(2,1)S(1)}, bf16[4,16384]{1,0:T(4,128)(2,1)S(1)}, u32[]{:S(2)}, u32[]{:S(2)}) %collective-permute-start.5) | collective-permute-done | bytes 131104 | tf_op jit(solution)/shard_map/ppermute | solution.py:410
  20.3 0.2 pack.3
  20.5 0.1 collective-permute-start.6
  20.6 3.1 %collective-permute-start.7 = (bf16[4,10240]{1,0:T(4,128)(2,1)S(1)}, bf16[4,10240]{1,0:T(4,128)(2,1)S(1)}, u32[]{:S(2)}, u32[]{:S(2)}) collective-permute-start(bf16[4,10240]{1,0:T(4,128)(2,1)S(1)} %get-tuple-element.37), channel_id=1, source_target_pairs={{0,16},{1,17},{2,18},{3,19},{4,20},{5,21},{6,22},{7,23},{8,24},{9,... | collective-permute-start | bytes 245768 | tf_op jit(solution)/shard_map/ppermute | solution.py:415
  23.7 0.0 collective-permute-done.2.refs_1_
  23.7 0.0 collective-permute-start.8
  23.7 0.0 collective-permute-done.3.refs_2_
  23.7 0.0 collective-permute-done.4.refs_3_
  23.7 1.3 %collective-permute-done.6.refs_5_ = bf16[4,10240]{1,0:T(4,128)(2,1)S(1)} collective-permute-done((bf16[4,10240]{1,0:T(4,128)(2,1)S(1)}, bf16[4,10240]{1,0:T(4,128)(2,1)S(1)}, u32[]{:S(2)}, u32[]{:S(2)}) %collective-permute-start.6) | collective-permute-done | bytes 81952 | tf_op jit(solution)/shard_map/ppermute | solution.py:415
  25.0 2.1 %collective-permute-done.7.refs_6_ = bf16[4,10240]{1,0:T(4,128)(2,1)S(1)} collective-permute-done((bf16[4,10240]{1,0:T(4,128)(2,1)S(1)}, bf16[4,10240]{1,0:T(4,128)(2,1)S(1)}, u32[]{:S(2)}, u32[]{:S(2)}) %collective-permute-start.7) | collective-permute-done | bytes 81952 | tf_op jit(solution)/shard_map/ppermute | solution.py:415
  27.1 0.2 collective-permute-done.8.refs_7_
  27.3 0.2 join.1
  27.4 2.7 %collective-permute-start.9 = (bf16[32,6144]{1,0:T(8,128)(2,1)S(1)}, bf16[32,6144]{1,0:T(8,128)(2,1)S(1)}, u32[]{:S(2)}, u32[]{:S(2)}) collective-permute-start(bf16[32,6144]{1,0:T(8,128)(2,1)S(1)} %get-tuple-element.40), channel_id=1, source_target_pairs={{0,8},{8,0},{16,24},{24,16},{1,9},{9,1},{17,25},{25,17},{2,10},{10... | collective-permute-start | bytes 1179656 | tf_op jit(solution)/shard_map/ppermute | solution.py:410
  30.1 1.3 %collective-permute-done.9.refs_1_ = bf16[32,6144]{1,0:T(8,128)(2,1)S(1)} collective-permute-done((bf16[32,6144]{1,0:T(8,128)(2,1)S(1)}, bf16[32,6144]{1,0:T(8,128)(2,1)S(1)}, u32[]{:S(2)}, u32[]{:S(2)}) %collective-permute-start.9) | collective-permute-done | bytes 393248 | tf_op jit(solution)/shard_map/ppermute | solution.py:410
  31.5 11.4 %outer.1 = f32[4096,2048]{1,0:T(8,128)} custom-call(bf16[32,6144]{1,0:T(8,128)(2,1)S(1)} %get-tuple-element.39.refs_0_, bf16[32,6144]{1,0:T(8,128)(2,1)S(1)} %collective-permute-done.9.refs_1_), custom_call_target="tpu_custom_call" | custom-call | flops 10000000000 | bytes 30000000 | tf_op jit(solution)/shard_map/outer/pallas_call | solution.py:387
Async XLA Ops:
  0.0 6.5 %collective-permute-start = (bf16[1,48,2304]{2,1,0:T(8,128)(2,1)}, bf16[1,48,2304]{2,1,0:T(8,128)(2,1)S(1)}, u32[]{:S(2)}, u32[]{:S(2)}) collective-permute-start(bf16[1,48,2304]{2,1,0:T(8,128)(2,1)} %param.7), channel_id=1, source_target_pairs={{0,8},{8,16},{16,24},{24,0},{1,9},{9,17},{17,25},{25,1},{2,10},{10... | collective-permute-start | bytes 663560 | tf_op jit(solution)/shard_map/ppermute | solution.py:405
  4.5 0.9 %copy-start = (s32[3,8192]{1,0:T(4,128)S(1)}, s32[3,8192]{1,0:T(4,128)}, u32[]{:S(2)}) copy-start(s32[3,8192]{1,0:T(4,128)} %sphere_ref.1) | copy-start | bytes 294916
  9.6 4.4 %collective-permute-start.1 = (bf16[2,16384]{1,0:T(2,128)(2,1)S(1)}, bf16[2,16384]{1,0:T(2,128)(2,1)S(1)}, u32[]{:S(2)}, u32[]{:S(2)}) collective-permute-start(bf16[2,16384]{1,0:T(2,128)(2,1)S(1)} %get-tuple-element.29.refs_0_), channel_id=1, source_target_pairs={{0,4},{1,5},{2,6},{3,7},{4,0},{5,1},{6,2},{7,3},{8,12},{9,13},{10,... | collective-permute-start | bytes 196616 | tf_op jit(solution)/shard_map/ppermute | solution.py:410
  14.3 6.0 %collective-permute-start.5 = (bf16[4,16384]{1,0:T(4,128)(2,1)S(1)}, bf16[4,16384]{1,0:T(4,128)(2,1)S(1)}, u32[]{:S(2)}, u32[]{:S(2)}) collective-permute-start(bf16[4,16384]{1,0:T(4,128)(2,1)S(1)} %get-tuple-element.34), channel_id=1, source_target_pairs={{0,2},{1,3},{2,0},{3,1},{4,6},{5,7},{6,4},{7,5},{8,10},{9,11},{10,... | collective-permute-start | bytes 393224 | tf_op jit(solution)/shard_map/ppermute | solution.py:410
  16.7 6.9 %collective-permute-start.2 = (bf16[4,10240]{1,0:T(4,128)(2,1)S(1)}, bf16[4,10240]{1,0:T(4,128)(2,1)S(1)}, u32[]{:S(2)}, u32[]{:S(2)}) collective-permute-start(bf16[4,10240]{1,0:T(4,128)(2,1)S(1)} %get-tuple-element.31), channel_id=1, source_target_pairs={{0,17},{1,16},{2,19},{3,18},{4,21},{5,20},{6,23},{7,22},{8,25},{9,... | collective-permute-start | bytes 245768 | tf_op jit(solution)/shard_map/ppermute | solution.py:415
  17.6 6.1 %collective-permute-start.3 = (bf16[4,10240]{1,0:T(4,128)(2,1)S(1)}, bf16[4,10240]{1,0:T(4,128)(2,1)S(1)}, u32[]{:S(2)}, u32[]{:S(2)}) collective-permute-start(bf16[4,10240]{1,0:T(4,128)(2,1)S(1)} %get-tuple-element.32), channel_id=1, source_target_pairs={{0,16},{1,17},{2,18},{3,19},{4,20},{5,21},{6,22},{7,23},{8,24},{9,... | collective-permute-start | bytes 245768 | tf_op jit(solution)/shard_map/ppermute | solution.py:415
  19.1 4.5 %collective-permute-start.4 = (bf16[4,10240]{1,0:T(4,128)(2,1)S(1)}, bf16[4,10240]{1,0:T(4,128)(2,1)S(1)}, u32[]{:S(2)}, u32[]{:S(2)}) collective-permute-start(bf16[4,10240]{1,0:T(4,128)(2,1)S(1)} %get-tuple-element.33), channel_id=1, source_target_pairs={{0,1},{1,0},{2,3},{3,2},{4,5},{5,4},{6,7},{7,6},{8,9},{9,8},{10,11... | collective-permute-start | bytes 245768 | tf_op jit(solution)/shard_map/ppermute | solution.py:415
  20.5 4.5 %collective-permute-start.6 = (bf16[4,10240]{1,0:T(4,128)(2,1)S(1)}, bf16[4,10240]{1,0:T(4,128)(2,1)S(1)}, u32[]{:S(2)}, u32[]{:S(2)}) collective-permute-start(bf16[4,10240]{1,0:T(4,128)(2,1)S(1)} %get-tuple-element.36), channel_id=1, source_target_pairs={{0,17},{1,16},{2,19},{3,18},{4,21},{5,20},{6,23},{7,22},{8,25},{9,... | collective-permute-start | bytes 245768 | tf_op jit(solution)/shard_map/ppermute | solution.py:415
  20.6 6.5 %collective-permute-start.7 = (bf16[4,10240]{1,0:T(4,128)(2,1)S(1)}, bf16[4,10240]{1,0:T(4,128)(2,1)S(1)}, u32[]{:S(2)}, u32[]{:S(2)}) collective-permute-start(bf16[4,10240]{1,0:T(4,128)(2,1)S(1)} %get-tuple-element.37), channel_id=1, source_target_pairs={{0,16},{1,17},{2,18},{3,19},{4,20},{5,21},{6,22},{7,23},{8,24},{9,... | collective-permute-start | bytes 245768 | tf_op jit(solution)/shard_map/ppermute | solution.py:415
  23.7 3.6 %collective-permute-start.8 = (bf16[4,10240]{1,0:T(4,128)(2,1)S(1)}, bf16[4,10240]{1,0:T(4,128)(2,1)S(1)}, u32[]{:S(2)}, u32[]{:S(2)}) collective-permute-start(bf16[4,10240]{1,0:T(4,128)(2,1)S(1)} %get-tuple-element.38), channel_id=1, source_target_pairs={{0,1},{1,0},{2,3},{3,2},{4,5},{5,4},{6,7},{7,6},{8,9},{9,8},{10,11... | collective-permute-start | bytes 245768 | tf_op jit(solution)/shard_map/ppermute | solution.py:415
  27.4 4.1 %collective-permute-start.9 = (bf16[32,6144]{1,0:T(8,128)(2,1)S(1)}, bf16[32,6144]{1,0:T(8,128)(2,1)S(1)}, u32[]{:S(2)}, u32[]{:S(2)}) collective-permute-start(bf16[32,6144]{1,0:T(8,128)(2,1)S(1)} %get-tuple-element.40), channel_id=1, source_target_pairs={{0,8},{8,0},{16,24},{24,16},{1,9},{9,1},{17,25},{25,17},{2,10},{10... | collective-permute-start | bytes 1179656 | tf_op jit(solution)/shard_map/ppermute | solution.py:410

commit v15 on v14

--- a/solution.py
+++ b/solution.py
@@ -291,14 +291,12 @@
     if merged:
         outs[-1][...] = mixed_ref[...].astype(jnp.bfloat16)
     weight = pair_weights([c ^ turn for turn in turns], levels_ref)
-    columns = []
-    for side in range(2):
-        start = pl.multiple_of((c ^ side) * col_width, LANES)
-        columns.append((weight * mixed_ref[:, pl.ds(start, col_width)]).astype(jnp.bfloat16))
-    for (turn, side), out_ref in zip(targets, outs):
+    for (even, odd), out_ref in zip(targets, outs):
+        turn, side = (jnp.where(on_even_core(), *choice) for choice in zip(even, odd))
         start = pl.multiple_of((r ^ turn) // 2 * (2 * row_width), LANES)
         out_ref[:, : 2 * row_width] = mixed_ref[:, pl.ds(start, 2 * row_width)].astype(jnp.bfloat16)
-        out_ref[:, 2 * row_width :] = columns[side]
+        start = pl.multiple_of((c ^ side) * col_width, LANES)
+        out_ref[:, 2 * row_width :] = (weight * mixed_ref[:, pl.ds(start, col_width)]).astype(jnp.bfloat16)
 
 
 def pack(arrived, levels, turns, targets, merged, plan):
@@ -410,8 +408,11 @@
     return lax.ppermute(value, axis, [(i, i ^ turn) for i in range(devices)])
 
 
-def sent_across(value, turn, side, rows, cols):
-    moves = [(r * cols + c, (r ^ turn) * cols + (c ^ side)) for r in range(rows) for c in range(cols)]
+def sent_across(value, target, rows, cols):
+    moves = []
+    for r in range(rows):
+        turn, side = target[r % 2]
+        moves += [(r * cols + c, (r ^ turn) * cols + (c ^ side)) for c in range(cols)]
     return lax.ppermute(value, ("row", "col"), moves)
 
 
@@ -423,11 +424,12 @@
     occ_second = shifted(occ_orbitals, "row", 1)
     own, later = transform(cond_orbitals, occ_orbitals, occ_second, sphere_index, occ_band.shape)
     levels = jnp.stack([cond_energy, occ_energy, (occ_band + later[0]).astype(jnp.float32)])
-    targets = [(0, 0)] + [(turn, side) for side in (1, 0) for turn in range(rows - 2, -2, -2) if turn or side]
-    targets.append(targets.pop(rows // 2))
+    even = [(0, 0)] + [(turn, 1) for turn in range(rows - 2, 0, -2)] + [(turn, 0) for turn in range(rows - 2, 0, -2)] + [(0, 1)]
+    odd = even[:-2] + even[:-3:-1]
+    targets = list(zip(even, odd))
 
     def sent(packed):
-        return [packed[0]] + [sent_across(value, *target, rows, cols) for value, target in zip(packed[1:], targets[1:])]
+        return [packed[0]] + [sent_across(value, target, rows, cols) for value, target in zip(packed[1:], targets[1:])]
 
     held, turns, bit = [own], [0], cols // 2
     while bit > 2:

time: 43.4 us -> 43.4 us (level)
  no operation moved by 1% of the time
where the time goes in v15:
time: 43.4 us; the launch traced here: 42.9 us
  starting transfers between devices  16.2 us (37%)
  Pallas kernels  16.1 us (37%)
  waiting for transfers between devices  6.41 us (15%)
  local copies, waits for them, and re-layouts  2.8 us (6%)
  other arithmetic  1.34 us (3%)
    pallas_call x1, Pallas kernels, outer(): pl.pallas_call(functools.partial(outer_kernel, row_width, block, slots),...  11.4 us
    ppermute x3, starting transfers between devices, turned(): return lax.ppermute(value, axis, [(i, i ^ turn) for i in range(devices)])  7.7 us
    ppermute x6, starting transfers between devices, sent_across(): return lax.ppermute(value, ('row', 'col'), moves)  5.83 us
    ppermute x6, waiting for transfers between devices, sent_across(): return lax.ppermute(value, ('row', 'col'), moves)  3.43 us
    pallas_call x1, Pallas kernels, transform(): pl.pallas_call(functools.partial(second_kernel, grid), out_shape=[jax.Sha...  3.06 us
    ppermute x3, waiting for transfers between devices, turned(): return lax.ppermute(value, axis, [(i, i ^ turn) for i in range(devices)])  2.98 us
    ppermute x1, starting transfers between devices, shifted(): lax.ppermute(value, axis, [(i, (i + by) % devices) for i in range(devices)])  2.63 us
    unnamed x3, local copies, waits for them, and re-layouts  1.85 us
  transfers between devices with their start and end apart: 10, of which 6 were waited for; matrix products, arithmetic and copies ran while one was open for 8% of the time, Pallas kernels for 3%

profile of v15, /device:TPU:1, one launch (start us, length us, event | category | flops | bytes accessed | tf_op | source)
XLA Modules:
  0.0 42.9 jit_solution(7794100781589649811)
XLA Ops:
  0.0 2.6 %collective-permute-start = (bf16[1,48,2304]{2,1,0:T(8,128)(2,1)}, bf16[1,48,2304]{2,1,0:T(8,128)(2,1)S(1)}, u32[]{:S(2)}, u32[]{:S(2)}) collective-permute-start(bf16[1,48,2304]{2,1,0:T(8,128)(2,1)} %param.7), channel_id=1, source_target_pairs={{0,8},{8,16},{16,24},{24,0},{1,9},{9,17},{17,25},{25,1},{2,10},{10... | collective-permute-start | bytes 663560 | tf_op jit(solution)/shard_map/ppermute | solution.py:403
  2.6 0.9 %constant_dynamic-update-slice_fusion.1 = bf16[2,48,2304]{2,1,0:T(8,128)(2,1)S(1)} fusion(bf16[1,48,2304]{2,1,0:T(8,128)(2,1)} %param.6), kind=kLoop, calls=%fused_computation.1 | loop fusion | bytes 442368
  3.6 1.0 %constant_dynamic-update-slice_fusion.orbitals_ref = bf16[2,48,2304]{2,1,0:T(8,128)(2,1)S(1)} fusion(bf16[2,48,2304]{2,1,0:T(8,128)(2,1)S(1)} %constant_dynamic-update-slice_fusion.1, bf16[1,48,2304]{2,1,0:T(8,128)(2,1)} %param.7), kind=kLoop, calls=%fused_computation | loop fusion | bytes 442368 | tf_op jit(solution)/shard_map/concatenate | solution.py:248
  4.5 0.0 copy-start
  4.6 0.9 %copy-done = s32[3,8192]{1,0:T(4,128)S(1)} copy-done((s32[3,8192]{1,0:T(4,128)S(1)}, s32[3,8192]{1,0:T(4,128)}, u32[]{:S(2)}) %copy-start) | copy-done | bytes 98328
  5.4 1.1 %first_pair.1 = (bf16[1,16384]{1,0:T(2,128)(2,1)S(1)}, s32[2,8192]{1,0:T(2,128)S(1)}, bf16[1616,128]{1,0:T(8,128)(2,1)S(1)}, f32[16,384]{1,0:T(8,128)S(1)}, bf16[240,256]{1,0:T(8,128)(2,1)S(1)}) custom-call(bf16[2,48,2304]{2,1,0:T(8,128)(2,1)S(1)} %constant_dynamic-update-slice_fusion.orbitals_ref, s32[3,8192]{1,0:T(4,128)S(1)} %copy-done), custom_call_target="tpu_custom_call" | custom-call | flops 2000000000 | bytes 2000000 | tf_op jit(solution)/shard_map/first_pair/pallas_call | solution.py:254
  6.5 0.0 collective-permute-done.occ_ref
  6.5 3.1 %second_pair.1 = (bf16[2,16384]{1,0:T(2,128)(2,1)S(1)}, s32[1,32]{1,0:T(1,128)S(1)}) custom-call(bf16[2,48,2304]{2,1,0:T(8,128)(2,1)S(1)} %constant_dynamic-update-slice_fusion.orbitals_ref, bf16[1,48,2304]{2,1,0:T(8,128)(2,1)S(1)} %collective-permute-done.occ_ref, bf16[1,16384]{1,0:T(2,128)(2,1)S(1)} %get-tuple-element.23.first_ref, ...), custom_call_target="tpu_custom_call" | custom-call | flops 2000000000 | bytes 2000000 | tf_op jit(solution)/shard_map/second_pair/pallas_call | solution.py:268
  9.6 2.4 %collective-permute-start.1 = (bf16[2,16384]{1,0:T(2,128)(2,1)S(1)}, bf16[2,16384]{1,0:T(2,128)(2,1)S(1)}, u32[]{:S(2)}, u32[]{:S(2)}) collective-permute-start(bf16[2,16384]{1,0:T(2,128)(2,1)S(1)} %get-tuple-element.29.refs_0_), channel_id=1, source_target_pairs={{0,4},{1,5},{2,6},{3,7},{4,0},{5,1},{6,2},{7,3},{8,12},{9,13},{10,... | collective-permute-start | bytes 196616 | tf_op jit(solution)/shard_map/ppermute | solution.py:408
  12.0 0.7 %fusion.1 = f32[1,32]{1,0:T(1,128)S(1)} fusion(s32[32]{0:T(128)} %param.10, s32[1,32]{1,0:T(1,128)S(1)} %get-tuple-element.28), kind=kLoop, calls=%fused_computation.5 | loop fusion | flops 64 | bytes 384 | tf_op jit(solution)/shard_map/stack | solution.py:426
  12.6 0.7 %pad_maximum_fusion.levels_ref = f32[3,32]{1,0:T(4,128)S(1)} fusion(f32[1,32]{1,0:T(1,128)S(1)} %fusion.1, f32[1,32]{1,0:T(1,128)} %bitcast.10, f32[1,32]{1,0:T(1,128)} %bitcast.11), kind=kLoop, calls=%fused_computation.2 | loop fusion | flops 192 | bytes 768 | tf_op jit(solution)/shard_map/stack | solution.py:426
  13.3 0.7 %collective-permute-done.1.refs_1_ = bf16[2,16384]{1,0:T(2,128)(2,1)S(1)} collective-permute-done((bf16[2,16384]{1,0:T(2,128)(2,1)S(1)}, bf16[2,16384]{1,0:T(2,128)(2,1)S(1)}, u32[]{:S(2)}, u32[]{:S(2)}) %collective-permute-start.1) | collective-permute-done | bytes 65568 | tf_op jit(solution)/shard_map/ppermute | solution.py:408
  14.0 0.3 pack.2
  14.3 2.5 %collective-permute-start.5 = (bf16[4,16384]{1,0:T(4,128)(2,1)S(1)}, bf16[4,16384]{1,0:T(4,128)(2,1)S(1)}, u32[]{:S(2)}, u32[]{:S(2)}) collective-permute-start(bf16[4,16384]{1,0:T(4,128)(2,1)S(1)} %get-tuple-element.34), channel_id=1, source_target_pairs={{0,2},{1,3},{2,0},{3,1},{4,6},{5,7},{6,4},{7,5},{8,10},{9,11},{10,... | collective-permute-start | bytes 393224 | tf_op jit(solution)/shard_map/ppermute | solution.py:408
  16.8 0.9 %collective-permute-start.2 = (bf16[4,10240]{1,0:T(4,128)(2,1)S(1)}, bf16[4,10240]{1,0:T(4,128)(2,1)S(1)}, u32[]{:S(2)}, u32[]{:S(2)}) collective-permute-start(bf16[4,10240]{1,0:T(4,128)(2,1)S(1)} %get-tuple-element.31), channel_id=1, source_target_pairs={{0,17},{1,16},{2,19},{3,18},{4,21},{5,20},{6,23},{7,22},{8,25},{9,... | collective-permute-start | bytes 245768 | tf_op jit(solution)/shard_map/ppermute | solution.py:416
  17.7 0.3 collective-permute-start.3
  18.0 1.4 %collective-permute-start.4 = (bf16[4,10240]{1,0:T(4,128)(2,1)S(1)}, bf16[4,10240]{1,0:T(4,128)(2,1)S(1)}, u32[]{:S(2)}, u32[]{:S(2)}) collective-permute-start(bf16[4,10240]{1,0:T(4,128)(2,1)S(1)} %get-tuple-element.33), channel_id=1, source_target_pairs={{0,1},{1,0},{2,3},{3,2},{4,5},{5,4},{6,7},{7,6},{8,24},{9,25},{10,... | collective-permute-start | bytes 245768 | tf_op jit(solution)/shard_map/ppermute | solution.py:416
  19.4 0.9 %collective-permute-done.5.refs_0_ = bf16[4,16384]{1,0:T(4,128)(2,1)S(1)} collective-permute-done((bf16[4,16384]{1,0:T(4,128)(2,1)S(1)}, bf16[4,16384]{1,0:T(4,128)(2,1)S(1)}, u32[]{:S(2)}, u32[]{:S(2)}) %collective-permute-start.5) | collective-permute-done | bytes 131104 | tf_op jit(solution)/shard_map/ppermute | solution.py:408
  20.3 0.2 pack.3
  20.5 0.1 collective-permute-start.6
  20.6 2.0 %collective-permute-start.7 = (bf16[4,10240]{1,0:T(4,128)(2,1)S(1)}, bf16[4,10240]{1,0:T(4,128)(2,1)S(1)}, u32[]{:S(2)}, u32[]{:S(2)}) collective-permute-start(bf16[4,10240]{1,0:T(4,128)(2,1)S(1)} %get-tuple-element.37), channel_id=1, source_target_pairs={{0,16},{1,17},{2,18},{3,19},{4,20},{5,21},{6,22},{7,23},{8,9},{9,8... | collective-permute-start | bytes 245768 | tf_op jit(solution)/shard_map/ppermute | solution.py:416
  22.6 0.0 collective-permute-done.2.refs_1_
  22.6 1.1 %collective-permute-start.8 = (bf16[4,10240]{1,0:T(4,128)(2,1)S(1)}, bf16[4,10240]{1,0:T(4,128)(2,1)S(1)}, u32[]{:S(2)}, u32[]{:S(2)}) collective-permute-start(bf16[4,10240]{1,0:T(4,128)(2,1)S(1)} %get-tuple-element.38), channel_id=1, source_target_pairs={{0,1},{1,0},{2,3},{3,2},{4,5},{5,4},{6,7},{7,6},{8,24},{9,25},{10,... | collective-permute-start | bytes 245768 | tf_op jit(solution)/shard_map/ppermute | solution.py:416
  23.7 0.0 collective-permute-done.3.refs_2_
  23.7 0.0 collective-permute-done.4.refs_3_
  23.7 1.3 %collective-permute-done.6.refs_5_ = bf16[4,10240]{1,0:T(4,128)(2,1)S(1)} collective-permute-done((bf16[4,10240]{1,0:T(4,128)(2,1)S(1)}, bf16[4,10240]{1,0:T(4,128)(2,1)S(1)}, u32[]{:S(2)}, u32[]{:S(2)}) %collective-permute-start.6) | collective-permute-done | bytes 81952 | tf_op jit(solution)/shard_map/ppermute | solution.py:416
  25.0 1.8 %collective-permute-done.7.refs_6_ = bf16[4,10240]{1,0:T(4,128)(2,1)S(1)} collective-permute-done((bf16[4,10240]{1,0:T(4,128)(2,1)S(1)}, bf16[4,10240]{1,0:T(4,128)(2,1)S(1)}, u32[]{:S(2)}, u32[]{:S(2)}) %collective-permute-start.7) | collective-permute-done | bytes 81952 | tf_op jit(solution)/shard_map/ppermute | solution.py:416
  26.8 0.3 collective-permute-done.8.refs_7_
  27.1 0.2 join.1
  27.3 2.9 %collective-permute-start.9 = (bf16[32,6144]{1,0:T(8,128)(2,1)S(1)}, bf16[32,6144]{1,0:T(8,128)(2,1)S(1)}, u32[]{:S(2)}, u32[]{:S(2)}) collective-permute-start(bf16[32,6144]{1,0:T(8,128)(2,1)S(1)} %get-tuple-element.40), channel_id=1, source_target_pairs={{0,8},{8,0},{16,24},{24,16},{1,9},{9,1},{17,25},{25,17},{2,10},{10... | collective-permute-start | bytes 1179656 | tf_op jit(solution)/shard_map/ppermute | solution.py:408
  30.2 1.3 %collective-permute-done.9.refs_1_ = bf16[32,6144]{1,0:T(8,128)(2,1)S(1)} collective-permute-done((bf16[32,6144]{1,0:T(8,128)(2,1)S(1)}, bf16[32,6144]{1,0:T(8,128)(2,1)S(1)}, u32[]{:S(2)}, u32[]{:S(2)}) %collective-permute-start.9) | collective-permute-done | bytes 393248 | tf_op jit(solution)/shard_map/ppermute | solution.py:408
  31.5 11.4 %outer.1 = f32[4096,2048]{1,0:T(8,128)} custom-call(bf16[32,6144]{1,0:T(8,128)(2,1)S(1)} %get-tuple-element.39.refs_0_, bf16[32,6144]{1,0:T(8,128)(2,1)S(1)} %collective-permute-done.9.refs_1_), custom_call_target="tpu_custom_call" | custom-call | flops 10000000000 | bytes 30000000 | tf_op jit(solution)/shard_map/outer/pallas_call | solution.py:385
Async XLA Ops:
  0.0 6.5 %collective-permute-start = (bf16[1,48,2304]{2,1,0:T(8,128)(2,1)}, bf16[1,48,2304]{2,1,0:T(8,128)(2,1)S(1)}, u32[]{:S(2)}, u32[]{:S(2)}) collective-permute-start(bf16[1,48,2304]{2,1,0:T(8,128)(2,1)} %param.7), channel_id=1, source_target_pairs={{0,8},{8,16},{16,24},{24,0},{1,9},{9,17},{17,25},{25,1},{2,10},{10... | collective-permute-start | bytes 663560 | tf_op jit(solution)/shard_map/ppermute | solution.py:403
  4.5 0.9 %copy-start = (s32[3,8192]{1,0:T(4,128)S(1)}, s32[3,8192]{1,0:T(4,128)}, u32[]{:S(2)}) copy-start(s32[3,8192]{1,0:T(4,128)} %sphere_ref.1) | copy-start | bytes 294916
  9.6 4.4 %collective-permute-start.1 = (bf16[2,16384]{1,0:T(2,128)(2,1)S(1)}, bf16[2,16384]{1,0:T(2,128)(2,1)S(1)}, u32[]{:S(2)}, u32[]{:S(2)}) collective-permute-start(bf16[2,16384]{1,0:T(2,128)(2,1)S(1)} %get-tuple-element.29.refs_0_), channel_id=1, source_target_pairs={{0,4},{1,5},{2,6},{3,7},{4,0},{5,1},{6,2},{7,3},{8,12},{9,13},{10,... | collective-permute-start | bytes 196616 | tf_op jit(solution)/shard_map/ppermute | solution.py:408
  14.3 6.0 %collective-permute-start.5 = (bf16[4,16384]{1,0:T(4,128)(2,1)S(1)}, bf16[4,16384]{1,0:T(4,128)(2,1)S(1)}, u32[]{:S(2)}, u32[]{:S(2)}) collective-permute-start(bf16[4,16384]{1,0:T(4,128)(2,1)S(1)} %get-tuple-element.34), channel_id=1, source_target_pairs={{0,2},{1,3},{2,0},{3,1},{4,6},{5,7},{6,4},{7,5},{8,10},{9,11},{10,... | collective-permute-start | bytes 393224 | tf_op jit(solution)/shard_map/ppermute | solution.py:408
  16.8 5.8 %collective-permute-start.2 = (bf16[4,10240]{1,0:T(4,128)(2,1)S(1)}, bf16[4,10240]{1,0:T(4,128)(2,1)S(1)}, u32[]{:S(2)}, u32[]{:S(2)}) collective-permute-start(bf16[4,10240]{1,0:T(4,128)(2,1)S(1)} %get-tuple-element.31), channel_id=1, source_target_pairs={{0,17},{1,16},{2,19},{3,18},{4,21},{5,20},{6,23},{7,22},{8,25},{9,... | collective-permute-start | bytes 245768 | tf_op jit(solution)/shard_map/ppermute | solution.py:416
  17.7 6.1 %collective-permute-start.3 = (bf16[4,10240]{1,0:T(4,128)(2,1)S(1)}, bf16[4,10240]{1,0:T(4,128)(2,1)S(1)}, u32[]{:S(2)}, u32[]{:S(2)}) collective-permute-start(bf16[4,10240]{1,0:T(4,128)(2,1)S(1)} %get-tuple-element.32), channel_id=1, source_target_pairs={{0,16},{1,17},{2,18},{3,19},{4,20},{5,21},{6,22},{7,23},{8,9},{9,8... | collective-permute-start | bytes 245768 | tf_op jit(solution)/shard_map/ppermute | solution.py:416
  18.0 5.7 %collective-permute-start.4 = (bf16[4,10240]{1,0:T(4,128)(2,1)S(1)}, bf16[4,10240]{1,0:T(4,128)(2,1)S(1)}, u32[]{:S(2)}, u32[]{:S(2)}) collective-permute-start(bf16[4,10240]{1,0:T(4,128)(2,1)S(1)} %get-tuple-element.33), channel_id=1, source_target_pairs={{0,1},{1,0},{2,3},{3,2},{4,5},{5,4},{6,7},{7,6},{8,24},{9,25},{10,... | collective-permute-start | bytes 245768 | tf_op jit(solution)/shard_map/ppermute | solution.py:416
  20.5 4.5 %collective-permute-start.6 = (bf16[4,10240]{1,0:T(4,128)(2,1)S(1)}, bf16[4,10240]{1,0:T(4,128)(2,1)S(1)}, u32[]{:S(2)}, u32[]{:S(2)}) collective-permute-start(bf16[4,10240]{1,0:T(4,128)(2,1)S(1)} %get-tuple-element.36), channel_id=1, source_target_pairs={{0,17},{1,16},{2,19},{3,18},{4,21},{5,20},{6,23},{7,22},{8,25},{9,... | collective-permute-start | bytes 245768 | tf_op jit(solution)/shard_map/ppermute | solution.py:416
  20.6 6.2 %collective-permute-start.7 = (bf16[4,10240]{1,0:T(4,128)(2,1)S(1)}, bf16[4,10240]{1,0:T(4,128)(2,1)S(1)}, u32[]{:S(2)}, u32[]{:S(2)}) collective-permute-start(bf16[4,10240]{1,0:T(4,128)(2,1)S(1)} %get-tuple-element.37), channel_id=1, source_target_pairs={{0,16},{1,17},{2,18},{3,19},{4,20},{5,21},{6,22},{7,23},{8,9},{9,8... | collective-permute-start | bytes 245768 | tf_op jit(solution)/shard_map/ppermute | solution.py:416
  22.6 4.5 %collective-permute-start.8 = (bf16[4,10240]{1,0:T(4,128)(2,1)S(1)}, bf16[4,10240]{1,0:T(4,128)(2,1)S(1)}, u32[]{:S(2)}, u32[]{:S(2)}) collective-permute-start(bf16[4,10240]{1,0:T(4,128)(2,1)S(1)} %get-tuple-element.38), channel_id=1, source_target_pairs={{0,1},{1,0},{2,3},{3,2},{4,5},{5,4},{6,7},{7,6},{8,24},{9,25},{10,... | collective-permute-start | bytes 245768 | tf_op jit(solution)/shard_map/ppermute | solution.py:416
  27.3 4.2 %collective-permute-start.9 = (bf16[32,6144]{1,0:T(8,128)(2,1)S(1)}, bf16[32,6144]{1,0:T(8,128)(2,1)S(1)}, u32[]{:S(2)}, u32[]{:S(2)}) collective-permute-start(bf16[32,6144]{1,0:T(8,128)(2,1)S(1)} %get-tuple-element.40), channel_id=1, source_target_pairs={{0,8},{8,0},{16,24},{24,16},{1,9},{9,1},{17,25},{25,17},{2,10},{10... | collective-permute-start | bytes 1179656 | tf_op jit(solution)/shard_map/ppermute | solution.py:408

commit v16 on v14

--- a/solution.py
+++ b/solution.py
@@ -279,17 +279,15 @@
     )(orbitals, occ_second, *handed)
 
 
-def pack_kernel(plan, turns, targets, merged, levels_ref, *refs):
+def pack_kernel(plan, turns, targets, levels_ref, *refs):
     rows, cols, row_width, col_width = plan
-    count = len(refs) - len(targets) - 1 - merged
+    count = len(refs) - len(targets) - 1
     arrived, outs, mixed_ref = refs[:count], refs[count:-1], refs[-1]
     r, c = own_place()
     first = 0
     for ref in arrived:
         mixed_ref[first : first + ref.shape[0], :] = ref[...].astype(jnp.float32)
         first += ref.shape[0]
-    if merged:
-        outs[-1][...] = mixed_ref[...].astype(jnp.bfloat16)
     weight = pair_weights([c ^ turn for turn in turns], levels_ref)
     columns = []
     for side in range(2):
@@ -301,13 +299,13 @@
         out_ref[:, 2 * row_width :] = columns[side]
 
 
-def pack(arrived, levels, turns, targets, merged, plan):
+def pack(arrived, levels, turns, targets, plan):
     rows, cols, row_width, col_width = plan
     pairs = STEPS * len(turns)
     entries = arrived[0].shape[1]
-    shapes = [(pairs, 2 * row_width + col_width)] * len(targets) + [(pairs, entries)] * merged
+    shapes = [(pairs, 2 * row_width + col_width)] * len(targets)
     return pl.pallas_call(
-        functools.partial(pack_kernel, plan, turns, targets, merged),
+        functools.partial(pack_kernel, plan, turns, targets),
         out_shape=[jax.ShapeDtypeStruct(shape, jnp.bfloat16) for shape in shapes],
         in_specs=in_vmem(1 + len(arrived)),
         out_specs=in_vmem(len(shapes)),
@@ -400,6 +398,22 @@
     )(*messages)
 
 
+def copy_kernel(value_ref, behind_ref, out_ref):
+    out_ref[...] = value_ref[...]
+
+
+def copied(value, behind):
+    return pl.pallas_call(
+        copy_kernel,
+        out_shape=jax.ShapeDtypeStruct(value.shape, value.dtype),
+        in_specs=in_vmem(2),
+        out_specs=in_vmem(1)[0],
+        compiler_params=pltpu.CompilerParams(vmem_limit_bytes=VMEM_LIMIT),
+        cost_estimate=cost(10**6, 10**5),
+        name="copied",
+    )(value, behind)
+
+
 def shifted(value, axis, by):
     devices = lax.axis_size(axis)
     return lax.ppermute(value, axis, [(i, (i + by) % devices) for i in range(devices)])
@@ -429,17 +443,17 @@
     def sent(packed):
         return [packed[0]] + [sent_across(value, *target, rows, cols) for value, target in zip(packed[1:], targets[1:])]
 
-    held, turns, bit = [own], [0], cols // 2
+    others, other_turns, bit = [], [], cols // 2
     while bit > 2:
-        if len(held) > 1:
-            held = [jnp.concatenate(held, axis=0)]
-        held.append(turned(held[0], "col", bit))
-        turns += [turn + bit for turn in turns]
+        held = jnp.concatenate([own, *others], axis=0) if others else own
+        others.append(turned(held, "col", bit))
+        other_turns += [turn + bit for turn in [0, *other_turns]]
         bit //= 2
-    *packed, merged = pack(held, levels, turns, targets, 1, plan)
-    messages = sent(packed)
-    far = turned(merged, "col", bit)
-    messages += sent(pack([far], levels, [turn + bit for turn in turns], targets, 0, plan))
+    turns = [0, *other_turns]
+    messages = sent(pack([own, *others], levels, turns, targets, plan))
+    relayed = turned(jnp.concatenate(others, axis=0) if len(others) > 1 else others[0], "col", bit)
+    beside = turned(copied(own, levels), "col", bit)
+    messages += sent(pack([beside, relayed], levels, [turn + bit for turn in turns], targets, plan))
     kept, passed = join(messages, plan)
     return outer([kept, turned(passed, "row", 1)], plan)
 

time: 43.4 us -> 42.1 us (0.970)
  waiting for transfers between devices: 6.56 us -> 5.29 us
    ppermute x3 -> x4, waiting for transfers between devices: 2.98 us -> 1.36 us  [turned(): return lax.ppermute(value, axis, [(i, i ^ turn) for i in range(devices)])]
    ppermute x3 -> x4, starting transfers between devices: 7.54 us -> 7.94 us  [turned(): return lax.ppermute(value, axis, [(i, i ^ turn) for i in range(devices)])]
  transfers between devices with their start and end apart: 10 -> 11, of which waited for: 6 -> 5; matrix products, arithmetic and copies ran while one was open for 8% -> 8% of each run, Pallas kernels for 3% -> 4%
where the time goes in v16:
time: 42.1 us; the launch traced here: 41.6 us
  Pallas kernels  16.1 us (38%)
  starting transfers between devices  16 us (38%)
  waiting for transfers between devices  5.29 us (13%)
  local copies, waits for them, and re-layouts  2.8 us (7%)
  other arithmetic  1.34 us (3%)
    pallas_call x1, Pallas kernels, outer(): pl.pallas_call(functools.partial(outer_kernel, row_width, block, slots),...  11.4 us
    ppermute x4, starting transfers between devices, turned(): return lax.ppermute(value, axis, [(i, i ^ turn) for i in range(devices)])  7.94 us
    ppermute x6, starting transfers between devices, sent_across(): return lax.ppermute(value, ('row', 'col'), moves)  5.43 us
    ppermute x6, waiting for transfers between devices, sent_across(): return lax.ppermute(value, ('row', 'col'), moves)  3.93 us
    pallas_call x1, Pallas kernels, transform(): pl.pallas_call(functools.partial(second_kernel, grid), out_shape=[jax.Sha...  3.05 us
    ppermute x1, starting transfers between devices, shifted(): lax.ppermute(value, axis, [(i, (i + by) % devices) for i in range(devices)])  2.63 us
    unnamed x3, local copies, waits for them, and re-layouts  1.85 us
    ppermute x4, waiting for transfers between devices, turned(): return lax.ppermute(value, axis, [(i, i ^ turn) for i in range(devices)])  1.36 us
  transfers between devices with their start and end apart: 11, of which 5 were waited for; matrix products, arithmetic and copies ran while one was open for 8% of the time, Pallas kernels for 4%

profile of v16, /device:TPU:1, one launch (start us, length us, event | category | flops | bytes accessed | tf_op | source)
XLA Modules:
  0.0 41.6 jit_solution(11242151199778682529)
XLA Ops:
  0.0 2.6 %collective-permute-start = (bf16[1,48,2304]{2,1,0:T(8,128)(2,1)}, bf16[1,48,2304]{2,1,0:T(8,128)(2,1)S(1)}, u32[]{:S(2)}, u32[]{:S(2)}) collective-permute-start(bf16[1,48,2304]{2,1,0:T(8,128)(2,1)} %param.7), channel_id=1, source_target_pairs={{0,8},{8,16},{16,24},{24,0},{1,9},{9,17},{17,25},{25,1},{2,10},{10... | collective-permute-start | bytes 663560 | tf_op jit(solution)/shard_map/ppermute | solution.py:419
  2.6 0.9 %constant_dynamic-update-slice_fusion.1 = bf16[2,48,2304]{2,1,0:T(8,128)(2,1)S(1)} fusion(bf16[1,48,2304]{2,1,0:T(8,128)(2,1)} %param.6), kind=kLoop, calls=%fused_computation.1 | loop fusion | bytes 442368
  3.6 1.0 %constant_dynamic-update-slice_fusion.orbitals_ref = bf16[2,48,2304]{2,1,0:T(8,128)(2,1)S(1)} fusion(bf16[2,48,2304]{2,1,0:T(8,128)(2,1)S(1)} %constant_dynamic-update-slice_fusion.1, bf16[1,48,2304]{2,1,0:T(8,128)(2,1)} %param.7), kind=kLoop, calls=%fused_computation | loop fusion | bytes 442368 | tf_op jit(solution)/shard_map/concatenate | solution.py:248
  4.5 0.0 copy-start
  4.6 0.9 %copy-done = s32[3,8192]{1,0:T(4,128)S(1)} copy-done((s32[3,8192]{1,0:T(4,128)S(1)}, s32[3,8192]{1,0:T(4,128)}, u32[]{:S(2)}) %copy-start) | copy-done | bytes 98328
  5.4 1.1 %first_pair.1 = (bf16[1,16384]{1,0:T(2,128)(2,1)S(1)}, s32[2,8192]{1,0:T(2,128)S(1)}, bf16[1616,128]{1,0:T(8,128)(2,1)S(1)}, f32[16,384]{1,0:T(8,128)S(1)}, bf16[240,256]{1,0:T(8,128)(2,1)S(1)}) custom-call(bf16[2,48,2304]{2,1,0:T(8,128)(2,1)S(1)} %constant_dynamic-update-slice_fusion.orbitals_ref, s32[3,8192]{1,0:T(4,128)S(1)} %copy-done), custom_call_target="tpu_custom_call" | custom-call | flops 2000000000 | bytes 2000000 | tf_op jit(solution)/shard_map/first_pair/pallas_call | solution.py:254
  6.5 0.0 collective-permute-done.occ_ref
  6.5 3.1 %second_pair.1 = (bf16[2,16384]{1,0:T(2,128)(2,1)S(1)}, s32[1,32]{1,0:T(1,128)S(1)}) custom-call(bf16[2,48,2304]{2,1,0:T(8,128)(2,1)S(1)} %constant_dynamic-update-slice_fusion.orbitals_ref, bf16[1,48,2304]{2,1,0:T(8,128)(2,1)S(1)} %collective-permute-done.occ_ref, bf16[1,16384]{1,0:T(2,128)(2,1)S(1)} %get-tuple-element.22.first_ref, ...), custom_call_target="tpu_custom_call" | custom-call | flops 2000000000 | bytes 2000000 | tf_op jit(solution)/shard_map/second_pair/pallas_call | solution.py:268
  9.6 2.4 %collective-permute-start.1 = (bf16[2,16384]{1,0:T(2,128)(2,1)S(1)}, bf16[2,16384]{1,0:T(2,128)(2,1)S(1)}, u32[]{:S(2)}, u32[]{:S(2)}) collective-permute-start(bf16[2,16384]{1,0:T(2,128)(2,1)S(1)} %get-tuple-element.28.refs_0_.value_ref), channel_id=1, source_target_pairs={{0,4},{1,5},{2,6},{3,7},{4,0},{5,1},{6,2},{7,3},{8,12},{9,13},{10,... | collective-permute-start | bytes 196616 | tf_op jit(solution)/shard_map/ppermute | solution.py:424
  12.0 0.7 %fusion.1 = f32[1,32]{1,0:T(1,128)S(1)} fusion(s32[32]{0:T(128)} %param.10, s32[1,32]{1,0:T(1,128)S(1)} %get-tuple-element.27), kind=kLoop, calls=%fused_computation.5 | loop fusion | flops 64 | bytes 384 | tf_op jit(solution)/shard_map/stack | solution.py:439
  12.6 0.7 %pad_maximum_fusion.levels_ref.behind_ref = f32[3,32]{1,0:T(4,128)S(1)} fusion(f32[1,32]{1,0:T(1,128)S(1)} %fusion.1, f32[1,32]{1,0:T(1,128)} %bitcast.10, f32[1,32]{1,0:T(1,128)} %bitcast.11), kind=kLoop, calls=%fused_computation.2 | loop fusion | flops 192 | bytes 768 | tf_op jit(solution)/shard_map/stack | solution.py:439
  13.3 1.4 %collective-permute-start.5 = (bf16[2,16384]{1,0:T(2,128)(2,1)S(1)}, bf16[2,16384]{1,0:T(2,128)(2,1)S(1)}, u32[]{:S(2)}, u32[]{:S(2)}) collective-permute-start(bf16[2,16384]{1,0:T(2,128)(2,1)S(1)} %copied.1), channel_id=1, source_target_pairs={{0,2},{1,3},{2,0},{3,1},{4,6},{5,7},{6,4},{7,5},{8,10},{9,11},{10,... | collective-permute-start | bytes 196616 | tf_op jit(solution)/shard_map/ppermute | solution.py:424
  14.7 0.0 collective-permute-done.1.refs_1_
  14.7 1.8 %collective-permute-start.6 = (bf16[2,16384]{1,0:T(2,128)(2,1)S(1)}, bf16[2,16384]{1,0:T(2,128)(2,1)S(1)}, u32[]{:S(2)}, u32[]{:S(2)}) collective-permute-start(bf16[2,16384]{1,0:T(2,128)(2,1)S(1)} %collective-permute-done.1.refs_1_), channel_id=1, source_target_pairs={{0,2},{1,3},{2,0},{3,1},{4,6},{5,7},{6,4},{7,5},{8,10},{9,11},{10,... | collective-permute-start | bytes 196616 | tf_op jit(solution)/shard_map/ppermute | solution.py:424
  16.5 0.2 pack.2
  16.7 0.9 %collective-permute-start.2 = (bf16[4,10240]{1,0:T(4,128)(2,1)S(1)}, bf16[4,10240]{1,0:T(4,128)(2,1)S(1)}, u32[]{:S(2)}, u32[]{:S(2)}) collective-permute-start(bf16[4,10240]{1,0:T(4,128)(2,1)S(1)} %get-tuple-element.30), channel_id=1, source_target_pairs={{0,17},{1,16},{2,19},{3,18},{4,21},{5,20},{6,23},{7,22},{8,25},{9,... | collective-permute-start | bytes 245768 | tf_op jit(solution)/shard_map/ppermute | solution.py:429
  17.6 1.6 %collective-permute-start.3 = (bf16[4,10240]{1,0:T(4,128)(2,1)S(1)}, bf16[4,10240]{1,0:T(4,128)(2,1)S(1)}, u32[]{:S(2)}, u32[]{:S(2)}) collective-permute-start(bf16[4,10240]{1,0:T(4,128)(2,1)S(1)} %get-tuple-element.31), channel_id=1, source_target_pairs={{0,16},{1,17},{2,18},{3,19},{4,20},{5,21},{6,22},{7,23},{8,24},{9,... | collective-permute-start | bytes 245768 | tf_op jit(solution)/shard_map/ppermute | solution.py:429
  19.2 0.3 collective-permute-start.4
  19.4 0.0 collective-permute-done.5.refs_0_
  19.4 0.0 collective-permute-done.6.refs_1_
  19.4 0.2 pack.3
  19.6 1.0 %collective-permute-start.7 = (bf16[4,10240]{1,0:T(4,128)(2,1)S(1)}, bf16[4,10240]{1,0:T(4,128)(2,1)S(1)}, u32[]{:S(2)}, u32[]{:S(2)}) collective-permute-start(bf16[4,10240]{1,0:T(4,128)(2,1)S(1)} %get-tuple-element.34), channel_id=1, source_target_pairs={{0,17},{1,16},{2,19},{3,18},{4,21},{5,20},{6,23},{7,22},{8,25},{9,... | collective-permute-start | bytes 245768 | tf_op jit(solution)/shard_map/ppermute | solution.py:429
  20.6 1.5 %collective-permute-start.8 = (bf16[4,10240]{1,0:T(4,128)(2,1)S(1)}, bf16[4,10240]{1,0:T(4,128)(2,1)S(1)}, u32[]{:S(2)}, u32[]{:S(2)}) collective-permute-start(bf16[4,10240]{1,0:T(4,128)(2,1)S(1)} %get-tuple-element.35), channel_id=1, source_target_pairs={{0,16},{1,17},{2,18},{3,19},{4,20},{5,21},{6,22},{7,23},{8,24},{9,... | collective-permute-start | bytes 245768 | tf_op jit(solution)/shard_map/ppermute | solution.py:429
  22.1 0.0 collective-permute-done.2.refs_1_
  22.1 0.3 collective-permute-start.9
  22.3 1.2 %collective-permute-done.3.refs_2_ = bf16[4,10240]{1,0:T(4,128)(2,1)S(1)} collective-permute-done((bf16[4,10240]{1,0:T(4,128)(2,1)S(1)}, bf16[4,10240]{1,0:T(4,128)(2,1)S(1)}, u32[]{:S(2)}, u32[]{:S(2)}) %collective-permute-start.3) | collective-permute-done | bytes 81952 | tf_op jit(solution)/shard_map/ppermute | solution.py:429
  23.6 0.0 collective-permute-done.4.refs_3_
  23.6 1.0 %collective-permute-done.7.refs_5_ = bf16[4,10240]{1,0:T(4,128)(2,1)S(1)} collective-permute-done((bf16[4,10240]{1,0:T(4,128)(2,1)S(1)}, bf16[4,10240]{1,0:T(4,128)(2,1)S(1)}, u32[]{:S(2)}, u32[]{:S(2)}) %collective-permute-start.7) | collective-permute-done | bytes 81952 | tf_op jit(solution)/shard_map/ppermute | solution.py:429
  24.6 1.4 %collective-permute-done.8.refs_6_ = bf16[4,10240]{1,0:T(4,128)(2,1)S(1)} collective-permute-done((bf16[4,10240]{1,0:T(4,128)(2,1)S(1)}, bf16[4,10240]{1,0:T(4,128)(2,1)S(1)}, u32[]{:S(2)}, u32[]{:S(2)}) %collective-permute-start.8) | collective-permute-done | bytes 81952 | tf_op jit(solution)/shard_map/ppermute | solution.py:429
  25.9 0.3 collective-permute-done.9.refs_7_
  26.3 0.2 join.1
  26.4 2.4 %collective-permute-start.10 = (bf16[32,6144]{1,0:T(8,128)(2,1)S(1)}, bf16[32,6144]{1,0:T(8,128)(2,1)S(1)}, u32[]{:S(2)}, u32[]{:S(2)}) collective-permute-start(bf16[32,6144]{1,0:T(8,128)(2,1)S(1)} %get-tuple-element.38), channel_id=1, source_target_pairs={{0,8},{8,0},{16,24},{24,16},{1,9},{9,1},{17,25},{25,17},{2,10},{10... | collective-permute-start | bytes 1179656 | tf_op jit(solution)/shard_map/ppermute | solution.py:424
  28.8 1.3 %collective-permute-done.10.refs_1_ = bf16[32,6144]{1,0:T(8,128)(2,1)S(1)} collective-permute-done((bf16[32,6144]{1,0:T(8,128)(2,1)S(1)}, bf16[32,6144]{1,0:T(8,128)(2,1)S(1)}, u32[]{:S(2)}, u32[]{:S(2)}) %collective-permute-start.10) | collective-permute-done | bytes 393248 | tf_op jit(solution)/shard_map/ppermute | solution.py:424
  30.2 11.4 %outer.1 = f32[4096,2048]{1,0:T(8,128)} custom-call(bf16[32,6144]{1,0:T(8,128)(2,1)S(1)} %get-tuple-element.37.refs_0_, bf16[32,6144]{1,0:T(8,128)(2,1)S(1)} %collective-permute-done.10.refs_1_), custom_call_target="tpu_custom_call" | custom-call | flops 10000000000 | bytes 30000000 | tf_op jit(solution)/shard_map/outer/pallas_call | solution.py:385
  (1 shorter events, 0.0 us)
Async XLA Ops:
  0.0 6.5 %collective-permute-start = (bf16[1,48,2304]{2,1,0:T(8,128)(2,1)}, bf16[1,48,2304]{2,1,0:T(8,128)(2,1)S(1)}, u32[]{:S(2)}, u32[]{:S(2)}) collective-permute-start(bf16[1,48,2304]{2,1,0:T(8,128)(2,1)} %param.7), channel_id=1, source_target_pairs={{0,8},{8,16},{16,24},{24,0},{1,9},{9,17},{17,25},{25,1},{2,10},{10... | collective-permute-start | bytes 663560 | tf_op jit(solution)/shard_map/ppermute | solution.py:419
  4.5 0.9 %copy-start = (s32[3,8192]{1,0:T(4,128)S(1)}, s32[3,8192]{1,0:T(4,128)}, u32[]{:S(2)}) copy-start(s32[3,8192]{1,0:T(4,128)} %sphere_ref.1) | copy-start | bytes 294916
  9.6 5.1 %collective-permute-start.1 = (bf16[2,16384]{1,0:T(2,128)(2,1)S(1)}, bf16[2,16384]{1,0:T(2,128)(2,1)S(1)}, u32[]{:S(2)}, u32[]{:S(2)}) collective-permute-start(bf16[2,16384]{1,0:T(2,128)(2,1)S(1)} %get-tuple-element.28.refs_0_.value_ref), channel_id=1, source_target_pairs={{0,4},{1,5},{2,6},{3,7},{4,0},{5,1},{6,2},{7,3},{8,12},{9,13},{10,... | collective-permute-start | bytes 196616 | tf_op jit(solution)/shard_map/ppermute | solution.py:424
  13.3 6.1 %collective-permute-start.5 = (bf16[2,16384]{1,0:T(2,128)(2,1)S(1)}, bf16[2,16384]{1,0:T(2,128)(2,1)S(1)}, u32[]{:S(2)}, u32[]{:S(2)}) collective-permute-start(bf16[2,16384]{1,0:T(2,128)(2,1)S(1)} %copied.1), channel_id=1, source_target_pairs={{0,2},{1,3},{2,0},{3,1},{4,6},{5,7},{6,4},{7,5},{8,10},{9,11},{10,... | collective-permute-start | bytes 196616 | tf_op jit(solution)/shard_map/ppermute | solution.py:424
  14.7 4.7 %collective-permute-start.6 = (bf16[2,16384]{1,0:T(2,128)(2,1)S(1)}, bf16[2,16384]{1,0:T(2,128)(2,1)S(1)}, u32[]{:S(2)}, u32[]{:S(2)}) collective-permute-start(bf16[2,16384]{1,0:T(2,128)(2,1)S(1)} %collective-permute-done.1.refs_1_), channel_id=1, source_target_pairs={{0,2},{1,3},{2,0},{3,1},{4,6},{5,7},{6,4},{7,5},{8,10},{9,11},{10,... | collective-permute-start | bytes 196616 | tf_op jit(solution)/shard_map/ppermute | solution.py:424
  16.7 5.4 %collective-permute-start.2 = (bf16[4,10240]{1,0:T(4,128)(2,1)S(1)}, bf16[4,10240]{1,0:T(4,128)(2,1)S(1)}, u32[]{:S(2)}, u32[]{:S(2)}) collective-permute-start(bf16[4,10240]{1,0:T(4,128)(2,1)S(1)} %get-tuple-element.30), channel_id=1, source_target_pairs={{0,17},{1,16},{2,19},{3,18},{4,21},{5,20},{6,23},{7,22},{8,25},{9,... | collective-permute-start | bytes 245768 | tf_op jit(solution)/shard_map/ppermute | solution.py:429
  17.6 6.0 %collective-permute-start.3 = (bf16[4,10240]{1,0:T(4,128)(2,1)S(1)}, bf16[4,10240]{1,0:T(4,128)(2,1)S(1)}, u32[]{:S(2)}, u32[]{:S(2)}) collective-permute-start(bf16[4,10240]{1,0:T(4,128)(2,1)S(1)} %get-tuple-element.31), channel_id=1, source_target_pairs={{0,16},{1,17},{2,18},{3,19},{4,20},{5,21},{6,22},{7,23},{8,24},{9,... | collective-permute-start | bytes 245768 | tf_op jit(solution)/shard_map/ppermute | solution.py:429
  19.2 4.4 %collective-permute-start.4 = (bf16[4,10240]{1,0:T(4,128)(2,1)S(1)}, bf16[4,10240]{1,0:T(4,128)(2,1)S(1)}, u32[]{:S(2)}, u32[]{:S(2)}) collective-permute-start(bf16[4,10240]{1,0:T(4,128)(2,1)S(1)} %get-tuple-element.32), channel_id=1, source_target_pairs={{0,1},{1,0},{2,3},{3,2},{4,5},{5,4},{6,7},{7,6},{8,9},{9,8},{10,11... | collective-permute-start | bytes 245768 | tf_op jit(solution)/shard_map/ppermute | solution.py:429
  19.6 5.0 %collective-permute-start.7 = (bf16[4,10240]{1,0:T(4,128)(2,1)S(1)}, bf16[4,10240]{1,0:T(4,128)(2,1)S(1)}, u32[]{:S(2)}, u32[]{:S(2)}) collective-permute-start(bf16[4,10240]{1,0:T(4,128)(2,1)S(1)} %get-tuple-element.34), channel_id=1, source_target_pairs={{0,17},{1,16},{2,19},{3,18},{4,21},{5,20},{6,23},{7,22},{8,25},{9,... | collective-permute-start | bytes 245768 | tf_op jit(solution)/shard_map/ppermute | solution.py:429
  20.6 5.3 %collective-permute-start.8 = (bf16[4,10240]{1,0:T(4,128)(2,1)S(1)}, bf16[4,10240]{1,0:T(4,128)(2,1)S(1)}, u32[]{:S(2)}, u32[]{:S(2)}) collective-permute-start(bf16[4,10240]{1,0:T(4,128)(2,1)S(1)} %get-tuple-element.35), channel_id=1, source_target_pairs={{0,16},{1,17},{2,18},{3,19},{4,20},{5,21},{6,22},{7,23},{8,24},{9,... | collective-permute-start | bytes 245768 | tf_op jit(solution)/shard_map/ppermute | solution.py:429
  22.1 4.2 %collective-permute-start.9 = (bf16[4,10240]{1,0:T(4,128)(2,1)S(1)}, bf16[4,10240]{1,0:T(4,128)(2,1)S(1)}, u32[]{:S(2)}, u32[]{:S(2)}) collective-permute-start(bf16[4,10240]{1,0:T(4,128)(2,1)S(1)} %get-tuple-element.36), channel_id=1, source_target_pairs={{0,1},{1,0},{2,3},{3,2},{4,5},{5,4},{6,7},{7,6},{8,9},{9,8},{10,11... | collective-permute-start | bytes 245768 | tf_op jit(solution)/shard_map/ppermute | solution.py:429
  26.4 3.7 %collective-permute-start.10 = (bf16[32,6144]{1,0:T(8,128)(2,1)S(1)}, bf16[32,6144]{1,0:T(8,128)(2,1)S(1)}, u32[]{:S(2)}, u32[]{:S(2)}) collective-permute-start(bf16[32,6144]{1,0:T(8,128)(2,1)S(1)} %get-tuple-element.38), channel_id=1, source_target_pairs={{0,8},{8,0},{16,24},{24,16},{1,9},{9,1},{17,25},{25,17},{2,10},{10... | collective-permute-start | bytes 1179656 | tf_op jit(solution)/shard_map/ppermute | solution.py:424

commit v17 on v16

--- a/solution.py
+++ b/solution.py
@@ -245,7 +245,8 @@
     grid = cond_orbitals.shape[1]
     half_count = sphere_index.shape[1]
     width, _, table_count = table_rows(grid)
-    orbitals = jnp.concatenate([cond_orbitals, occ_orbitals], axis=0)
+    which = lax.broadcasted_iota(jnp.int32, (2, *cond_orbitals.shape[1:]), 0)
+    orbitals = jnp.where(which == 0, cond_orbitals, occ_orbitals)
     picks = RADIX * KX_ROWS
     params = dict(
         compiler_params=pltpu.CompilerParams(vmem_limit_bytes=VMEM_LIMIT),

time: 42.1 us -> 41.3 us (0.981)
  local copies, waits for them, and re-layouts: 2.8 us -> 0.9 us
  waiting for transfers between devices: 5.29 us -> 6.82 us
  starting transfers between devices: 16 us -> 14.5 us
  other arithmetic: 1.34 us -> 2.49 us
    ppermute x4, starting transfers between devices: 7.94 us -> 6.45 us  [turned(): return lax.ppermute(value, axis, [(i, i ^ turn) for i in range(devices)])]
    select_n x0 -> x1, other arithmetic: none -> 1.15 us  [transform(): orbitals = jnp.where(which == 0, cond_orbitals, occ_orbitals)]
    ppermute x4, waiting for transfers between devices: 1.36 us -> 2.48 us  [turned(): return lax.ppermute(value, axis, [(i, i ^ turn) for i in range(devices)])]
    concatenate x1 -> x0, local copies, waits for them, and re-layouts: 0.95 us -> none  [transform(): orbitals = jnp.concatenate([cond_orbitals, occ_orbitals], axis=0)]
    unnamed x3 -> x2, local copies, waits for them, and re-layouts: 1.85 us -> 0.9 us
  transfers between devices with their start and end apart: 11 -> 11, of which waited for: 5 -> 8; matrix products, arithmetic and copies ran while one was open for 8% -> 6% of each run, Pallas kernels for 4% -> 4%
where the time goes in v17:
time: 41.3 us; the launch traced here: 40.8 us
  Pallas kernels  16.1 us (39%)
  starting transfers between devices  14.5 us (35%)
  waiting for transfers between devices  6.82 us (17%)
  other arithmetic  2.49 us (6%)
  local copies, waits for them, and re-layouts  0.9 us (2%)
    pallas_call x1, Pallas kernels, outer(): pl.pallas_call(functools.partial(outer_kernel, row_width, block, slots),...  11.4 us
    ppermute x4, starting transfers between devices, turned(): return lax.ppermute(value, axis, [(i, i ^ turn) for i in range(devices)])  6.45 us
    ppermute x6, starting transfers between devices, sent_across(): return lax.ppermute(value, ('row', 'col'), moves)  5.42 us
    ppermute x6, waiting for transfers between devices, sent_across(): return lax.ppermute(value, ('row', 'col'), moves)  4.29 us
    pallas_call x1, Pallas kernels, transform(): pl.pallas_call(functools.partial(second_kernel, grid), out_shape=[jax.Sha...  3.05 us
    ppermute x1, starting transfers between devices, shifted(): lax.ppermute(value, axis, [(i, (i + by) % devices) for i in range(devices)])  2.63 us
    ppermute x4, waiting for transfers between devices, turned(): return lax.ppermute(value, axis, [(i, i ^ turn) for i in range(devices)])  2.48 us
    another operation x2, other arithmetic, on_device(): jnp.stack([cond_energy, occ_energy, (occ_band + later[0]).astype(jnp.floa...  1.34 us
  transfers between devices with their start and end apart: 11, of which 8 were waited for; matrix products, arithmetic and copies ran while one was open for 6% of the time, Pallas kernels for 4%

profile of v17, /device:TPU:1, one launch (start us, length us, event | category | flops | bytes accessed | tf_op | source)
XLA Modules:
  0.0 40.8 jit_solution(11109764272305774834)
XLA Ops:
  0.0 2.6 %collective-permute-start = (bf16[1,48,2304]{2,1,0:T(8,128)(2,1)}, bf16[1,48,2304]{2,1,0:T(8,128)(2,1)S(1)}, u32[]{:S(2)}, u32[]{:S(2)}) collective-permute-start(bf16[1,48,2304]{2,1,0:T(8,128)(2,1)} %param.7), channel_id=1, source_target_pairs={{0,8},{8,16},{16,24},{24,0},{1,9},{9,17},{17,25},{25,1},{2,10},{10... | collective-permute-start | bytes 663560 | tf_op jit(solution)/shard_map/ppermute | solution.py:420
  2.6 1.2 %broadcast_select_fusion.orbitals_ref = bf16[2,48,2304]{2,1,0:T(8,128)(2,1)S(1)} fusion(pred[2]{0:T(512)(128)(4,1)S(1)} %iota_compare_fusion, bf16[48,2304]{1,0:T(8,128)(2,1)} %bitcast.13, bf16[48,2304]{1,0:T(8,128)(2,1)} %bitcast.12), kind=kLoop, calls=%fused_computation | loop fusion | flops 221184 | bytes 884738 | tf_op jit(solution)/shard_map/jit(_where)/select_n | solution.py:249
  3.8 0.0 copy-start
  3.8 0.9 %copy-done = s32[3,8192]{1,0:T(4,128)S(1)} copy-done((s32[3,8192]{1,0:T(4,128)S(1)}, s32[3,8192]{1,0:T(4,128)}, u32[]{:S(2)}) %copy-start) | copy-done | bytes 98328
  4.7 1.1 %first_pair.1 = (bf16[1,16384]{1,0:T(2,128)(2,1)S(1)}, s32[2,8192]{1,0:T(2,128)S(1)}, bf16[1616,128]{1,0:T(8,128)(2,1)S(1)}, f32[16,384]{1,0:T(8,128)S(1)}, bf16[240,256]{1,0:T(8,128)(2,1)S(1)}) custom-call(bf16[2,48,2304]{2,1,0:T(8,128)(2,1)S(1)} %broadcast_select_fusion.orbitals_ref, s32[3,8192]{1,0:T(4,128)S(1)} %copy-done), custom_call_target="tpu_custom_call" | custom-call | flops 2000000000 | bytes 2000000 | tf_op jit(solution)/shard_map/first_pair/pallas_call | solution.py:255
  5.8 0.1 collective-permute-done.occ_ref
  5.8 3.1 %second_pair.1 = (bf16[2,16384]{1,0:T(2,128)(2,1)S(1)}, s32[1,32]{1,0:T(1,128)S(1)}) custom-call(bf16[2,48,2304]{2,1,0:T(8,128)(2,1)S(1)} %broadcast_select_fusion.orbitals_ref, bf16[1,48,2304]{2,1,0:T(8,128)(2,1)S(1)} %collective-permute-done.occ_ref, bf16[1,16384]{1,0:T(2,128)(2,1)S(1)} %get-tuple-element.22.first_ref, ...), custom_call_target="tpu_custom_call" | custom-call | flops 2000000000 | bytes 2000000 | tf_op jit(solution)/shard_map/second_pair/pallas_call | solution.py:269
  8.9 2.4 %collective-permute-start.1 = (bf16[2,16384]{1,0:T(2,128)(2,1)S(1)}, bf16[2,16384]{1,0:T(2,128)(2,1)S(1)}, u32[]{:S(2)}, u32[]{:S(2)}) collective-permute-start(bf16[2,16384]{1,0:T(2,128)(2,1)S(1)} %get-tuple-element.28.refs_0_.value_ref), channel_id=1, source_target_pairs={{0,4},{1,5},{2,6},{3,7},{4,0},{5,1},{6,2},{7,3},{8,12},{9,13},{10,... | collective-permute-start | bytes 196616 | tf_op jit(solution)/shard_map/ppermute | solution.py:425
  11.3 0.7 %fusion.1 = f32[1,32]{1,0:T(1,128)S(1)} fusion(s32[32]{0:T(128)} %param.10, s32[1,32]{1,0:T(1,128)S(1)} %get-tuple-element.27), kind=kLoop, calls=%fused_computation.4 | loop fusion | flops 64 | bytes 384 | tf_op jit(solution)/shard_map/stack | solution.py:440
  11.9 0.7 %pad_maximum_fusion.levels_ref.behind_ref = f32[3,32]{1,0:T(4,128)S(1)} fusion(f32[1,32]{1,0:T(1,128)S(1)} %fusion.1, f32[1,32]{1,0:T(1,128)} %bitcast.14, f32[1,32]{1,0:T(1,128)} %bitcast.15), kind=kLoop, calls=%fused_computation.1 | loop fusion | flops 192 | bytes 768 | tf_op jit(solution)/shard_map/stack | solution.py:440
  12.6 1.4 %collective-permute-start.5 = (bf16[2,16384]{1,0:T(2,128)(2,1)S(1)}, bf16[2,16384]{1,0:T(2,128)(2,1)S(1)}, u32[]{:S(2)}, u32[]{:S(2)}) collective-permute-start(bf16[2,16384]{1,0:T(2,128)(2,1)S(1)} %copied.1), channel_id=1, source_target_pairs={{0,2},{1,3},{2,0},{3,1},{4,6},{5,7},{6,4},{7,5},{8,10},{9,11},{10,... | collective-permute-start | bytes 196616 | tf_op jit(solution)/shard_map/ppermute | solution.py:425
  14.0 1.1 %collective-permute-done.1.refs_1_ = bf16[2,16384]{1,0:T(2,128)(2,1)S(1)} collective-permute-done((bf16[2,16384]{1,0:T(2,128)(2,1)S(1)}, bf16[2,16384]{1,0:T(2,128)(2,1)S(1)}, u32[]{:S(2)}, u32[]{:S(2)}) %collective-permute-start.1) | collective-permute-done | bytes 65568 | tf_op jit(solution)/shard_map/ppermute | solution.py:425
  15.1 0.6 %collective-permute-start.6 = (bf16[2,16384]{1,0:T(2,128)(2,1)S(1)}, bf16[2,16384]{1,0:T(2,128)(2,1)S(1)}, u32[]{:S(2)}, u32[]{:S(2)}) collective-permute-start(bf16[2,16384]{1,0:T(2,128)(2,1)S(1)} %collective-permute-done.1.refs_1_), channel_id=1, source_target_pairs={{0,2},{1,3},{2,0},{3,1},{4,6},{5,7},{6,4},{7,5},{8,10},{9,11},{10,... | collective-permute-start | bytes 196616 | tf_op jit(solution)/shard_map/ppermute | solution.py:425
  15.7 0.2 pack.2
  15.9 0.1 collective-permute-start.2
  16.0 2.4 %collective-permute-start.3 = (bf16[4,10240]{1,0:T(4,128)(2,1)S(1)}, bf16[4,10240]{1,0:T(4,128)(2,1)S(1)}, u32[]{:S(2)}, u32[]{:S(2)}) collective-permute-start(bf16[4,10240]{1,0:T(4,128)(2,1)S(1)} %get-tuple-element.31), channel_id=1, source_target_pairs={{0,16},{1,17},{2,18},{3,19},{4,20},{5,21},{6,22},{7,23},{8,24},{9,... | collective-permute-start | bytes 245768 | tf_op jit(solution)/shard_map/ppermute | solution.py:430
  18.4 0.3 collective-permute-start.4
  18.6 0.0 collective-permute-done.5.refs_0_
  18.6 0.0 collective-permute-done.6.refs_1_
  18.6 0.2 pack.3
  18.8 1.0 %collective-permute-start.7 = (bf16[4,10240]{1,0:T(4,128)(2,1)S(1)}, bf16[4,10240]{1,0:T(4,128)(2,1)S(1)}, u32[]{:S(2)}, u32[]{:S(2)}) collective-permute-start(bf16[4,10240]{1,0:T(4,128)(2,1)S(1)} %get-tuple-element.34), channel_id=1, source_target_pairs={{0,17},{1,16},{2,19},{3,18},{4,21},{5,20},{6,23},{7,22},{8,25},{9,... | collective-permute-start | bytes 245768 | tf_op jit(solution)/shard_map/ppermute | solution.py:430
  19.8 1.5 %collective-permute-start.8 = (bf16[4,10240]{1,0:T(4,128)(2,1)S(1)}, bf16[4,10240]{1,0:T(4,128)(2,1)S(1)}, u32[]{:S(2)}, u32[]{:S(2)}) collective-permute-start(bf16[4,10240]{1,0:T(4,128)(2,1)S(1)} %get-tuple-element.35), channel_id=1, source_target_pairs={{0,16},{1,17},{2,18},{3,19},{4,20},{5,21},{6,22},{7,23},{8,24},{9,... | collective-permute-start | bytes 245768 | tf_op jit(solution)/shard_map/ppermute | solution.py:430
  21.3 0.0 collective-permute-done.2.refs_1_
  21.3 0.3 collective-permute-start.9
  21.5 0.3 collective-permute-done.3.refs_2_
  21.9 0.7 %collective-permute-done.4.refs_3_ = bf16[4,10240]{1,0:T(4,128)(2,1)S(1)} collective-permute-done((bf16[4,10240]{1,0:T(4,128)(2,1)S(1)}, bf16[4,10240]{1,0:T(4,128)(2,1)S(1)}, u32[]{:S(2)}, u32[]{:S(2)}) %collective-permute-start.4) | collective-permute-done | bytes 81952 | tf_op jit(solution)/shard_map/ppermute | solution.py:430
  22.6 0.6 %collective-permute-done.7.refs_5_ = bf16[4,10240]{1,0:T(4,128)(2,1)S(1)} collective-permute-done((bf16[4,10240]{1,0:T(4,128)(2,1)S(1)}, bf16[4,10240]{1,0:T(4,128)(2,1)S(1)}, u32[]{:S(2)}, u32[]{:S(2)}) %collective-permute-start.7) | collective-permute-done | bytes 81952 | tf_op jit(solution)/shard_map/ppermute | solution.py:430
  23.2 1.8 %collective-permute-done.8.refs_6_ = bf16[4,10240]{1,0:T(4,128)(2,1)S(1)} collective-permute-done((bf16[4,10240]{1,0:T(4,128)(2,1)S(1)}, bf16[4,10240]{1,0:T(4,128)(2,1)S(1)}, u32[]{:S(2)}, u32[]{:S(2)}) %collective-permute-start.8) | collective-permute-done | bytes 81952 | tf_op jit(solution)/shard_map/ppermute | solution.py:430
  25.0 0.8 %collective-permute-done.9.refs_7_ = bf16[4,10240]{1,0:T(4,128)(2,1)S(1)} collective-permute-done((bf16[4,10240]{1,0:T(4,128)(2,1)S(1)}, bf16[4,10240]{1,0:T(4,128)(2,1)S(1)}, u32[]{:S(2)}, u32[]{:S(2)}) %collective-permute-start.9) | collective-permute-done | bytes 81952 | tf_op jit(solution)/shard_map/ppermute | solution.py:430
  25.8 0.2 join.1
  26.0 2.1 %collective-permute-start.10 = (bf16[32,6144]{1,0:T(8,128)(2,1)S(1)}, bf16[32,6144]{1,0:T(8,128)(2,1)S(1)}, u32[]{:S(2)}, u32[]{:S(2)}) collective-permute-start(bf16[32,6144]{1,0:T(8,128)(2,1)S(1)} %get-tuple-element.38), channel_id=1, source_target_pairs={{0,8},{8,0},{16,24},{24,16},{1,9},{9,1},{17,25},{25,17},{2,10},{10... | collective-permute-start | bytes 1179656 | tf_op jit(solution)/shard_map/ppermute | solution.py:425
  28.1 1.3 %collective-permute-done.10.refs_1_ = bf16[32,6144]{1,0:T(8,128)(2,1)S(1)} collective-permute-done((bf16[32,6144]{1,0:T(8,128)(2,1)S(1)}, bf16[32,6144]{1,0:T(8,128)(2,1)S(1)}, u32[]{:S(2)}, u32[]{:S(2)}) %collective-permute-start.10) | collective-permute-done | bytes 393248 | tf_op jit(solution)/shard_map/ppermute | solution.py:425
  29.4 11.4 %outer.1 = f32[4096,2048]{1,0:T(8,128)} custom-call(bf16[32,6144]{1,0:T(8,128)(2,1)S(1)} %get-tuple-element.37.refs_0_, bf16[32,6144]{1,0:T(8,128)(2,1)S(1)} %collective-permute-done.10.refs_1_), custom_call_target="tpu_custom_call" | custom-call | flops 10000000000 | bytes 30000000 | tf_op jit(solution)/shard_map/outer/pallas_call | solution.py:386
  (2 shorter events, 0.0 us)
Async XLA Ops:
  0.0 5.8 %collective-permute-start = (bf16[1,48,2304]{2,1,0:T(8,128)(2,1)}, bf16[1,48,2304]{2,1,0:T(8,128)(2,1)S(1)}, u32[]{:S(2)}, u32[]{:S(2)}) collective-permute-start(bf16[1,48,2304]{2,1,0:T(8,128)(2,1)} %param.7), channel_id=1, source_target_pairs={{0,8},{8,16},{16,24},{24,0},{1,9},{9,17},{17,25},{25,1},{2,10},{10... | collective-permute-start | bytes 663560 | tf_op jit(solution)/shard_map/ppermute | solution.py:420
  3.8 0.9 %copy-start = (s32[3,8192]{1,0:T(4,128)S(1)}, s32[3,8192]{1,0:T(4,128)}, u32[]{:S(2)}) copy-start(s32[3,8192]{1,0:T(4,128)} %sphere_ref.1) | copy-start | bytes 294916
  8.9 6.2 %collective-permute-start.1 = (bf16[2,16384]{1,0:T(2,128)(2,1)S(1)}, bf16[2,16384]{1,0:T(2,128)(2,1)S(1)}, u32[]{:S(2)}, u32[]{:S(2)}) collective-permute-start(bf16[2,16384]{1,0:T(2,128)(2,1)S(1)} %get-tuple-element.28.refs_0_.value_ref), channel_id=1, source_target_pairs={{0,4},{1,5},{2,6},{3,7},{4,0},{5,1},{6,2},{7,3},{8,12},{9,13},{10,... | collective-permute-start | bytes 196616 | tf_op jit(solution)/shard_map/ppermute | solution.py:425
  12.6 6.0 %collective-permute-start.5 = (bf16[2,16384]{1,0:T(2,128)(2,1)S(1)}, bf16[2,16384]{1,0:T(2,128)(2,1)S(1)}, u32[]{:S(2)}, u32[]{:S(2)}) collective-permute-start(bf16[2,16384]{1,0:T(2,128)(2,1)S(1)} %copied.1), channel_id=1, source_target_pairs={{0,2},{1,3},{2,0},{3,1},{4,6},{5,7},{6,4},{7,5},{8,10},{9,11},{10,... | collective-permute-start | bytes 196616 | tf_op jit(solution)/shard_map/ppermute | solution.py:425
  15.1 3.5 %collective-permute-start.6 = (bf16[2,16384]{1,0:T(2,128)(2,1)S(1)}, bf16[2,16384]{1,0:T(2,128)(2,1)S(1)}, u32[]{:S(2)}, u32[]{:S(2)}) collective-permute-start(bf16[2,16384]{1,0:T(2,128)(2,1)S(1)} %collective-permute-done.1.refs_1_), channel_id=1, source_target_pairs={{0,2},{1,3},{2,0},{3,1},{4,6},{5,7},{6,4},{7,5},{8,10},{9,11},{10,... | collective-permute-start | bytes 196616 | tf_op jit(solution)/shard_map/ppermute | solution.py:425
  15.9 5.4 %collective-permute-start.2 = (bf16[4,10240]{1,0:T(4,128)(2,1)S(1)}, bf16[4,10240]{1,0:T(4,128)(2,1)S(1)}, u32[]{:S(2)}, u32[]{:S(2)}) collective-permute-start(bf16[4,10240]{1,0:T(4,128)(2,1)S(1)} %get-tuple-element.30), channel_id=1, source_target_pairs={{0,17},{1,16},{2,19},{3,18},{4,21},{5,20},{6,23},{7,22},{8,25},{9,... | collective-permute-start | bytes 245768 | tf_op jit(solution)/shard_map/ppermute | solution.py:430
  16.0 5.9 %collective-permute-start.3 = (bf16[4,10240]{1,0:T(4,128)(2,1)S(1)}, bf16[4,10240]{1,0:T(4,128)(2,1)S(1)}, u32[]{:S(2)}, u32[]{:S(2)}) collective-permute-start(bf16[4,10240]{1,0:T(4,128)(2,1)S(1)} %get-tuple-element.31), channel_id=1, source_target_pairs={{0,16},{1,17},{2,18},{3,19},{4,20},{5,21},{6,22},{7,23},{8,24},{9,... | collective-permute-start | bytes 245768 | tf_op jit(solution)/shard_map/ppermute | solution.py:430
  18.4 4.3 %collective-permute-start.4 = (bf16[4,10240]{1,0:T(4,128)(2,1)S(1)}, bf16[4,10240]{1,0:T(4,128)(2,1)S(1)}, u32[]{:S(2)}, u32[]{:S(2)}) collective-permute-start(bf16[4,10240]{1,0:T(4,128)(2,1)S(1)} %get-tuple-element.32), channel_id=1, source_target_pairs={{0,1},{1,0},{2,3},{3,2},{4,5},{5,4},{6,7},{7,6},{8,9},{9,8},{10,11... | collective-permute-start | bytes 245768 | tf_op jit(solution)/shard_map/ppermute | solution.py:430
  18.8 4.4 %collective-permute-start.7 = (bf16[4,10240]{1,0:T(4,128)(2,1)S(1)}, bf16[4,10240]{1,0:T(4,128)(2,1)S(1)}, u32[]{:S(2)}, u32[]{:S(2)}) collective-permute-start(bf16[4,10240]{1,0:T(4,128)(2,1)S(1)} %get-tuple-element.34), channel_id=1, source_target_pairs={{0,17},{1,16},{2,19},{3,18},{4,21},{5,20},{6,23},{7,22},{8,25},{9,... | collective-permute-start | bytes 245768 | tf_op jit(solution)/shard_map/ppermute | solution.py:430
  19.8 5.2 %collective-permute-start.8 = (bf16[4,10240]{1,0:T(4,128)(2,1)S(1)}, bf16[4,10240]{1,0:T(4,128)(2,1)S(1)}, u32[]{:S(2)}, u32[]{:S(2)}) collective-permute-start(bf16[4,10240]{1,0:T(4,128)(2,1)S(1)} %get-tuple-element.35), channel_id=1, source_target_pairs={{0,16},{1,17},{2,18},{3,19},{4,20},{5,21},{6,22},{7,23},{8,24},{9,... | collective-permute-start | bytes 245768 | tf_op jit(solution)/shard_map/ppermute | solution.py:430
  21.3 4.5 %collective-permute-start.9 = (bf16[4,10240]{1,0:T(4,128)(2,1)S(1)}, bf16[4,10240]{1,0:T(4,128)(2,1)S(1)}, u32[]{:S(2)}, u32[]{:S(2)}) collective-permute-start(bf16[4,10240]{1,0:T(4,128)(2,1)S(1)} %get-tuple-element.36), channel_id=1, source_target_pairs={{0,1},{1,0},{2,3},{3,2},{4,5},{5,4},{6,7},{7,6},{8,9},{9,8},{10,11... | collective-permute-start | bytes 245768 | tf_op jit(solution)/shard_map/ppermute | solution.py:430
  26.0 3.5 %collective-permute-start.10 = (bf16[32,6144]{1,0:T(8,128)(2,1)S(1)}, bf16[32,6144]{1,0:T(8,128)(2,1)S(1)}, u32[]{:S(2)}, u32[]{:S(2)}) collective-permute-start(bf16[32,6144]{1,0:T(8,128)(2,1)S(1)} %get-tuple-element.38), channel_id=1, source_target_pairs={{0,8},{8,0},{16,24},{24,16},{1,9},{9,1},{17,25},{25,17},{2,10},{10... | collective-permute-start | bytes 1179656 | tf_op jit(solution)/shard_map/ppermute | solution.py:425

commit v18 on v17

--- a/solution.py
+++ b/solution.py
@@ -360,6 +360,10 @@
         rows = pl.ds(pl.multiple_of(i * block, block), block)
         return pltpu.make_async_copy(held_ref.at[slot], out_ref.at[rows], sems.at[slot])
 
+    def product(first, size):
+        left = jnp.concatenate([ref[:, pl.ds(first, size)] for ref in messages], axis=0)
+        return lax.dot_general(left, right_ref[...], (((0,), (0,)), ((), ())), preferred_element_type=jnp.float32)
+
     def step(i, carry):
         slot = lax.rem(i, slots)
 
@@ -367,13 +371,16 @@
         def _():
             copy_out(i - slots, slot).wait()
 
-        here = pl.ds(pl.multiple_of(i * block, block), block)
-        left = jnp.concatenate([ref[:, here] for ref in messages], axis=0)
-        held_ref[slot] = lax.dot_general(left, right_ref[...], (((0,), (0,)), ((), ())), preferred_element_type=jnp.float32)
+        held_ref[slot] = product(pl.multiple_of(i * block, block), block)
         copy_out(i, slot).start()
         return carry
 
-    lax.fori_loop(0, count, step, 0)
+    half = block // 2
+    for part in range(2):
+        here = pl.ds(part * half, half)
+        held_ref[0, part * half : (part + 1) * half, :] = product(part * half, half)
+        pltpu.make_async_copy(held_ref.at[0, here], out_ref.at[here], sems.at[0]).start()
+    lax.fori_loop(1, count, step, 0)
     for i in range(max(0, count - slots), count):
         copy_out(i, i % slots).wait()
 
@@ -451,12 +458,15 @@
         other_turns += [turn + bit for turn in [0, *other_turns]]
         bit //= 2
     turns = [0, *other_turns]
-    messages = sent(pack([own, *others], levels, turns, targets, plan))
+    early = sent(pack([own, *others], levels, turns, targets, plan))
     relayed = turned(jnp.concatenate(others, axis=0) if len(others) > 1 else others[0], "col", bit)
     beside = turned(copied(own, levels), "col", bit)
-    messages += sent(pack([beside, relayed], levels, [turn + bit for turn in turns], targets, plan))
-    kept, passed = join(messages, plan)
-    return outer([kept, turned(passed, "row", 1)], plan)
+    late = sent(pack([beside, relayed], levels, [turn + bit for turn in turns], targets, plan))
+    joined = []
+    for messages in (early, late):
+        kept, passed = join(messages, plan)
+        joined += [kept, turned(passed, "row", 1)]
+    return outer(joined, plan)
 
 
 def solution(mesh):

time: 41.3 us -> 40.8 us (0.988)
  waiting for transfers between devices: 6.82 us -> 3.59 us
  starting transfers between devices: 14.5 us -> 17.4 us
    ppermute x6, waiting for transfers between devices: 4.29 us -> 1.33 us  [sent_across(): return lax.ppermute(value, ('row', 'col'), moves)]
    ppermute x4 -> x5, starting transfers between devices: 6.45 us -> 9.32 us  [turned(): return lax.ppermute(value, axis, [(i, i ^ turn) for i in range(devices)])]
    ppermute x4 -> x5, waiting for transfers between devices: 2.48 us -> 2.2 us  [turned(): return lax.ppermute(value, axis, [(i, i ^ turn) for i in range(devices)])]
  transfers between devices with their start and end apart: 11 -> 12, of which waited for: 8 -> 6; matrix products, arithmetic and copies ran while one was open for 6% -> 6% of each run, Pallas kernels for 4% -> 4%
where the time goes in v18:
time: 40.8 us; the launch traced here: 40.3 us
  starting transfers between devices  17.4 us (43%)
  Pallas kernels  15.9 us (39%)
  waiting for transfers between devices  3.59 us (9%)
  other arithmetic  2.49 us (6%)
  local copies, waits for them, and re-layouts  0.9 us (2%)
    pallas_call x1, Pallas kernels, outer(): pl.pallas_call(functools.partial(outer_kernel, row_width, block, slots),...  11.2 us
    ppermute x5, starting transfers between devices, turned(): return lax.ppermute(value, axis, [(i, i ^ turn) for i in range(devices)])  9.32 us
    ppermute x6, starting transfers between devices, sent_across(): return lax.ppermute(value, ('row', 'col'), moves)  5.42 us
    pallas_call x1, Pallas kernels, transform(): pl.pallas_call(functools.partial(second_kernel, grid), out_shape=[jax.Sha...  3.05 us
    ppermute x1, starting transfers between devices, shifted(): lax.ppermute(value, axis, [(i, (i + by) % devices) for i in range(devices)])  2.63 us
    ppermute x5, waiting for transfers between devices, turned(): return lax.ppermute(value, axis, [(i, i ^ turn) for i in range(devices)])  2.2 us
    another operation x2, other arithmetic, on_device(): jnp.stack([cond_energy, occ_energy, (occ_band + later[0]).astype(jnp.floa...  1.34 us
    ppermute x6, waiting for transfers between devices, sent_across(): return lax.ppermute(value, ('row', 'col'), moves)  1.33 us
  transfers between devices with their start and end apart: 12, of which 6 were waited for; matrix products, arithmetic and copies ran while one was open for 6% of the time, Pallas kernels for 4%

profile of v18, /device:TPU:1, one launch (start us, length us, event | category | flops | bytes accessed | tf_op | source)
XLA Modules:
  0.0 40.3 jit_solution(8332464544007139451)
XLA Ops:
  0.0 2.6 %collective-permute-start = (bf16[1,48,2304]{2,1,0:T(8,128)(2,1)}, bf16[1,48,2304]{2,1,0:T(8,128)(2,1)S(1)}, u32[]{:S(2)}, u32[]{:S(2)}) collective-permute-start(bf16[1,48,2304]{2,1,0:T(8,128)(2,1)} %param.7), channel_id=1, source_target_pairs={{0,8},{8,16},{16,24},{24,0},{1,9},{9,17},{17,25},{25,1},{2,10},{10... | collective-permute-start | bytes 663560 | tf_op jit(solution)/shard_map/ppermute | solution.py:427
  2.6 1.2 %broadcast_select_fusion.orbitals_ref = bf16[2,48,2304]{2,1,0:T(8,128)(2,1)S(1)} fusion(pred[2]{0:T(512)(128)(4,1)S(1)} %iota_compare_fusion, bf16[48,2304]{1,0:T(8,128)(2,1)} %bitcast.13, bf16[48,2304]{1,0:T(8,128)(2,1)} %bitcast.12), kind=kLoop, calls=%fused_computation | loop fusion | flops 221184 | bytes 884738 | tf_op jit(solution)/shard_map/jit(_where)/select_n | solution.py:249
  3.8 0.0 copy-start
  3.8 0.9 %copy-done = s32[3,8192]{1,0:T(4,128)S(1)} copy-done((s32[3,8192]{1,0:T(4,128)S(1)}, s32[3,8192]{1,0:T(4,128)}, u32[]{:S(2)}) %copy-start) | copy-done | bytes 98328
  4.7 1.1 %first_pair.1 = (bf16[1,16384]{1,0:T(2,128)(2,1)S(1)}, s32[2,8192]{1,0:T(2,128)S(1)}, bf16[1616,128]{1,0:T(8,128)(2,1)S(1)}, f32[16,384]{1,0:T(8,128)S(1)}, bf16[240,256]{1,0:T(8,128)(2,1)S(1)}) custom-call(bf16[2,48,2304]{2,1,0:T(8,128)(2,1)S(1)} %broadcast_select_fusion.orbitals_ref, s32[3,8192]{1,0:T(4,128)S(1)} %copy-done), custom_call_target="tpu_custom_call" | custom-call | flops 2000000000 | bytes 2000000 | tf_op jit(solution)/shard_map/first_pair/pallas_call | solution.py:255
  5.8 0.1 collective-permute-done.occ_ref
  5.8 3.1 %second_pair.1 = (bf16[2,16384]{1,0:T(2,128)(2,1)S(1)}, s32[1,32]{1,0:T(1,128)S(1)}) custom-call(bf16[2,48,2304]{2,1,0:T(8,128)(2,1)S(1)} %broadcast_select_fusion.orbitals_ref, bf16[1,48,2304]{2,1,0:T(8,128)(2,1)S(1)} %collective-permute-done.occ_ref, bf16[1,16384]{1,0:T(2,128)(2,1)S(1)} %get-tuple-element.24.first_ref, ...), custom_call_target="tpu_custom_call" | custom-call | flops 2000000000 | bytes 2000000 | tf_op jit(solution)/shard_map/second_pair/pallas_call | solution.py:269
  8.9 2.4 %collective-permute-start.1 = (bf16[2,16384]{1,0:T(2,128)(2,1)S(1)}, bf16[2,16384]{1,0:T(2,128)(2,1)S(1)}, u32[]{:S(2)}, u32[]{:S(2)}) collective-permute-start(bf16[2,16384]{1,0:T(2,128)(2,1)S(1)} %get-tuple-element.30.refs_0_.value_ref), channel_id=1, source_target_pairs={{0,4},{1,5},{2,6},{3,7},{4,0},{5,1},{6,2},{7,3},{8,12},{9,13},{10,... | collective-permute-start | bytes 196616 | tf_op jit(solution)/shard_map/ppermute | solution.py:432
  11.3 0.7 %fusion.1 = f32[1,32]{1,0:T(1,128)S(1)} fusion(s32[32]{0:T(128)} %param.10, s32[1,32]{1,0:T(1,128)S(1)} %get-tuple-element.29), kind=kLoop, calls=%fused_computation.4 | loop fusion | flops 64 | bytes 384 | tf_op jit(solution)/shard_map/stack | solution.py:447
  11.9 0.7 %pad_maximum_fusion.levels_ref.behind_ref = f32[3,32]{1,0:T(4,128)S(1)} fusion(f32[1,32]{1,0:T(1,128)S(1)} %fusion.1, f32[1,32]{1,0:T(1,128)} %bitcast.14, f32[1,32]{1,0:T(1,128)} %bitcast.15), kind=kLoop, calls=%fused_computation.1 | loop fusion | flops 192 | bytes 768 | tf_op jit(solution)/shard_map/stack | solution.py:447
  12.6 1.4 %collective-permute-start.6 = (bf16[2,16384]{1,0:T(2,128)(2,1)S(1)}, bf16[2,16384]{1,0:T(2,128)(2,1)S(1)}, u32[]{:S(2)}, u32[]{:S(2)}) collective-permute-start(bf16[2,16384]{1,0:T(2,128)(2,1)S(1)} %copied.1), channel_id=1, source_target_pairs={{0,2},{1,3},{2,0},{3,1},{4,6},{5,7},{6,4},{7,5},{8,10},{9,11},{10,... | collective-permute-start | bytes 196616 | tf_op jit(solution)/shard_map/ppermute | solution.py:432
  14.0 1.1 %collective-permute-done.1.refs_1_ = bf16[2,16384]{1,0:T(2,128)(2,1)S(1)} collective-permute-done((bf16[2,16384]{1,0:T(2,128)(2,1)S(1)}, bf16[2,16384]{1,0:T(2,128)(2,1)S(1)}, u32[]{:S(2)}, u32[]{:S(2)}) %collective-permute-start.1) | collective-permute-done | bytes 65568 | tf_op jit(solution)/shard_map/ppermute | solution.py:432
  15.1 0.6 %collective-permute-start.7 = (bf16[2,16384]{1,0:T(2,128)(2,1)S(1)}, bf16[2,16384]{1,0:T(2,128)(2,1)S(1)}, u32[]{:S(2)}, u32[]{:S(2)}) collective-permute-start(bf16[2,16384]{1,0:T(2,128)(2,1)S(1)} %collective-permute-done.1.refs_1_), channel_id=1, source_target_pairs={{0,2},{1,3},{2,0},{3,1},{4,6},{5,7},{6,4},{7,5},{8,10},{9,11},{10,... | collective-permute-start | bytes 196616 | tf_op jit(solution)/shard_map/ppermute | solution.py:432
  15.7 0.2 pack.2
  15.9 0.1 collective-permute-start.2
  16.0 2.4 %collective-permute-start.3 = (bf16[4,10240]{1,0:T(4,128)(2,1)S(1)}, bf16[4,10240]{1,0:T(4,128)(2,1)S(1)}, u32[]{:S(2)}, u32[]{:S(2)}) collective-permute-start(bf16[4,10240]{1,0:T(4,128)(2,1)S(1)} %get-tuple-element.33), channel_id=1, source_target_pairs={{0,16},{1,17},{2,18},{3,19},{4,20},{5,21},{6,22},{7,23},{8,24},{9,... | collective-permute-start | bytes 245768 | tf_op jit(solution)/shard_map/ppermute | solution.py:437
  18.4 0.3 collective-permute-start.4
  18.6 0.0 collective-permute-done.6.refs_0_
  18.6 0.0 collective-permute-done.7.refs_1_
  18.6 0.2 pack.3
  18.8 1.0 %collective-permute-start.8 = (bf16[4,10240]{1,0:T(4,128)(2,1)S(1)}, bf16[4,10240]{1,0:T(4,128)(2,1)S(1)}, u32[]{:S(2)}, u32[]{:S(2)}) collective-permute-start(bf16[4,10240]{1,0:T(4,128)(2,1)S(1)} %get-tuple-element.38), channel_id=1, source_target_pairs={{0,17},{1,16},{2,19},{3,18},{4,21},{5,20},{6,23},{7,22},{8,25},{9,... | collective-permute-start | bytes 245768 | tf_op jit(solution)/shard_map/ppermute | solution.py:437
  19.8 1.5 %collective-permute-start.9 = (bf16[4,10240]{1,0:T(4,128)(2,1)S(1)}, bf16[4,10240]{1,0:T(4,128)(2,1)S(1)}, u32[]{:S(2)}, u32[]{:S(2)}) collective-permute-start(bf16[4,10240]{1,0:T(4,128)(2,1)S(1)} %get-tuple-element.39), channel_id=1, source_target_pairs={{0,16},{1,17},{2,18},{3,19},{4,20},{5,21},{6,22},{7,23},{8,24},{9,... | collective-permute-start | bytes 245768 | tf_op jit(solution)/shard_map/ppermute | solution.py:437
  21.3 0.0 collective-permute-done.2.refs_1_
  21.3 0.3 collective-permute-start.10
  21.5 0.3 collective-permute-done.3.refs_2_
  21.9 0.7 %collective-permute-done.4.refs_3_ = bf16[4,10240]{1,0:T(4,128)(2,1)S(1)} collective-permute-done((bf16[4,10240]{1,0:T(4,128)(2,1)S(1)}, bf16[4,10240]{1,0:T(4,128)(2,1)S(1)}, u32[]{:S(2)}, u32[]{:S(2)}) %collective-permute-start.4) | collective-permute-done | bytes 81952 | tf_op jit(solution)/shard_map/ppermute | solution.py:437
  22.6 0.1 join.2
  22.7 2.9 %collective-permute-start.5 = (bf16[16,6144]{1,0:T(8,128)(2,1)S(1)}, bf16[16,6144]{1,0:T(8,128)(2,1)S(1)}, u32[]{:S(2)}, u32[]{:S(2)}) collective-permute-start(bf16[16,6144]{1,0:T(8,128)(2,1)S(1)} %get-tuple-element.36), channel_id=1, source_target_pairs={{0,8},{8,0},{16,24},{24,16},{1,9},{9,1},{17,25},{25,17},{2,10},{10... | collective-permute-start | bytes 589832 | tf_op jit(solution)/shard_map/ppermute | solution.py:432
  25.6 0.0 collective-permute-done.8.refs_1_
  25.6 0.0 collective-permute-done.9.refs_2_
  25.6 0.3 collective-permute-done.10.refs_3_
  25.8 0.1 join.3
  25.9 2.1 %collective-permute-start.11 = (bf16[16,6144]{1,0:T(8,128)(2,1)S(1)}, bf16[16,6144]{1,0:T(8,128)(2,1)S(1)}, u32[]{:S(2)}, u32[]{:S(2)}) collective-permute-start(bf16[16,6144]{1,0:T(8,128)(2,1)S(1)} %get-tuple-element.42), channel_id=1, source_target_pairs={{0,8},{8,0},{16,24},{24,16},{1,9},{9,1},{17,25},{25,17},{2,10},{10... | collective-permute-start | bytes 589832 | tf_op jit(solution)/shard_map/ppermute | solution.py:432
  28.0 0.0 collective-permute-done.5.refs_1_
  28.0 1.1 %collective-permute-done.11.refs_3_ = bf16[16,6144]{1,0:T(8,128)(2,1)S(1)} collective-permute-done((bf16[16,6144]{1,0:T(8,128)(2,1)S(1)}, bf16[16,6144]{1,0:T(8,128)(2,1)S(1)}, u32[]{:S(2)}, u32[]{:S(2)}) %collective-permute-start.11) | collective-permute-done | bytes 196640 | tf_op jit(solution)/shard_map/ppermute | solution.py:432
  29.1 11.2 %outer.1 = f32[4096,2048]{1,0:T(8,128)} custom-call(bf16[16,6144]{1,0:T(8,128)(2,1)S(1)} %get-tuple-element.35.refs_0_, bf16[16,6144]{1,0:T(8,128)(2,1)S(1)} %collective-permute-done.5.refs_1_, bf16[16,6144]{1,0:T(8,128)(2,1)S(1)} %get-tuple-element.41.refs_2_, bf16[16,6144]{1,0:T(8,128)(2,1)S(1)} %collective-permute-done.11.refs_3_), custom_call_target="tpu_custom_call" | custom-call | flops 10000000000 | bytes 30000000 | tf_op jit(solution)/shard_map/outer/pallas_call | solution.py:393
  (2 shorter events, 0.0 us)
Async XLA Ops:
  0.0 5.8 %collective-permute-start = (bf16[1,48,2304]{2,1,0:T(8,128)(2,1)}, bf16[1,48,2304]{2,1,0:T(8,128)(2,1)S(1)}, u32[]{:S(2)}, u32[]{:S(2)}) collective-permute-start(bf16[1,48,2304]{2,1,0:T(8,128)(2,1)} %param.7), channel_id=1, source_target_pairs={{0,8},{8,16},{16,24},{24,0},{1,9},{9,17},{17,25},{25,1},{2,10},{10... | collective-permute-start | bytes 663560 | tf_op jit(solution)/shard_map/ppermute | solution.py:427
  3.8 0.9 %copy-start = (s32[3,8192]{1,0:T(4,128)S(1)}, s32[3,8192]{1,0:T(4,128)}, u32[]{:S(2)}) copy-start(s32[3,8192]{1,0:T(4,128)} %sphere_ref.1) | copy-start | bytes 294916
  8.9 6.2 %collective-permute-start.1 = (bf16[2,16384]{1,0:T(2,128)(2,1)S(1)}, bf16[2,16384]{1,0:T(2,128)(2,1)S(1)}, u32[]{:S(2)}, u32[]{:S(2)}) collective-permute-start(bf16[2,16384]{1,0:T(2,128)(2,1)S(1)} %get-tuple-element.30.refs_0_.value_ref), channel_id=1, source_target_pairs={{0,4},{1,5},{2,6},{3,7},{4,0},{5,1},{6,2},{7,3},{8,12},{9,13},{10,... | collective-permute-start | bytes 196616 | tf_op jit(solution)/shard_map/ppermute | solution.py:432
  12.6 6.0 %collective-permute-start.6 = (bf16[2,16384]{1,0:T(2,128)(2,1)S(1)}, bf16[2,16384]{1,0:T(2,128)(2,1)S(1)}, u32[]{:S(2)}, u32[]{:S(2)}) collective-permute-start(bf16[2,16384]{1,0:T(2,128)(2,1)S(1)} %copied.1), channel_id=1, source_target_pairs={{0,2},{1,3},{2,0},{3,1},{4,6},{5,7},{6,4},{7,5},{8,10},{9,11},{10,... | collective-permute-start | bytes 196616 | tf_op jit(solution)/shard_map/ppermute | solution.py:432
  15.1 3.5 %collective-permute-start.7 = (bf16[2,16384]{1,0:T(2,128)(2,1)S(1)}, bf16[2,16384]{1,0:T(2,128)(2,1)S(1)}, u32[]{:S(2)}, u32[]{:S(2)}) collective-permute-start(bf16[2,16384]{1,0:T(2,128)(2,1)S(1)} %collective-permute-done.1.refs_1_), channel_id=1, source_target_pairs={{0,2},{1,3},{2,0},{3,1},{4,6},{5,7},{6,4},{7,5},{8,10},{9,11},{10,... | collective-permute-start | bytes 196616 | tf_op jit(solution)/shard_map/ppermute | solution.py:432
  15.9 5.4 %collective-permute-start.2 = (bf16[4,10240]{1,0:T(4,128)(2,1)S(1)}, bf16[4,10240]{1,0:T(4,128)(2,1)S(1)}, u32[]{:S(2)}, u32[]{:S(2)}) collective-permute-start(bf16[4,10240]{1,0:T(4,128)(2,1)S(1)} %get-tuple-element.32), channel_id=1, source_target_pairs={{0,17},{1,16},{2,19},{3,18},{4,21},{5,20},{6,23},{7,22},{8,25},{9,... | collective-permute-start | bytes 245768 | tf_op jit(solution)/shard_map/ppermute | solution.py:437
  16.0 5.9 %collective-permute-start.3 = (bf16[4,10240]{1,0:T(4,128)(2,1)S(1)}, bf16[4,10240]{1,0:T(4,128)(2,1)S(1)}, u32[]{:S(2)}, u32[]{:S(2)}) collective-permute-start(bf16[4,10240]{1,0:T(4,128)(2,1)S(1)} %get-tuple-element.33), channel_id=1, source_target_pairs={{0,16},{1,17},{2,18},{3,19},{4,20},{5,21},{6,22},{7,23},{8,24},{9,... | collective-permute-start | bytes 245768 | tf_op jit(solution)/shard_map/ppermute | solution.py:437
  18.4 4.3 %collective-permute-start.4 = (bf16[4,10240]{1,0:T(4,128)(2,1)S(1)}, bf16[4,10240]{1,0:T(4,128)(2,1)S(1)}, u32[]{:S(2)}, u32[]{:S(2)}) collective-permute-start(bf16[4,10240]{1,0:T(4,128)(2,1)S(1)} %get-tuple-element.34), channel_id=1, source_target_pairs={{0,1},{1,0},{2,3},{3,2},{4,5},{5,4},{6,7},{7,6},{8,9},{9,8},{10,11... | collective-permute-start | bytes 245768 | tf_op jit(solution)/shard_map/ppermute | solution.py:437
  18.8 6.7 %collective-permute-start.8 = (bf16[4,10240]{1,0:T(4,128)(2,1)S(1)}, bf16[4,10240]{1,0:T(4,128)(2,1)S(1)}, u32[]{:S(2)}, u32[]{:S(2)}) collective-permute-start(bf16[4,10240]{1,0:T(4,128)(2,1)S(1)} %get-tuple-element.38), channel_id=1, source_target_pairs={{0,17},{1,16},{2,19},{3,18},{4,21},{5,20},{6,23},{7,22},{8,25},{9,... | collective-permute-start | bytes 245768 | tf_op jit(solution)/shard_map/ppermute | solution.py:437
  19.8 5.8 %collective-permute-start.9 = (bf16[4,10240]{1,0:T(4,128)(2,1)S(1)}, bf16[4,10240]{1,0:T(4,128)(2,1)S(1)}, u32[]{:S(2)}, u32[]{:S(2)}) collective-permute-start(bf16[4,10240]{1,0:T(4,128)(2,1)S(1)} %get-tuple-element.39), channel_id=1, source_target_pairs={{0,16},{1,17},{2,18},{3,19},{4,20},{5,21},{6,22},{7,23},{8,24},{9,... | collective-permute-start | bytes 245768 | tf_op jit(solution)/shard_map/ppermute | solution.py:437
  21.3 4.5 %collective-permute-start.10 = (bf16[4,10240]{1,0:T(4,128)(2,1)S(1)}, bf16[4,10240]{1,0:T(4,128)(2,1)S(1)}, u32[]{:S(2)}, u32[]{:S(2)}) collective-permute-start(bf16[4,10240]{1,0:T(4,128)(2,1)S(1)} %get-tuple-element.40), channel_id=1, source_target_pairs={{0,1},{1,0},{2,3},{3,2},{4,5},{5,4},{6,7},{7,6},{8,9},{9,8},{10,11... | collective-permute-start | bytes 245768 | tf_op jit(solution)/shard_map/ppermute | solution.py:437
  22.7 5.3 %collective-permute-start.5 = (bf16[16,6144]{1,0:T(8,128)(2,1)S(1)}, bf16[16,6144]{1,0:T(8,128)(2,1)S(1)}, u32[]{:S(2)}, u32[]{:S(2)}) collective-permute-start(bf16[16,6144]{1,0:T(8,128)(2,1)S(1)} %get-tuple-element.36), channel_id=1, source_target_pairs={{0,8},{8,0},{16,24},{24,16},{1,9},{9,1},{17,25},{25,17},{2,10},{10... | collective-permute-start | bytes 589832 | tf_op jit(solution)/shard_map/ppermute | solution.py:432
  25.9 3.2 %collective-permute-start.11 = (bf16[16,6144]{1,0:T(8,128)(2,1)S(1)}, bf16[16,6144]{1,0:T(8,128)(2,1)S(1)}, u32[]{:S(2)}, u32[]{:S(2)}) collective-permute-start(bf16[16,6144]{1,0:T(8,128)(2,1)S(1)} %get-tuple-element.42), channel_id=1, source_target_pairs={{0,8},{8,0},{16,24},{24,16},{1,9},{9,1},{17,25},{25,17},{2,10},{10... | collective-permute-start | bytes 589832 | tf_op jit(solution)/shard_map/ppermute | solution.py:432

commit v19 on v18

--- a/solution.py
+++ b/solution.py
@@ -445,8 +445,7 @@
     occ_second = shifted(occ_orbitals, "row", 1)
     own, later = transform(cond_orbitals, occ_orbitals, occ_second, sphere_index, occ_band.shape)
     levels = jnp.stack([cond_energy, occ_energy, (occ_band + later[0]).astype(jnp.float32)])
-    targets = [(0, 0)] + [(turn, side) for side in (1, 0) for turn in range(rows - 2, -2, -2) if turn or side]
-    targets.append(targets.pop(rows // 2))
+    targets = [(0, 0)] + [(turn, side) for side in range(2) for turn in range(rows - 2, 0, -2)] + [(0, 1)]
 
     def sent(packed):
         return [packed[0]] + [sent_across(value, *target, rows, cols) for value, target in zip(packed[1:], targets[1:])]

time: 40.8 us -> 40.8 us (level)
  transfers between devices with their start and end apart: 12 -> 12, of which waited for: 6 -> 5; matrix products, arithmetic and copies ran while one was open for 6% -> 6% of each run, Pallas kernels for 4% -> 4%
where the time goes in v19:
time: 40.8 us; the launch traced here: 40.3 us
  starting transfers between devices  17.4 us (43%)
  Pallas kernels  15.9 us (39%)
  waiting for transfers between devices  3.55 us (9%)
  other arithmetic  2.49 us (6%)
  local copies, waits for them, and re-layouts  0.9 us (2%)
    pallas_call x1, Pallas kernels, outer(): pl.pallas_call(functools.partial(outer_kernel, row_width, block, slots),...  11.2 us
    ppermute x5, starting transfers between devices, turned(): return lax.ppermute(value, axis, [(i, i ^ turn) for i in range(devices)])  9.36 us
    ppermute x6, starting transfers between devices, sent_across(): return lax.ppermute(value, ('row', 'col'), moves)  5.42 us
    pallas_call x1, Pallas kernels, transform(): pl.pallas_call(functools.partial(second_kernel, grid), out_shape=[jax.Sha...  3.05 us
    ppermute x1, starting transfers between devices, shifted(): lax.ppermute(value, axis, [(i, (i + by) % devices) for i in range(devices)])  2.63 us
    ppermute x5, waiting for transfers between devices, turned(): return lax.ppermute(value, axis, [(i, i ^ turn) for i in range(devices)])  2.2 us
    another operation x2, other arithmetic, on_device(): jnp.stack([cond_energy, occ_energy, (occ_band + later[0]).astype(jnp.floa...  1.34 us
    ppermute x6, waiting for transfers between devices, sent_across(): return lax.ppermute(value, ('row', 'col'), moves)  1.3 us
  transfers between devices with their start and end apart: 12, of which 5 were waited for; matrix products, arithmetic and copies ran while one was open for 6% of the time, Pallas kernels for 4%

profile of v19, /device:TPU:1, one launch (start us, length us, event | category | flops | bytes accessed | tf_op | source)
XLA Modules:
  0.0 40.3 jit_solution(5095831173187997137)
XLA Ops:
  0.0 2.6 %collective-permute-start = (bf16[1,48,2304]{2,1,0:T(8,128)(2,1)}, bf16[1,48,2304]{2,1,0:T(8,128)(2,1)S(1)}, u32[]{:S(2)}, u32[]{:S(2)}) collective-permute-start(bf16[1,48,2304]{2,1,0:T(8,128)(2,1)} %param.7), channel_id=1, source_target_pairs={{0,8},{8,16},{16,24},{24,0},{1,9},{9,17},{17,25},{25,1},{2,10},{10... | collective-permute-start | bytes 663560 | tf_op jit(solution)/shard_map/ppermute | solution.py:427
  2.6 1.2 %broadcast_select_fusion.orbitals_ref = bf16[2,48,2304]{2,1,0:T(8,128)(2,1)S(1)} fusion(pred[2]{0:T(512)(128)(4,1)S(1)} %iota_compare_fusion, bf16[48,2304]{1,0:T(8,128)(2,1)} %bitcast.13, bf16[48,2304]{1,0:T(8,128)(2,1)} %bitcast.12), kind=kLoop, calls=%fused_computation | loop fusion | flops 221184 | bytes 884738 | tf_op jit(solution)/shard_map/jit(_where)/select_n | solution.py:249
  3.8 0.0 copy-start
  3.8 0.9 %copy-done = s32[3,8192]{1,0:T(4,128)S(1)} copy-done((s32[3,8192]{1,0:T(4,128)S(1)}, s32[3,8192]{1,0:T(4,128)}, u32[]{:S(2)}) %copy-start) | copy-done | bytes 98328
  4.7 1.1 %first_pair.1 = (bf16[1,16384]{1,0:T(2,128)(2,1)S(1)}, s32[2,8192]{1,0:T(2,128)S(1)}, bf16[1616,128]{1,0:T(8,128)(2,1)S(1)}, f32[16,384]{1,0:T(8,128)S(1)}, bf16[240,256]{1,0:T(8,128)(2,1)S(1)}) custom-call(bf16[2,48,2304]{2,1,0:T(8,128)(2,1)S(1)} %broadcast_select_fusion.orbitals_ref, s32[3,8192]{1,0:T(4,128)S(1)} %copy-done), custom_call_target="tpu_custom_call" | custom-call | flops 2000000000 | bytes 2000000 | tf_op jit(solution)/shard_map/first_pair/pallas_call | solution.py:255
  5.8 0.1 collective-permute-done.occ_ref
  5.8 3.1 %second_pair.1 = (bf16[2,16384]{1,0:T(2,128)(2,1)S(1)}, s32[1,32]{1,0:T(1,128)S(1)}) custom-call(bf16[2,48,2304]{2,1,0:T(8,128)(2,1)S(1)} %broadcast_select_fusion.orbitals_ref, bf16[1,48,2304]{2,1,0:T(8,128)(2,1)S(1)} %collective-permute-done.occ_ref, bf16[1,16384]{1,0:T(2,128)(2,1)S(1)} %get-tuple-element.24.first_ref, ...), custom_call_target="tpu_custom_call" | custom-call | flops 2000000000 | bytes 2000000 | tf_op jit(solution)/shard_map/second_pair/pallas_call | solution.py:269
  8.9 2.4 %collective-permute-start.1 = (bf16[2,16384]{1,0:T(2,128)(2,1)S(1)}, bf16[2,16384]{1,0:T(2,128)(2,1)S(1)}, u32[]{:S(2)}, u32[]{:S(2)}) collective-permute-start(bf16[2,16384]{1,0:T(2,128)(2,1)S(1)} %get-tuple-element.30.refs_0_.value_ref), channel_id=1, source_target_pairs={{0,4},{1,5},{2,6},{3,7},{4,0},{5,1},{6,2},{7,3},{8,12},{9,13},{10,... | collective-permute-start | bytes 196616 | tf_op jit(solution)/shard_map/ppermute | solution.py:432
  11.3 0.7 %fusion.1 = f32[1,32]{1,0:T(1,128)S(1)} fusion(s32[32]{0:T(128)} %param.10, s32[1,32]{1,0:T(1,128)S(1)} %get-tuple-element.29), kind=kLoop, calls=%fused_computation.4 | loop fusion | flops 64 | bytes 384 | tf_op jit(solution)/shard_map/stack | solution.py:447
  11.9 0.7 %pad_maximum_fusion.levels_ref.behind_ref = f32[3,32]{1,0:T(4,128)S(1)} fusion(f32[1,32]{1,0:T(1,128)S(1)} %fusion.1, f32[1,32]{1,0:T(1,128)} %bitcast.14, f32[1,32]{1,0:T(1,128)} %bitcast.15), kind=kLoop, calls=%fused_computation.1 | loop fusion | flops 192 | bytes 768 | tf_op jit(solution)/shard_map/stack | solution.py:447
  12.6 1.4 %collective-permute-start.6 = (bf16[2,16384]{1,0:T(2,128)(2,1)S(1)}, bf16[2,16384]{1,0:T(2,128)(2,1)S(1)}, u32[]{:S(2)}, u32[]{:S(2)}) collective-permute-start(bf16[2,16384]{1,0:T(2,128)(2,1)S(1)} %copied.1), channel_id=1, source_target_pairs={{0,2},{1,3},{2,0},{3,1},{4,6},{5,7},{6,4},{7,5},{8,10},{9,11},{10,... | collective-permute-start | bytes 196616 | tf_op jit(solution)/shard_map/ppermute | solution.py:432
  14.0 1.1 %collective-permute-done.1.refs_1_ = bf16[2,16384]{1,0:T(2,128)(2,1)S(1)} collective-permute-done((bf16[2,16384]{1,0:T(2,128)(2,1)S(1)}, bf16[2,16384]{1,0:T(2,128)(2,1)S(1)}, u32[]{:S(2)}, u32[]{:S(2)}) %collective-permute-start.1) | collective-permute-done | bytes 65568 | tf_op jit(solution)/shard_map/ppermute | solution.py:432
  15.1 0.6 %collective-permute-start.7 = (bf16[2,16384]{1,0:T(2,128)(2,1)S(1)}, bf16[2,16384]{1,0:T(2,128)(2,1)S(1)}, u32[]{:S(2)}, u32[]{:S(2)}) collective-permute-start(bf16[2,16384]{1,0:T(2,128)(2,1)S(1)} %collective-permute-done.1.refs_1_), channel_id=1, source_target_pairs={{0,2},{1,3},{2,0},{3,1},{4,6},{5,7},{6,4},{7,5},{8,10},{9,11},{10,... | collective-permute-start | bytes 196616 | tf_op jit(solution)/shard_map/ppermute | solution.py:432
  15.7 0.2 pack.2
  15.9 0.1 collective-permute-start.2
  16.0 2.4 %collective-permute-start.3 = (bf16[4,10240]{1,0:T(4,128)(2,1)S(1)}, bf16[4,10240]{1,0:T(4,128)(2,1)S(1)}, u32[]{:S(2)}, u32[]{:S(2)}) collective-permute-start(bf16[4,10240]{1,0:T(4,128)(2,1)S(1)} %get-tuple-element.33), channel_id=1, source_target_pairs={{0,17},{1,16},{2,19},{3,18},{4,21},{5,20},{6,23},{7,22},{8,25},{9,... | collective-permute-start | bytes 245768 | tf_op jit(solution)/shard_map/ppermute | solution.py:437
  18.4 0.3 collective-permute-start.4
  18.6 0.0 collective-permute-done.6.refs_0_
  18.6 0.0 collective-permute-done.7.refs_1_
  18.6 0.2 pack.3
  18.8 0.1 collective-permute-start.8
  19.0 2.3 %collective-permute-start.9 = (bf16[4,10240]{1,0:T(4,128)(2,1)S(1)}, bf16[4,10240]{1,0:T(4,128)(2,1)S(1)}, u32[]{:S(2)}, u32[]{:S(2)}) collective-permute-start(bf16[4,10240]{1,0:T(4,128)(2,1)S(1)} %get-tuple-element.39), channel_id=1, source_target_pairs={{0,17},{1,16},{2,19},{3,18},{4,21},{5,20},{6,23},{7,22},{8,25},{9,... | collective-permute-start | bytes 245768 | tf_op jit(solution)/shard_map/ppermute | solution.py:437
  21.3 0.0 collective-permute-done.2.refs_1_
  21.3 0.3 collective-permute-start.10
  21.5 0.0 collective-permute-done.3.refs_2_
  21.5 1.0 %collective-permute-done.4.refs_3_ = bf16[4,10240]{1,0:T(4,128)(2,1)S(1)} collective-permute-done((bf16[4,10240]{1,0:T(4,128)(2,1)S(1)}, bf16[4,10240]{1,0:T(4,128)(2,1)S(1)}, u32[]{:S(2)}, u32[]{:S(2)}) %collective-permute-start.4) | collective-permute-done | bytes 81952 | tf_op jit(solution)/shard_map/ppermute | solution.py:437
  22.5 0.1 join.2
  22.6 2.5 %collective-permute-start.5 = (bf16[16,6144]{1,0:T(8,128)(2,1)S(1)}, bf16[16,6144]{1,0:T(8,128)(2,1)S(1)}, u32[]{:S(2)}, u32[]{:S(2)}) collective-permute-start(bf16[16,6144]{1,0:T(8,128)(2,1)S(1)} %get-tuple-element.36), channel_id=1, source_target_pairs={{0,8},{8,0},{16,24},{24,16},{1,9},{9,1},{17,25},{25,17},{2,10},{10... | collective-permute-start | bytes 589832 | tf_op jit(solution)/shard_map/ppermute | solution.py:432
  25.1 0.0 collective-permute-done.8.refs_1_
  25.1 0.0 collective-permute-done.9.refs_2_
  25.1 0.3 collective-permute-done.10.refs_3_
  25.4 0.1 join.3
  25.5 2.5 %collective-permute-start.11 = (bf16[16,6144]{1,0:T(8,128)(2,1)S(1)}, bf16[16,6144]{1,0:T(8,128)(2,1)S(1)}, u32[]{:S(2)}, u32[]{:S(2)}) collective-permute-start(bf16[16,6144]{1,0:T(8,128)(2,1)S(1)} %get-tuple-element.42), channel_id=1, source_target_pairs={{0,8},{8,0},{16,24},{24,16},{1,9},{9,1},{17,25},{25,17},{2,10},{10... | collective-permute-start | bytes 589832 | tf_op jit(solution)/shard_map/ppermute | solution.py:432
  28.0 0.0 collective-permute-done.5.refs_1_
  28.0 1.1 %collective-permute-done.11.refs_3_ = bf16[16,6144]{1,0:T(8,128)(2,1)S(1)} collective-permute-done((bf16[16,6144]{1,0:T(8,128)(2,1)S(1)}, bf16[16,6144]{1,0:T(8,128)(2,1)S(1)}, u32[]{:S(2)}, u32[]{:S(2)}) %collective-permute-start.11) | collective-permute-done | bytes 196640 | tf_op jit(solution)/shard_map/ppermute | solution.py:432
  29.1 11.2 %outer.1 = f32[4096,2048]{1,0:T(8,128)} custom-call(bf16[16,6144]{1,0:T(8,128)(2,1)S(1)} %get-tuple-element.35.refs_0_, bf16[16,6144]{1,0:T(8,128)(2,1)S(1)} %collective-permute-done.5.refs_1_, bf16[16,6144]{1,0:T(8,128)(2,1)S(1)} %get-tuple-element.41.refs_2_, bf16[16,6144]{1,0:T(8,128)(2,1)S(1)} %collective-permute-done.11.refs_3_), custom_call_target="tpu_custom_call" | custom-call | flops 10000000000 | bytes 30000000 | tf_op jit(solution)/shard_map/outer/pallas_call | solution.py:393
  (2 shorter events, 0.0 us)
Async XLA Ops:
  0.0 5.8 %collective-permute-start = (bf16[1,48,2304]{2,1,0:T(8,128)(2,1)}, bf16[1,48,2304]{2,1,0:T(8,128)(2,1)S(1)}, u32[]{:S(2)}, u32[]{:S(2)}) collective-permute-start(bf16[1,48,2304]{2,1,0:T(8,128)(2,1)} %param.7), channel_id=1, source_target_pairs={{0,8},{8,16},{16,24},{24,0},{1,9},{9,17},{17,25},{25,1},{2,10},{10... | collective-permute-start | bytes 663560 | tf_op jit(solution)/shard_map/ppermute | solution.py:427
  3.8 0.9 %copy-start = (s32[3,8192]{1,0:T(4,128)S(1)}, s32[3,8192]{1,0:T(4,128)}, u32[]{:S(2)}) copy-start(s32[3,8192]{1,0:T(4,128)} %sphere_ref.1) | copy-start | bytes 294916
  8.9 6.2 %collective-permute-start.1 = (bf16[2,16384]{1,0:T(2,128)(2,1)S(1)}, bf16[2,16384]{1,0:T(2,128)(2,1)S(1)}, u32[]{:S(2)}, u32[]{:S(2)}) collective-permute-start(bf16[2,16384]{1,0:T(2,128)(2,1)S(1)} %get-tuple-element.30.refs_0_.value_ref), channel_id=1, source_target_pairs={{0,4},{1,5},{2,6},{3,7},{4,0},{5,1},{6,2},{7,3},{8,12},{9,13},{10,... | collective-permute-start | bytes 196616 | tf_op jit(solution)/shard_map/ppermute | solution.py:432
  12.6 6.0 %collective-permute-start.6 = (bf16[2,16384]{1,0:T(2,128)(2,1)S(1)}, bf16[2,16384]{1,0:T(2,128)(2,1)S(1)}, u32[]{:S(2)}, u32[]{:S(2)}) collective-permute-start(bf16[2,16384]{1,0:T(2,128)(2,1)S(1)} %copied.1), channel_id=1, source_target_pairs={{0,2},{1,3},{2,0},{3,1},{4,6},{5,7},{6,4},{7,5},{8,10},{9,11},{10,... | collective-permute-start | bytes 196616 | tf_op jit(solution)/shard_map/ppermute | solution.py:432
  15.1 3.5 %collective-permute-start.7 = (bf16[2,16384]{1,0:T(2,128)(2,1)S(1)}, bf16[2,16384]{1,0:T(2,128)(2,1)S(1)}, u32[]{:S(2)}, u32[]{:S(2)}) collective-permute-start(bf16[2,16384]{1,0:T(2,128)(2,1)S(1)} %collective-permute-done.1.refs_1_), channel_id=1, source_target_pairs={{0,2},{1,3},{2,0},{3,1},{4,6},{5,7},{6,4},{7,5},{8,10},{9,11},{10,... | collective-permute-start | bytes 196616 | tf_op jit(solution)/shard_map/ppermute | solution.py:432
  15.9 5.4 %collective-permute-start.2 = (bf16[4,10240]{1,0:T(4,128)(2,1)S(1)}, bf16[4,10240]{1,0:T(4,128)(2,1)S(1)}, u32[]{:S(2)}, u32[]{:S(2)}) collective-permute-start(bf16[4,10240]{1,0:T(4,128)(2,1)S(1)} %get-tuple-element.32), channel_id=1, source_target_pairs={{0,16},{1,17},{2,18},{3,19},{4,20},{5,21},{6,22},{7,23},{8,24},{9,... | collective-permute-start | bytes 245768 | tf_op jit(solution)/shard_map/ppermute | solution.py:437
  16.0 5.6 %collective-permute-start.3 = (bf16[4,10240]{1,0:T(4,128)(2,1)S(1)}, bf16[4,10240]{1,0:T(4,128)(2,1)S(1)}, u32[]{:S(2)}, u32[]{:S(2)}) collective-permute-start(bf16[4,10240]{1,0:T(4,128)(2,1)S(1)} %get-tuple-element.33), channel_id=1, source_target_pairs={{0,17},{1,16},{2,19},{3,18},{4,21},{5,20},{6,23},{7,22},{8,25},{9,... | collective-permute-start | bytes 245768 | tf_op jit(solution)/shard_map/ppermute | solution.py:437
  18.4 4.2 %collective-permute-start.4 = (bf16[4,10240]{1,0:T(4,128)(2,1)S(1)}, bf16[4,10240]{1,0:T(4,128)(2,1)S(1)}, u32[]{:S(2)}, u32[]{:S(2)}) collective-permute-start(bf16[4,10240]{1,0:T(4,128)(2,1)S(1)} %get-tuple-element.34), channel_id=1, source_target_pairs={{0,1},{1,0},{2,3},{3,2},{4,5},{5,4},{6,7},{7,6},{8,9},{9,8},{10,11... | collective-permute-start | bytes 245768 | tf_op jit(solution)/shard_map/ppermute | solution.py:437
  18.8 6.3 %collective-permute-start.8 = (bf16[4,10240]{1,0:T(4,128)(2,1)S(1)}, bf16[4,10240]{1,0:T(4,128)(2,1)S(1)}, u32[]{:S(2)}, u32[]{:S(2)}) collective-permute-start(bf16[4,10240]{1,0:T(4,128)(2,1)S(1)} %get-tuple-element.38), channel_id=1, source_target_pairs={{0,16},{1,17},{2,18},{3,19},{4,20},{5,21},{6,22},{7,23},{8,24},{9,... | collective-permute-start | bytes 245768 | tf_op jit(solution)/shard_map/ppermute | solution.py:437
  19.0 6.2 %collective-permute-start.9 = (bf16[4,10240]{1,0:T(4,128)(2,1)S(1)}, bf16[4,10240]{1,0:T(4,128)(2,1)S(1)}, u32[]{:S(2)}, u32[]{:S(2)}) collective-permute-start(bf16[4,10240]{1,0:T(4,128)(2,1)S(1)} %get-tuple-element.39), channel_id=1, source_target_pairs={{0,17},{1,16},{2,19},{3,18},{4,21},{5,20},{6,23},{7,22},{8,25},{9,... | collective-permute-start | bytes 245768 | tf_op jit(solution)/shard_map/ppermute | solution.py:437
  21.3 4.1 %collective-permute-start.10 = (bf16[4,10240]{1,0:T(4,128)(2,1)S(1)}, bf16[4,10240]{1,0:T(4,128)(2,1)S(1)}, u32[]{:S(2)}, u32[]{:S(2)}) collective-permute-start(bf16[4,10240]{1,0:T(4,128)(2,1)S(1)} %get-tuple-element.40), channel_id=1, source_target_pairs={{0,1},{1,0},{2,3},{3,2},{4,5},{5,4},{6,7},{7,6},{8,9},{9,8},{10,11... | collective-permute-start | bytes 245768 | tf_op jit(solution)/shard_map/ppermute | solution.py:437
  22.6 5.4 %collective-permute-start.5 = (bf16[16,6144]{1,0:T(8,128)(2,1)S(1)}, bf16[16,6144]{1,0:T(8,128)(2,1)S(1)}, u32[]{:S(2)}, u32[]{:S(2)}) collective-permute-start(bf16[16,6144]{1,0:T(8,128)(2,1)S(1)} %get-tuple-element.36), channel_id=1, source_target_pairs={{0,8},{8,0},{16,24},{24,16},{1,9},{9,1},{17,25},{25,17},{2,10},{10... | collective-permute-start | bytes 589832 | tf_op jit(solution)/shard_map/ppermute | solution.py:432
  25.5 3.6 %collective-permute-start.11 = (bf16[16,6144]{1,0:T(8,128)(2,1)S(1)}, bf16[16,6144]{1,0:T(8,128)(2,1)S(1)}, u32[]{:S(2)}, u32[]{:S(2)}) collective-permute-start(bf16[16,6144]{1,0:T(8,128)(2,1)S(1)} %get-tuple-element.42), channel_id=1, source_target_pairs={{0,8},{8,0},{16,24},{24,16},{1,9},{9,1},{17,25},{25,17},{2,10},{10... | collective-permute-start | bytes 589832 | tf_op jit(solution)/shard_map/ppermute | solution.py:432

commit v20 on v18

--- a/solution.py
+++ b/solution.py
@@ -270,7 +270,7 @@
         functools.partial(second_kernel, grid),
         out_shape=[
             jax.ShapeDtypeStruct((STEPS, 2 * half_count), jnp.bfloat16),
-            jax.ShapeDtypeStruct((1, *band_shape), jnp.int32),
+            jax.ShapeDtypeStruct((3, *band_shape), jnp.int32),
         ],
         in_specs=in_vmem(7),
         out_specs=in_vmem(2),
@@ -444,7 +444,9 @@
     plan = (rows, cols, entries // rows, entries // cols)
     occ_second = shifted(occ_orbitals, "row", 1)
     own, later = transform(cond_orbitals, occ_orbitals, occ_second, sphere_index, occ_band.shape)
-    levels = jnp.stack([cond_energy, occ_energy, (occ_band + later[0]).astype(jnp.float32)])
+    line = lax.broadcasted_iota(jnp.int32, (3, occ_band.shape[0]), 0)
+    bands = (occ_band + later).astype(jnp.float32)
+    levels = jnp.where(line == 0, cond_energy, jnp.where(line == 1, occ_energy, bands))
     targets = [(0, 0)] + [(turn, side) for side in (1, 0) for turn in range(rows - 2, -2, -2) if turn or side]
     targets.append(targets.pop(rows // 2))
 

time: 40.8 us -> 40.9 us (level)
  starting transfers between devices: 17.4 us -> 18 us
  other arithmetic: 2.49 us -> 1.92 us
    another operation x2 -> x0, other arithmetic: 1.34 us -> none  [on_device(): jnp.stack([cond_energy, occ_energy, (occ_band + later[0]).astype(jnp.floa...]
    select_n x0 -> x1, other arithmetic: none -> 0.76 us  [on_device(): jnp.where(line == 0, cond_energy, jnp.where(line == 1, occ_energy, bands))]
    ppermute x5, starting transfers between devices: 9.32 us -> 9.94 us  [turned(): return lax.ppermute(value, axis, [(i, i ^ turn) for i in range(devices)])]
  transfers between devices with their start and end apart: 12 -> 12, of which waited for: 6 -> 5; matrix products, arithmetic and copies ran while one was open for 6% -> 5% of each run, Pallas kernels for 4% -> 4%
where the time goes in v20:
time: 40.9 us; the launch traced here: 40.4 us
  starting transfers between devices  18 us (44%)
  Pallas kernels  15.9 us (39%)
  waiting for transfers between devices  3.58 us (9%)
  other arithmetic  1.92 us (5%)
  local copies, waits for them, and re-layouts  0.9 us (2%)
    pallas_call x1, Pallas kernels, outer(): pl.pallas_call(functools.partial(outer_kernel, row_width, block, slots),...  11.3 us
    ppermute x5, starting transfers between devices, turned(): return lax.ppermute(value, axis, [(i, i ^ turn) for i in range(devices)])  9.94 us
    ppermute x6, starting transfers between devices, sent_across(): return lax.ppermute(value, ('row', 'col'), moves)  5.42 us
    pallas_call x1, Pallas kernels, transform(): pl.pallas_call(functools.partial(second_kernel, grid), out_shape=[jax.Sha...  3.05 us
    ppermute x1, starting transfers between devices, shifted(): lax.ppermute(value, axis, [(i, (i + by) % devices) for i in range(devices)])  2.63 us
    ppermute x5, waiting for transfers between devices, turned(): return lax.ppermute(value, axis, [(i, i ^ turn) for i in range(devices)])  2.42 us
    select_n x1, other arithmetic, transform(): orbitals = jnp.where(which == 0, cond_orbitals, occ_orbitals)  1.15 us
    ppermute x6, waiting for transfers between devices, sent_across(): return lax.ppermute(value, ('row', 'col'), moves)  1.12 us
  transfers between devices with their start and end apart: 12, of which 5 were waited for; matrix products, arithmetic and copies ran while one was open for 5% of the time, Pallas kernels for 4%

profile of v20, /device:TPU:1, one launch (start us, length us, event | category | flops | bytes accessed | tf_op | source)
XLA Modules:
  0.0 40.4 jit_solution(7871694254133347275)
XLA Ops:
  0.0 2.6 %collective-permute-start = (bf16[1,48,2304]{2,1,0:T(8,128)(2,1)}, bf16[1,48,2304]{2,1,0:T(8,128)(2,1)S(1)}, u32[]{:S(2)}, u32[]{:S(2)}) collective-permute-start(bf16[1,48,2304]{2,1,0:T(8,128)(2,1)} %param.7), channel_id=1, source_target_pairs={{0,8},{8,16},{16,24},{24,0},{1,9},{9,17},{17,25},{25,1},{2,10},{10... | collective-permute-start | bytes 663560 | tf_op jit(solution)/shard_map/ppermute | solution.py:427
  2.6 1.2 %broadcast_select_fusion.orbitals_ref = bf16[2,48,2304]{2,1,0:T(8,128)(2,1)S(1)} fusion(pred[2]{0:T(512)(128)(4,1)S(1)} %iota_compare_fusion, bf16[48,2304]{1,0:T(8,128)(2,1)} %bitcast.3, bf16[48,2304]{1,0:T(8,128)(2,1)} %bitcast.2), kind=kLoop, calls=%fused_computation | loop fusion | flops 221184 | bytes 884738 | tf_op jit(solution)/shard_map/jit(_where)/select_n | solution.py:249
  3.8 0.0 copy-start
  3.8 0.9 %copy-done = s32[3,8192]{1,0:T(4,128)S(1)} copy-done((s32[3,8192]{1,0:T(4,128)S(1)}, s32[3,8192]{1,0:T(4,128)}, u32[]{:S(2)}) %copy-start) | copy-done | bytes 98328
  4.7 1.1 %first_pair.1 = (bf16[1,16384]{1,0:T(2,128)(2,1)S(1)}, s32[2,8192]{1,0:T(2,128)S(1)}, bf16[1616,128]{1,0:T(8,128)(2,1)S(1)}, f32[16,384]{1,0:T(8,128)S(1)}, bf16[240,256]{1,0:T(8,128)(2,1)S(1)}) custom-call(bf16[2,48,2304]{2,1,0:T(8,128)(2,1)S(1)} %broadcast_select_fusion.orbitals_ref, s32[3,8192]{1,0:T(4,128)S(1)} %copy-done), custom_call_target="tpu_custom_call" | custom-call | flops 2000000000 | bytes 2000000 | tf_op jit(solution)/shard_map/first_pair/pallas_call | solution.py:255
  5.8 0.0 collective-permute-done.occ_ref
  5.8 3.1 %second_pair.1 = (bf16[2,16384]{1,0:T(2,128)(2,1)S(1)}, s32[3,32]{1,0:T(4,128)S(1)}) custom-call(bf16[2,48,2304]{2,1,0:T(8,128)(2,1)S(1)} %broadcast_select_fusion.orbitals_ref, bf16[1,48,2304]{2,1,0:T(8,128)(2,1)S(1)} %collective-permute-done.occ_ref, bf16[1,16384]{1,0:T(2,128)(2,1)S(1)} %get-tuple-element.24.first_ref, ...), custom_call_target="tpu_custom_call" | custom-call | flops 2000000000 | bytes 2000000 | tf_op jit(solution)/shard_map/second_pair/pallas_call | solution.py:269
  8.9 2.4 %collective-permute-start.1 = (bf16[2,16384]{1,0:T(2,128)(2,1)S(1)}, bf16[2,16384]{1,0:T(2,128)(2,1)S(1)}, u32[]{:S(2)}, u32[]{:S(2)}) collective-permute-start(bf16[2,16384]{1,0:T(2,128)(2,1)S(1)} %get-tuple-element.30.refs_0_.value_ref), channel_id=1, source_target_pairs={{0,4},{1,5},{2,6},{3,7},{4,0},{5,1},{6,2},{7,3},{8,12},{9,13},{10,... | collective-permute-start | bytes 196616 | tf_op jit(solution)/shard_map/ppermute | solution.py:432
  11.3 0.8 %select_select_fusion.levels_ref.behind_ref = f32[3,32]{1,0:T(4,128)S(1)} fusion(s32[3,32]{1,0:T(4,128)S(1)} %get-tuple-element.29, s32[32]{0:T(128)} %param.10, f32[32]{0:T(128)} %param.9, f32[32]{0:T(128)} %param.8, pred[3]{0:T(512)(128)(4,1)S(1)} %get-tuple-element.43, pred[3]{0:T(512)(128)(4,1)S(1)} %get-tuple-element.44), kind=kLoop, calls=%fused_computation.1 | loop fusion | flops 384 | bytes 1158 | tf_op jit(solution)/shard_map/jit(_where)/select_n | solution.py:449
  12.0 1.4 %collective-permute-start.6 = (bf16[2,16384]{1,0:T(2,128)(2,1)S(1)}, bf16[2,16384]{1,0:T(2,128)(2,1)S(1)}, u32[]{:S(2)}, u32[]{:S(2)}) collective-permute-start(bf16[2,16384]{1,0:T(2,128)(2,1)S(1)} %copied.1), channel_id=1, source_target_pairs={{0,2},{1,3},{2,0},{3,1},{4,6},{5,7},{6,4},{7,5},{8,10},{9,11},{10,... | collective-permute-start | bytes 196616 | tf_op jit(solution)/shard_map/ppermute | solution.py:432
  13.4 1.3 %collective-permute-done.1.refs_1_ = bf16[2,16384]{1,0:T(2,128)(2,1)S(1)} collective-permute-done((bf16[2,16384]{1,0:T(2,128)(2,1)S(1)}, bf16[2,16384]{1,0:T(2,128)(2,1)S(1)}, u32[]{:S(2)}, u32[]{:S(2)}) %collective-permute-start.1) | collective-permute-done | bytes 65568 | tf_op jit(solution)/shard_map/ppermute | solution.py:432
  14.7 1.0 %collective-permute-start.7 = (bf16[2,16384]{1,0:T(2,128)(2,1)S(1)}, bf16[2,16384]{1,0:T(2,128)(2,1)S(1)}, u32[]{:S(2)}, u32[]{:S(2)}) collective-permute-start(bf16[2,16384]{1,0:T(2,128)(2,1)S(1)} %collective-permute-done.1.refs_1_), channel_id=1, source_target_pairs={{0,2},{1,3},{2,0},{3,1},{4,6},{5,7},{6,4},{7,5},{8,10},{9,11},{10,... | collective-permute-start | bytes 196616 | tf_op jit(solution)/shard_map/ppermute | solution.py:432
  15.7 0.2 pack.2
  15.9 0.1 collective-permute-start.2
  16.0 2.4 %collective-permute-start.3 = (bf16[4,10240]{1,0:T(4,128)(2,1)S(1)}, bf16[4,10240]{1,0:T(4,128)(2,1)S(1)}, u32[]{:S(2)}, u32[]{:S(2)}) collective-permute-start(bf16[4,10240]{1,0:T(4,128)(2,1)S(1)} %get-tuple-element.33), channel_id=1, source_target_pairs={{0,16},{1,17},{2,18},{3,19},{4,20},{5,21},{6,22},{7,23},{8,24},{9,... | collective-permute-start | bytes 245768 | tf_op jit(solution)/shard_map/ppermute | solution.py:437
  18.4 0.3 collective-permute-start.4
  18.7 0.0 collective-permute-done.6.refs_0_
  18.7 0.0 collective-permute-done.7.refs_1_
  18.7 0.2 pack.3
  18.9 1.0 %collective-permute-start.8 = (bf16[4,10240]{1,0:T(4,128)(2,1)S(1)}, bf16[4,10240]{1,0:T(4,128)(2,1)S(1)}, u32[]{:S(2)}, u32[]{:S(2)}) collective-permute-start(bf16[4,10240]{1,0:T(4,128)(2,1)S(1)} %get-tuple-element.38), channel_id=1, source_target_pairs={{0,17},{1,16},{2,19},{3,18},{4,21},{5,20},{6,23},{7,22},{8,25},{9,... | collective-permute-start | bytes 245768 | tf_op jit(solution)/shard_map/ppermute | solution.py:437
  19.9 1.5 %collective-permute-start.9 = (bf16[4,10240]{1,0:T(4,128)(2,1)S(1)}, bf16[4,10240]{1,0:T(4,128)(2,1)S(1)}, u32[]{:S(2)}, u32[]{:S(2)}) collective-permute-start(bf16[4,10240]{1,0:T(4,128)(2,1)S(1)} %get-tuple-element.39), channel_id=1, source_target_pairs={{0,16},{1,17},{2,18},{3,19},{4,20},{5,21},{6,22},{7,23},{8,24},{9,... | collective-permute-start | bytes 245768 | tf_op jit(solution)/shard_map/ppermute | solution.py:437
  21.3 0.0 collective-permute-done.2.refs_1_
  21.3 0.3 collective-permute-start.10
  21.6 0.3 collective-permute-done.3.refs_2_
  21.9 0.2 collective-permute-done.4.refs_3_
  22.1 0.1 join.2
  22.1 3.0 %collective-permute-start.5 = (bf16[16,6144]{1,0:T(8,128)(2,1)S(1)}, bf16[16,6144]{1,0:T(8,128)(2,1)S(1)}, u32[]{:S(2)}, u32[]{:S(2)}) collective-permute-start(bf16[16,6144]{1,0:T(8,128)(2,1)S(1)} %get-tuple-element.36), channel_id=1, source_target_pairs={{0,8},{8,0},{16,24},{24,16},{1,9},{9,1},{17,25},{25,17},{2,10},{10... | collective-permute-start | bytes 589832 | tf_op jit(solution)/shard_map/ppermute | solution.py:432
  25.1 0.0 collective-permute-done.8.refs_1_
  25.1 0.0 collective-permute-done.9.refs_2_
  25.1 0.6 %collective-permute-done.10.refs_3_ = bf16[4,10240]{1,0:T(4,128)(2,1)S(1)} collective-permute-done((bf16[4,10240]{1,0:T(4,128)(2,1)S(1)}, bf16[4,10240]{1,0:T(4,128)(2,1)S(1)}, u32[]{:S(2)}, u32[]{:S(2)}) %collective-permute-start.10) | collective-permute-done | bytes 81952 | tf_op jit(solution)/shard_map/ppermute | solution.py:437
  25.7 0.1 join.3
  25.8 2.2 %collective-permute-start.11 = (bf16[16,6144]{1,0:T(8,128)(2,1)S(1)}, bf16[16,6144]{1,0:T(8,128)(2,1)S(1)}, u32[]{:S(2)}, u32[]{:S(2)}) collective-permute-start(bf16[16,6144]{1,0:T(8,128)(2,1)S(1)} %get-tuple-element.42), channel_id=1, source_target_pairs={{0,8},{8,0},{16,24},{24,16},{1,9},{9,1},{17,25},{25,17},{2,10},{10... | collective-permute-start | bytes 589832 | tf_op jit(solution)/shard_map/ppermute | solution.py:432
  28.1 0.0 collective-permute-done.5.refs_1_
  28.1 1.1 %collective-permute-done.11.refs_3_ = bf16[16,6144]{1,0:T(8,128)(2,1)S(1)} collective-permute-done((bf16[16,6144]{1,0:T(8,128)(2,1)S(1)}, bf16[16,6144]{1,0:T(8,128)(2,1)S(1)}, u32[]{:S(2)}, u32[]{:S(2)}) %collective-permute-start.11) | collective-permute-done | bytes 196640 | tf_op jit(solution)/shard_map/ppermute | solution.py:432
  29.1 11.3 %outer.1 = f32[4096,2048]{1,0:T(8,128)} custom-call(bf16[16,6144]{1,0:T(8,128)(2,1)S(1)} %get-tuple-element.35.refs_0_, bf16[16,6144]{1,0:T(8,128)(2,1)S(1)} %collective-permute-done.5.refs_1_, bf16[16,6144]{1,0:T(8,128)(2,1)S(1)} %get-tuple-element.41.refs_2_, bf16[16,6144]{1,0:T(8,128)(2,1)S(1)} %collective-permute-done.11.refs_3_), custom_call_target="tpu_custom_call" | custom-call | flops 10000000000 | bytes 30000000 | tf_op jit(solution)/shard_map/outer/pallas_call | solution.py:393
  (3 shorter events, 0.0 us)
Async XLA Ops:
  0.0 5.8 %collective-permute-start = (bf16[1,48,2304]{2,1,0:T(8,128)(2,1)}, bf16[1,48,2304]{2,1,0:T(8,128)(2,1)S(1)}, u32[]{:S(2)}, u32[]{:S(2)}) collective-permute-start(bf16[1,48,2304]{2,1,0:T(8,128)(2,1)} %param.7), channel_id=1, source_target_pairs={{0,8},{8,16},{16,24},{24,0},{1,9},{9,17},{17,25},{25,1},{2,10},{10... | collective-permute-start | bytes 663560 | tf_op jit(solution)/shard_map/ppermute | solution.py:427
  3.8 0.9 %copy-start = (s32[3,8192]{1,0:T(4,128)S(1)}, s32[3,8192]{1,0:T(4,128)}, u32[]{:S(2)}) copy-start(s32[3,8192]{1,0:T(4,128)} %sphere_ref.1) | copy-start | bytes 294916
  8.9 5.9 %collective-permute-start.1 = (bf16[2,16384]{1,0:T(2,128)(2,1)S(1)}, bf16[2,16384]{1,0:T(2,128)(2,1)S(1)}, u32[]{:S(2)}, u32[]{:S(2)}) collective-permute-start(bf16[2,16384]{1,0:T(2,128)(2,1)S(1)} %get-tuple-element.30.refs_0_.value_ref), channel_id=1, source_target_pairs={{0,4},{1,5},{2,6},{3,7},{4,0},{5,1},{6,2},{7,3},{8,12},{9,13},{10,... | collective-permute-start | bytes 196616 | tf_op jit(solution)/shard_map/ppermute | solution.py:432
  12.0 6.6 %collective-permute-start.6 = (bf16[2,16384]{1,0:T(2,128)(2,1)S(1)}, bf16[2,16384]{1,0:T(2,128)(2,1)S(1)}, u32[]{:S(2)}, u32[]{:S(2)}) collective-permute-start(bf16[2,16384]{1,0:T(2,128)(2,1)S(1)} %copied.1), channel_id=1, source_target_pairs={{0,2},{1,3},{2,0},{3,1},{4,6},{5,7},{6,4},{7,5},{8,10},{9,11},{10,... | collective-permute-start | bytes 196616 | tf_op jit(solution)/shard_map/ppermute | solution.py:432
  14.7 3.9 %collective-permute-start.7 = (bf16[2,16384]{1,0:T(2,128)(2,1)S(1)}, bf16[2,16384]{1,0:T(2,128)(2,1)S(1)}, u32[]{:S(2)}, u32[]{:S(2)}) collective-permute-start(bf16[2,16384]{1,0:T(2,128)(2,1)S(1)} %collective-permute-done.1.refs_1_), channel_id=1, source_target_pairs={{0,2},{1,3},{2,0},{3,1},{4,6},{5,7},{6,4},{7,5},{8,10},{9,11},{10,... | collective-permute-start | bytes 196616 | tf_op jit(solution)/shard_map/ppermute | solution.py:432
  15.9 5.4 %collective-permute-start.2 = (bf16[4,10240]{1,0:T(4,128)(2,1)S(1)}, bf16[4,10240]{1,0:T(4,128)(2,1)S(1)}, u32[]{:S(2)}, u32[]{:S(2)}) collective-permute-start(bf16[4,10240]{1,0:T(4,128)(2,1)S(1)} %get-tuple-element.32), channel_id=1, source_target_pairs={{0,17},{1,16},{2,19},{3,18},{4,21},{5,20},{6,23},{7,22},{8,25},{9,... | collective-permute-start | bytes 245768 | tf_op jit(solution)/shard_map/ppermute | solution.py:437
  16.0 5.9 %collective-permute-start.3 = (bf16[4,10240]{1,0:T(4,128)(2,1)S(1)}, bf16[4,10240]{1,0:T(4,128)(2,1)S(1)}, u32[]{:S(2)}, u32[]{:S(2)}) collective-permute-start(bf16[4,10240]{1,0:T(4,128)(2,1)S(1)} %get-tuple-element.33), channel_id=1, source_target_pairs={{0,16},{1,17},{2,18},{3,19},{4,20},{5,21},{6,22},{7,23},{8,24},{9,... | collective-permute-start | bytes 245768 | tf_op jit(solution)/shard_map/ppermute | solution.py:437
  18.4 3.7 %collective-permute-start.4 = (bf16[4,10240]{1,0:T(4,128)(2,1)S(1)}, bf16[4,10240]{1,0:T(4,128)(2,1)S(1)}, u32[]{:S(2)}, u32[]{:S(2)}) collective-permute-start(bf16[4,10240]{1,0:T(4,128)(2,1)S(1)} %get-tuple-element.34), channel_id=1, source_target_pairs={{0,1},{1,0},{2,3},{3,2},{4,5},{5,4},{6,7},{7,6},{8,9},{9,8},{10,11... | collective-permute-start | bytes 245768 | tf_op jit(solution)/shard_map/ppermute | solution.py:437
  18.9 6.2 %collective-permute-start.8 = (bf16[4,10240]{1,0:T(4,128)(2,1)S(1)}, bf16[4,10240]{1,0:T(4,128)(2,1)S(1)}, u32[]{:S(2)}, u32[]{:S(2)}) collective-permute-start(bf16[4,10240]{1,0:T(4,128)(2,1)S(1)} %get-tuple-element.38), channel_id=1, source_target_pairs={{0,17},{1,16},{2,19},{3,18},{4,21},{5,20},{6,23},{7,22},{8,25},{9,... | collective-permute-start | bytes 245768 | tf_op jit(solution)/shard_map/ppermute | solution.py:437
  19.9 5.2 %collective-permute-start.9 = (bf16[4,10240]{1,0:T(4,128)(2,1)S(1)}, bf16[4,10240]{1,0:T(4,128)(2,1)S(1)}, u32[]{:S(2)}, u32[]{:S(2)}) collective-permute-start(bf16[4,10240]{1,0:T(4,128)(2,1)S(1)} %get-tuple-element.39), channel_id=1, source_target_pairs={{0,16},{1,17},{2,18},{3,19},{4,20},{5,21},{6,22},{7,23},{8,24},{9,... | collective-permute-start | bytes 245768 | tf_op jit(solution)/shard_map/ppermute | solution.py:437
  21.3 4.4 %collective-permute-start.10 = (bf16[4,10240]{1,0:T(4,128)(2,1)S(1)}, bf16[4,10240]{1,0:T(4,128)(2,1)S(1)}, u32[]{:S(2)}, u32[]{:S(2)}) collective-permute-start(bf16[4,10240]{1,0:T(4,128)(2,1)S(1)} %get-tuple-element.40), channel_id=1, source_target_pairs={{0,1},{1,0},{2,3},{3,2},{4,5},{5,4},{6,7},{7,6},{8,9},{9,8},{10,11... | collective-permute-start | bytes 245768 | tf_op jit(solution)/shard_map/ppermute | solution.py:437
  22.1 5.9 %collective-permute-start.5 = (bf16[16,6144]{1,0:T(8,128)(2,1)S(1)}, bf16[16,6144]{1,0:T(8,128)(2,1)S(1)}, u32[]{:S(2)}, u32[]{:S(2)}) collective-permute-start(bf16[16,6144]{1,0:T(8,128)(2,1)S(1)} %get-tuple-element.36), channel_id=1, source_target_pairs={{0,8},{8,0},{16,24},{24,16},{1,9},{9,1},{17,25},{25,17},{2,10},{10... | collective-permute-start | bytes 589832 | tf_op jit(solution)/shard_map/ppermute | solution.py:432
  25.8 3.3 %collective-permute-start.11 = (bf16[16,6144]{1,0:T(8,128)(2,1)S(1)}, bf16[16,6144]{1,0:T(8,128)(2,1)S(1)}, u32[]{:S(2)}, u32[]{:S(2)}) collective-permute-start(bf16[16,6144]{1,0:T(8,128)(2,1)S(1)} %get-tuple-element.42), channel_id=1, source_target_pairs={{0,8},{8,0},{16,24},{24,16},{1,9},{9,1},{17,25},{25,17},{2,10},{10... | collective-permute-start | bytes 589832 | tf_op jit(solution)/shard_map/ppermute | solution.py:432
